TPU v7x, 32 devices: a whole 2x2x4 slice. The times are simulated.
32 devices in a mesh: dp: 8 (over z, x), mp: 4 (over y, core).
Axes of the slice: x: 2, y: 2, z: 4, core: 2. Of those that a mesh axis runs over, the one named last changes fastest.
Arguments:
- tokens: bfloat16 [32, 197, 768], P(('dp', 'mp')), may hold values from -6 to 6
- keep_mask: int32 [32, 197], P(('dp', 'mp')), may hold values from 0 to 1, as said below
- cotangent: bfloat16 [32, 197, 768], P(('dp', 'mp')), may hold values from -6 to 6
- w_attn: float32 [16, 384, 384], P('mp', 'dp')
- w_fc1: float32 [16, 384, 384], P('mp', 'dp'), may hold values from -0.21875 to 0.21875
- w_fc2: float32 [16, 384, 384], P('mp', 'dp'), may hold values from -0.109375 to 0.109375
- vectors: float32 [13, 768], replicated, as said below
- left_attn: float32 [16, 384, 384], P('mp', 'dp'), as said below
- right_attn: float32 [16, 384, 384], P('mp', 'dp'), as said below
- root_left_attn: float32 [16, 384, 384], P('mp', 'dp'), as said below
- root_right_attn: float32 [16, 384, 384], P('mp', 'dp'), as said below
- left_fc1: float32 [16, 384, 384], P('mp', 'dp'), as said below
- right_fc1: float32 [16, 384, 384], P('mp', 'dp'), as said below
- root_left_fc1: float32 [16, 384, 384], P('mp', 'dp'), as said below
- root_right_fc1: float32 [16, 384, 384], P('mp', 'dp'), as said below
- left_fc2: float32 [16, 384, 384], P('mp', 'dp'), as said below
- right_fc2: float32 [16, 384, 384], P('mp', 'dp'), as said below
- root_left_fc2: float32 [16, 384, 384], P('mp', 'dp'), as said below
- root_right_fc2: float32 [16, 384, 384], P('mp', 'dp'), as said below
Outputs:
- block_out: bfloat16 [32, 197, 768], P(('dp', 'mp'))
- input_grad: float32 [32, 197, 768], P(('dp', 'mp'))
- grad_attn: float32 [16, 384, 384], P('mp', 'dp')
- grad_fc1: float32 [16, 384, 384], P('mp', 'dp')
- grad_fc2: float32 [16, 384, 384], P('mp', 'dp')
- new_left_attn: float32 [16, 384, 384], P('mp', 'dp')
- new_right_attn: float32 [16, 384, 384], P('mp', 'dp')
- new_left_fc1: float32 [16, 384, 384], P('mp', 'dp')
- new_right_fc1: float32 [16, 384, 384], P('mp', 'dp')
- new_left_fc2: float32 [16, 384, 384], P('mp', 'dp')
- new_right_fc2: float32 [16, 384, 384], P('mp', 'dp')
- new_attn: float32 [16, 384, 384], P('mp', 'dp')
- new_fc1: float32 [16, 384, 384], P('mp', 'dp')
- new_fc2: float32 [16, 384, 384], P('mp', 'dp')
- half_attn: bfloat16 [16, 384, 384], P('mp', 'dp')
- half_fc1: bfloat16 [16, 384, 384], P('mp', 'dp')
- half_fc2: bfloat16 [16, 384, 384], P('mp', 'dp')
- vector_grad: float32 [13, 768], replicated
- new_vectors: float32 [13, 768], replicated
Inputs may be any that keep to these rules, and one draw needn't show every extreme that they name: `keep_mask`: each image keeps at least a fifth of its 197 patches, rounded up, and at most 157; both counts occur in every draw. `vectors`: rows as listed in its meaning. `left_attn`: every block is symmetric. `right_attn`: every block is symmetric. `root_left_attn`: every block is symmetric. `root_right_attn`: every block is symmetric. `left_fc1`: every block is symmetric. `right_fc1`: every block is symmetric. `root_left_fc1`: every block is symmetric. `root_right_fc1`: every block is symmetric. `left_fc2`: every block is symmetric. `right_fc2`: every block is symmetric. `root_left_fc2`: every block is symmetric. `root_right_fc2`: every block is symmetric.
All inputs are finite; a program needn't handle non-finite values.
Results may differ from a plain program's by a relative error of at most 0.014.
Values may be sent and summed in bfloat16 or wider, within the bound.
No kernel may reach another device: no remote copies, remote signals or barrier semaphores. Data moves between devices by JAX's collectives and lax.ppermute only.
A program may use at most 128 MiB of HBM per device.

v0:
```python
import jax
import jax.numpy as jnp
from jax import lax
from jax.sharding import PartitionSpec as P

D = 768
HEADS = 12
FF = 3072
BLOCK_VEC = 128
KEPT_MOST = 157


highest = lax.Precision.HIGHEST
masked_score = -1e30


def to_half(values):
    return values.astype(jnp.bfloat16)


def layer_norm(values, gain_row, shift_row):
    centered = values - jnp.mean(values, axis=-1, keepdims=True)
    variance = jnp.mean(centered * centered, axis=-1, keepdims=True)
    return centered * lax.rsqrt(variance + 1e-06) * gain_row + shift_row


def exact_gelu(values):
    return jax.nn.gelu(values, approximate=False)


def row_product(left_half, right_half):
    return lax.dot_general(
        left_half, right_half, (((0,), (0,)), ((), ())), preferred_element_type=jnp.float32
    )


def times_transpose(left_half, right_half):
    return lax.dot_general(
        left_half, right_half, (((1,), (1,)), ((), ())), preferred_element_type=jnp.float32
    )


def cols_whole(blocks, row_blocks):
    block_count, block_order, _ = blocks.shape
    col_blocks = block_count // row_blocks
    return (
        blocks.reshape(col_blocks, row_blocks, block_order, block_order)
        .transpose(1, 2, 0, 3)
        .reshape(row_blocks * block_order, col_blocks * block_order)
    )


def rows_whole(blocks, col_blocks):
    block_count, block_order, _ = blocks.shape
    row_blocks = block_count // col_blocks
    return (
        blocks.reshape(row_blocks, col_blocks, block_order, block_order)
        .transpose(0, 2, 1, 3)
        .reshape(row_blocks * block_order, col_blocks * block_order)
    )


def blocks_of_cols(matrix, row_blocks, block_order):
    row_total, col_total = matrix.shape
    col_blocks = col_total // block_order
    return (
        matrix.reshape(row_blocks, block_order, col_blocks, block_order)
        .transpose(2, 0, 1, 3)
        .reshape(col_blocks * row_blocks, block_order, block_order)
    )


def blocks_of_rows(matrix, col_blocks, block_order):
    row_total, col_total = matrix.shape
    row_blocks = row_total // block_order
    return (
        matrix.reshape(row_blocks, block_order, col_blocks, block_order)
        .transpose(0, 2, 1, 3)
        .reshape(row_blocks * col_blocks, block_order, block_order)
    )


def from_devices(device_stack, data_count, model_count):
    total_devices, local_blocks, piece_rows, block_order = device_stack.shape
    return (
        device_stack.reshape(data_count, model_count, local_blocks, piece_rows, block_order)
        .transpose(1, 2, 0, 3, 4)
        .reshape(model_count * local_blocks, data_count * piece_rows, block_order)
    )


def to_devices(blocks, data_count, model_count):
    block_count, block_order, _ = blocks.shape
    local_blocks = block_count // model_count
    piece_rows = block_order // data_count
    return (
        blocks.reshape(model_count, local_blocks, data_count, piece_rows, block_order)
        .transpose(2, 0, 1, 3, 4)
        .reshape(data_count * model_count, local_blocks, piece_rows, block_order)
    )


def masked_scores(queries, key_part, allowed):
    scale_factor = queries.shape[-1] ** (-0.5)
    scores = (
        jnp.einsum("qhd,khd->hqk", queries, key_part, preferred_element_type=jnp.float32)
        * scale_factor
    )
    return (jnp.where(allowed[None, None, :] > 0, scores, masked_score), scale_factor)


def attend(queries, key_part, values, allowed):
    scores, scale_factor = masked_scores(queries, key_part, allowed)
    highest_score = jnp.max(scores, axis=-1, keepdims=True)
    exp_total = jnp.sum(jnp.exp(scores - highest_score), axis=-1, keepdims=True)
    log_total = highest_score + jnp.log(exp_total)
    weights = to_half(jnp.exp(scores - log_total))
    attended = jnp.einsum("hqk,khd->qhd", weights, values, preferred_element_type=jnp.float32)
    return (to_half(attended), log_total)


def attend_back(queries, key_part, values, allowed, log_total, grad_attended):
    scores, scale_factor = masked_scores(queries, key_part, allowed)
    probs = jnp.exp(scores - log_total)
    grad_values = jnp.einsum(
        "hqk,qhd->khd", to_half(probs), grad_attended, preferred_element_type=jnp.float32
    )
    grad_probs = jnp.einsum(
        "qhd,khd->hqk", grad_attended, values, preferred_element_type=jnp.float32
    )
    row_inner = jnp.sum(probs * grad_probs, axis=-1, keepdims=True)
    grad_scores = to_half(probs * (grad_probs - row_inner))
    grad_queries = (
        jnp.einsum("hqk,khd->qhd", grad_scores, key_part, preferred_element_type=jnp.float32)
        * scale_factor
    )
    grad_keys = (
        jnp.einsum("hqk,qhd->khd", grad_scores, queries, preferred_element_type=jnp.float32)
        * scale_factor
    )
    return jnp.stack([grad_queries, grad_keys, grad_values], axis=1)


def shampoo_rows(
    grad_rows, grad_whole, left_stat, right_stat, left_root, right_root_whole, row_offset
):
    new_left = 0.95 * left_stat + 0.05 * jnp.einsum(
        "bij,bkj->bik", grad_rows, grad_whole, precision=highest
    )
    grad_cols = lax.dynamic_slice_in_dim(grad_whole, row_offset, grad_rows.shape[1], 2)
    new_right = 0.95 * right_stat + 0.05 * jnp.einsum(
        "bji,bjk->bik", grad_cols, grad_whole, precision=highest
    )
    step_rows = jnp.einsum("bij,bjk->bik", left_root, grad_whole, precision=highest)
    step_rows = jnp.einsum("bij,bjk->bik", step_rows, right_root_whole, precision=highest)
    return (new_left, new_right, step_rows, jnp.sum(step_rows * step_rows, axis=(1, 2)))


def apply_step(weight, step_rows, square_total, step_rates):
    block_order = weight.shape[2]
    update_scale = lax.rsqrt(square_total / (block_order * block_order) + 1e-06)
    return weight - step_rates[:, None, None] * step_rows * update_scale[:, None, None]


def body(
    tokens,
    keep_mask,
    cotangent,
    w_attn,
    w_fc1,
    w_fc2,
    vectors,
    left_attn,
    right_attn,
    root_left_attn,
    root_right_attn,
    left_fc1,
    right_fc1,
    root_left_fc1,
    root_right_fc1,
    left_fc2,
    right_fc2,
    root_left_fc2,
    root_right_fc2,
):
    data_count = lax.axis_size("dp")
    model_count = lax.axis_size("mp")
    image_count, patch_count, width = tokens.shape
    row_count = image_count * patch_count
    block_order = w_attn.shape[2]
    piece_rows = w_attn.shape[1]
    row_blocks = width // block_order
    attn_stack = lax.all_gather(to_half(w_attn)[None], ("dp", "mp"), axis=0, tiled=True)
    fc1_blocks, fc2_blocks = (
        lax.all_gather(to_half(w_fc1), "dp", axis=1, tiled=True),
        lax.all_gather(to_half(w_fc2), "dp", axis=1, tiled=True),
    )
    fc1_used = cols_whole(fc1_blocks, row_blocks)
    fc2_used = rows_whole(fc2_blocks, row_blocks)
    attn_used = cols_whole(from_devices(attn_stack, data_count, model_count), row_blocks)
    qkv_full = attn_used[:, : 3 * width]
    out_full = attn_used[:, 3 * width :]
    hidden_local = fc1_used.shape[1]
    flat = tokens.reshape(row_count, width).astype(jnp.float32)
    keep_rows = keep_mask.reshape(row_count).astype(jnp.float32)
    row_gate = jax.nn.sigmoid(jnp.dot(flat, vectors[8], precision=highest))
    normed, first_norm_back = jax.vjp(layer_norm, flat, vectors[0], vectors[1])
    normed_half = to_half(normed)
    qkv_bias = jnp.concatenate([vectors[4], jnp.zeros_like(vectors[4]), vectors[5]])
    mixed_half = to_half(
        jnp.dot(normed_half, qkv_full, preferred_element_type=jnp.float32) + qkv_bias
    )
    heads_view = mixed_half.reshape(image_count, patch_count, 3, HEADS, width // HEADS)
    queries = heads_view[:, :, 0]
    key_part = heads_view[:, :, 1]
    values = heads_view[:, :, 2]
    attended_half, log_totals = lax.map(
        lambda members: attend(*members), (queries, key_part, values, keep_mask)
    )
    attended_flat = attended_half.reshape(row_count, width)
    branch = jnp.dot(attended_flat, out_full, preferred_element_type=jnp.float32) + vectors[6]
    middle = flat + branch
    normed_two, second_norm_back = jax.vjp(layer_norm, middle, vectors[2], vectors[3])
    normed_two_half = to_half(normed_two)
    up_bias = vectors[9:].reshape(-1)
    picked_rows = jax.vmap(lambda mask_row: jnp.nonzero(mask_row, size=KEPT_MOST, fill_value=0)[0])(
        keep_mask
    )
    image_base = lax.broadcasted_iota(jnp.int32, (image_count, 1), 0)
    gather_index = (picked_rows.astype(jnp.int32) + image_base * patch_count).reshape(-1)
    slot_index = (
        jnp.maximum(jnp.cumsum(keep_mask, axis=1) - 1, 0) + image_base * KEPT_MOST
    ).reshape(-1)
    kept_counts = jnp.sum(keep_mask, axis=1, keepdims=True)
    slot_live = (
        lax.broadcasted_iota(jnp.int32, (image_count, KEPT_MOST), 1) < kept_counts
    ).reshape(-1)
    mlp_rows = jnp.take(normed_two_half, gather_index, axis=0)
    mlp_count = mlp_rows.shape[0]
    group_rows = lax.all_gather(mlp_rows, "mp", axis=0, tiled=True)
    offset = lax.axis_index("mp") * hidden_local
    local_bias = lax.dynamic_slice_in_dim(up_bias, offset, hidden_local)
    hidden = jnp.dot(group_rows, fc1_used, preferred_element_type=jnp.float32) + local_bias
    activated = to_half(exact_gelu(hidden))
    row_piece = lax.slice_in_dim(activated, 0, mlp_count * lax.axis_size("mp"), axis=0)
    feed_rows = lax.psum_scatter(
        jnp.dot(row_piece, fc2_used, preferred_element_type=jnp.float32).astype(jnp.bfloat16),
        "mp",
        scatter_dimension=0,
        tiled=True,
    ).astype(jnp.float32)
    feed = jnp.take(feed_rows, slot_index, axis=0) + vectors[7]
    change = branch + feed
    row_scale = keep_rows * row_gate
    block_out = to_half(flat + row_scale[:, None] * change).reshape(tokens.shape)
    grad_output = cotangent.reshape(row_count, width).astype(jnp.float32)
    grad_change = row_scale[:, None] * grad_output
    grad_logit = keep_rows * row_gate * (1.0 - row_gate) * jnp.sum(grad_output * change, axis=-1)
    grad_feed = to_half(grad_change)
    grad_sent = jnp.where(
        slot_live[:, None], jnp.take(grad_feed, gather_index, axis=0), jnp.zeros((), jnp.bfloat16)
    )
    group_grads = lax.all_gather(grad_sent, "mp", axis=0, tiled=True)
    grad_active = times_transpose(group_grads, fc2_used)
    grad_hidden = to_half(jax.vjp(exact_gelu, hidden)[1](grad_active)[0])
    grad_fc2_part = row_product(activated, group_grads)
    grad_fc1_part = row_product(group_rows, grad_hidden)
    up_part = jnp.sum(grad_hidden, axis=0, dtype=jnp.float32)
    up_bias_grad = lax.dynamic_update_slice_in_dim(jnp.zeros_like(up_bias), up_part, offset, 0)
    row_piece = lax.slice_in_dim(grad_hidden, 0, mlp_count * lax.axis_size("mp"), axis=0)
    grad_rows_back = lax.psum_scatter(
        times_transpose(row_piece, fc1_used).astype(jnp.bfloat16),
        "mp",
        scatter_dimension=0,
        tiled=True,
    ).astype(jnp.float32)
    fc1_owned, fc2_owned = (
        lax.psum_scatter(
            blocks_of_cols(grad_fc1_part, row_blocks, block_order).astype(jnp.bfloat16),
            "dp",
            scatter_dimension=1,
            tiled=True,
        ).astype(jnp.float32),
        lax.psum_scatter(
            blocks_of_rows(grad_fc2_part, row_blocks, block_order).astype(jnp.bfloat16),
            "dp",
            scatter_dimension=1,
            tiled=True,
        ).astype(jnp.float32),
    )
    grad_normed_two = jnp.take(grad_rows_back, slot_index, axis=0) * keep_rows[:, None]
    grad_middle, grad_gain_two, grad_shift_two = second_norm_back(grad_normed_two)
    grad_branch = to_half(grad_change + grad_middle)
    grad_attended = to_half(times_transpose(grad_branch, out_full))
    grad_out_full = row_product(attended_flat, grad_branch)
    grad_heads = lax.map(
        lambda members: attend_back(*members),
        (
            queries,
            key_part,
            values,
            keep_mask,
            log_totals,
            grad_attended.reshape(image_count, patch_count, HEADS, -1),
        ),
    )
    grad_mixed = to_half(grad_heads.reshape(row_count, 3 * width))
    grad_qkv_full = row_product(normed_half, grad_mixed)
    grad_normed = times_transpose(grad_mixed, qkv_full)
    grad_flat, grad_gain_one, grad_shift_one = first_norm_back(grad_normed)
    input_grad = (grad_output + grad_middle + grad_flat + grad_logit[:, None] * vectors[8]).reshape(
        tokens.shape
    )
    mixed_sums = jnp.sum(grad_mixed, axis=0, dtype=jnp.float32)
    vector_rows = jnp.stack(
        [
            grad_gain_one,
            grad_shift_one,
            grad_gain_two,
            grad_shift_two,
            mixed_sums[:width],
            mixed_sums[2 * width :],
            jnp.sum(grad_branch, axis=0, dtype=jnp.float32),
            jnp.sum(grad_feed, axis=0, dtype=jnp.float32),
            jnp.dot(grad_logit, flat, precision=highest),
        ]
    )
    vector_part = jnp.concatenate([vector_rows, up_bias_grad.reshape(-1, width)], axis=0)
    attn_blocks_grad = blocks_of_cols(
        jnp.concatenate([grad_qkv_full, grad_out_full], axis=1), row_blocks, block_order
    )
    attn_owned = lax.psum_scatter(
        to_devices(attn_blocks_grad, data_count, model_count),
        ("dp", "mp"),
        scatter_dimension=0,
        tiled=True,
    )[0]
    vector_grad = lax.psum(vector_part, ("dp", "mp"))
    attn_whole, fc1_whole, fc2_whole, right_root_attn, right_root_fc1, right_root_fc2 = (
        lax.all_gather(attn_owned.astype(jnp.bfloat16), "dp", axis=1, tiled=True).astype(
            attn_owned.dtype
        ),
        lax.all_gather(fc1_owned.astype(jnp.bfloat16), "dp", axis=1, tiled=True).astype(
            fc1_owned.dtype
        ),
        lax.all_gather(fc2_owned.astype(jnp.bfloat16), "dp", axis=1, tiled=True).astype(
            fc2_owned.dtype
        ),
        lax.all_gather(root_right_attn.astype(jnp.bfloat16), "dp", axis=1, tiled=True).astype(
            root_right_attn.dtype
        ),
        lax.all_gather(root_right_fc1.astype(jnp.bfloat16), "dp", axis=1, tiled=True).astype(
            root_right_fc1.dtype
        ),
        lax.all_gather(root_right_fc2.astype(jnp.bfloat16), "dp", axis=1, tiled=True).astype(
            root_right_fc2.dtype
        ),
    )
    row_offset = lax.axis_index("dp") * piece_rows
    new_left_attn, new_right_attn, step_attn, square_attn = shampoo_rows(
        attn_owned, attn_whole, left_attn, right_attn, root_left_attn, right_root_attn, row_offset
    )
    new_left_fc1, new_right_fc1, step_fc1, square_fc1 = shampoo_rows(
        fc1_owned, fc1_whole, left_fc1, right_fc1, root_left_fc1, right_root_fc1, row_offset
    )
    new_left_fc2, new_right_fc2, step_fc2, square_fc2 = shampoo_rows(
        fc2_owned, fc2_whole, left_fc2, right_fc2, root_left_fc2, right_root_fc2, row_offset
    )
    total_attn, total_fc1, total_fc2 = lax.psum((square_attn, square_fc1, square_fc2), "dp")
    attn_local = w_attn.shape[0]
    block_index = lax.axis_index("mp") * attn_local + lax.broadcasted_iota(
        jnp.int32, (attn_local,), 0
    )
    attn_rates = jnp.where(
        block_index // row_blocks < 3 * row_blocks, 0.5 * D ** (-0.5), 0.5 * (D // 16) ** (-0.5)
    )
    fc1_rates = jnp.full((w_fc1.shape[0],), 0.5 * D ** (-0.5), jnp.float32)
    fc2_rates = jnp.full((w_fc2.shape[0],), 0.5 * FF ** (-0.5), jnp.float32)
    new_attn = apply_step(w_attn, step_attn, total_attn, attn_rates)
    new_fc1 = apply_step(w_fc1, step_fc1, total_fc1, fc1_rates)
    new_fc2 = apply_step(w_fc2, step_fc2, total_fc2, fc2_rates)
    vector_blocks = vector_grad.reshape(vector_grad.shape[0], -1, BLOCK_VEC)
    block_scale = lax.rsqrt(jnp.mean(vector_blocks * vector_blocks, axis=-1, keepdims=True) + 1e-06)
    new_vectors = vectors - 0.05 * (vector_blocks * block_scale).reshape(vectors.shape)
    return (
        block_out,
        input_grad,
        attn_owned,
        fc1_owned,
        fc2_owned,
        new_left_attn,
        new_right_attn,
        new_left_fc1,
        new_right_fc1,
        new_left_fc2,
        new_right_fc2,
        new_attn,
        new_fc1,
        new_fc2,
        to_half(new_attn),
        to_half(new_fc1),
        to_half(new_fc2),
        vector_grad,
        new_vectors,
    )


def solution(mesh):
    placed = (
        P(("dp", "mp"), None, None),
        P(("dp", "mp"), None),
        P(("dp", "mp"), None, None),
        P("mp", "dp", None),
        P("mp", "dp", None),
        P("mp", "dp", None),
        P(),
        P("mp", "dp", None),
        P("mp", "dp", None),
        P("mp", "dp", None),
        P("mp", "dp", None),
        P("mp", "dp", None),
        P("mp", "dp", None),
        P("mp", "dp", None),
        P("mp", "dp", None),
        P("mp", "dp", None),
        P("mp", "dp", None),
        P("mp", "dp", None),
        P("mp", "dp", None),
    )
    return jax.shard_map(
        body,
        mesh=mesh,
        in_specs=placed,
        out_specs=(
            P(("dp", "mp"), None, None),
            P(("dp", "mp"), None, None),
            P("mp", "dp", None),
            P("mp", "dp", None),
            P("mp", "dp", None),
            P("mp", "dp", None),
            P("mp", "dp", None),
            P("mp", "dp", None),
            P("mp", "dp", None),
            P("mp", "dp", None),
            P("mp", "dp", None),
            P("mp", "dp", None),
            P("mp", "dp", None),
            P("mp", "dp", None),
            P("mp", "dp", None),
            P("mp", "dp", None),
            P("mp", "dp", None),
            P(),
            P(),
        ),
        check_vma=False,
    )
```

profile of v0, /device:TPU:0, one launch (start us, length us, event | category | flops | bytes accessed | tf_op | source)
XLA Modules:
  0.0 783.7 jit_solution(17085322839996233641)
XLA Ops:
  23.7 31.0 %all-gather.13.cloned.1.call-done = bf16[4,384,384]{2,1,0:T(8,128)(2,1)} async-done(((bf16[4,48,384]{2,1,0:T(8,128)(2,1)}), bf16[4,384,384]{2,1,0:T(8,128)(2,1)}) %all-gather.13.cloned.1.call-update) | async-done | bytes 1179664 | tf_op jit(solution)/shard_map/all_gather | solution.py:195
  54.7 2.5 copy.95
  58.6 39.0 %all-gather.15.cloned.1.call-done = bf16[4,384,384]{2,1,0:T(8,128)(2,1)} async-done(((bf16[4,48,384]{2,1,0:T(8,128)(2,1)}), bf16[4,384,384]{2,1,0:T(8,128)(2,1)}) %all-gather.15.cloned.1.call-update) | async-done | bytes 1179664 | tf_op jit(solution)/shard_map/all_gather | solution.py:196
  97.5 2.5 copy.96
  101.3 62.1 %all-gather.29.cloned.1.call-done = bf16[128,48,384]{2,1,0:T(8,128)(2,1)} async-done(((bf16[4,48,384]{2,1,0:T(8,128)(2,1)}), bf16[128,48,384]{2,1,0:T(8,128)(2,1)}) %all-gather.29.cloned.1.call-update) | async-done | bytes 4718608 | tf_op jit(solution)/shard_map/all_gather | solution.py:193
  163.5 3.0 copy.91
  166.5 2.8 copy.92
  170.5 2.1 copy-done.10
  172.6 2.0 fusion.2
  178.5 2.8 fusion.97
  182.8 9.7 %all-gather.1 = bf16[4,157,768]{2,1,0:T(8,128)(2,1)S(1)} all-gather(bf16[1,157,768]{2,1,0:T(8,128)(2,1)S(1)} %get-tuple-element.193), channel_id=1, replica_groups=mesh['dp'=8,'mp'=4] {'mp'}, dimensions={0}, use_global_device_ids=true | all-gather | bytes 1205760 | tf_op jit(solution)/shard_map/all_gather | solution.py:240
  193.7 9.8 %all-gather.2 = bf16[4,157,768]{2,1,0:T(8,128)(2,1)S(1)} all-gather(bf16[1,157,768]{2,1,0:T(8,128)(2,1)S(1)} %get-tuple-element.194), channel_id=1, replica_groups=mesh['dp'=8,'mp'=4] {'mp'}, dimensions={0}, use_global_device_ids=true | all-gather | bytes 1205760 | tf_op jit(solution)/shard_map/all_gather | solution.py:263
  204.7 2.6 fusion.99
  207.4 6.3 convert_reduce_fusion.1
  214.6 2.2 convolution_convert_fusion.1
  216.8 2.8 convert_element_type.215
  222.1 3.6 convolution_convert_fusion.2
  229.1 21.6 %fusion.89 = (bf16[160,768]{1,0:T(8,128)(2,1)S(1)}, bf16[160,768]{1,0:T(8,128)(2,1)S(1)}) fusion(bf16[628,768]{1,0:T(8,128)(2,1)} %convolution_convert_fusion.3, bf16[628,768]{1,0:T(8,128)(2,1)} %convolution_convert_fusion.2), kind=kCustom, calls=%all-reduce-scatter.2 | all-reduce-scatter fusion | flops 983041 | bytes 2421248
  252.1 3.4 convolution_convert_fusion
  255.5 2.8 convert_element_type.220
  259.5 4.1 collective-permute-start.1
  264.4 9.1 %concatenate.18 = bf16[169,768]{1,0:T(8,128)(2,1)S(1)} concatenate(bf16[9,768]{1,0:T(8,128)(2,1)S(1)} %collective-permute-done.1, bf16[160,768]{1,0:T(8,128)(2,1)S(1)} %get-tuple-element.167), dimensions={0} | concatenate | bytes 519168
  276.3 2.5 multiply_reduce_fusion.1
  281.0 2.6 convolution_convert_fusion.5
  284.7 2.0 multiply_reduce_fusion
  291.7 4.2 fusion.51
  295.9 8.0 %pad_maximum_fusion = f32[768,3072]{1,0:T(8,128)} fusion(f32[768,768]{1,0:T(8,128)S(1)} %fusion.100, f32[768,2304]{1,0:T(8,128)} %fusion.51), kind=kLoop, calls=%fused_computation.5 | loop fusion | flops 2359296 | bytes 18874368 | tf_op jit(solution)/shard_map/concatenate | solution.py:330
  303.9 6.0 copy.121
  309.9 2.0 copy.102
  311.9 4.9 copy.103
  317.7 32.4 %reduce-scatter.12.cloned.1.call-done = bf16[4,48,384]{2,1,0:T(8,128)(2,1)} async-done(((bf16[4,384,384]{2,1,0:T(8,128)(2,1)}), bf16[4,48,384]{2,1,0:T(8,128)(2,1)}) %reduce-scatter.12.cloned.1.call-update) | async-done | bytes 147472 | tf_op jit(solution)/shard_map/reduce_scatter | solution.py:284
  351.7 139.5 %reduce-scatter.8.cloned.1.call-done = f32[1,4,48,384]{3,2,1,0:T(8,128)} async-done(((f32[32,4,48,384]{3,2,1,0:T(8,128)}), f32[1,4,48,384]{3,2,1,0:T(8,128)}) %reduce-scatter.8.cloned.1.call-update) | async-done | bytes 294928 | tf_op jit(solution)/shard_map/reduce_scatter | solution.py:332
  494.1 3.5 fusion.87
  500.3 40.5 %psum.31 = f32[13,768]{1,0:T(8,128)S(1)} all-reduce(f32[13,768]{1,0:T(8,128)S(1)} %concatenate.15), channel_id=1, replica_groups=mesh['dp'=8,'mp'=4] {'dp','mp'}, use_global_device_ids=true, to_apply=%region_40.43 | all-reduce | flops 9984 | bytes 79872 | tf_op jit(solution)/shard_map/psum | solution.py:338
  543.2 2.7 fusion.102
  547.2 29.0 %all-gather.21.cloned.1.call-done = bf16[4,384,384]{2,1,0:T(8,128)(2,1)} async-done(((bf16[4,48,384]{2,1,0:T(8,128)(2,1)}), bf16[4,384,384]{2,1,0:T(8,128)(2,1)}) %all-gather.21.cloned.1.call-update) | async-done | bytes 1179664 | tf_op jit(solution)/shard_map/all_gather | solution.py:346
  576.2 2.9 fusion.16
  580.5 38.7 %all-gather.25.cloned.1.call-done = bf16[4,384,384]{2,1,0:T(8,128)(2,1)} async-done(((bf16[4,48,384]{2,1,0:T(8,128)(2,1)}), bf16[4,384,384]{2,1,0:T(8,128)(2,1)}) %all-gather.25.cloned.1.call-update) | async-done | bytes 1179664 | tf_op jit(solution)/shard_map/all_gather | solution.py:352
  619.3 2.1 multiply_reduce_fusion.5
  621.4 40.8 %all-gather.27.cloned.1.call-done = bf16[4,384,384]{2,1,0:T(8,128)(2,1)} async-done(((bf16[4,48,384]{2,1,0:T(8,128)(2,1)}), bf16[4,384,384]{2,1,0:T(8,128)(2,1)}) %all-gather.27.cloned.1.call-update) | async-done | bytes 1179664 | tf_op jit(solution)/shard_map/all_gather | solution.py:355
  662.2 2.8 multiply_reduce_fusion.4
  665.0 2.2 fusion.21
  668.4 36.9 %all-gather.17.cloned.1.call-done = bf16[4,384,384]{2,1,0:T(8,128)(2,1)} async-done(((bf16[4,48,384]{2,1,0:T(8,128)(2,1)}), bf16[4,384,384]{2,1,0:T(8,128)(2,1)}) %all-gather.17.cloned.1.call-update) | async-done | bytes 1179664 | tf_op jit(solution)/shard_map/all_gather | solution.py:340
  707.2 41.0 %all-gather.23.cloned.1.call-done = bf16[4,384,384]{2,1,0:T(8,128)(2,1)} async-done(((bf16[4,48,384]{2,1,0:T(8,128)(2,1)}), bf16[4,384,384]{2,1,0:T(8,128)(2,1)}) %all-gather.23.cloned.1.call-update) | async-done | bytes 1179664 | tf_op jit(solution)/shard_map/all_gather | solution.py:349
  748.2 2.0 multiply_reduce_fusion.6
  750.2 19.4 %all-reduce.8 = (f32[4]{0:T(128)S(1)}, f32[4]{0:T(128)S(1)}, f32[4]{0:T(128)S(1)}) all-reduce(f32[4]{0:T(128)S(1)} %get-tuple-element.201, f32[4]{0:T(128)S(1)} %get-tuple-element.203, f32[4]{0:T(128)S(1)} %get-tuple-element.205), channel_id=1, replica_groups=mesh['dp'=8,'mp'=4] {'dp'}, use_global_device_ids=true, to_apply=%region_27.30 | all-reduce | flops 12 | bytes 96 | tf_op jit(solution)/shard_map/psum | solution.py:369
  772.2 2.2 fusion.18
  774.5 2.0 fusion.19
  (262 shorter events, 66.9 us)
Async XLA Ops:
  7.2 536.0 %copy-start = (f32[4,48,384]{2,1,0:T(8,128)S(1)}, f32[4,48,384]{2,1,0:T(8,128)}, u32[]{:S(2)}) copy-start(f32[4,48,384]{2,1,0:T(8,128)} %param.36) | copy-start | bytes 884740
  7.2 13.8 %copy-start.46 = (f32[13,768]{1,0:T(8,128)S(1)}, f32[13,768]{1,0:T(8,128)}, u32[]{:S(2)}) copy-start(f32[13,768]{1,0:T(8,128)} %param.29) | copy-start | bytes 119812
  7.2 13.8 %copy-start.3 = (bf16[1,197,768]{2,1,0:T(8,128)(2,1)S(1)}, bf16[1,197,768]{2,1,0:T(8,128)(2,1)}, u32[]{:S(2)}) copy-start(bf16[1,197,768]{2,1,0:T(8,128)(2,1)} %param.23) | copy-start | bytes 907780
  7.2 14.2 %copy-start.13 = (bf16[1,197,768]{2,1,0:T(8,128)(2,1)S(1)}, bf16[1,197,768]{2,1,0:T(8,128)(2,1)}, u32[]{:S(2)}) copy-start(bf16[1,197,768]{2,1,0:T(8,128)(2,1)} %param.25) | copy-start | bytes 907780
  7.2 47.5 %all-gather.13.cloned.1.call-start = ((), (), s32[]{:S(2)}) async-start(), calls=%async_computation.3 | async-start | bytes 1327104 | tf_op jit(solution)/shard_map/all_gather | solution.py:195
  9.0 88.5 %all-gather.15.cloned.1.call-start = ((), (), s32[]{:S(2)}) async-start(), calls=%async_computation.4 | async-start | bytes 1327104 | tf_op jit(solution)/shard_map/all_gather | solution.py:196
  10.7 152.7 %all-gather.29.cloned.1.call-start = ((), (), s32[]{:S(2)}) async-start(), calls=%async_computation.14 | async-start | bytes 4866048 | tf_op jit(solution)/shard_map/all_gather | solution.py:193
  12.5 304.5 %reduce-scatter.10.cloned.1.call-start = ((), (), s32[]{:S(2)}) async-start(), calls=%async_computation.6 | async-start | bytes 1327104 | tf_op jit(solution)/shard_map/reduce_scatter | solution.py:278
  178.5 3.2 copy-start.20
  207.3 6.3 copy-start.17
  207.4 7.2 copy-start.36
  220.8 129.3 %reduce-scatter.12.cloned.1.call-start = ((), (), s32[]{:S(2)}) async-start(), calls=%async_computation.7 | async-start | bytes 1327104 | tf_op jit(solution)/shard_map/reduce_scatter | solution.py:284
  222.1 3.7 copy-start.18
  222.1 3.7 copy-start.19
  229.1 23.0 %copy-start.34 = (bf16[628,768]{1,0:T(8,128)(2,1)S(1)}, bf16[628,768]{1,0:T(8,128)(2,1)}, u32[]{:S(2)}) copy-start(bf16[628,768]{1,0:T(8,128)(2,1)} %reshape.532) | copy-start | bytes 2893828
  250.8 12.9 %collective-permute-start = (bf16[9,768]{1,0:T(8,128)(2,1)S(1)}, bf16[9,768]{1,0:T(8,128)(2,1)S(1)}, u32[]{:S(2)}, u32[]{:S(2)}) collective-permute-start(bf16[9,768]{1,0:T(8,128)(2,1)S(1)} %slice.127), channel_id=1, source_target_pairs={{0,1},{1,2},{2,3},{4,5},{5,6},{6,7},{8,9},{9,10},{10,11},{12,13},{... | collective-permute-start | bytes 41480
  259.5 5.0 collective-permute-start.1
  263.6 227.6 %reduce-scatter.8.cloned.1.call-start = ((), (), s32[]{:S(2)}) async-start(), calls=%async_computation.5 | async-start | bytes 9732096 | tf_op jit(solution)/shard_map/reduce_scatter | solution.py:332
  280.1 4.6 copy-start.2
  316.8 33.4 %copy-start.40 = (f32[4,48,384]{2,1,0:T(8,128)S(1)}, f32[4,48,384]{2,1,0:T(8,128)}, u32[]{:S(2)}) copy-start(f32[4,48,384]{2,1,0:T(8,128)} %param.37) | copy-start | bytes 884740
  316.8 34.1 %copy-start.41 = (f32[4,48,384]{2,1,0:T(8,128)S(1)}, f32[4,48,384]{2,1,0:T(8,128)}, u32[]{:S(2)}) copy-start(f32[4,48,384]{2,1,0:T(8,128)} %param.41) | copy-start | bytes 884740
  316.8 176.1 %copy-start.42 = (f32[4,48,384]{2,1,0:T(8,128)S(1)}, f32[4,48,384]{2,1,0:T(8,128)}, u32[]{:S(2)}) copy-start(f32[4,48,384]{2,1,0:T(8,128)} %param.33) | copy-start | bytes 884740
  316.8 177.2 %copy-start.4 = (bf16[1,197,768]{2,1,0:T(8,128)(2,1)S(1)}, bf16[1,197,768]{2,1,0:T(8,128)(2,1)}, u32[]{:S(2)}) copy-start(bf16[1,197,768]{2,1,0:T(8,128)(2,1)} %param.23) | copy-start | bytes 907780
  316.9 177.2 %copy-start.16 = (bf16[197,3,12,64]{0,3,2,1:T(8,128)(2,1)S(1)}, bf16[197,3,12,64]{0,3,2,1:T(8,128)(2,1)}, u32[]{:S(2)}) copy-start(bf16[197,3,12,64]{0,3,2,1:T(8,128)(2,1)} %copy-done.15) | copy-start | bytes 2723332
  316.9 226.3 %all-gather.19.cloned.1.call-start = ((), (), s32[]{:S(2)}) async-start(), calls=%async_computation.9 | async-start | bytes 1327104 | tf_op jit(solution)/shard_map/all_gather | solution.py:343
  317.6 258.6 %all-gather.21.cloned.1.call-start = ((), (), s32[]{:S(2)}) async-start(), calls=%async_computation.10 | async-start | bytes 1327104 | tf_op jit(solution)/shard_map/all_gather | solution.py:346
  350.1 269.2 %all-gather.25.cloned.1.call-start = ((), (), s32[]{:S(2)}) async-start(), calls=%async_computation.12 | async-start | bytes 1327104 | tf_op jit(solution)/shard_map/all_gather | solution.py:352
  350.9 311.3 %all-gather.27.cloned.1.call-start = ((), (), s32[]{:S(2)}) async-start(), calls=%async_computation.13 | async-start | bytes 1327104 | tf_op jit(solution)/shard_map/all_gather | solution.py:355
  351.7 353.6 %all-gather.17.cloned.1.call-start = ((), (), s32[]{:S(2)}) async-start(), calls=%async_computation.8 | async-start | bytes 1327104 | tf_op jit(solution)/shard_map/all_gather | solution.py:340
  492.9 255.3 %all-gather.23.cloned.1.call-start = ((), (), s32[]{:S(2)}) async-start(), calls=%async_computation.11 | async-start | bytes 1327104 | tf_op jit(solution)/shard_map/all_gather | solution.py:349
  494.0 4.4 copy-start.12
  494.1 4.4 copy-start.14
  498.4 42.7 %copy-start.47 = (f32[13,768]{1,0:T(8,128)S(1)}, f32[13,768]{1,0:T(8,128)}, u32[]{:S(2)}) copy-start(f32[13,768]{1,0:T(8,128)} %param.29) | copy-start | bytes 119812
  498.4 43.3 %copy-start.22 = (bf16[4,48,384]{2,1,0:T(8,128)(2,1)S(1)}, bf16[4,48,384]{2,1,0:T(8,128)(2,1)}, u32[]{:S(2)}) copy-start(bf16[4,48,384]{2,1,0:T(8,128)(2,1)} %reduce-scatter.10.cloned.1.call-done) | copy-start | bytes 442372
  498.8 43.6 %copy-start.23 = (bf16[4,48,384]{2,1,0:T(8,128)(2,1)S(1)}, bf16[4,48,384]{2,1,0:T(8,128)(2,1)}, u32[]{:S(2)}) copy-start(bf16[4,48,384]{2,1,0:T(8,128)(2,1)} %reduce-scatter.12.cloned.1.call-done) | copy-start | bytes 442372
  500.3 45.7 %copy-start.43 = (f32[4,48,384]{2,1,0:T(8,128)S(1)}, f32[4,48,384]{2,1,0:T(8,128)}, u32[]{:S(2)}) copy-start(f32[4,48,384]{2,1,0:T(8,128)} %param.35) | copy-start | bytes 884740
  540.8 6.4 copy-start.37
  545.9 33.3 %copy-start.38 = (f32[4,48,384]{2,1,0:T(8,128)S(1)}, f32[4,48,384]{2,1,0:T(8,128)}, u32[]{:S(2)}) copy-start(f32[4,48,384]{2,1,0:T(8,128)} %param.40) | copy-start | bytes 884740
  576.2 3.0 copy-start.7
  662.2 4.9 copy-start.45
  667.1 38.1 %copy-start.39 = (f32[4,48,384]{2,1,0:T(8,128)S(1)}, f32[4,48,384]{2,1,0:T(8,128)}, u32[]{:S(2)}) copy-start(f32[4,48,384]{2,1,0:T(8,128)} %param.32) | copy-start | bytes 884740
  668.4 101.2 %copy-start.26 = (f32[4,48,384]{2,1,0:T(8,128)S(1)}, f32[4,48,384]{2,1,0:T(8,128)}, u32[]{:S(2)}) copy-start(f32[4,48,384]{2,1,0:T(8,128)} %param.28) | copy-start | bytes 884740
  668.4 101.2 %copy-start.31 = (f32[4,48,384]{2,1,0:T(8,128)S(1)}, f32[4,48,384]{2,1,0:T(8,128)}, u32[]{:S(2)}) copy-start(f32[4,48,384]{2,1,0:T(8,128)} %get-tuple-element.206) | copy-start | bytes 884740
  668.4 102.1 %copy-start.27 = (f32[4,48,384]{2,1,0:T(8,128)S(1)}, f32[4,48,384]{2,1,0:T(8,128)}, u32[]{:S(2)}) copy-start(f32[4,48,384]{2,1,0:T(8,128)} %param.27) | copy-start | bytes 884740
  707.2 64.2 %copy-start.28 = (f32[4,48,384]{2,1,0:T(8,128)S(1)}, f32[4,48,384]{2,1,0:T(8,128)}, u32[]{:S(2)}) copy-start(f32[4,48,384]{2,1,0:T(8,128)} %param.26) | copy-start | bytes 884740
  750.2 22.1 %copy-start.5 = (bf16[4,384,384]{2,1,0:T(8,128)(2,1)S(1)}, bf16[4,384,384]{2,1,0:T(8,128)(2,1)}, u32[]{:S(2)}) copy-start(bf16[4,384,384]{2,1,0:T(8,128)(2,1)} %all-gather.17.cloned.1.call-done) | copy-start | bytes 3538948
  770.5 4.0 copy-start.32
  770.5 4.0 copy-start.44
  (16 other events, 23.6 us)
Sparse Core Ops, SparseCore 0:
  10.9 43.7 all-gather.12
  57.5 39.9 all-gather.14
  101.0 62.4 all-gather.28
  220.9 62.8 reduce-scatter.9
  287.1 63.0 reduce-scatter.11
  356.4 134.7 reduce-scatter.7
  493.7 39.9 all-gather.18
  536.2 40.0 all-gather.20
  579.3 39.9 all-gather.24
  622.2 39.9 all-gather.26
  665.3 39.9 all-gather.16
  708.2 39.9 all-gather.22
where the time goes:
time: 793 us; the launch traced here: 784 us
  waiting for transfers between devices  492 us (62%)
  blocking collectives  101 us (13%)
  local copies, waits for them, and re-layouts  67.5 us (9%)
  matrix products  65.6 us (8%)
  other arithmetic  35.8 us (5%)
  between operations  16.2 us (2%)
    reduce_scatter x1, waiting for transfers between devices, body(): lax.psum_scatter(to_devices(attn_blocks_grad, data_count, model_count), (...  140 us
    all_gather x1, waiting for transfers between devices, body(): lax.all_gather(to_half(w_attn)[None], ('dp', 'mp'), axis=0, tiled=True)  62.1 us
    all_gather x1, waiting for transfers between devices, body(): lax.all_gather(root_right_attn.astype(jnp.bfloat16), 'dp', axis=1, tiled=...  41 us
    all_gather x1, waiting for transfers between devices, body(): lax.all_gather(root_right_fc2.astype(jnp.bfloat16), 'dp', axis=1, tiled=T...  40.8 us
    psum x1, blocking collectives, body(): vector_grad = lax.psum(vector_part, ('dp', 'mp'))  40.5 us
    all_gather x1, waiting for transfers between devices, body(): lax.all_gather(to_half(w_fc2), 'dp', axis=1, tiled=True)  39 us
    all_gather x1, waiting for transfers between devices, body(): lax.all_gather(root_right_fc1.astype(jnp.bfloat16), 'dp', axis=1, tiled=T...  38.7 us
    all_gather x1, waiting for transfers between devices, body(): lax.all_gather(attn_owned.astype(jnp.bfloat16), 'dp', axis=1, tiled=True)  36.9 us
  transfers between devices with their start and end apart: 14, of which 11 were waited for; matrix products, arithmetic and copies ran while one was open for 18% of the time, Pallas kernels for 0%

commit v1 on v0

v1 whole, which is shorter than its diff:
```python
import jax
import jax.numpy as jnp
from jax import lax
from jax.sharding import PartitionSpec as P

D = 768
HEADS = 12
FF = 3072
BLOCK_VEC = 128
KEPT_MOST = 157
SLOTS = 160
PAIR = 2

highest = lax.Precision.HIGHEST
masked_score = -1e30
half = jnp.bfloat16
full = jnp.float32


def to_half(values):
    return values.astype(half)


def layer_norm(values, gain_row, shift_row):
    centered = values - jnp.mean(values, axis=-1, keepdims=True)
    variance = jnp.mean(centered * centered, axis=-1, keepdims=True)
    return centered * lax.rsqrt(variance + 1e-06) * gain_row + shift_row


def exact_gelu(values):
    return jax.nn.gelu(values, approximate=False)


def dot32(left, right):
    return jnp.dot(left, right, preferred_element_type=full)


def row_product(left_half, right_half):
    return lax.dot_general(
        left_half, right_half, (((0,), (0,)), ((), ())), preferred_element_type=full
    )


def times_transpose(left_half, right_half):
    return lax.dot_general(
        left_half, right_half, (((1,), (1,)), ((), ())), preferred_element_type=full
    )


def swap_low(values, axis):
    count = lax.axis_size(axis)
    return lax.ppermute(values, axis, [(s, s ^ 1) for s in range(count)])


def shift_high(values, axis, step):
    count = lax.axis_size(axis)
    return lax.ppermute(values, axis, [(s, (s + step * PAIR) % count) for s in range(count)])


def high_index(axis):
    return lax.axis_index(axis) // PAIR


def low_index(axis):
    return lax.axis_index(axis) % PAIR


def high_size(axis):
    return lax.axis_size(axis) // PAIR


def pick(values, index, dim=0):
    return lax.dynamic_index_in_dim(values, index, dim, keepdims=False)


def ordered(pieces, index):
    count = len(pieces)
    if count == 2:
        first = index == 0
        return jnp.stack(
            [jnp.where(first, pieces[0], pieces[1]), jnp.where(first, pieces[1], pieces[0])]
        )
    return lax.dynamic_slice_in_dim(jnp.stack(pieces + pieces), (count - index) % count, count, 0)


def gather_low(values, axis):
    return ordered([values, swap_low(values, axis)], low_index(axis))


def gather_high(values, axis):
    count = high_size(axis)
    pieces = [values] + [shift_high(values, axis, -k) for k in range(1, count)]
    return ordered(pieces, high_index(axis))


def scatter_low(values, axis):
    low = low_index(axis)
    arrived = swap_low(pick(values, 1 - low), axis)
    return pick(values, low).astype(full) + arrived.astype(full)


def scatter_high(values, axis):
    count, high = high_size(axis), high_index(axis)
    total = pick(values, high).astype(full)
    for k in range(1, count):
        total = total + shift_high(pick(values, (high + k) % count), axis, k).astype(full)
    return total


def attend(queries, key_part, values, allowed):
    scale_factor = queries.shape[-1] ** (-0.5)
    scores = jnp.einsum("qhd,khd->hqk", queries, key_part, preferred_element_type=full)
    scores = jnp.where(allowed[None, None, :] > 0, scores * scale_factor, masked_score)
    shifted = jnp.exp(scores - jnp.max(scores, axis=-1, keepdims=True))
    probs = shifted / jnp.sum(shifted, axis=-1, keepdims=True)
    attended = jnp.einsum("hqk,khd->qhd", to_half(probs), values, preferred_element_type=full)
    return (to_half(attended), probs)


def attend_back(queries, key_part, values, probs, grad_attended):
    scale_factor = queries.shape[-1] ** (-0.5)
    grad_values = jnp.einsum(
        "hqk,qhd->khd", to_half(probs), grad_attended, preferred_element_type=full
    )
    grad_probs = jnp.einsum("qhd,khd->hqk", grad_attended, values, preferred_element_type=full)
    row_inner = jnp.sum(probs * grad_probs, axis=-1, keepdims=True)
    grad_scores = to_half(probs * (grad_probs - row_inner))
    grad_queries = (
        jnp.einsum("hqk,khd->qhd", grad_scores, key_part, preferred_element_type=full)
        * scale_factor
    )
    grad_keys = (
        jnp.einsum("hqk,qhd->khd", grad_scores, queries, preferred_element_type=full)
        * scale_factor
    )
    return jnp.stack([grad_queries, grad_keys, grad_values], axis=1)


def gather_group(rows):
    pair = jnp.stack([rows, swap_low(rows, "mp")])
    pieces = [pair] + [shift_high(pair, "mp", -k) for k in range(1, high_size("mp"))]
    return jnp.concatenate(pieces, axis=0).reshape(-1, rows.shape[-1])


def scatter_group(rows, row_count):
    pieces = rows.reshape(high_size("mp"), PAIR, row_count, rows.shape[-1])
    pairs = pieces[:, 0].astype(full) + swap_low(pieces[:, 1], "mp").astype(full)
    total = pairs[0]
    for k in range(1, high_size("mp")):
        total = total + shift_high(to_half(pairs[k]), "mp", k).astype(full)
    return total


def halves(values, dim):
    count = values.shape[dim] // 2
    return (
        lax.slice_in_dim(values, 0, count, axis=dim),
        lax.slice_in_dim(values, count, 2 * count, axis=dim),
    )


def gather_attn(blocks):
    local, piece, order = blocks.shape
    lines = gather_high(to_half(blocks), "dp")
    first, second = halves(lines, 0)
    first = gather_high(gather_low(first, "dp"), "mp")
    second = gather_low(gather_high(second, "mp"), "dp")
    both = jnp.concatenate([first, second.swapaxes(0, 1)], axis=2)
    both = gather_low(both, "mp")
    row_blocks = D // order
    both = both.transpose(1, 0, 4, 3, 2, 5, 6)
    both = both.reshape(-1, row_blocks, order, order)
    return both.transpose(1, 2, 0, 3).reshape(D, -1)


def gather_fc(blocks):
    lines = gather_low(gather_high(to_half(blocks), "dp"), "dp")
    lines = lines.transpose(2, 1, 0, 3, 4)
    return lines.reshape(blocks.shape[0], -1, blocks.shape[2])


def split_cols(matrix, order):
    rows, cols = matrix.shape
    return (
        matrix.reshape(rows // order, order, cols // order, order)
        .transpose(2, 0, 1, 3)
        .reshape(-1, order, order)
    )


def split_rows(matrix, order):
    rows, cols = matrix.shape
    return (
        matrix.reshape(rows // order, order, cols // order, order)
        .transpose(0, 2, 1, 3)
        .reshape(-1, order, order)
    )


def join_cols(blocks, row_blocks):
    count, order, _ = blocks.shape
    return (
        blocks.reshape(-1, row_blocks, order, order)
        .transpose(1, 2, 0, 3)
        .reshape(row_blocks * order, -1)
    )


def join_rows(blocks, col_blocks):
    count, order, _ = blocks.shape
    return (
        blocks.reshape(-1, col_blocks, order, order)
        .transpose(0, 2, 1, 3)
        .reshape(-1, col_blocks * order)
    )


def scatter_z(blocks):
    local, order, _ = blocks.shape
    count = high_size("dp")
    by_rows = to_half(blocks).reshape(local, count, order // count, order).swapaxes(0, 1)
    return scatter_high(by_rows, "dp")


def scatter_fc(blocks):
    local, order, _ = blocks.shape
    by_x = to_half(blocks).reshape(PAIR, local // PAIR, order, order)
    return scatter_z(scatter_low(by_x, "dp"))


def scatter_attn(blocks):
    count, order, _ = blocks.shape
    y_count = high_size("mp")
    local = count // (y_count * PAIR)
    by_core = to_half(blocks).reshape(y_count, PAIR, local, order, order).swapaxes(0, 1)
    kept = to_half(scatter_low(by_core, "mp")).reshape(
        y_count, PAIR, local // PAIR, order, order
    )
    first, second = halves(kept, 3)
    first = to_half(scatter_low(first.swapaxes(0, 1), "dp"))
    second = to_half(scatter_high(second, "mp"))
    first = scatter_high(first, "mp")
    second = scatter_low(second, "dp")
    return scatter_z(jnp.concatenate([first, second], axis=1))


def gather_z(rows):
    local, _, order = rows.shape
    return gather_high(to_half(rows), "dp").swapaxes(0, 1).reshape(local, -1, order)


def to_pair(pieces):
    local, piece, order = pieces.shape
    by_x = to_half(pieces).reshape(PAIR, local // PAIR, piece, order)
    low = low_index("dp")
    both = ordered([pick(by_x, low), swap_low(pick(by_x, 1 - low), "dp")], low)
    return both.swapaxes(0, 1).reshape(local // PAIR, PAIR * piece, order)


def from_pair(rows):
    n, local, piece, order = rows.shape
    by_x = to_half(rows).reshape(n, local, PAIR, piece // PAIR, order)
    low = low_index("dp")
    both = ordered([pick(by_x, low, 2), swap_low(pick(by_x, 1 - low, 2), "dp")], low)
    return both.swapaxes(0, 1).reshape(n, PAIR * local, piece // PAIR, order)


def shampoo_rows(grad_rows, left_root, right_root):
    grad_half = to_half(grad_rows)
    whole = gather_z(grad_half)
    rows = grad_rows.shape[1]
    cols = lax.dynamic_slice_in_dim(whole, high_index("dp") * rows, rows, 2)
    left_term = jnp.einsum("bij,bkj->bik", grad_half, whole, preferred_element_type=full)
    right_term = jnp.einsum("bji,bjk->bik", cols, whole, preferred_element_type=full)
    step = to_half(jnp.einsum("bij,bjk->bik", left_root, whole, preferred_element_type=full))
    step = jnp.einsum("bij,bjk->bik", step, right_root, preferred_element_type=full)
    squares = jnp.sum(step * step, axis=(1, 2))
    squares = gather_low(squares, "dp").reshape(-1)
    total = squares
    for k in range(1, high_size("dp")):
        total = total + shift_high(squares, "dp", k)
    sent = from_pair(jnp.stack([grad_rows, left_term, right_term, step]))
    return sent, total


def apply_step(weight, left_stat, right_stat, sent, square_total, step_rates):
    order = weight.shape[2]
    sent = sent.astype(full)
    update_scale = lax.rsqrt(square_total / (order * order) + 1e-06) * step_rates
    return (
        sent[0],
        0.95 * left_stat + 0.05 * sent[1],
        0.95 * right_stat + 0.05 * sent[2],
        weight - sent[3] * update_scale[:, None, None],
    )


def sum_all(values):
    values = values + swap_low(values, "mp")
    for axis in ("mp", "dp"):
        if axis == "dp":
            values = values + swap_low(values, "dp")
        base = values
        for k in range(1, high_size(axis)):
            values = values + shift_high(base, axis, k)
    return values


def body(
    tokens,
    keep_mask,
    cotangent,
    w_attn,
    w_fc1,
    w_fc2,
    vectors,
    left_attn,
    right_attn,
    root_left_attn,
    root_right_attn,
    left_fc1,
    right_fc1,
    root_left_fc1,
    root_right_fc1,
    left_fc2,
    right_fc2,
    root_left_fc2,
    root_right_fc2,
):
    image_count, patch_count, width = tokens.shape
    row_count = image_count * patch_count
    order = w_attn.shape[2]
    row_blocks = width // order
    attn_used = gather_attn(w_attn)
    qkv_full = attn_used[:, : 3 * width]
    out_full = attn_used[:, 3 * width :]
    fc1_used = join_cols(gather_fc(w_fc1), row_blocks)
    fc2_used = join_rows(gather_fc(w_fc2), row_blocks)
    left_roots = [to_pair(v) for v in (root_left_attn, root_left_fc1, root_left_fc2)]
    right_roots = [gather_z(to_pair(v)) for v in (root_right_attn, root_right_fc1, root_right_fc2)]
    hidden_local = fc1_used.shape[1]
    flat = tokens.reshape(row_count, width).astype(full)
    keep_rows = keep_mask.reshape(row_count).astype(full)
    row_gate = jax.nn.sigmoid(jnp.sum(flat * vectors[8], axis=-1))
    row_scale = keep_rows * row_gate
    grad_output = cotangent.reshape(row_count, width).astype(full)
    grad_change = row_scale[:, None] * grad_output
    grad_feed = to_half(grad_change)
    slot = jnp.cumsum(keep_mask, axis=1) - 1
    chosen = (
        (slot[:, None, :] == lax.broadcasted_iota(jnp.int32, (1, SLOTS, 1), 1))
        & (keep_mask[:, None, :] > 0)
    ).astype(half)

    def compact(rows):
        rows = rows.reshape(image_count, patch_count, width)
        picked = jnp.einsum("bsr,brd->bsd", chosen, rows, preferred_element_type=full)
        return to_half(picked).reshape(image_count * SLOTS, width)

    def spread(rows):
        rows = rows.reshape(image_count, SLOTS, width)
        return jnp.einsum(
            "bsr,bsd->brd", chosen.astype(full), rows, precision=highest
        ).reshape(row_count, width)

    group_grads = gather_group(compact(grad_feed))
    normed, first_norm_back = jax.vjp(layer_norm, flat, vectors[0], vectors[1])
    normed_half = to_half(normed)
    qkv_bias = jnp.concatenate([vectors[4], jnp.zeros_like(vectors[4]), vectors[5]])
    mixed_half = to_half(dot32(normed_half, qkv_full) + qkv_bias)
    heads_view = mixed_half.reshape(image_count, patch_count, 3, HEADS, width // HEADS)
    queries = heads_view[:, :, 0]
    key_part = heads_view[:, :, 1]
    values = heads_view[:, :, 2]
    attended_half, probs = jax.vmap(attend)(queries, key_part, values, keep_mask)
    attended_flat = attended_half.reshape(row_count, width)
    branch = dot32(attended_flat, out_full) + vectors[6]
    middle = flat + branch
    normed_two, second_norm_back = jax.vjp(layer_norm, middle, vectors[2], vectors[3])
    group_rows = gather_group(compact(to_half(normed_two)))
    up_bias = vectors[9:].reshape(-1)
    offset = lax.axis_index("mp") * hidden_local
    local_bias = lax.dynamic_slice_in_dim(up_bias, offset, hidden_local)
    hidden = dot32(group_rows, fc1_used) + local_bias
    activated, gelu_back = jax.vjp(exact_gelu, hidden)
    activated = to_half(activated)
    grad_active = times_transpose(group_grads, fc2_used)
    grad_hidden = to_half(gelu_back(grad_active)[0])
    mlp_count = image_count * SLOTS
    grad_rows_back = scatter_group(to_half(times_transpose(grad_hidden, fc1_used)), mlp_count)
    feed = spread(scatter_group(to_half(dot32(activated, fc2_used)), mlp_count)) + vectors[7]
    change = branch + feed
    block_out = to_half(flat + row_scale[:, None] * change).reshape(tokens.shape)
    grad_logit = keep_rows * row_gate * (1.0 - row_gate) * jnp.sum(grad_output * change, axis=-1)
    fc1_rows = scatter_fc(split_cols(row_product(group_rows, grad_hidden), order))
    fc2_rows = scatter_fc(split_rows(row_product(activated, group_grads), order))
    up_part = jnp.sum(grad_hidden, axis=0, dtype=full)
    up_bias_grad = lax.dynamic_update_slice_in_dim(jnp.zeros_like(up_bias), up_part, offset, 0)
    sent_fc1, total_fc1 = shampoo_rows(fc1_rows, left_roots[1], right_roots[1])
    sent_fc2, total_fc2 = shampoo_rows(fc2_rows, left_roots[2], right_roots[2])

    grad_normed_two = spread(grad_rows_back)
    grad_middle, grad_gain_two, grad_shift_two = second_norm_back(grad_normed_two)
    grad_branch = to_half(grad_change + grad_middle)
    grad_attended = to_half(times_transpose(grad_branch, out_full))
    grad_out_full = row_product(attended_flat, grad_branch)
    grad_heads = jax.vmap(attend_back)(
        queries,
        key_part,
        values,
        probs,
        grad_attended.reshape(image_count, patch_count, HEADS, -1),
    )
    grad_mixed = to_half(grad_heads.reshape(row_count, 3 * width))
    grad_qkv_full = row_product(normed_half, grad_mixed)
    attn_rows = scatter_attn(
        split_cols(jnp.concatenate([grad_qkv_full, grad_out_full], axis=1), order)
    )
    sent_attn, total_attn = shampoo_rows(attn_rows, left_roots[0], right_roots[0])
    grad_normed = times_transpose(grad_mixed, qkv_full)
    grad_flat, grad_gain_one, grad_shift_one = first_norm_back(grad_normed)
    input_grad = (grad_output + grad_middle + grad_flat + grad_logit[:, None] * vectors[8]).reshape(
        tokens.shape
    )
    mixed_sums = jnp.sum(grad_mixed, axis=0, dtype=full)
    vector_rows = jnp.stack(
        [
            grad_gain_one,
            grad_shift_one,
            grad_gain_two,
            grad_shift_two,
            mixed_sums[:width],
            mixed_sums[2 * width :],
            jnp.sum(grad_branch, axis=0, dtype=full),
            jnp.sum(grad_feed, axis=0, dtype=full),
            jnp.sum(grad_logit[:, None] * flat, axis=0),
        ]
    )
    vector_part = jnp.concatenate([vector_rows, up_bias_grad.reshape(-1, width)], axis=0)
    vector_grad = sum_all(vector_part)

    attn_local = w_attn.shape[0]
    block_index = lax.axis_index("mp") * attn_local + lax.broadcasted_iota(
        jnp.int32, (attn_local,), 0
    )
    attn_rates = jnp.where(
        block_index // row_blocks < 3 * row_blocks, 0.5 * D ** (-0.5), 0.5 * (D // 16) ** (-0.5)
    )
    fc1_rates = jnp.full((w_fc1.shape[0],), 0.5 * D ** (-0.5), full)
    fc2_rates = jnp.full((w_fc2.shape[0],), 0.5 * FF ** (-0.5), full)
    grad_attn, new_left_attn, new_right_attn, new_attn = apply_step(
        w_attn, left_attn, right_attn, sent_attn, total_attn, attn_rates
    )
    grad_fc1, new_left_fc1, new_right_fc1, new_fc1 = apply_step(
        w_fc1, left_fc1, right_fc1, sent_fc1, total_fc1, fc1_rates
    )
    grad_fc2, new_left_fc2, new_right_fc2, new_fc2 = apply_step(
        w_fc2, left_fc2, right_fc2, sent_fc2, total_fc2, fc2_rates
    )
    vector_blocks = vector_grad.reshape(vector_grad.shape[0], -1, BLOCK_VEC)
    block_scale = lax.rsqrt(jnp.mean(vector_blocks * vector_blocks, axis=-1, keepdims=True) + 1e-06)
    new_vectors = vectors - 0.05 * (vector_blocks * block_scale).reshape(vectors.shape)
    return (
        block_out,
        input_grad,
        grad_attn,
        grad_fc1,
        grad_fc2,
        new_left_attn,
        new_right_attn,
        new_left_fc1,
        new_right_fc1,
        new_left_fc2,
        new_right_fc2,
        new_attn,
        new_fc1,
        new_fc2,
        to_half(new_attn),
        to_half(new_fc1),
        to_half(new_fc2),
        vector_grad,
        new_vectors,
    )


def solution(mesh):
    rows = P(("dp", "mp"), None, None)
    blocks = P("mp", "dp", None)
    return jax.shard_map(
        body,
        mesh=mesh,
        in_specs=(rows, P(("dp", "mp"), None), rows)
        + (blocks,) * 3
        + (P(),)
        + (blocks,) * 12,
        out_specs=(rows, rows) + (blocks,) * 15 + (P(), P()),
        check_vma=False,
    )
```

time: 793 us -> 413 us (0.52)
  waiting for transfers between devices: 492 us -> 112 us
  blocking collectives: 101 us -> 0 us
  starting transfers between devices: 5.9 us -> 106 us
  local copies, waits for them, and re-layouts: 67.5 us -> 84.7 us
  matrix products: 65.6 us -> 50.3 us
  other arithmetic: 35.8 us -> 50.7 us
  between operations: 16.2 us -> 3.41 us
    all_gather x9 -> x0, waiting for transfers between devices: 319 us -> none  [the longest x1 62.1 us: body(): lax.all_gather(to_half(w_attn)[None], ('dp', 'mp'), axis=0, tiled=True)]
    reduce_scatter x3 -> x0, waiting for transfers between devices: 172 us -> none  [the longest x1 140 us: body(): lax.psum_scatter(to_devices(attn_blocks_grad, data_count, model_count), (...]
    ppermute x0 -> x85, waiting for transfers between devices: none -> 112 us  [the longest x57 57.1 us: shift_high(): lax.ppermute(values, axis, [(s, (s + step * PAIR) % count) for s in range...]
    ppermute x0 -> x85, starting transfers between devices: none -> 106 us  [the longest x57 83.4 us: shift_high(): lax.ppermute(values, axis, [(s, (s + step * PAIR) % count) for s in range...]
    psum x2 -> x0, blocking collectives: 59.9 us -> none  [the longest x1 40.5 us: body(): vector_grad = lax.psum(vector_part, ('dp', 'mp'))]
    unnamed x1 -> x0, blocking collectives: 21.6 us -> none
    all_gather x2 -> x0, blocking collectives: 19.5 us -> none  [the longest x1 9.78 us: body(): group_grads = lax.all_gather(grad_sent, 'mp', axis=0, tiled=True)]
    dot_general x21 -> x19, matrix products: 36.4 us -> 23.7 us  [the longest x4 12.1 us: dot32(): return jnp.dot(left, right, preferred_element_type=full)]
  transfers between devices with their start and end apart: 14 -> 85, of which waited for: 11 -> 31; matrix products, arithmetic and copies ran while one was open for 18% -> 38% of each run, Pallas kernels for 0% -> 0%
where the time goes in v1:
time: 413 us; the launch traced here: 406 us
  waiting for transfers between devices  112 us (27%)
  starting transfers between devices  106 us (26%)
  local copies, waits for them, and re-layouts  84.7 us (21%)
  other arithmetic  50.7 us (12%)
  matrix products  50.3 us (12%)
    ppermute x57, starting transfers between devices, shift_high(): lax.ppermute(values, axis, [(s, (s + step * PAIR) % count) for s in range...  83.4 us
    ppermute x57, waiting for transfers between devices, shift_high(): lax.ppermute(values, axis, [(s, (s + step * PAIR) % count) for s in range...  57.1 us
    ppermute x28, waiting for transfers between devices, swap_low(): return lax.ppermute(values, axis, [(s, s ^ 1) for s in range(count)])  54.7 us
    unnamed x288, local copies, waits for them, and re-layouts  33.2 us
    ppermute x28, starting transfers between devices, swap_low(): return lax.ppermute(values, axis, [(s, s ^ 1) for s in range(count)])  22.2 us
    convert_element_type x16, other arithmetic, to_half(): return values.astype(half)  12.7 us
    dot_general x4, matrix products, times_transpose(): lax.dot_general(left_half, right_half, (((1,), (1,)), ((), ())), preferre...  12.5 us
    dot_general x4, matrix products, dot32(): return jnp.dot(left, right, preferred_element_type=full)  12.1 us
  transfers between devices with their start and end apart: 85, of which 31 were waited for; matrix products, arithmetic and copies ran while one was open for 38% of the time, Pallas kernels for 0%

profile of v1, /device:TPU:0, one launch (start us, length us, event | category | flops | bytes accessed | tf_op | source)
XLA Modules:
  0.0 406.4 jit_solution(17887297602228421344)
XLA Ops:
  2.4 5.0 %collective-permute-start.14 = (bf16[4,48,384]{2,1,0:T(8,128)(2,1)}, bf16[4,48,384]{2,1,0:T(8,128)(2,1)}, u32[]{:S(2)}, u32[]{:S(2)}) collective-permute-start(bf16[4,48,384]{2,1,0:T(8,128)(2,1)} %get-tuple-element.127), channel_id=1, source_target_pairs={{0,24},{4,28},{8,0},{12,4},{16,8},{20,12},{24,16},{28,20},{1,25},{... | collective-permute-start | bytes 442376 | tf_op jit(solution)/shard_map/ppermute | solution.py:57
  10.2 2.8 collective-permute-start.10
  31.8 3.0 collective-permute-done.62
  35.5 4.3 %collective-permute-done.36 = bf16[2,48,384]{2,1,0:T(8,128)(2,1)S(1)} collective-permute-done((bf16[2,48,384]{2,1,0:T(8,128)(2,1)S(1)}, bf16[2,48,384]{2,1,0:T(8,128)(2,1)S(1)}, u32[]{:S(2)}, u32[]{:S(2)}) %collective-permute-start.36) | collective-permute-done | bytes 73760 | tf_op jit(solution)/shard_map/ppermute | solution.py:52
  40.5 3.7 collective-permute-done.61
  44.8 3.8 collective-permute-done.48
  49.1 3.8 collective-permute-done.35
  57.1 3.7 collective-permute-start
  82.9 4.6 %collective-permute-done.51 = bf16[2,96,384]{2,1,0:T(8,128)(2,1)S(1)} collective-permute-done((bf16[2,96,384]{2,1,0:T(8,128)(2,1)S(1)}, bf16[2,96,384]{2,1,0:T(8,128)(2,1)S(1)}, u32[]{:S(2)}, u32[]{:S(2)}) %collective-permute-start.51) | collective-permute-done | bytes 147488 | tf_op jit(solution)/shard_map/ppermute | solution.py:57
  89.1 2.9 collective-permute-start.37
  92.1 2.6 collective-permute-start.38
  94.8 4.9 %collective-permute-done.64 = bf16[2,96,384]{2,1,0:T(8,128)(2,1)S(1)} collective-permute-done((bf16[2,96,384]{2,1,0:T(8,128)(2,1)S(1)}, bf16[2,96,384]{2,1,0:T(8,128)(2,1)S(1)}, u32[]{:S(2)}, u32[]{:S(2)}) %collective-permute-start.64) | collective-permute-done | bytes 147488 | tf_op jit(solution)/shard_map/ppermute | solution.py:57
  101.9 6.1 %collective-permute-done.5 = bf16[2,4,48,384]{3,2,0,1:T(8,128)(2,1)S(1)} collective-permute-done((bf16[2,4,48,384]{3,2,0,1:T(8,128)(2,1)S(1)}, bf16[2,4,48,384]{3,2,0,1:T(8,128)(2,1)S(1)}, u32[]{:S(2)}, u32[]{:S(2)}) %collective-permute-start.5) | collective-permute-done | bytes 294944 | tf_op jit(solution)/shard_map/ppermute | solution.py:57
  111.5 9.9 %collective-permute-done.6 = bf16[2,2,4,48,384]{4,3,1,2,0:T(8,128)(2,1)S(1)} collective-permute-done((bf16[2,2,4,48,384]{4,3,1,2,0:T(8,128)(2,1)S(1)}, bf16[2,2,4,48,384]{4,3,1,2,0:T(8,128)(2,1)S(1)}, u32[]{:S(2)}, u32[]{:S(2)}) %collective-permute-start.6) | collective-permute-done | bytes 589856 | tf_op jit(solution)/shard_map/ppermute | solution.py:52
  121.3 3.5 collective-permute-start.39
  134.8 2.8 copy.163
  137.7 3.4 copy.235
  141.0 3.0 fusion.2
  144.8 2.5 fusion.206
  164.4 6.6 %collective-permute-done.9 = bf16[2,160,768]{2,1,0:T(8,128)(2,1)} collective-permute-done((bf16[2,160,768]{2,1,0:T(8,128)(2,1)}, bf16[2,160,768]{2,1,0:T(8,128)(2,1)}, u32[]{:S(2)}, u32[]{:S(2)}) %collective-permute-start.9) | collective-permute-done | bytes 491552 | tf_op jit(solution)/shard_map/ppermute | solution.py:57
  172.2 6.1 %fusion.17 = (bf16[768,640]{0,1:T(8,128)(2,1)}, f32[768,640]{0,1:T(8,128)}, f32[640,768]{1,0:T(8,128)S(1)}) fusion(f32[768]{0:T(1024)S(1)} %copy-done.81, bf16[640,768]{1,0:T(8,128)(2,1)S(1)} %bitcast.859, bf16[768,768]{1,0:T(8,128)(2,1)S(1)} %bitcast.901), kind=kOutput, calls=%fused_computation.41 | convolution fusion | flops 787415040 | bytes 7080960 | tf_op jit(solution)/shard_map/dot_general | solution.py:35
  178.3 6.1 %convert_reduce_fusion.1 = (f32[768]{0:T(1024)S(1)}, bf16[640,768]{1,0:T(8,128)(2,1)S(1)}, f32[640,768]{1,0:T(8,128)S(1)}, f32[640,768]{1,0:T(8,128)}) fusion(f32[640,768]{1,0:T(8,128)S(1)} %get-tuple-element.212, f32[768]{0:T(1024)S(1)} %copy-done.81, bf16[640,768]{1,0:T(8,128)(2,1)S(1)} %bitcast.862, bf16[768,768]{1,0:T(8,128)(2,1)S(1)} %bitcast.855), kind=kOutput, calls=%fused_computation.42 | convolution fusion | flops 791837952 | bytes 9050112 | tf_op jit(solution)/shard_map/dot_general | solution.py:45
  190.9 2.3 copy.230
  193.2 2.8 convolution_convert_fusion.2
  200.2 2.3 copy.229
  203.9 2.6 convolution_convert_fusion.3
  216.5 2.5 collective-permute-start.55
  219.0 7.0 %collective-permute-done.41 = bf16[2,384,384]{2,1,0:T(8,128)(2,1)S(1)} collective-permute-done((bf16[2,384,384]{2,1,0:T(8,128)(2,1)S(1)}, bf16[2,384,384]{2,1,0:T(8,128)(2,1)S(1)}, u32[]{:S(2)}, u32[]{:S(2)}) %collective-permute-start.41) | collective-permute-done | bytes 589856 | tf_op jit(solution)/shard_map/ppermute | solution.py:52
  237.1 2.4 multiply_reduce_fusion
  243.7 3.4 fusion.184
  258.3 2.7 concatenate.46
  262.6 2.8 collective-permute-start.44
  285.1 3.5 collective-permute-start.82
  307.9 4.7 %collective-permute-done.76 = f32[4]{0:T(128)S(1)} collective-permute-done((f32[4]{0:T(128)S(1)}, f32[4]{0:T(128)S(1)}, u32[]{:S(2)}, u32[]{:S(2)}) %collective-permute-start.76) | collective-permute-done | bytes 48 | tf_op jit(solution)/shard_map/ppermute | solution.py:57
  312.7 4.4 %collective-permute-done.77 = f32[4]{0:T(128)S(1)} collective-permute-done((f32[4]{0:T(128)S(1)}, f32[4]{0:T(128)S(1)}, u32[]{:S(2)}, u32[]{:S(2)}) %collective-permute-start.77) | collective-permute-done | bytes 48 | tf_op jit(solution)/shard_map/ppermute | solution.py:57
  317.1 3.5 collective-permute-done.78
  324.8 2.2 fusion.1
  332.0 8.1 %collective-permute-done.25 = bf16[2,2,192,384]{3,2,1,0:T(8,128)(2,1)S(1)} collective-permute-done((bf16[2,2,192,384]{3,2,1,0:T(8,128)(2,1)S(1)}, bf16[2,2,192,384]{3,2,1,0:T(8,128)(2,1)S(1)}, u32[]{:S(2)}, u32[]{:S(2)}) %collective-permute-start.25) | collective-permute-done | bytes 589856 | tf_op jit(solution)/shard_map/ppermute | solution.py:52
  342.6 2.9 collective-permute-start.28
  347.3 2.9 collective-permute-done.28
  352.0 2.3 collective-permute-start.31
  355.0 2.6 collective-permute-done.29
  357.6 2.7 collective-permute-done.30
  361.4 4.8 %collective-permute-start.32 = (bf16[2,96,384]{2,1,0:T(8,128)(2,1)S(1)}, bf16[2,96,384]{2,1,0:T(8,128)(2,1)S(1)}, u32[]{:S(2)}, u32[]{:S(2)}) collective-permute-start(bf16[2,96,384]{2,1,0:T(8,128)(2,1)S(1)} %get-tuple-element.119), channel_id=1, source_target_pairs={{0,24},{4,28},{8,0},{12,4},{16,8},{20,12},{24,16},{28,20},{1,25},{... | collective-permute-start | bytes 442376 | tf_op jit(solution)/shard_map/ppermute | solution.py:57
  367.0 2.6 collective-permute-start.33
  370.5 6.2 %collective-permute-done.33 = bf16[2,96,384]{2,1,0:T(8,128)(2,1)S(1)} collective-permute-done((bf16[2,96,384]{2,1,0:T(8,128)(2,1)S(1)}, bf16[2,96,384]{2,1,0:T(8,128)(2,1)S(1)}, u32[]{:S(2)}, u32[]{:S(2)}) %collective-permute-start.33) | collective-permute-done | bytes 147488 | tf_op jit(solution)/shard_map/ppermute | solution.py:57
  386.7 4.8 %collective-permute-done.67 = f32[2]{0:T(128)S(1)} collective-permute-done((f32[2]{0:T(128)S(1)}, f32[2]{0:T(128)S(1)}, u32[]{:S(2)}, u32[]{:S(2)}) %collective-permute-start.67) | collective-permute-done | bytes 40 | tf_op jit(solution)/shard_map/ppermute | solution.py:52
  393.6 2.3 collective-permute-start.69
  (646 shorter events, 216.8 us)
Async XLA Ops:
  2.4 53.5 %collective-permute-start.14 = (bf16[4,48,384]{2,1,0:T(8,128)(2,1)}, bf16[4,48,384]{2,1,0:T(8,128)(2,1)}, u32[]{:S(2)}, u32[]{:S(2)}) collective-permute-start(bf16[4,48,384]{2,1,0:T(8,128)(2,1)} %get-tuple-element.127), channel_id=1, source_target_pairs={{0,24},{4,28},{8,0},{12,4},{16,8},{20,12},{24,16},{28,20},{1,25},{... | collective-permute-start | bytes 442376 | tf_op jit(solution)/shard_map/ppermute | solution.py:57
  7.5 49.6 %collective-permute-start.15 = (bf16[4,48,384]{2,1,0:T(8,128)(2,1)}, bf16[4,48,384]{2,1,0:T(8,128)(2,1)}, u32[]{:S(2)}, u32[]{:S(2)}) collective-permute-start(bf16[4,48,384]{2,1,0:T(8,128)(2,1)} %get-tuple-element.127), channel_id=1, source_target_pairs={{0,16},{4,20},{8,24},{12,28},{16,0},{20,4},{24,8},{28,12},{1,17},{... | collective-permute-start | bytes 442376 | tf_op jit(solution)/shard_map/ppermute | solution.py:57
  7.5 54.2 %collective-permute-start.16 = (bf16[4,48,384]{2,1,0:T(8,128)(2,1)}, bf16[4,48,384]{2,1,0:T(8,128)(2,1)}, u32[]{:S(2)}, u32[]{:S(2)}) collective-permute-start(bf16[4,48,384]{2,1,0:T(8,128)(2,1)} %get-tuple-element.127), channel_id=1, source_target_pairs={{0,8},{4,12},{8,16},{12,20},{16,24},{20,28},{24,0},{28,4},{1,9},{5... | collective-permute-start | bytes 442376 | tf_op jit(solution)/shard_map/ppermute | solution.py:57
  10.2 53.8 %collective-permute-start.10 = (bf16[4,48,384]{2,1,0:T(8,128)(2,1)}, bf16[4,48,384]{2,1,0:T(8,128)(2,1)}, u32[]{:S(2)}, u32[]{:S(2)}) collective-permute-start(bf16[4,48,384]{2,1,0:T(8,128)(2,1)} %get-tuple-element.123), channel_id=1, source_target_pairs={{0,24},{4,28},{8,0},{12,4},{16,8},{20,12},{24,16},{28,20},{1,25},{... | collective-permute-start | bytes 442376 | tf_op jit(solution)/shard_map/ppermute | solution.py:57
  13.0 17.2 %collective-permute-start.49 = (bf16[2,48,384]{2,1,0:T(8,128)(2,1)S(1)}, bf16[2,48,384]{2,1,0:T(8,128)(2,1)}, u32[]{:S(2)}, u32[]{:S(2)}) collective-permute-start(bf16[2,48,384]{2,1,0:T(8,128)(2,1)S(1)} %dynamic-slice_bitcast_fusion.27), channel_id=1, source_target_pairs={{0,4},{4,0},{8,12},{12,8},{16,20},{20,16},{24,28},{28,24},{1,5},{5... | collective-permute-start | bytes 221192 | tf_op jit(solution)/shard_map/ppermute | solution.py:52
  52.9 14.6 %collective-permute-start.11 = (bf16[4,48,384]{2,1,0:T(8,128)(2,1)}, bf16[4,48,384]{2,1,0:T(8,128)(2,1)S(1)}, u32[]{:S(2)}, u32[]{:S(2)}) collective-permute-start(bf16[4,48,384]{2,1,0:T(8,128)(2,1)} %get-tuple-element.123), channel_id=1, source_target_pairs={{0,16},{4,20},{8,24},{12,28},{16,0},{20,4},{24,8},{28,12},{1,17},{... | collective-permute-start | bytes 442376 | tf_op jit(solution)/shard_map/ppermute | solution.py:57
  57.1 15.7 %collective-permute-start = (bf16[4,48,384]{2,1,0:T(8,128)(2,1)S(1)}, bf16[4,48,384]{2,1,0:T(8,128)(2,1)S(1)}, u32[]{:S(2)}, u32[]{:S(2)}) collective-permute-start(bf16[4,48,384]{2,1,0:T(8,128)(2,1)S(1)} %copy-done.58), channel_id=1, source_target_pairs={{0,24},{4,28},{8,0},{12,4},{16,8},{20,12},{24,16},{28,20},{1,25},{... | collective-permute-start | bytes 442376 | tf_op jit(solution)/shard_map/ppermute | solution.py:57
  61.7 13.2 %collective-permute-start.1 = (bf16[4,48,384]{2,1,0:T(8,128)(2,1)S(1)}, bf16[4,48,384]{2,1,0:T(8,128)(2,1)S(1)}, u32[]{:S(2)}, u32[]{:S(2)}) collective-permute-start(bf16[4,48,384]{2,1,0:T(8,128)(2,1)S(1)} %copy-done.58), channel_id=1, source_target_pairs={{0,16},{4,20},{8,24},{12,28},{16,0},{20,4},{24,8},{28,12},{1,17},{... | collective-permute-start | bytes 442376 | tf_op jit(solution)/shard_map/ppermute | solution.py:57
  64.0 13.9 %collective-permute-start.2 = (bf16[4,48,384]{2,1,0:T(8,128)(2,1)S(1)}, bf16[4,48,384]{2,1,0:T(8,128)(2,1)S(1)}, u32[]{:S(2)}, u32[]{:S(2)}) collective-permute-start(bf16[4,48,384]{2,1,0:T(8,128)(2,1)S(1)} %copy-done.58), channel_id=1, source_target_pairs={{0,8},{4,12},{8,16},{12,20},{16,24},{20,28},{24,0},{28,4},{1,9},{5... | collective-permute-start | bytes 442376 | tf_op jit(solution)/shard_map/ppermute | solution.py:57
  67.6 63.4 %collective-permute-start.20 = (bf16[160,768]{1,0:T(8,128)(2,1)S(1)}, bf16[160,768]{1,0:T(8,128)(2,1)S(1)}, u32[]{:S(2)}, u32[]{:S(2)}) collective-permute-start(bf16[160,768]{1,0:T(8,128)(2,1)S(1)} %convolution_convert_fusion.8), channel_id=1, source_target_pairs={{0,1},{1,0},{2,3},{3,2},{4,5},{5,4},{6,7},{7,6},{8,9},{9,8},{10,11... | collective-permute-start | bytes 737288 | tf_op jit(solution)/shard_map/ppermute | solution.py:52
  67.6 14.4 %collective-permute-start.50 = (bf16[2,96,384]{2,1,0:T(8,128)(2,1)S(1)}, bf16[2,96,384]{2,1,0:T(8,128)(2,1)S(1)}, u32[]{:S(2)}, u32[]{:S(2)}) collective-permute-start(bf16[2,96,384]{2,1,0:T(8,128)(2,1)S(1)} %bitcast.897), channel_id=1, source_target_pairs={{0,24},{4,28},{8,0},{12,4},{16,8},{20,12},{24,16},{28,20},{1,25},{... | collective-permute-start | bytes 442376 | tf_op jit(solution)/shard_map/ppermute | solution.py:57
  72.8 14.7 %collective-permute-start.51 = (bf16[2,96,384]{2,1,0:T(8,128)(2,1)S(1)}, bf16[2,96,384]{2,1,0:T(8,128)(2,1)S(1)}, u32[]{:S(2)}, u32[]{:S(2)}) collective-permute-start(bf16[2,96,384]{2,1,0:T(8,128)(2,1)S(1)} %bitcast.898), channel_id=1, source_target_pairs={{0,16},{4,20},{8,24},{12,28},{16,0},{20,4},{24,8},{28,12},{1,17},{... | collective-permute-start | bytes 442376 | tf_op jit(solution)/shard_map/ppermute | solution.py:57
  74.9 14.2 %collective-permute-start.52 = (bf16[2,96,384]{2,1,0:T(8,128)(2,1)S(1)}, bf16[2,96,384]{2,1,0:T(8,128)(2,1)S(1)}, u32[]{:S(2)}, u32[]{:S(2)}) collective-permute-start(bf16[2,96,384]{2,1,0:T(8,128)(2,1)S(1)} %bitcast.899), channel_id=1, source_target_pairs={{0,8},{4,12},{8,16},{12,20},{16,24},{20,28},{24,0},{28,4},{1,9},{5... | collective-permute-start | bytes 442376 | tf_op jit(solution)/shard_map/ppermute | solution.py:57
  77.9 14.2 %collective-permute-start.63 = (bf16[2,96,384]{2,1,0:T(8,128)(2,1)S(1)}, bf16[2,96,384]{2,1,0:T(8,128)(2,1)S(1)}, u32[]{:S(2)}, u32[]{:S(2)}) collective-permute-start(bf16[2,96,384]{2,1,0:T(8,128)(2,1)S(1)} %bitcast.892), channel_id=1, source_target_pairs={{0,24},{4,28},{8,0},{12,4},{16,8},{20,12},{24,16},{28,20},{1,25},{... | collective-permute-start | bytes 442376 | tf_op jit(solution)/shard_map/ppermute | solution.py:57
  82.0 17.7 %collective-permute-start.64 = (bf16[2,96,384]{2,1,0:T(8,128)(2,1)S(1)}, bf16[2,96,384]{2,1,0:T(8,128)(2,1)S(1)}, u32[]{:S(2)}, u32[]{:S(2)}) collective-permute-start(bf16[2,96,384]{2,1,0:T(8,128)(2,1)S(1)} %bitcast.893), channel_id=1, source_target_pairs={{0,16},{4,20},{8,24},{12,28},{16,0},{20,4},{24,8},{28,12},{1,17},{... | collective-permute-start | bytes 442376 | tf_op jit(solution)/shard_map/ppermute | solution.py:57
  87.5 12.8 %collective-permute-start.65 = (bf16[2,96,384]{2,1,0:T(8,128)(2,1)S(1)}, bf16[2,96,384]{2,1,0:T(8,128)(2,1)S(1)}, u32[]{:S(2)}, u32[]{:S(2)}) collective-permute-start(bf16[2,96,384]{2,1,0:T(8,128)(2,1)S(1)} %bitcast.894), channel_id=1, source_target_pairs={{0,8},{4,12},{8,16},{12,20},{16,24},{20,28},{24,0},{28,4},{1,9},{5... | collective-permute-start | bytes 442376 | tf_op jit(solution)/shard_map/ppermute | solution.py:57
  89.1 38.5 %collective-permute-start.37 = (bf16[2,96,384]{2,1,0:T(8,128)(2,1)S(1)}, bf16[2,96,384]{2,1,0:T(8,128)(2,1)S(1)}, u32[]{:S(2)}, u32[]{:S(2)}) collective-permute-start(bf16[2,96,384]{2,1,0:T(8,128)(2,1)S(1)} %bitcast.887), channel_id=1, source_target_pairs={{0,24},{4,28},{8,0},{12,4},{16,8},{20,12},{24,16},{28,20},{1,25},{... | collective-permute-start | bytes 442376 | tf_op jit(solution)/shard_map/ppermute | solution.py:57
  92.1 36.0 %collective-permute-start.38 = (bf16[2,96,384]{2,1,0:T(8,128)(2,1)S(1)}, bf16[2,96,384]{2,1,0:T(8,128)(2,1)S(1)}, u32[]{:S(2)}, u32[]{:S(2)}) collective-permute-start(bf16[2,96,384]{2,1,0:T(8,128)(2,1)S(1)} %bitcast.888), channel_id=1, source_target_pairs={{0,16},{4,20},{8,24},{12,28},{16,0},{20,4},{24,8},{28,12},{1,17},{... | collective-permute-start | bytes 442376 | tf_op jit(solution)/shard_map/ppermute | solution.py:57
  108.2 13.2 %collective-permute-start.6 = (bf16[2,2,4,48,384]{4,3,1,2,0:T(8,128)(2,1)S(1)}, bf16[2,2,4,48,384]{4,3,1,2,0:T(8,128)(2,1)S(1)}, u32[]{:S(2)}, u32[]{:S(2)}) collective-permute-start(bf16[2,2,4,48,384]{4,3,1,2,0:T(8,128)(2,1)S(1)} %pad_maximum_fusion.8), channel_id=1, source_target_pairs={{0,4},{4,0},{8,12},{12,8},{16,20},{20,16},{24,28},{28,24},{1,5},{5... | collective-permute-start | bytes 1769480 | tf_op jit(solution)/shard_map/ppermute | solution.py:52
  109.9 15.3 %collective-permute-start.4 = (bf16[2,2,4,48,384]{4,3,1,2,0:T(8,128)(2,1)S(1)}, bf16[2,2,4,48,384]{4,3,1,2,0:T(8,128)(2,1)S(1)}, u32[]{:S(2)}, u32[]{:S(2)}) collective-permute-start(bf16[2,2,4,48,384]{4,3,1,2,0:T(8,128)(2,1)S(1)} %pad_maximum_fusion.7), channel_id=1, source_target_pairs={{0,2},{1,3},{2,0},{3,1},{4,6},{5,7},{6,4},{7,5},{8,10},{9,11},{10,... | collective-permute-start | bytes 1769480 | tf_op jit(solution)/shard_map/ppermute | solution.py:57
  127.6 24.6 %collective-permute-start.17 = (bf16[4,4,48,384]{3,2,0,1:T(8,128)(2,1)}, bf16[4,4,48,384]{3,2,0,1:T(8,128)(2,1)}, u32[]{:S(2)}, u32[]{:S(2)}) collective-permute-start(bf16[4,4,48,384]{3,2,0,1:T(8,128)(2,1)} %constant_dynamic-slice_fusion.1), channel_id=1, source_target_pairs={{0,4},{4,0},{8,12},{12,8},{16,20},{20,16},{24,28},{28,24},{1,5},{5... | collective-permute-start | bytes 1769480 | tf_op jit(solution)/shard_map/ppermute | solution.py:52
  128.2 29.9 %collective-permute-start.13 = (bf16[4,4,48,384]{3,2,0,1:T(8,128)(2,1)}, bf16[4,4,48,384]{3,2,0,1:T(8,128)(2,1)}, u32[]{:S(2)}, u32[]{:S(2)}) collective-permute-start(bf16[4,4,48,384]{3,2,0,1:T(8,128)(2,1)} %constant_dynamic-slice_fusion.2), channel_id=1, source_target_pairs={{0,4},{4,0},{8,12},{12,8},{16,20},{20,16},{24,28},{28,24},{1,5},{5... | collective-permute-start | bytes 1769480 | tf_op jit(solution)/shard_map/ppermute | solution.py:52
  131.8 30.1 %collective-permute-start.21 = (bf16[2,160,768]{2,1,0:T(8,128)(2,1)}, bf16[2,160,768]{2,1,0:T(8,128)(2,1)}, u32[]{:S(2)}, u32[]{:S(2)}) collective-permute-start(bf16[2,160,768]{2,1,0:T(8,128)(2,1)} %pad_maximum_fusion.14), channel_id=1, source_target_pairs={{0,2},{1,3},{2,0},{3,1},{4,6},{5,7},{6,4},{7,5},{8,10},{9,11},{10,... | collective-permute-start | bytes 1474568 | tf_op jit(solution)/shard_map/ppermute | solution.py:57
  157.6 13.4 %collective-permute-start.9 = (bf16[2,160,768]{2,1,0:T(8,128)(2,1)}, bf16[2,160,768]{2,1,0:T(8,128)(2,1)}, u32[]{:S(2)}, u32[]{:S(2)}) collective-permute-start(bf16[2,160,768]{2,1,0:T(8,128)(2,1)} %pad_maximum_fusion.13), channel_id=1, source_target_pairs={{0,2},{1,3},{2,0},{3,1},{4,6},{5,7},{6,4},{7,5},{8,10},{9,11},{10,... | collective-permute-start | bytes 1474568 | tf_op jit(solution)/shard_map/ppermute | solution.py:57
  186.4 21.8 %collective-permute-start.18 = (bf16[2,160,768]{2,1,0:T(8,128)(2,1)}, bf16[2,160,768]{2,1,0:T(8,128)(2,1)}, u32[]{:S(2)}, u32[]{:S(2)}) collective-permute-start(bf16[2,160,768]{2,1,0:T(8,128)(2,1)} %slice_bitcast_fusion.4), channel_id=1, source_target_pairs={{0,1},{1,0},{2,3},{3,2},{4,5},{5,4},{6,7},{7,6},{8,9},{9,8},{10,11... | collective-permute-start | bytes 1474568 | tf_op jit(solution)/shard_map/ppermute | solution.py:52
  189.1 20.8 %collective-permute-start.22 = (bf16[2,160,768]{2,1,0:T(8,128)(2,1)}, bf16[2,160,768]{2,1,0:T(8,128)(2,1)}, u32[]{:S(2)}, u32[]{:S(2)}) collective-permute-start(bf16[2,160,768]{2,1,0:T(8,128)(2,1)} %slice_bitcast_fusion.1), channel_id=1, source_target_pairs={{0,1},{1,0},{2,3},{3,2},{4,5},{5,4},{6,7},{7,6},{8,9},{9,8},{10,11... | collective-permute-start | bytes 1474568 | tf_op jit(solution)/shard_map/ppermute | solution.py:52
  197.9 16.5 %collective-permute-start.54 = (bf16[2,384,384]{2,1,0:T(8,128)(2,1)}, bf16[2,384,384]{2,1,0:T(8,128)(2,1)}, u32[]{:S(2)}, u32[]{:S(2)}) collective-permute-start(bf16[2,384,384]{2,1,0:T(8,128)(2,1)} %dynamic-slice_bitcast_fusion.3), channel_id=1, source_target_pairs={{0,4},{4,0},{8,12},{12,8},{16,20},{20,16},{24,28},{28,24},{1,5},{5... | collective-permute-start | bytes 1769480 | tf_op jit(solution)/shard_map/ppermute | solution.py:52
  206.6 19.3 %collective-permute-start.41 = (bf16[2,384,384]{2,1,0:T(8,128)(2,1)S(1)}, bf16[2,384,384]{2,1,0:T(8,128)(2,1)S(1)}, u32[]{:S(2)}, u32[]{:S(2)}) collective-permute-start(bf16[2,384,384]{2,1,0:T(8,128)(2,1)S(1)} %dynamic-slice_bitcast_fusion.6), channel_id=1, source_target_pairs={{0,4},{4,0},{8,12},{12,8},{16,20},{20,16},{24,28},{28,24},{1,5},{5... | collective-permute-start | bytes 1769480 | tf_op jit(solution)/shard_map/ppermute | solution.py:52
  209.3 21.8 %collective-permute-start.19 = (bf16[160,768]{1,0:T(8,128)(2,1)S(1)}, bf16[160,768]{1,0:T(8,128)(2,1)S(1)}, u32[]{:S(2)}, u32[]{:S(2)}) collective-permute-start(bf16[160,768]{1,0:T(8,128)(2,1)S(1)} %fusion.136), channel_id=1, source_target_pairs={{0,2},{1,3},{2,0},{3,1},{4,6},{5,7},{6,4},{7,5},{8,10},{9,11},{10,... | collective-permute-start | bytes 737288 | tf_op jit(solution)/shard_map/ppermute | solution.py:57
  211.1 17.5 %collective-permute-start.23 = (bf16[160,768]{1,0:T(8,128)(2,1)S(1)}, bf16[160,768]{1,0:T(8,128)(2,1)S(1)}, u32[]{:S(2)}, u32[]{:S(2)}) collective-permute-start(bf16[160,768]{1,0:T(8,128)(2,1)S(1)} %fusion.137), channel_id=1, source_target_pairs={{0,2},{1,3},{2,0},{3,1},{4,6},{5,7},{6,4},{7,5},{8,10},{9,11},{10,... | collective-permute-start | bytes 737288 | tf_op jit(solution)/shard_map/ppermute | solution.py:57
  216.5 46.1 %collective-permute-start.55 = (bf16[2,96,384]{2,1,0:T(8,128)(2,1)}, bf16[2,96,384]{2,1,0:T(8,128)(2,1)}, u32[]{:S(2)}, u32[]{:S(2)}) collective-permute-start(bf16[2,96,384]{2,1,0:T(8,128)(2,1)} %get-tuple-element.163), channel_id=1, source_target_pairs={{0,8},{4,12},{8,16},{12,20},{16,24},{20,28},{24,0},{28,4},{1,9},{5... | collective-permute-start | bytes 442376 | tf_op jit(solution)/shard_map/ppermute | solution.py:57
  218.9 46.5 %collective-permute-start.56 = (bf16[2,96,384]{2,1,0:T(8,128)(2,1)}, bf16[2,96,384]{2,1,0:T(8,128)(2,1)}, u32[]{:S(2)}, u32[]{:S(2)}) collective-permute-start(bf16[2,96,384]{2,1,0:T(8,128)(2,1)} %get-tuple-element.165), channel_id=1, source_target_pairs={{0,16},{4,20},{8,24},{12,28},{16,0},{20,4},{24,8},{28,12},{1,17},{... | collective-permute-start | bytes 442376 | tf_op jit(solution)/shard_map/ppermute | solution.py:57
  225.9 39.5 %collective-permute-start.57 = (bf16[2,96,384]{2,1,0:T(8,128)(2,1)}, bf16[2,96,384]{2,1,0:T(8,128)(2,1)}, u32[]{:S(2)}, u32[]{:S(2)}) collective-permute-start(bf16[2,96,384]{2,1,0:T(8,128)(2,1)} %get-tuple-element.164), channel_id=1, source_target_pairs={{0,24},{4,28},{8,0},{12,4},{16,8},{20,12},{24,16},{28,20},{1,25},{... | collective-permute-start | bytes 442376 | tf_op jit(solution)/shard_map/ppermute | solution.py:57
  228.6 40.8 %collective-permute-start.42 = (bf16[2,96,384]{2,1,0:T(8,128)(2,1)}, bf16[2,96,384]{2,1,0:T(8,128)(2,1)}, u32[]{:S(2)}, u32[]{:S(2)}) collective-permute-start(bf16[2,96,384]{2,1,0:T(8,128)(2,1)} %get-tuple-element.166), channel_id=1, source_target_pairs={{0,8},{4,12},{8,16},{12,20},{16,24},{20,28},{24,0},{28,4},{1,9},{5... | collective-permute-start | bytes 442376 | tf_op jit(solution)/shard_map/ppermute | solution.py:57
  231.1 40.2 %collective-permute-start.43 = (bf16[2,96,384]{2,1,0:T(8,128)(2,1)}, bf16[2,96,384]{2,1,0:T(8,128)(2,1)}, u32[]{:S(2)}, u32[]{:S(2)}) collective-permute-start(bf16[2,96,384]{2,1,0:T(8,128)(2,1)} %get-tuple-element.168), channel_id=1, source_target_pairs={{0,16},{4,20},{8,24},{12,28},{16,0},{20,4},{24,8},{28,12},{1,17},{... | collective-permute-start | bytes 442376 | tf_op jit(solution)/shard_map/ppermute | solution.py:57
  266.7 16.4 %collective-permute-start.58 = (bf16[2,96,384]{2,1,0:T(8,128)(2,1)S(1)}, bf16[2,96,384]{2,1,0:T(8,128)(2,1)S(1)}, u32[]{:S(2)}, u32[]{:S(2)}) collective-permute-start(bf16[2,96,384]{2,1,0:T(8,128)(2,1)S(1)} %get-tuple-element.113), channel_id=1, source_target_pairs={{0,24},{4,28},{8,0},{12,4},{16,8},{20,12},{24,16},{28,20},{1,25},{... | collective-permute-start | bytes 442376 | tf_op jit(solution)/shard_map/ppermute | solution.py:57
  268.7 16.3 %collective-permute-start.59 = (bf16[2,96,384]{2,1,0:T(8,128)(2,1)S(1)}, bf16[2,96,384]{2,1,0:T(8,128)(2,1)S(1)}, u32[]{:S(2)}, u32[]{:S(2)}) collective-permute-start(bf16[2,96,384]{2,1,0:T(8,128)(2,1)S(1)} %get-tuple-element.113), channel_id=1, source_target_pairs={{0,16},{4,20},{8,24},{12,28},{16,0},{20,4},{24,8},{28,12},{1,17},{... | collective-permute-start | bytes 442376 | tf_op jit(solution)/shard_map/ppermute | solution.py:57
  269.4 15.7 %collective-permute-start.60 = (bf16[2,96,384]{2,1,0:T(8,128)(2,1)S(1)}, bf16[2,96,384]{2,1,0:T(8,128)(2,1)S(1)}, u32[]{:S(2)}, u32[]{:S(2)}) collective-permute-start(bf16[2,96,384]{2,1,0:T(8,128)(2,1)S(1)} %get-tuple-element.113), channel_id=1, source_target_pairs={{0,8},{4,12},{8,16},{12,20},{16,24},{20,28},{24,0},{28,4},{1,9},{5... | collective-permute-start | bytes 442376 | tf_op jit(solution)/shard_map/ppermute | solution.py:57
  275.5 15.9 %collective-permute-start.45 = (bf16[2,96,384]{2,1,0:T(8,128)(2,1)S(1)}, bf16[2,96,384]{2,1,0:T(8,128)(2,1)}, u32[]{:S(2)}, u32[]{:S(2)}) collective-permute-start(bf16[2,96,384]{2,1,0:T(8,128)(2,1)S(1)} %get-tuple-element.117), channel_id=1, source_target_pairs={{0,24},{4,28},{8,0},{12,4},{16,8},{20,12},{24,16},{28,20},{1,25},{... | collective-permute-start | bytes 442376 | tf_op jit(solution)/shard_map/ppermute | solution.py:57
  282.0 14.5 %collective-permute-start.46 = (bf16[2,96,384]{2,1,0:T(8,128)(2,1)S(1)}, bf16[2,96,384]{2,1,0:T(8,128)(2,1)}, u32[]{:S(2)}, u32[]{:S(2)}) collective-permute-start(bf16[2,96,384]{2,1,0:T(8,128)(2,1)S(1)} %get-tuple-element.117), channel_id=1, source_target_pairs={{0,16},{4,20},{8,24},{12,28},{16,0},{20,4},{24,8},{28,12},{1,17},{... | collective-permute-start | bytes 442376 | tf_op jit(solution)/shard_map/ppermute | solution.py:57
  283.0 16.6 %collective-permute-start.47 = (bf16[2,96,384]{2,1,0:T(8,128)(2,1)S(1)}, bf16[2,96,384]{2,1,0:T(8,128)(2,1)}, u32[]{:S(2)}, u32[]{:S(2)}) collective-permute-start(bf16[2,96,384]{2,1,0:T(8,128)(2,1)S(1)} %get-tuple-element.117), channel_id=1, source_target_pairs={{0,8},{4,12},{8,16},{12,20},{16,24},{20,28},{24,0},{28,4},{1,9},{5... | collective-permute-start | bytes 442376 | tf_op jit(solution)/shard_map/ppermute | solution.py:57
  285.0 39.8 %collective-permute-start.24 = (bf16[2,4,384,384]{3,2,1,0:T(8,128)(2,1)}, bf16[2,4,384,384]{3,2,1,0:T(8,128)(2,1)S(1)}, u32[]{:S(2)}, u32[]{:S(2)}) collective-permute-start(bf16[2,4,384,384]{3,2,1,0:T(8,128)(2,1)} %dynamic-slice_bitcast_fusion), channel_id=1, source_target_pairs={{0,1},{1,0},{2,3},{3,2},{4,5},{5,4},{6,7},{7,6},{8,9},{9,8},{10,11... | collective-permute-start | bytes 7077896 | tf_op jit(solution)/shard_map/ppermute | solution.py:52
  285.1 37.1 %collective-permute-start.82 = (f32[13,768]{1,0:T(8,128)}, f32[13,768]{1,0:T(8,128)}, u32[]{:S(2)}, u32[]{:S(2)}) collective-permute-start(f32[13,768]{1,0:T(8,128)} %add.533), channel_id=1, source_target_pairs={{0,8},{4,12},{8,16},{12,20},{16,24},{20,28},{24,0},{28,4},{1,9},{5... | collective-permute-start | bytes 119816 | tf_op jit(solution)/shard_map/ppermute | solution.py:57
  291.4 30.8 %collective-permute-start.83 = (f32[13,768]{1,0:T(8,128)}, f32[13,768]{1,0:T(8,128)}, u32[]{:S(2)}, u32[]{:S(2)}) collective-permute-start(f32[13,768]{1,0:T(8,128)} %add.533), channel_id=1, source_target_pairs={{0,16},{4,20},{8,24},{12,28},{16,0},{20,4},{24,8},{28,12},{1,17},{... | collective-permute-start | bytes 119816 | tf_op jit(solution)/shard_map/ppermute | solution.py:57
  296.5 25.7 %collective-permute-start.84 = (f32[13,768]{1,0:T(8,128)}, f32[13,768]{1,0:T(8,128)}, u32[]{:S(2)}, u32[]{:S(2)}) collective-permute-start(f32[13,768]{1,0:T(8,128)} %add.533), channel_id=1, source_target_pairs={{0,24},{4,28},{8,0},{12,4},{16,8},{20,12},{24,16},{28,20},{1,25},{... | collective-permute-start | bytes 119816 | tf_op jit(solution)/shard_map/ppermute | solution.py:57
  327.4 12.8 %collective-permute-start.25 = (bf16[2,2,192,384]{3,2,1,0:T(8,128)(2,1)S(1)}, bf16[2,2,192,384]{3,2,1,0:T(8,128)(2,1)S(1)}, u32[]{:S(2)}, u32[]{:S(2)}) collective-permute-start(bf16[2,2,192,384]{3,2,1,0:T(8,128)(2,1)S(1)} %dynamic-slice_bitcast_fusion.10), channel_id=1, source_target_pairs={{0,4},{4,0},{8,12},{12,8},{16,20},{20,16},{24,28},{28,24},{1,5},{5... | collective-permute-start | bytes 1769480 | tf_op jit(solution)/shard_map/ppermute | solution.py:52
  381.4 17.9 %collective-permute-start.53 = (bf16[4,2,48,384]{3,2,1,0:T(8,128)(2,1)S(1)}, bf16[4,2,48,384]{3,2,1,0:T(8,128)(2,1)S(1)}, u32[]{:S(2)}, u32[]{:S(2)}) collective-permute-start(bf16[4,2,48,384]{3,2,1,0:T(8,128)(2,1)S(1)} %dynamic-slice_bitcast_fusion.12), channel_id=1, source_target_pairs={{0,4},{4,0},{8,12},{12,8},{16,20},{20,16},{24,28},{28,24},{1,5},{5... | collective-permute-start | bytes 884744 | tf_op jit(solution)/shard_map/ppermute | solution.py:52
  384.2 16.1 %collective-permute-start.40 = (bf16[4,2,48,384]{3,2,1,0:T(8,128)(2,1)S(1)}, bf16[4,2,48,384]{3,2,1,0:T(8,128)(2,1)S(1)}, u32[]{:S(2)}, u32[]{:S(2)}) collective-permute-start(bf16[4,2,48,384]{3,2,1,0:T(8,128)(2,1)S(1)} %dynamic-slice_bitcast_fusion.13), channel_id=1, source_target_pairs={{0,4},{4,0},{8,12},{12,8},{16,20},{20,16},{24,28},{28,24},{1,5},{5... | collective-permute-start | bytes 884744 | tf_op jit(solution)/shard_map/ppermute | solution.py:52
  (149 other events, 1096.8 us)

commit v2 on v1

--- a/solution.py
+++ b/solution.py
@@ -1,6 +1,8 @@
 import jax
 import jax.numpy as jnp
 from jax import lax
+from jax.experimental import pallas as pl
+from jax.experimental.pallas import tpu as pltpu
 from jax.sharding import PartitionSpec as P
 
 D = 768
@@ -306,7 +308,7 @@
     return values
 
 
-def body(
+def body_plain(
     tokens,
     keep_mask,
     cotangent,
@@ -483,6 +485,961 @@
     )
 
 
+def normalized(values):
+    centered = values - jnp.mean(values, axis=-1, keepdims=True)
+    variance = jnp.mean(centered * centered, axis=-1, keepdims=True)
+    scale = lax.rsqrt(variance + 1e-06)
+    return centered * scale, scale
+
+
+def norm_back(grad_hat, hat, scale):
+    first = jnp.mean(grad_hat, axis=-1, keepdims=True)
+    second = jnp.mean(grad_hat * hat, axis=-1, keepdims=True)
+    return scale * (grad_hat - first - hat * second)
+
+
+def col_sum(values):
+    return jnp.sum(values, axis=0, keepdims=True)
+
+
+def shape(dims, kind=half):
+    return jax.ShapeDtypeStruct(dims, kind)
+
+
+def local_call(kernel, args, outs, scratch=(), in_hbm=(), out_hbm=(), in_smem=(0,), mib=12, micros=1):
+    def place_of(index, hbm, smem):
+        if index in hbm:
+            return pl.BlockSpec(memory_space=pltpu.HBM)
+        if index in smem:
+            return pl.BlockSpec(memory_space=pltpu.SMEM)
+        return pl.BlockSpec(memory_space=pltpu.VMEM)
+
+    moved = sum(v.size * v.dtype.itemsize for v in list(args) + list(outs))
+    return pl.pallas_call(
+        kernel,
+        out_shape=list(outs),
+        in_specs=[place_of(i, in_hbm, in_smem) for i in range(len(args))],
+        out_specs=[place_of(i, out_hbm, ()) for i in range(len(outs))],
+        scratch_shapes=list(scratch),
+        compiler_params=pltpu.CompilerParams(vmem_limit_bytes=mib * 2**20),
+        cost_estimate=pl.CostEstimate(
+            flops=int(micros * 1e9), bytes_accessed=moved, transcendentals=0
+        ),
+    )(*args)
+
+
+def gate_of(tokens, vec_ref):
+    return jax.nn.sigmoid(jnp.sum(tokens * vec_ref[8:9, :], axis=-1, keepdims=True))
+
+
+def keep_of(chosen):
+    ones = jnp.ones((chosen.shape[0], 128), half)
+    return row_product(chosen, ones)[:, :1]
+
+
+def prepare_kernel(mask_ref, tok_ref, cot_ref, vec_ref, normed_ref, grad_ref, chosen_ref):
+    rows = tok_ref.shape[0]
+    tokens = tok_ref[...].astype(full)
+    hat, _ = normalized(tokens)
+    normed_ref[...] = to_half(hat * vec_ref[0:1, :] + vec_ref[1:2, :])
+    mask = mask_ref[...].astype(full)
+    upper = lax.broadcasted_iota(jnp.int32, (rows, rows), 0) <= lax.broadcasted_iota(
+        jnp.int32, (rows, rows), 1
+    )
+    count = dot32(
+        to_half(jnp.broadcast_to(mask, (16, rows))), jnp.where(upper, 1.0, 0.0).astype(half)
+    )
+    slot = count[0:1, :] - 1.0
+    wanted = lax.broadcasted_iota(jnp.int32, (SLOTS, rows), 0).astype(full)
+    chosen = jnp.where((slot == wanted) & (mask > 0.0), 1.0, 0.0).astype(half)
+    chosen_ref[...] = chosen
+    scale = keep_of(chosen) * gate_of(tokens, vec_ref)
+    grad_feed = to_half(scale * cot_ref[...].astype(full))
+    grad_ref[...] = to_half(dot32(chosen, grad_feed))
+
+
+def head_parts(values):
+    lane = lax.broadcasted_iota(jnp.int32, values.shape, 1)
+    first = lane < values.shape[1] // 2
+    zero = jnp.zeros_like(values)
+    return jnp.where(first, values, zero), jnp.where(first, zero, values)
+
+
+def copy_all(copies):
+    for copy in copies:
+        copy.start()
+    for copy in copies:
+        copy.wait()
+
+
+def forward_kernel(order, pieces, place_ref, *refs):
+    piece_refs, refs = refs[: len(pieces)], refs[len(pieces) :]
+    normed_ref, tok_ref, mask_ref, chosen_ref, vec_ref = refs[:5]
+    rows_ref, qkv_ref, probs_ref, attended_ref, branch_ref, weights_hbm = refs[5:11]
+    weights, probs_all, sems, out_sem, probs_sems = refs[11:]
+    z, x, m = place_ref[0], place_ref[1], place_ref[2]
+    local, piece = piece_refs[0].shape[1], piece_refs[0].shape[2]
+    copies = []
+    for ref, (slots, dx, dm) in zip(piece_refs, pieces):
+        for index, slot in enumerate(slots):
+            row = pl.multiple_of(((z ^ slot) * PAIR + (x ^ dx)) * piece, 16)
+            target = weights.at[pl.ds((m ^ dm) * local, local), pl.ds(row, piece), :]
+            copies.append(pltpu.make_async_copy(ref.at[index], target, sems.at[len(copies)]))
+    copy_all(copies)
+    keep_whole = pltpu.make_async_copy(weights, weights_hbm, out_sem)
+    keep_whole.start()
+    width = normed_ref.shape[1]
+    row_blocks = width // order
+    normed = normed_ref[...]
+    for col in range(3 * row_blocks):
+        part = jnp.zeros((normed.shape[0], order), full)
+        for row in range(row_blocks):
+            part = part + dot32(
+                normed[:, row * order : (row + 1) * order], weights[col * row_blocks + row]
+            )
+        kind, start = col // row_blocks, (col % row_blocks) * order
+        if kind != 1:
+            bias_row = 4 if kind == 0 else 5
+            part = part + vec_ref[bias_row : bias_row + 1, start : start + order]
+        qkv_ref[:, col * order : (col + 1) * order] = to_half(part)
+    keep_probs = []
+    head = width // HEADS
+    scale = head ** (-0.5)
+    allowed = mask_ref[...] > 0
+    for slab in range(width // (2 * head)):
+        lanes = slice(slab * 2 * head, (slab + 1) * 2 * head)
+        queries = head_parts(qkv_ref[:, lanes])
+        keys = qkv_ref[:, width + lanes.start : width + lanes.stop]
+        values = head_parts(qkv_ref[:, 2 * width + lanes.start : 2 * width + lanes.stop])
+        total = None
+        for index in range(2):
+            scores = times_transpose(queries[index], keys) * scale
+            scores = jnp.where(allowed, scores, masked_score)
+            raised = jnp.exp(scores - jnp.max(scores, axis=-1, keepdims=True))
+            probs = raised / jnp.sum(raised, axis=-1, keepdims=True)
+            probs_all[2 * slab + index] = probs
+            part = dot32(to_half(probs), values[index])
+            total = part if total is None else total + part
+        attended_ref[:, lanes] = to_half(total)
+        pair = pl.ds(2 * slab, 2)
+        keep_probs.append(
+            pltpu.make_async_copy(probs_all.at[pair], probs_ref.at[pair], probs_sems.at[slab])
+        )
+        keep_probs[-1].start()
+    attended = attended_ref[...]
+    for col in range(row_blocks):
+        part = jnp.zeros((normed.shape[0], order), full)
+        for row in range(row_blocks):
+            part = part + dot32(
+                attended[:, row * order : (row + 1) * order],
+                weights[(3 * row_blocks + col) * row_blocks + row],
+            )
+        lanes = slice(col * order, (col + 1) * order)
+        branch_ref[:, lanes] = part + vec_ref[6:7, lanes]
+    hat, _ = normalized(tok_ref[...].astype(full) + branch_ref[...])
+    second = to_half(hat * vec_ref[2:3, :] + vec_ref[3:4, :])
+    rows_ref[...] = to_half(dot32(chosen_ref[...], second))
+    keep_whole.wait()
+    for copy in keep_probs:
+        copy.wait()
+
+
+def bias_row(m, values, count):
+    row = lax.broadcasted_iota(jnp.int32, (count, values.shape[1]), 0)
+    return jnp.where(row == m, values, 0.0)
+
+
+def gelu_parts(values):
+    cdf = 0.5 * (1.0 + lax.erf(values * 0.7071067811865476))
+    density = jnp.exp(-0.5 * values * values) * 0.3989422804014327
+    return values * cdf, cdf + values * density
+
+
+def hidden_kernel(order, group, pieces, place_ref, *refs):
+    piece_refs, refs = refs[: len(pieces)], refs[len(pieces) :]
+    row_refs, refs = refs[:group], refs[group:]
+    grad_refs, refs = refs[:group], refs[group:]
+    vec_ref = refs[0]
+    back_refs, refs = refs[1 : 1 + group], refs[1 + group :]
+    rows_ref, grads_ref, active_ref, hidden_ref, down_hbm = refs[:5]
+    weights, sems, out_sem = refs[5:]
+    z, x, m = place_ref[0], place_ref[1], place_ref[2]
+    piece = piece_refs[0].shape[2]
+    bias = jnp.sum(bias_row(m, vec_ref[9:, :], vec_ref.shape[0] - 9), axis=0, keepdims=True)
+    copies = []
+    for ref, (slots, dx) in zip(piece_refs, pieces):
+        for index, slot in enumerate(slots):
+            row = pl.multiple_of(((z ^ slot) * PAIR + (x ^ dx)) * piece, 16)
+            target = weights.at[:, pl.ds(row, piece), :]
+            copies.append(pltpu.make_async_copy(ref.at[index], target, sems.at[len(copies)]))
+    for copy in copies:
+        copy.start()
+    count = row_refs[0].shape[0]
+    for index in range(group):
+        rows_ref[index * count : (index + 1) * count, :] = row_refs[index][...]
+        grads_ref[index * count : (index + 1) * count, :] = grad_refs[index][...]
+    for copy in copies:
+        copy.wait()
+    local = weights.shape[0] // 2
+    keep_down = pltpu.make_async_copy(weights.at[pl.ds(local, local)], down_hbm, out_sem)
+    keep_down.start()
+    row_blocks = rows_ref.shape[1] // order
+    for col in range(local // row_blocks):
+        lanes = slice(col * order, (col + 1) * order)
+        hidden = bias[:, lanes]
+        for row in range(row_blocks):
+            hidden = hidden + dot32(
+                rows_ref[:, row * order : (row + 1) * order], weights[col * row_blocks + row]
+            )
+        active, slope = gelu_parts(hidden)
+        active_ref[:, lanes] = to_half(active)
+        grad = jnp.zeros_like(slope)
+        for row in range(row_blocks):
+            grad = grad + times_transpose(
+                grads_ref[:, row * order : (row + 1) * order],
+                weights[local + col * row_blocks + row],
+            )
+        hidden_ref[:, lanes] = to_half(grad * slope)
+    for row in range(row_blocks):
+        total = None
+        for col in range(local // row_blocks):
+            part = times_transpose(
+                hidden_ref[:, col * order : (col + 1) * order], weights[col * row_blocks + row]
+            )
+            total = part if total is None else total + part
+        for index in range(group):
+            back_refs[index][:, row * order : (row + 1) * order] = to_half(
+                total[index * count : (index + 1) * count, :]
+            )
+    keep_down.wait()
+
+
+def share_blocks(place_ref, blocks, kept_ref, sent_ref):
+    own, x = kept_ref.shape[0], place_ref[1]
+    kept_ref[...] = blocks[pl.ds(x * own, own)]
+    sent_ref[...] = blocks[pl.ds((1 - x) * own, own)]
+
+
+def up_grads_kernel(order, place_ref, rows_ref, hidden_ref, kept_ref, sent_ref, bias_ref, blocks):
+    row_blocks = rows_ref.shape[1] // order
+    for col in range(blocks.shape[0] // row_blocks):
+        lanes = slice(col * order, (col + 1) * order)
+        for row in range(row_blocks):
+            others = slice(row * order, (row + 1) * order)
+            blocks[col * row_blocks + row] = to_half(
+                row_product(rows_ref[:, others], hidden_ref[:, lanes])
+            )
+    share_blocks(place_ref, blocks, kept_ref, sent_ref)
+    bias_ref[...] = col_sum(hidden_ref[...].astype(full))
+
+
+def down_grads_kernel(order, group, place_ref, grads_ref, active_ref, down_ref, *refs):
+    feed_refs, (kept_ref, sent_ref, blocks) = refs[:group], refs[group:]
+    count = grads_ref.shape[0] // group
+    row_blocks = grads_ref.shape[1] // order
+    col_blocks = down_ref.shape[0] // row_blocks
+    for row in range(row_blocks):
+        total = None
+        for col in range(col_blocks):
+            part = dot32(
+                active_ref[:, col * order : (col + 1) * order], down_ref[col * row_blocks + row]
+            )
+            total = part if total is None else total + part
+        for index in range(group):
+            feed_refs[index][:, row * order : (row + 1) * order] = to_half(
+                total[index * count : (index + 1) * count, :]
+            )
+    for col in range(col_blocks):
+        lanes = slice(col * order, (col + 1) * order)
+        for row in range(row_blocks):
+            others = slice(row * order, (row + 1) * order)
+            blocks[col * row_blocks + row] = to_half(
+                row_product(active_ref[:, lanes], grads_ref[:, others])
+            )
+    share_blocks(place_ref, blocks, kept_ref, sent_ref)
+
+
+def backward_kernel(order, group, place_ref, *refs):
+    back_refs, refs = refs[:group], refs[group:]
+    chosen_ref, tok_ref, cot_ref, branch_ref, vec_ref = refs[:5]
+    qkv_ref, probs_ref, attended_ref, normed_ref, weights_hbm = refs[5:10]
+    kept_ref, sent_ref, mixed_ref, middle_ref, sums_ref = refs[10:15]
+    weights, left, right, grad_attended, probs_all, sem, probs_sem = refs[15:]
+    width = tok_ref.shape[1]
+    row_blocks = width // order
+    local = weights.shape[0]
+    fetch = pltpu.make_async_copy(weights_hbm.at[pl.ds(3 * local, local)], weights, sem)
+    fetch.start()
+    fetch_probs = pltpu.make_async_copy(probs_ref, probs_all, probs_sem)
+    fetch_probs.start()
+    chosen = chosen_ref[...]
+    arrived = back_refs[0][...].astype(full)
+    for ref in back_refs[1:]:
+        arrived = arrived + ref[...].astype(full)
+    high = to_half(arrived)
+    low = to_half(arrived - high.astype(full))
+    grad_second = row_product(chosen, high) + row_product(chosen, low)
+    tokens = tok_ref[...].astype(full)
+    hat, scale = normalized(tokens + branch_ref[...])
+    grad_middle = norm_back(grad_second * vec_ref[2:3, :], hat, scale)
+    middle_ref[...] = grad_middle
+    change = keep_of(chosen) * gate_of(tokens, vec_ref) * cot_ref[...].astype(full)
+    grad_branch = to_half(change + grad_middle)
+    sums_ref[0:1, :] = col_sum(grad_second * hat)
+    sums_ref[1:2, :] = col_sum(grad_second)
+    sums_ref[2:3, :] = col_sum(grad_branch.astype(full))
+    sums_ref[3:4, :] = col_sum(to_half(change).astype(full))
+    left[0] = normed_ref[...]
+    left[1] = attended_ref[...]
+    right[3] = grad_branch
+    fetch.wait()
+    for row in range(row_blocks):
+        total = None
+        for col in range(row_blocks):
+            part = times_transpose(
+                grad_branch[:, col * order : (col + 1) * order], weights[col * row_blocks + row]
+            )
+            total = part if total is None else total + part
+        grad_attended[:, row * order : (row + 1) * order] = to_half(total)
+    fetch_probs.wait()
+    head = width // HEADS
+    factor = head ** (-0.5)
+    for slab in range(width // (2 * head)):
+        start, stop = slab * 2 * head, (slab + 1) * 2 * head
+        queries = head_parts(qkv_ref[:, start:stop])
+        key_pair = qkv_ref[:, width + start : width + stop]
+        keys = head_parts(key_pair)
+        values = qkv_ref[:, 2 * width + start : 2 * width + stop]
+        grads = head_parts(grad_attended[:, start:stop])
+        sums = [None] * 3
+        for index in range(2):
+            probs = probs_all[2 * slab + index]
+            grad_probs = times_transpose(grads[index], values)
+            inner = jnp.sum(probs * grad_probs, axis=-1, keepdims=True)
+            grad_scores = to_half(probs * (grad_probs - inner))
+            parts = (
+                dot32(grad_scores, keys[index]),
+                row_product(grad_scores, queries[index]),
+                row_product(to_half(probs), grads[index]),
+            )
+            sums = [p if s is None else s + p for s, p in zip(sums, parts)]
+        right[0, :, start:stop] = to_half(sums[0] * factor)
+        right[1, :, start:stop] = to_half(sums[1] * factor)
+        right[2, :, start:stop] = to_half(sums[2])
+    for kind in range(3):
+        mixed_ref[:, kind * width : (kind + 1) * width] = right[kind]
+    core = place_ref[3]
+    for high_part in range(kept_ref.shape[0]):
+        for target, low_part in ((kept_ref, core), (sent_ref, 1 - core)):
+            kind = high_part * PAIR + low_part
+            rows = left[kind // 3]
+            cols = right[kind]
+            for col in range(row_blocks):
+                for row in range(row_blocks):
+                    target[high_part, col * row_blocks + row] = to_half(
+                        row_product(
+                            rows[:, row * order : (row + 1) * order],
+                            cols[:, col * order : (col + 1) * order],
+                        )
+                    )
+
+
+def input_kernel(order, group, *refs):
+    feed_refs, refs = refs[:group], refs[group:]
+    mixed_ref, middle_ref, tok_ref, cot_ref, chosen_ref, vec_ref, branch_ref, weights_hbm = refs[:8]
+    out_ref, grad_ref, sums_ref, weights, sem = refs[8:]
+    width = tok_ref.shape[1]
+    row_blocks = width // order
+    fetch = pltpu.make_async_copy(weights_hbm.at[pl.ds(0, weights.shape[0])], weights, sem)
+    fetch.start()
+    patches = out_ref.shape[0]
+    chosen = chosen_ref[...]
+    tokens = tok_ref[...].astype(full)
+    cotangent = cot_ref[...].astype(full)
+    arrived = feed_refs[0][...].astype(full)
+    for ref in feed_refs[1:]:
+        arrived = arrived + ref[...].astype(full)
+    high = to_half(arrived)
+    low = to_half(arrived - high.astype(full))
+    feed = row_product(chosen, high) + row_product(chosen, low) + vec_ref[7:8, :]
+    change = branch_ref[...] + feed
+    gate = gate_of(tokens, vec_ref)
+    keep = keep_of(chosen)
+    out_ref[...] = to_half(tokens + keep * gate * change)[:patches]
+    logit = keep * gate * (1.0 - gate) * jnp.sum(cotangent * change, axis=-1, keepdims=True)
+    base = cotangent + middle_ref[...] + logit * vec_ref[8:9, :]
+    sums_ref[4:5, :] = col_sum(logit * tokens)
+    sums_ref[2:3, :] = col_sum(mixed_ref[:, :width].astype(full))
+    sums_ref[3:4, :] = col_sum(mixed_ref[:, 2 * width :].astype(full))
+    hat, scale = normalized(tokens)
+    fetch.wait()
+    parts = []
+    for row in range(row_blocks):
+        total = None
+        for col in range(3 * row_blocks):
+            part = times_transpose(
+                mixed_ref[:, col * order : (col + 1) * order], weights[col * row_blocks + row]
+            )
+            total = part if total is None else total + part
+        parts.append(total)
+    grad_normed = jnp.concatenate(parts, axis=1)
+    sums_ref[0:1, :] = col_sum(grad_normed * hat)
+    sums_ref[1:2, :] = col_sum(grad_normed)
+    grad = base + norm_back(grad_normed * vec_ref[0:1, :], hat, scale)
+    grad_ref[...] = grad[:patches]
+
+
+def core_sum_kernel(place_ref, kept_ref, came_ref, *out_refs):
+    x, m = place_ref[1], place_ref[2]
+    own = kept_ref.shape[1] // PAIR
+    for index, out_ref in enumerate(out_refs):
+        dy, dx = index // PAIR, index % PAIR
+        high = (m // PAIR) ^ dy
+        for block in range(own):
+            at = (x ^ dx) * own + block
+            out_ref[block] = to_half(
+                kept_ref[high, at].astype(full) + came_ref[high, at].astype(full)
+            )
+
+
+def row_sum_kernel(count, place_ref, *refs):
+    ins, outs = refs[:count], refs[count:]
+    rows = outs[0].shape[1]
+    for slot, out_ref in enumerate(outs):
+        start = pl.multiple_of((place_ref[0] ^ slot) * rows, 16)
+        for block in range(out_ref.shape[0]):
+            total = ins[0][block, pl.ds(start, rows), :].astype(full)
+            for ref in ins[1:]:
+                total = total + ref[block, pl.ds(start, rows), :].astype(full)
+            out_ref[block] = to_half(total)
+
+
+def whole_step_kernel(count, first, place_ref, *refs):
+    grad_refs, refs = refs[:count], refs[count:]
+    root_refs, refs = refs[:count], refs[count:]
+    kept_ref, sent_ref, grads, rights, lefts, terms, found = refs
+    z, x = place_ref[0], place_ref[1]
+    blocks, rows, order = grad_refs[0].shape
+    for slot in range(count):
+        start = pl.multiple_of((z ^ slot) * rows, 16)
+        for block in range(blocks):
+            grads[block, pl.ds(start, rows), :] = grad_refs[slot][block]
+            rights[block, pl.ds(start, rows), :] = root_refs[slot][block]
+            lefts[block, pl.ds(start, rows), :] = root_refs[slot][first + block]
+    mine = pl.multiple_of(z * rows, 16)
+    for block in range(blocks):
+        whole = grads[block]
+        own = grad_refs[0][block]
+        step = to_half(dot32(lefts[block], whole))
+        step = dot32(step, rights[block])
+        mean = jnp.mean(jnp.mean(step * step, axis=1, keepdims=True), axis=0, keepdims=True)
+        terms[0] = row_product(whole, whole)
+        terms[1] = step * lax.rsqrt(mean + 1e-06)
+        found[0] = own.astype(full)
+        found[1] = times_transpose(own, whole)
+        found[2] = terms[0, pl.ds(mine, rows), :]
+        found[3] = terms[1, pl.ds(mine, rows), :]
+        half_rows = rows // PAIR
+        for target, part in ((kept_ref, x), (sent_ref, 1 - x)):
+            start = pl.multiple_of(part * half_rows, 16)
+            for kind in range(4):
+                target[kind, block] = to_half(found[kind, pl.ds(start, half_rows), :])
+
+
+def step_kernel(count, first, place_ref, *refs):
+    grad_refs, refs = refs[:count], refs[count:]
+    right_refs, refs = refs[:count], refs[count:]
+    left_ref, kept_ref, sent_ref, square_ref, grads, rights, terms, found = refs
+    z, x = place_ref[0], place_ref[1]
+    blocks, rows, order = grad_refs[0].shape
+    for slot in range(count):
+        start = pl.multiple_of((z ^ slot) * rows, 16)
+        for block in range(blocks):
+            grads[block, pl.ds(start, rows), :] = grad_refs[slot][block]
+            rights[block, pl.ds(start, rows), :] = right_refs[slot][first + block]
+    mine = pl.multiple_of(z * rows, 16)
+    square_ref[...] = jnp.zeros_like(square_ref)
+    for block in range(blocks):
+        whole = grads[block]
+        own = grad_refs[0][block]
+        step = to_half(dot32(left_ref[first + block], whole))
+        step = dot32(step, rights[block])
+        square_ref[block : block + 1, :] = jnp.broadcast_to(
+            jnp.sum(jnp.sum(step * step, axis=1, keepdims=True), axis=0, keepdims=True), (1, 128)
+        )
+        terms[...] = row_product(whole, whole)
+        found[0] = own.astype(full)
+        found[1] = times_transpose(own, whole)
+        found[2] = terms[pl.ds(mine, rows), :]
+        found[3] = step
+        half_rows = rows // PAIR
+        for target, part in ((kept_ref, x), (sent_ref, 1 - x)):
+            start = pl.multiple_of(part * half_rows, 16)
+            for kind in range(4):
+                target[kind, block] = to_half(found[kind, pl.ds(start, half_rows), :])
+
+
+def apply_kernel(
+    first, order, rates, place_ref, weight_ref, left_ref, right_ref, kept_ref, came_ref, *refs
+):
+    total_ref = refs[0] if len(refs) == 6 else None
+    grad_ref, new_left_ref, new_right_ref, new_ref, half_ref = refs[-5:]
+    x, m = place_ref[1], place_ref[2]
+    local = weight_ref.shape[0]
+    own = local // PAIR
+    for side, ref in ((0, kept_ref), (1, came_ref)):
+        for block in range(own):
+            at = (x ^ side) * own + block
+            index = first + block
+            rate = jnp.where(m * local + at < rates[0], rates[1], rates[2])
+            scale = 1.0
+            if total_ref is not None:
+                scale = lax.rsqrt(total_ref[side, index : index + 1, 0:1] / (order * order) + 1e-06)
+            grad_ref[at] = ref[0, index].astype(full)
+            new_left_ref[at] = 0.95 * left_ref[at] + 0.05 * ref[1, index].astype(full)
+            new_right_ref[at] = 0.95 * right_ref[at] + 0.05 * ref[2, index].astype(full)
+            new = weight_ref[at] - (rate * scale) * ref[3, index].astype(full)
+            new_ref[at] = new
+            half_ref[at] = to_half(new)
+
+
+def vector_part_kernel(place_ref, one_ref, two_ref, bias_ref, out_ref):
+    out_ref[0:2, :] = one_ref[0:2, :]
+    out_ref[2:4, :] = two_ref[0:2, :]
+    out_ref[4:6, :] = one_ref[2:4, :]
+    out_ref[6:8, :] = two_ref[2:4, :]
+    out_ref[8:9, :] = one_ref[4:5, :]
+    out_ref[9:, :] = bias_row(place_ref[2], bias_ref[...], out_ref.shape[0] - 9)
+
+
+def vector_step_kernel(vec_ref, *refs):
+    part_refs, (grad_ref, new_ref) = refs[:-2], refs[-2:]
+    grad = part_refs[0][...]
+    for ref in part_refs[1:]:
+        grad = grad + ref[...]
+    grad_ref[...] = grad
+    for start in range(0, grad.shape[1], BLOCK_VEC):
+        lanes = slice(start, start + BLOCK_VEC)
+        block = grad[:, lanes]
+        scale = lax.rsqrt(jnp.mean(block * block, axis=-1, keepdims=True) + 1e-06)
+        new_ref[:, lanes] = vec_ref[:, lanes] - 0.05 * (block * scale)
+
+
+def weights_kernel(attn_ref, up_ref, down_ref, attn_out, feed_out):
+    attn_out[...] = to_half(attn_ref[...])
+    local = up_ref.shape[0]
+    feed_out[:local] = to_half(up_ref[...])
+    feed_out[local:] = to_half(down_ref[...])
+
+
+def roots_kernel(place_ref, *refs):
+    ins, (kept_ref, sent_ref) = refs[:6], refs[6:]
+    x = place_ref[1]
+    own = ins[0].shape[0] // PAIR
+    for index, ref in enumerate(ins):
+        kept_ref[index] = to_half(ref[pl.ds(x * own, own)])
+        sent_ref[index] = to_half(ref[pl.ds((1 - x) * own, own)])
+
+
+def roots_join_kernel(place_ref, kept_ref, came_ref, left_ref, right_ref):
+    x = place_ref[1]
+    kinds, own, piece, order = kept_ref.shape
+    for index in range(kinds):
+        for block in range(own):
+            at = (index % 3) * own + block
+            targets = [(left_ref, at)] if index < 3 else [(right_ref, at)]
+            if index == 0:
+                targets.append((right_ref, 3 * own + block))
+            for target, place in targets:
+                for side, ref in ((0, kept_ref), (1, came_ref)):
+                    start = pl.multiple_of((x ^ side) * piece, 16)
+                    target[place, pl.ds(start, piece), :] = ref[index, block]
+
+
+def move(values, dp_mask, mp_mask):
+    dp, mp = lax.axis_size("dp"), lax.axis_size("mp")
+    if mp_mask == 0:
+        return lax.ppermute(values, "dp", [(s, s ^ dp_mask) for s in range(dp)])
+    if dp_mask == 0:
+        return lax.ppermute(values, "mp", [(s, s ^ mp_mask) for s in range(mp)])
+    mask = dp_mask * mp + mp_mask
+    return lax.ppermute(values, ("dp", "mp"), [(s, s ^ mask) for s in range(dp * mp)])
+
+
+def phase(*values):
+    return lax.optimization_barrier(values)
+
+
+def after(values, *others):
+    return lax.optimization_barrier((values,) + others)[0]
+
+
+def body_lines(
+    tokens,
+    keep_mask,
+    cotangent,
+    w_attn,
+    w_fc1,
+    w_fc2,
+    vectors,
+    left_attn,
+    right_attn,
+    root_left_attn,
+    root_right_attn,
+    left_fc1,
+    right_fc1,
+    root_left_fc1,
+    root_right_fc1,
+    left_fc2,
+    right_fc2,
+    root_left_fc2,
+    root_right_fc2,
+):
+    _, patches, width = tokens.shape
+    local, piece, order = w_attn.shape
+    z_count, group = high_size("dp"), lax.axis_size("mp")
+    row_blocks = width // order
+    own = local // PAIR
+    rows = patches
+    line_rows = order // z_count
+    total_rows = group * SLOTS
+    hidden_width = local // row_blocks * order
+    heads = (HEADS, rows, rows)
+    others = range(1, group)
+    lines = range(1, z_count)
+    tok, cot, mask = tokens[0], cotangent[0], keep_mask
+    line, member = lax.axis_index("dp"), lax.axis_index("mp")
+    place = jnp.stack([line >> 1, line & 1, member, member & 1]).astype(jnp.int32)
+    w_attn_first, place = phase(w_attn, place)
+
+    attn_half, feed_half = local_call(
+        weights_kernel,
+        (w_attn_first, w_fc1, w_fc2),
+        (shape((local, piece, order)), shape((2 * local, piece, order))),
+        in_smem=(),
+    )
+    line_came = [move(attn_half, k * PAIR, 0) for k in lines]
+    plane = [(dx, high * PAIR) for high in range(group // PAIR) for dx in range(PAIR)]
+    first = attn_half[None]
+    first_pieces = [first] + [move(first, dx, dm) for dx, dm in plane[1:]]
+    root_kept, root_sent = local_call(
+        roots_kernel,
+        (
+            place,
+            root_left_attn,
+            root_left_fc1,
+            root_left_fc2,
+            root_right_attn,
+            root_right_fc1,
+            root_right_fc2,
+        ),
+        (shape((6, own, piece, order)),) * 2,
+    )
+    root_came = move(root_sent, 1, 0)
+    second = jnp.stack(line_came)
+    second, first_pieces, root_came, feed_half = phase(
+        second, first_pieces, root_came, feed_half
+    )
+
+    feed_far, feed_near = move(feed_half, 2 * PAIR, 0), move(feed_half, PAIR, 0)
+    second_pieces = [second] + [move(second, dx, dm) for dx, dm in plane[1:]]
+    pieces, piece_info = [], []
+    for slots, found in (((0,), first_pieces), (tuple(lines), second_pieces)):
+        for (dx, dm), part in zip(plane, found):
+            pieces += [part, move(part, 0, 1)]
+            piece_info += [(slots, dx, dm), (slots, dx, dm + 1)]
+    normed, grad_sent, chosen = local_call(
+        prepare_kernel,
+        (mask, tok, cot, vectors),
+        (shape((rows, width)), shape((SLOTS, width)), shape((SLOTS, rows))),
+        in_smem=(),
+        micros=1.5,
+    )
+    feed_near = jnp.stack([feed_half, feed_near])
+    pieces, feed_near, feed_far, normed, grad_sent, chosen = phase(
+        pieces, feed_near, feed_far, normed, grad_sent, chosen
+    )
+
+    near_came = move(feed_near, 1, 0)
+    feed_last = move(feed_far, PAIR, 0)
+    group_grads = [grad_sent] + [move(grad_sent, 0, k) for k in others]
+    count = len(pieces)
+    rows_sent, qkv, probs, attended, branch, weights = local_call(
+        lambda *refs: forward_kernel(order, piece_info, *refs),
+        (place, *pieces, normed, tok, mask, chosen, vectors),
+        (
+            shape((SLOTS, width)),
+            shape((rows, 3 * width)),
+            shape(heads, full),
+            shape((rows, width)),
+            shape((rows, width), full),
+            shape((group * local, order, order)),
+        ),
+        scratch=(
+            pltpu.VMEM((group * local, order, order), half),
+            pltpu.VMEM(heads, full),
+            pltpu.SemaphoreType.DMA((count * z_count // 2,)),
+            pltpu.SemaphoreType.DMA(()),
+            pltpu.SemaphoreType.DMA((HEADS // 2,)),
+        ),
+        in_hbm=range(1, 1 + count),
+        out_hbm=(2, 5),
+        micros=8,
+    )
+    feed_far = jnp.stack([feed_far, feed_last])
+    rows_sent, near_came, feed_far, group_grads = phase(
+        rows_sent, near_came, feed_far, group_grads
+    )
+
+    group_rows = [rows_sent] + [move(rows_sent, 0, k) for k in others]
+    far_came = move(feed_far, 1, 0)
+    left_roots, right_root = local_call(
+        roots_join_kernel,
+        (place, root_kept, root_came),
+        (shape((3 * own, PAIR * piece, order)), shape((4 * own, PAIR * piece, order))),
+    )
+    roots_far = move(right_root, 2 * PAIR, 0)
+    roots_near = move(right_root, PAIR, 0)
+    group_rows, far_came, roots_far, roots_near = phase(
+        group_rows, far_came, roots_far, roots_near
+    )
+
+    feed_pieces = [feed_near, near_came, feed_far, far_came]
+    near_slots, far_slots = (0, 1), (2, 3)
+    feed_info = [(near_slots, 0), (near_slots, 1), (far_slots, 0), (far_slots, 1)]
+    count = len(feed_pieces)
+    outs = local_call(
+        lambda *refs: hidden_kernel(order, group, feed_info, *refs),
+        (place, *feed_pieces, *group_rows, *group_grads, vectors),
+        (shape((SLOTS, width)),) * group
+        + (shape((total_rows, width)),) * 2
+        + (shape((total_rows, hidden_width)),) * 2
+        + (shape((local, order, order)),),
+        scratch=(
+            pltpu.VMEM((2 * local, order, order), half),
+            pltpu.SemaphoreType.DMA((PAIR * z_count,)),
+            pltpu.SemaphoreType.DMA(()),
+        ),
+        in_hbm=range(1, 1 + count),
+        out_hbm=(group + 4,),
+        micros=5,
+    )
+    back, (all_rows, all_grads, active, grad_hidden, down) = outs[:group], outs[group:]
+    back, all_rows = phase(back, all_rows)
+
+    back = [back[0]] + [move(back[k], 0, k) for k in others]
+    roots_last = move(roots_far, PAIR, 0)
+    right_roots = [right_root, roots_near, roots_far, roots_last]
+    up_kept, up_sent, bias_sums = local_call(
+        lambda *refs: up_grads_kernel(order, *refs),
+        (place, all_rows, grad_hidden),
+        (shape((own, order, order)),) * 2 + (shape((1, hidden_width), full),),
+        scratch=(pltpu.VMEM((local, order, order), half),),
+        micros=1,
+    )
+    up_came = move(up_sent, 1, 0)
+    outs = local_call(
+        lambda *refs: down_grads_kernel(order, group, *refs),
+        (place, all_grads, active, down),
+        (shape((SLOTS, width)),) * group + (shape((own, order, order)),) * 2,
+        scratch=(pltpu.VMEM((local, order, order), half),),
+        micros=2,
+    )
+    feed, down_kept, down_sent = outs[:group], outs[group], outs[group + 1]
+    back, up_came, down_sent, feed, roots_last = phase(back, up_came, down_sent, feed, roots_last)
+
+    def split_rows_of(parts):
+        return local_call(
+            lambda *refs: row_sum_kernel(len(parts), *refs),
+            (place, *parts),
+            (shape((own, line_rows, order)),) * z_count,
+        )
+
+    def total_of(split):
+        parts = [split[0]] + [move(split[k], k * PAIR, 0) for k in lines]
+        total = parts[0].astype(full)
+        for part in parts[1:]:
+            total = total + part.astype(full)
+        return to_half(total)
+
+    up_rows = total_of(split_rows_of([up_kept, up_came]))
+    down_came = move(down_sent, 1, 0)
+    feed = [feed[0]] + [move(feed[k], 0, k) for k in others]
+    attn_kept, attn_sent, mixed, grad_middle, sums_two = local_call(
+        lambda *refs: backward_kernel(order, group, *refs),
+        (place, *back, chosen, tok, cot, branch, vectors, qkv, probs, attended, normed, weights),
+        (
+            shape((group // PAIR, local, order, order)),
+            shape((group // PAIR, local, order, order)),
+            shape((rows, 3 * width)),
+            shape((rows, width), full),
+            shape((4, width), full),
+        ),
+        scratch=(
+            pltpu.VMEM((local, order, order), half),
+            pltpu.VMEM((2, rows, width), half),
+            pltpu.VMEM((4, rows, width), half),
+            pltpu.VMEM((rows, width), half),
+            pltpu.VMEM(heads, full),
+            pltpu.SemaphoreType.DMA(()),
+            pltpu.SemaphoreType.DMA(()),
+        ),
+        in_hbm=(1 + group + 6, 1 + group + 9),
+        micros=8,
+    )
+    attn_sent, up_rows, down_came, feed = phase(attn_sent, up_rows, down_came, feed)
+
+    attn_came = move(attn_sent, 0, 1)
+    block_out, input_grad, sums_one = local_call(
+        lambda *refs: input_kernel(order, group, *refs),
+        (*feed, mixed, grad_middle, tok, cot, chosen, vectors, branch, weights),
+        (
+            shape((patches, width)),
+            shape((patches, width), full),
+            shape((5, width), full),
+        ),
+        scratch=(
+            pltpu.VMEM((3 * local, order, order), half),
+            pltpu.SemaphoreType.DMA(()),
+        ),
+        in_hbm=(group + 7,),
+        in_smem=(),
+        micros=4,
+    )
+    (vector_sum,) = local_call(
+        vector_part_kernel,
+        (place, sums_one, sums_two, bias_sums),
+        (shape(vectors.shape, full),),
+    )
+    down_split = split_rows_of([down_kept, down_came])
+    core_parts = local_call(
+        core_sum_kernel,
+        (place, attn_kept, attn_came),
+        (shape((own, order, order)),) * group,
+    )
+    core_parts, down_split, vector_sum = phase(core_parts, down_split, vector_sum)
+
+    attn_parts = [core_parts[0]]
+    for (dx, dm), part in zip(plane[1:], core_parts[1:]):
+        attn_parts.append(move(part, dx, dm))
+    up_near, up_far = move(up_rows, PAIR, 0), move(up_rows, 2 * PAIR, 0)
+    down_rows = total_of(down_split)
+    up_last = move(up_far, PAIR, 0)
+    vector_sum = vector_sum + move(vector_sum, 0, 1)
+    attn_split = split_rows_of(attn_parts)
+    up_parts = [up_rows, up_near, up_far, up_last]
+    attn_split, up_parts, down_rows, vector_sum = phase(
+        attn_split, up_parts, down_rows, vector_sum
+    )
+
+    def step_of(parts, first):
+        return local_call(
+            lambda *refs: step_kernel(z_count, first, *refs),
+            (place, *parts, *right_roots, left_roots),
+            (shape((4, own, line_rows // PAIR, order)),) * 2 + (shape((8, 128), full),),
+            scratch=(
+                pltpu.VMEM((own, order, order), half),
+                pltpu.VMEM((own, order, order), half),
+                pltpu.VMEM((order, order), full),
+                pltpu.VMEM((4, line_rows, order), full),
+            ),
+            micros=2,
+        )
+
+    def line_total(values):
+        total = values
+        for k in lines:
+            total = total + move(values, k * PAIR, 0)
+        return total
+
+    attn_rows = total_of(attn_split)
+    down_near, down_far = move(down_rows, PAIR, 0), move(down_rows, 2 * PAIR, 0)
+    up_mine, up_sent, up_squares = step_of(up_parts, own)
+    up_squares = jnp.stack([up_squares, move(up_squares, 1, 0)])
+    up_found = move(up_sent, 1, 0)
+    for dm in range(PAIR, group, PAIR):
+        vector_sum = vector_sum + move(vector_sum, 0, dm)
+    attn_rows, down_near, down_far, up_squares, up_found, vector_sum = phase(
+        attn_rows, down_near, down_far, up_squares, up_found, vector_sum
+    )
+
+    attn_near, attn_far = move(attn_rows, PAIR, 0), move(attn_rows, 2 * PAIR, 0)
+    down_last = move(down_far, PAIR, 0)
+    attn_last = move(attn_far, PAIR, 0)
+    vector_sum = vector_sum + move(vector_sum, 1, 0)
+    up_total = line_total(up_squares)
+    attn_near, attn_far, attn_last, down_last, vector_sum, up_total = phase(
+        attn_near, attn_far, attn_last, down_last, vector_sum, up_total
+    )
+
+    kept, sent = local_call(
+        lambda *refs: whole_step_kernel(z_count, 3 * own, *refs),
+        (place, attn_rows, attn_near, attn_far, attn_last, *right_roots),
+        (shape((4, own, line_rows // PAIR, order)),) * 2,
+        scratch=(pltpu.VMEM((own, order, order), half),) * 3
+        + (pltpu.VMEM((2, order, order), full), pltpu.VMEM((4, line_rows, order), full)),
+        micros=2,
+    )
+    down_mine, down_sent, down_squares = step_of(
+        [down_rows, down_near, down_far, down_last], 2 * own
+    )
+    down_squares = jnp.stack([down_squares, move(down_squares, 1, 0)])
+    came = move(after(sent, down_squares), 1, 0)
+    down_found = move(after(down_sent, down_squares), 1, 0)
+    vector_parts = [vector_sum] + [move(vector_sum, k * PAIR, 0) for k in lines]
+    down_total = line_total(down_squares)
+
+    def apply(first, rates, weight, left, right, found):
+        stat = shape(weight.shape, full)
+        return local_call(
+            lambda *refs: apply_kernel(first, order, rates, *refs),
+            (place, weight, left, right, *found),
+            (stat,) * 4 + (shape(weight.shape),),
+        )
+
+    attn_rates = (3 * row_blocks * row_blocks, 0.5 * D ** (-0.5), 0.5 * (D // 16) ** (-0.5))
+    fc1_rates = (0, 0.0, 0.5 * D ** (-0.5))
+    fc2_rates = (0, 0.0, 0.5 * FF ** (-0.5))
+    vector_grad, new_vectors = local_call(
+        vector_step_kernel,
+        (vectors, *vector_parts),
+        (shape(vectors.shape, full),) * 2,
+        in_smem=(),
+    )
+    done_attn = apply(0, attn_rates, w_attn, left_attn, right_attn, (kept, came))
+    done_fc1 = apply(0, fc1_rates, w_fc1, left_fc1, right_fc1, (up_mine, up_found, up_total))
+    done_fc2 = apply(
+        0, fc2_rates, w_fc2, left_fc2, right_fc2, (down_mine, down_found, down_total)
+    )
+    return (
+        block_out[None],
+        input_grad[None],
+        done_attn[0],
+        done_fc1[0],
+        done_fc2[0],
+        *done_attn[1:3],
+        *done_fc1[1:3],
+        *done_fc2[1:3],
+        done_attn[3],
+        done_fc1[3],
+        done_fc2[3],
+        done_attn[4],
+        done_fc1[4],
+        done_fc2[4],
+        vector_grad,
+        new_vectors,
+    )
+
+
+def body(tokens, keep_mask, cotangent, w_attn, *rest):
+    local, piece, _ = w_attn.shape
+    group = lax.axis_size("mp")
+    tiled = piece % 16 == 0 and tokens.shape[0] == 1 and local % (2 * PAIR) == 0
+    tiled = tiled and group == 4 and high_size("dp") == 4
+    chosen_body = body_lines if tiled else body_plain
+    return chosen_body(tokens, keep_mask, cotangent, w_attn, *rest)
+
+
 def solution(mesh):
     rows = P(("dp", "mp"), None, None)
     blocks = P("mp", "dp", None)

time: 413 us -> 274 us (0.66); the launches traced: 406 us -> 273 us
  local copies, waits for them, and re-layouts: 84.7 us -> 7.27 us
  Pallas kernels: 0 us -> 50.4 us
  matrix products: 50.3 us -> 0 us
  other arithmetic: 50.7 us -> 0.55 us
  starting transfers between devices: 106 us -> 76.8 us
  waiting for transfers between devices: 112 us -> 137 us
    pallas_call x0 -> x22, Pallas kernels: none -> 50.4 us  [local_call(): pl.pallas_call(kernel, out_shape=list(outs), in_specs=[place_of(i, in_hbm...]
    dot_general x30 -> x0, matrix products: 47.8 us -> none  [the longest x4 12.5 us: times_transpose(): lax.dot_general(left_half, right_half, (((1,), (1,)), ((), ())), preferre...]
    ppermute x85 -> x79, starting transfers between devices: 106 us -> 76.8 us  [the longest x50 59.1 us: move(): return lax.ppermute(values, 'dp', [(s, s ^ dp_mask) for s in range(dp)])]
    unnamed x288 -> x39, local copies, waits for them, and re-layouts: 33.2 us -> 7.27 us
    ppermute x85 -> x79, waiting for transfers between devices: 112 us -> 137 us  [the longest x50 111 us: move(): return lax.ppermute(values, 'dp', [(s, s ^ dp_mask) for s in range(dp)])]
    convert_element_type x16 -> x3, other arithmetic: 12.7 us -> 0.24 us  [to_half(): return values.astype(half)]
    transpose x19 -> x0, local copies, waits for them, and re-layouts: 11 us -> none  [the longest x10 4.27 us: gather_z(): gather_high(to_half(rows), 'dp').swapaxes(0, 1).reshape(local, -1, order)]
    another operation x36 -> x6, other arithmetic: 10.1 us -> 0.28 us  [the longest x1 0.08 us: body_lines(): jnp.stack([line >> 1, line & 1, member, member & 1]).astype(jnp.int32)]
  transfers between devices with their start and end apart: 85 -> 79, of which waited for: 31 -> 36; matrix products, arithmetic and copies ran while one was open for 38% -> 1% of each run, Pallas kernels for 0% -> 14%
where the time goes in v2:
time: 274 us; the launch traced here: 273 us
  waiting for transfers between devices  137 us (50%)
  starting transfers between devices  76.8 us (28%)
  Pallas kernels  50.4 us (18%)
  local copies, waits for them, and re-layouts  7.27 us (3%)
    ppermute x50, waiting for transfers between devices, move(): return lax.ppermute(values, 'dp', [(s, s ^ dp_mask) for s in range(dp)])  111 us
    ppermute x50, starting transfers between devices, move(): return lax.ppermute(values, 'dp', [(s, s ^ dp_mask) for s in range(dp)])  59.1 us
    pallas_call x22, Pallas kernels, local_call(): pl.pallas_call(kernel, out_shape=list(outs), in_specs=[place_of(i, in_hbm...  50.4 us
    ppermute x26, waiting for transfers between devices, move(): return lax.ppermute(values, 'mp', [(s, s ^ mp_mask) for s in range(mp)])  20.6 us
    ppermute x26, starting transfers between devices, move(): return lax.ppermute(values, 'mp', [(s, s ^ mp_mask) for s in range(mp)])  13 us
    unnamed x39, local copies, waits for them, and re-layouts  7.27 us
    ppermute x3, waiting for transfers between devices, move(): lax.ppermute(values, ('dp', 'mp'), [(s, s ^ mask) for s in range(dp * mp)])  5.88 us
  transfers between devices with their start and end apart: 79, of which 36 were waited for; matrix products, arithmetic and copies ran while one was open for 1% of the time, Pallas kernels for 14%

profile of v2, /device:TPU:0, one launch (start us, length us, event | category | flops | bytes accessed | tf_op | source)
XLA Modules:
  0.0 273.5 jit_solution(5620223305250600812)
XLA Ops:
  7.2 3.0 %collective-permute-start.6 = (bf16[6,2,48,384]{3,2,1,0:T(8,128)(2,1)S(1)}, bf16[6,2,48,384]{3,2,1,0:T(8,128)(2,1)S(1)}, u32[]{:S(2)}, u32[]{:S(2)}) collective-permute-start(bf16[6,2,48,384]{3,2,1,0:T(8,128)(2,1)S(1)} %get-tuple-element.203), channel_id=1, source_target_pairs={{0,4},{4,0},{8,12},{12,8},{16,20},{20,16},{24,28},{28,24},{1,5},{5... | collective-permute-start | bytes 1327112 | tf_op jit(solution)/shard_map/ppermute | solution.py:1062
  11.9 2.6 collective-permute-start.1
  15.1 2.4 collective-permute-done
  19.0 6.8 %collective-permute-done.1 = bf16[4,48,384]{2,1,0:T(8,128)(2,1)S(1)} collective-permute-done((bf16[4,48,384]{2,1,0:T(8,128)(2,1)S(1)}, bf16[4,48,384]{2,1,0:T(8,128)(2,1)S(1)}, u32[]{:S(2)}, u32[]{:S(2)}) %collective-permute-start.1) | collective-permute-done | bytes 147488 | tf_op jit(solution)/shard_map/ppermute | solution.py:1062
  27.5 4.4 %collective-permute-done.5.refs_7_ = bf16[1,4,48,384]{3,2,1,0:T(8,128)(2,1)S(1)} collective-permute-done((bf16[1,4,48,384]{3,2,1,0:T(8,128)(2,1)S(1)}, bf16[1,4,48,384]{3,2,1,0:T(8,128)(2,1)S(1)}, u32[]{:S(2)}, u32[]{:S(2)}) %collective-permute-start.5) | collective-permute-done | bytes 147488 | tf_op jit(solution)/shard_map/ppermute | solution.py:1066
  38.2 6.6 %collective-permute-done.12.refs_11_ = bf16[3,4,48,384]{3,2,1,0:T(8,128)(2,1)S(1)} collective-permute-done((bf16[3,4,48,384]{3,2,1,0:T(8,128)(2,1)S(1)}, bf16[3,4,48,384]{3,2,1,0:T(8,128)(2,1)S(1)}, u32[]{:S(2)}, u32[]{:S(2)}) %collective-permute-start.12) | collective-permute-done | bytes 442400 | tf_op jit(solution)/shard_map/ppermute | solution.py:1062
  44.8 8.5 %collective-permute-done.14.refs_13_ = bf16[3,4,48,384]{3,2,1,0:T(8,128)(2,1)S(1)} collective-permute-done((bf16[3,4,48,384]{3,2,1,0:T(8,128)(2,1)S(1)}, bf16[3,4,48,384]{3,2,1,0:T(8,128)(2,1)S(1)}, u32[]{:S(2)}, u32[]{:S(2)}) %collective-permute-start.14) | collective-permute-done | bytes 442400 | tf_op jit(solution)/shard_map/ppermute | solution.py:1064
  55.7 15.4 %collective-permute-done.19 = bf16[8,48,384]{2,1,0:T(8,128)(2,1)S(1)} collective-permute-done((bf16[8,48,384]{2,1,0:T(8,128)(2,1)S(1)}, bf16[8,48,384]{2,1,0:T(8,128)(2,1)S(1)}, u32[]{:S(2)}, u32[]{:S(2)}) %collective-permute-start.19) | collective-permute-done | bytes 294944 | tf_op jit(solution)/shard_map/ppermute | solution.py:1062
  71.9 2.2 collective-permute-start.29
  75.9 8.9 %collective-permute-done.21 = bf16[8,48,384]{2,1,0:T(8,128)(2,1)S(1)} collective-permute-done((bf16[8,48,384]{2,1,0:T(8,128)(2,1)S(1)}, bf16[8,48,384]{2,1,0:T(8,128)(2,1)S(1)}, u32[]{:S(2)}, u32[]{:S(2)}) %collective-permute-start.21) | collective-permute-done | bytes 294944 | tf_op jit(solution)/shard_map/ppermute | solution.py:1062
  85.6 10.9 %shard_map.333 = (bf16[160,768]{1,0:T(8,128)(2,1)S(1)}, bf16[197,2304]{1,0:T(8,128)(2,1)S(1)}, f32[12,197,197]{2,1,0:T(8,128)S(1)}, bf16[197,768]{1,0:T(8,128)(2...) custom-call(s32[4]{0:T(128)S(1)} %pad_add_fusion.place_ref.refs_0_, ...), custom_call_target="tpu_custom_call" | custom-call | flops 8000000000 | bytes 14070292 | tf_op jit(solution)/shard_map/pallas_call | solution.py:518
  96.7 2.5 collective-permute-done.20.refs_2_
  101.9 11.6 %collective-permute-done.30.refs_6_ = bf16[8,96,384]{2,1,0:T(8,128)(2,1)S(1)} collective-permute-done((bf16[8,96,384]{2,1,0:T(8,128)(2,1)S(1)}, bf16[8,96,384]{2,1,0:T(8,128)(2,1)S(1)}, u32[]{:S(2)}, u32[]{:S(2)}) %collective-permute-start.30) | collective-permute-done | bytes 589856 | tf_op jit(solution)/shard_map/ppermute | solution.py:1062
  113.5 5.3 %shard_map.335 = (bf16[160,768]{1,0:T(8,128)(2,1)S(1)}, bf16[160,768]{1,0:T(8,128)(2,1)S(1)}, bf16[160,768]{1,0:T(8,128)(2,1)S(1)}, bf16[160,768]{1,0:T(8,128)(2...) custom-call(s32[4]{0:T(128)S(1)} %pad_add_fusion.place_ref.refs_0_, ...), custom_call_target="tpu_custom_call" | custom-call | flops 5000000000 | bytes 10460176 | tf_op jit(solution)/shard_map/pallas_call | solution.py:518
  118.8 2.0 shard_map.336
  123.7 3.1 %shard_map.337 = (bf16[160,768]{1,0:T(8,128)(2,1)S(1)}, bf16[160,768]{1,0:T(8,128)(2,1)S(1)}, bf16[160,768]{1,0:T(8,128)(2,1)S(1)}, bf16[160,768]{1,0:T(8,128)(2...) custom-call(s32[4]{0:T(128)S(1)} %pad_add_fusion.place_ref.refs_0_, ...), custom_call_target="tpu_custom_call" | custom-call | flops 2000000000 | bytes 5308432 | tf_op jit(solution)/shard_map/pallas_call | solution.py:518
  126.9 3.7 %collective-permute-done.32.refs_3_ = bf16[160,768]{1,0:T(8,128)(2,1)S(1)} collective-permute-done((bf16[160,768]{1,0:T(8,128)(2,1)S(1)}, bf16[160,768]{1,0:T(8,128)(2,1)S(1)}, u32[]{:S(2)}, u32[]{:S(2)}) %collective-permute-start.32) | collective-permute-done | bytes 245792 | tf_op jit(solution)/shard_map/ppermute | solution.py:1064
  130.6 4.5 %collective-permute-done.33.refs_4_ = bf16[160,768]{1,0:T(8,128)(2,1)S(1)} collective-permute-done((bf16[160,768]{1,0:T(8,128)(2,1)S(1)}, bf16[160,768]{1,0:T(8,128)(2,1)S(1)}, u32[]{:S(2)}, u32[]{:S(2)}) %collective-permute-start.33) | collective-permute-done | bytes 245792 | tf_op jit(solution)/shard_map/ppermute | solution.py:1064
  138.1 2.5 collective-permute-start.37
  143.1 2.3 collective-permute-done.36
  146.4 5.6 %collective-permute-done.37 = bf16[2,96,384]{2,1,0:T(8,128)(2,1)S(1)} collective-permute-done((bf16[2,96,384]{2,1,0:T(8,128)(2,1)S(1)}, bf16[2,96,384]{2,1,0:T(8,128)(2,1)S(1)}, u32[]{:S(2)}, u32[]{:S(2)}) %collective-permute-start.37) | collective-permute-done | bytes 147488 | tf_op jit(solution)/shard_map/ppermute | solution.py:1062
  152.0 8.0 %shard_map.338 = (bf16[2,4,384,384]{3,2,1,0:T(8,128)(2,1)S(1)}, bf16[2,4,384,384]{3,2,1,0:T(8,128)(2,1)S(1)}, bf16[197,2304]{1,0:T(8,128)(2,1)S(1)}, f32[197,768]{1,0:T(8,128)S(1)}, f32[4,768]{1,0:T(4,128)S(1)}) custom-call(s32[4]{0:T(128)S(1)} %pad_add_fusion.place_ref.refs_0_, bf16[160,768]{1,0:T(8,128)(2,1)S(1)} %get-tuple-element.272.refs_1_, ...), custom_call_target="tpu_custom_call" | custom-call | flops 8000000000 | bytes 16634624 | tf_op jit(solution)/shard_map/pallas_call | solution.py:518
  162.2 3.5 %shard_map.340 = (bf16[197,768]{1,0:T(8,128)(2,1)}, f32[197,768]{1,0:T(8,128)S(1)}, f32[5,768]{1,0:T(8,128)S(1)}) custom-call(bf16[160,768]{1,0:T(8,128)(2,1)S(1)} %get-tuple-element.293.refs_0_, bf16[160,768]{1,0:T(8,128)(2,1)S(1)} %collective-permute-done.40.refs_1_, bf16[160,768]{1,0:T(8,128)(2,1)S(1)} %collective-permute-done.41.refs_2_, ...), custom_call_target="tpu_custom_call" | custom-call | flops 4000000000 | bytes 9451072 | tf_op jit(solution)/shard_map/pallas_call | solution.py:518
  169.2 1.8 collective-permute-start.46
  171.0 2.5 collective-permute-start.50
  173.5 5.9 %collective-permute-done.48.refs_3_ = bf16[2,96,384]{2,1,0:T(8,128)(2,1)S(1)} collective-permute-done((bf16[2,96,384]{2,1,0:T(8,128)(2,1)S(1)}, bf16[2,96,384]{2,1,0:T(8,128)(2,1)S(1)}, u32[]{:S(2)}, u32[]{:S(2)}) %collective-permute-start.48) | collective-permute-done | bytes 147488 | tf_op jit(solution)/shard_map/ppermute | solution.py:1062
  180.6 1.9 collective-permute-start.52
  182.5 10.5 %collective-permute-done.51 = bf16[2,96,384]{2,1,0:T(8,128)(2,1)S(1)} collective-permute-done((bf16[2,96,384]{2,1,0:T(8,128)(2,1)S(1)}, bf16[2,96,384]{2,1,0:T(8,128)(2,1)S(1)}, u32[]{:S(2)}, u32[]{:S(2)}) %collective-permute-start.51) | collective-permute-done | bytes 147488 | tf_op jit(solution)/shard_map/ppermute | solution.py:1062
  193.1 3.6 %collective-permute-start.49 = (bf16[2,96,384]{2,1,0:T(8,128)(2,1)S(1)}, bf16[2,96,384]{2,1,0:T(8,128)(2,1)S(1)}, u32[]{:S(2)}, u32[]{:S(2)}) collective-permute-start(bf16[2,96,384]{2,1,0:T(8,128)(2,1)S(1)} %collective-permute-done.48.refs_3_), channel_id=1, source_target_pairs={{0,8},{4,12},{8,0},{12,4},{16,24},{20,28},{24,16},{28,20},{1,9},{5... | collective-permute-start | bytes 442376 | tf_op jit(solution)/shard_map/ppermute | solution.py:1062
  197.7 2.1 collective-permute-done.47.refs_2_
  199.8 2.2 collective-permute-done.49.refs_4_
  202.5 1.9 collective-permute-start.55
  204.4 1.9 collective-permute-start.56
  209.9 1.9 collective-permute-done.59
  213.4 2.9 %collective-permute-start.58 = (bf16[2,96,384]{2,1,0:T(8,128)(2,1)S(1)}, bf16[2,96,384]{2,1,0:T(8,128)(2,1)S(1)}, u32[]{:S(2)}, u32[]{:S(2)}) collective-permute-start(bf16[2,96,384]{2,1,0:T(8,128)(2,1)S(1)} %add_convert_fusion.1.refs_1_), channel_id=1, source_target_pairs={{0,16},{4,20},{8,24},{12,28},{16,0},{20,4},{24,8},{28,12},{1,17},{... | collective-permute-start | bytes 442376 | tf_op jit(solution)/shard_map/ppermute | solution.py:1062
  217.5 2.1 collective-permute-done.57.refs_2_
  219.6 4.3 %collective-permute-done.58.refs_3_ = bf16[2,96,384]{2,1,0:T(8,128)(2,1)S(1)} collective-permute-done((bf16[2,96,384]{2,1,0:T(8,128)(2,1)S(1)}, bf16[2,96,384]{2,1,0:T(8,128)(2,1)S(1)}, u32[]{:S(2)}, u32[]{:S(2)}) %collective-permute-start.58) | collective-permute-done | bytes 147488 | tf_op jit(solution)/shard_map/ppermute | solution.py:1062
  223.9 2.5 collective-permute-start.67
  226.8 1.9 collective-permute-start.69
  236.5 3.2 %collective-permute-done.65.refs_4_ = bf16[2,96,384]{2,1,0:T(8,128)(2,1)S(1)} collective-permute-done((bf16[2,96,384]{2,1,0:T(8,128)(2,1)S(1)}, bf16[2,96,384]{2,1,0:T(8,128)(2,1)S(1)}, u32[]{:S(2)}, u32[]{:S(2)}) %collective-permute-start.65) | collective-permute-done | bytes 147488 | tf_op jit(solution)/shard_map/ppermute | solution.py:1062
  239.6 2.1 collective-permute-done.64.refs_4_
  244.2 1.8 shard_map.347
  247.1 2.3 shard_map.346
  250.5 1.8 collective-permute-start.74
  252.3 1.8 collective-permute-start.75
  255.8 2.1 collective-permute-start.78
  259.9 1.8 collective-permute-done.78.refs_3_
  262.5 7.6 %collective-permute-done.71.refs_5_ = bf16[4,2,48,384]{3,2,1,0:T(8,128)(2,1)S(1)} collective-permute-done((bf16[4,2,48,384]{3,2,1,0:T(8,128)(2,1)S(1)}, bf16[4,2,48,384]{3,2,1,0:T(8,128)(2,1)S(1)}, u32[]{:S(2)}, u32[]{:S(2)}) %collective-permute-start.71) | collective-permute-done | bytes 294944 | tf_op jit(solution)/shard_map/ppermute | solution.py:1062
  (185 shorter events, 71.7 us)
Async XLA Ops:
  7.2 24.6 %collective-permute-start.6 = (bf16[6,2,48,384]{3,2,1,0:T(8,128)(2,1)S(1)}, bf16[6,2,48,384]{3,2,1,0:T(8,128)(2,1)S(1)}, u32[]{:S(2)}, u32[]{:S(2)}) collective-permute-start(bf16[6,2,48,384]{3,2,1,0:T(8,128)(2,1)S(1)} %get-tuple-element.203), channel_id=1, source_target_pairs={{0,4},{4,0},{8,12},{12,8},{16,20},{20,16},{24,28},{28,24},{1,5},{5... | collective-permute-start | bytes 1327112 | tf_op jit(solution)/shard_map/ppermute | solution.py:1062
  11.9 13.9 %collective-permute-start.1 = (bf16[4,48,384]{2,1,0:T(8,128)(2,1)S(1)}, bf16[4,48,384]{2,1,0:T(8,128)(2,1)S(1)}, u32[]{:S(2)}, u32[]{:S(2)}) collective-permute-start(bf16[4,48,384]{2,1,0:T(8,128)(2,1)S(1)} %get-tuple-element.202), channel_id=1, source_target_pairs={{0,16},{4,20},{8,24},{12,28},{16,0},{20,4},{24,8},{28,12},{1,17},{... | collective-permute-start | bytes 442376 | tf_op jit(solution)/shard_map/ppermute | solution.py:1062
  14.5 12.9 %collective-permute-start.2 = (bf16[4,48,384]{2,1,0:T(8,128)(2,1)S(1)}, bf16[4,48,384]{2,1,0:T(8,128)(2,1)S(1)}, u32[]{:S(2)}, u32[]{:S(2)}) collective-permute-start(bf16[4,48,384]{2,1,0:T(8,128)(2,1)S(1)} %get-tuple-element.202), channel_id=1, source_target_pairs={{0,24},{4,28},{8,16},{12,20},{16,8},{20,12},{24,0},{28,4},{1,25},{... | collective-permute-start | bytes 442376 | tf_op jit(solution)/shard_map/ppermute | solution.py:1062
  14.7 12.7 %collective-permute-start.3 = (bf16[1,4,48,384]{3,2,1,0:T(8,128)(2,1)S(1)}, bf16[1,4,48,384]{3,2,1,0:T(8,128)(2,1)S(1)}, u32[]{:S(2)}, u32[]{:S(2)}) collective-permute-start(bf16[1,4,48,384]{3,2,1,0:T(8,128)(2,1)S(1)} %bitcast.32), channel_id=1, source_target_pairs={{0,4},{4,0},{8,12},{12,8},{16,20},{20,16},{24,28},{28,24},{1,5},{5... | collective-permute-start | bytes 442376 | tf_op jit(solution)/shard_map/ppermute | solution.py:1062
  17.5 10.0 %collective-permute-start.4 = (bf16[1,4,48,384]{3,2,1,0:T(8,128)(2,1)S(1)}, bf16[1,4,48,384]{3,2,1,0:T(8,128)(2,1)S(1)}, u32[]{:S(2)}, u32[]{:S(2)}) collective-permute-start(bf16[1,4,48,384]{3,2,1,0:T(8,128)(2,1)S(1)} %bitcast.33), channel_id=1, source_target_pairs={{0,2},{1,3},{2,0},{3,1},{4,6},{5,7},{6,4},{7,5},{8,10},{9,11},{10,... | collective-permute-start | bytes 442376 | tf_op jit(solution)/shard_map/ppermute | solution.py:1064
  31.8 13.0 %collective-permute-start.12 = (bf16[3,4,48,384]{3,2,1,0:T(8,128)(2,1)S(1)}, bf16[3,4,48,384]{3,2,1,0:T(8,128)(2,1)S(1)}, u32[]{:S(2)}, u32[]{:S(2)}) collective-permute-start(bf16[3,4,48,384]{3,2,1,0:T(8,128)(2,1)S(1)} %pad_maximum_fusion.2.refs_9_), channel_id=1, source_target_pairs={{0,4},{4,0},{8,12},{12,8},{16,20},{20,16},{24,28},{28,24},{1,5},{5... | collective-permute-start | bytes 1327112 | tf_op jit(solution)/shard_map/ppermute | solution.py:1062
  32.5 20.9 %collective-permute-start.14 = (bf16[3,4,48,384]{3,2,1,0:T(8,128)(2,1)S(1)}, bf16[3,4,48,384]{3,2,1,0:T(8,128)(2,1)S(1)}, u32[]{:S(2)}, u32[]{:S(2)}) collective-permute-start(bf16[3,4,48,384]{3,2,1,0:T(8,128)(2,1)S(1)} %pad_maximum_fusion.2.refs_9_), channel_id=1, source_target_pairs={{0,2},{1,3},{2,0},{3,1},{4,6},{5,7},{6,4},{7,5},{8,10},{9,11},{10,... | collective-permute-start | bytes 1327112 | tf_op jit(solution)/shard_map/ppermute | solution.py:1064
  34.0 20.9 %collective-permute-start.16 = (bf16[3,4,48,384]{3,2,1,0:T(8,128)(2,1)S(1)}, bf16[3,4,48,384]{3,2,1,0:T(8,128)(2,1)S(1)}, u32[]{:S(2)}, u32[]{:S(2)}) collective-permute-start(bf16[3,4,48,384]{3,2,1,0:T(8,128)(2,1)S(1)} %pad_maximum_fusion.2.refs_9_), channel_id=1, source_target_pairs={{0,6},{1,7},{2,4},{3,5},{4,2},{5,3},{6,0},{7,1},{8,14},{9,15},{10,... | collective-permute-start | bytes 1327112 | tf_op jit(solution)/shard_map/ppermute | solution.py:1066
  36.9 17.9 %collective-permute-start.18 = (bf16[8,48,384]{2,1,0:T(8,128)(2,1)S(1)}, bf16[8,48,384]{2,1,0:T(8,128)(2,1)S(1)}, u32[]{:S(2)}, u32[]{:S(2)}) collective-permute-start(bf16[8,48,384]{2,1,0:T(8,128)(2,1)S(1)} %get-tuple-element.210), channel_id=1, source_target_pairs={{0,8},{4,12},{8,0},{12,4},{16,24},{20,28},{24,16},{28,20},{1,9},{5... | collective-permute-start | bytes 884744 | tf_op jit(solution)/shard_map/ppermute | solution.py:1062
  38.1 33.0 %collective-permute-start.11 = (bf16[3,4,48,384]{3,2,1,0:T(8,128)(2,1)S(1)}, bf16[3,4,48,384]{3,2,1,0:T(8,128)(2,1)S(1)}, u32[]{:S(2)}, u32[]{:S(2)}) collective-permute-start(bf16[3,4,48,384]{3,2,1,0:T(8,128)(2,1)S(1)} %pad_maximum_fusion.2.refs_9_), channel_id=1, source_target_pairs={{0,1},{1,0},{2,3},{3,2},{4,5},{5,4},{6,7},{7,6},{8,9},{9,8},{10,11... | collective-permute-start | bytes 1327112 | tf_op jit(solution)/shard_map/ppermute | solution.py:1064
  44.8 26.3 %collective-permute-start.13 = (bf16[3,4,48,384]{3,2,1,0:T(8,128)(2,1)S(1)}, bf16[3,4,48,384]{3,2,1,0:T(8,128)(2,1)S(1)}, u32[]{:S(2)}, u32[]{:S(2)}) collective-permute-start(bf16[3,4,48,384]{3,2,1,0:T(8,128)(2,1)S(1)} %collective-permute-done.12.refs_11_), channel_id=1, source_target_pairs={{0,1},{1,0},{2,3},{3,2},{4,5},{5,4},{6,7},{7,6},{8,9},{9,8},{10,11... | collective-permute-start | bytes 1327112 | tf_op jit(solution)/shard_map/ppermute | solution.py:1064
  53.3 17.8 %collective-permute-start.15 = (bf16[3,4,48,384]{3,2,1,0:T(8,128)(2,1)S(1)}, bf16[3,4,48,384]{3,2,1,0:T(8,128)(2,1)S(1)}, u32[]{:S(2)}, u32[]{:S(2)}) collective-permute-start(bf16[3,4,48,384]{3,2,1,0:T(8,128)(2,1)S(1)} %collective-permute-done.14.refs_13_), channel_id=1, source_target_pairs={{0,1},{1,0},{2,3},{3,2},{4,5},{5,4},{6,7},{7,6},{8,9},{9,8},{10,11... | collective-permute-start | bytes 1327112 | tf_op jit(solution)/shard_map/ppermute | solution.py:1064
  54.9 16.3 %collective-permute-start.17 = (bf16[3,4,48,384]{3,2,1,0:T(8,128)(2,1)S(1)}, bf16[3,4,48,384]{3,2,1,0:T(8,128)(2,1)S(1)}, u32[]{:S(2)}, u32[]{:S(2)}) collective-permute-start(bf16[3,4,48,384]{3,2,1,0:T(8,128)(2,1)S(1)} %collective-permute-done.16.refs_15_), channel_id=1, source_target_pairs={{0,1},{1,0},{2,3},{3,2},{4,5},{5,4},{6,7},{7,6},{8,9},{9,8},{10,11... | collective-permute-start | bytes 1327112 | tf_op jit(solution)/shard_map/ppermute | solution.py:1064
  54.9 16.3 %collective-permute-start.19 = (bf16[8,48,384]{2,1,0:T(8,128)(2,1)S(1)}, bf16[8,48,384]{2,1,0:T(8,128)(2,1)S(1)}, u32[]{:S(2)}, u32[]{:S(2)}) collective-permute-start(bf16[8,48,384]{2,1,0:T(8,128)(2,1)S(1)} %get-tuple-element.210), channel_id=1, source_target_pairs={{0,16},{4,20},{8,24},{12,28},{16,0},{20,4},{24,8},{28,12},{1,17},{... | collective-permute-start | bytes 884744 | tf_op jit(solution)/shard_map/ppermute | solution.py:1062
  71.2 13.6 %collective-permute-start.21 = (bf16[8,48,384]{2,1,0:T(8,128)(2,1)S(1)}, bf16[8,48,384]{2,1,0:T(8,128)(2,1)S(1)}, u32[]{:S(2)}, u32[]{:S(2)}) collective-permute-start(bf16[8,48,384]{2,1,0:T(8,128)(2,1)S(1)} %collective-permute-done.19), channel_id=1, source_target_pairs={{0,8},{4,12},{8,0},{12,4},{16,24},{20,28},{24,16},{28,20},{1,9},{5... | collective-permute-start | bytes 884744 | tf_op jit(solution)/shard_map/ppermute | solution.py:1062
  71.9 29.7 %collective-permute-start.29 = (bf16[8,96,384]{2,1,0:T(8,128)(2,1)S(1)}, bf16[8,96,384]{2,1,0:T(8,128)(2,1)S(1)}, u32[]{:S(2)}, u32[]{:S(2)}) collective-permute-start(bf16[8,96,384]{2,1,0:T(8,128)(2,1)S(1)} %get-tuple-element.241.refs_5_), channel_id=1, source_target_pairs={{0,16},{4,20},{8,24},{12,28},{16,0},{20,4},{24,8},{28,12},{1,17},{... | collective-permute-start | bytes 1769480 | tf_op jit(solution)/shard_map/ppermute | solution.py:1062
  74.1 22.6 %collective-permute-start.22 = (bf16[160,768]{1,0:T(8,128)(2,1)S(1)}, bf16[160,768]{1,0:T(8,128)(2,1)S(1)}, u32[]{:S(2)}, u32[]{:S(2)}) collective-permute-start(bf16[160,768]{1,0:T(8,128)(2,1)S(1)} %get-tuple-element.247.refs_9_), channel_id=1, source_target_pairs={{0,1},{1,0},{2,3},{3,2},{4,5},{5,4},{6,7},{7,6},{8,9},{9,8},{10,11... | collective-permute-start | bytes 737288 | tf_op jit(solution)/shard_map/ppermute | solution.py:1064
  74.1 22.7 %collective-permute-start.23 = (bf16[160,768]{1,0:T(8,128)(2,1)S(1)}, bf16[160,768]{1,0:T(8,128)(2,1)S(1)}, u32[]{:S(2)}, u32[]{:S(2)}) collective-permute-start(bf16[160,768]{1,0:T(8,128)(2,1)S(1)} %get-tuple-element.247.refs_9_), channel_id=1, source_target_pairs={{0,2},{1,3},{2,0},{3,1},{4,6},{5,7},{6,4},{7,5},{8,10},{9,11},{10,... | collective-permute-start | bytes 737288 | tf_op jit(solution)/shard_map/ppermute | solution.py:1064
  75.1 21.7 %collective-permute-start.24 = (bf16[160,768]{1,0:T(8,128)(2,1)S(1)}, bf16[160,768]{1,0:T(8,128)(2,1)S(1)}, u32[]{:S(2)}, u32[]{:S(2)}) collective-permute-start(bf16[160,768]{1,0:T(8,128)(2,1)S(1)} %get-tuple-element.247.refs_9_), channel_id=1, source_target_pairs={{0,3},{1,2},{2,1},{3,0},{4,7},{5,6},{6,5},{7,4},{8,11},{9,10},{10,... | collective-permute-start | bytes 737288 | tf_op jit(solution)/shard_map/ppermute | solution.py:1064
  84.8 14.5 %collective-permute-start.20 = (bf16[2,8,48,384]{3,2,1,0:T(8,128)(2,1)S(1)}, bf16[2,8,48,384]{3,2,1,0:T(8,128)(2,1)S(1)}, u32[]{:S(2)}, u32[]{:S(2)}) collective-permute-start(bf16[2,8,48,384]{3,2,1,0:T(8,128)(2,1)S(1)} %pad_maximum_fusion.refs_1_), channel_id=1, source_target_pairs={{0,4},{4,0},{8,12},{12,8},{16,20},{20,16},{24,28},{28,24},{1,5},{5... | collective-permute-start | bytes 1769480 | tf_op jit(solution)/shard_map/ppermute | solution.py:1062
  96.6 16.8 %collective-permute-start.30 = (bf16[8,96,384]{2,1,0:T(8,128)(2,1)S(1)}, bf16[8,96,384]{2,1,0:T(8,128)(2,1)S(1)}, u32[]{:S(2)}, u32[]{:S(2)}) collective-permute-start(bf16[8,96,384]{2,1,0:T(8,128)(2,1)S(1)} %get-tuple-element.241.refs_5_), channel_id=1, source_target_pairs={{0,8},{4,12},{8,0},{12,4},{16,24},{20,28},{24,16},{28,20},{1,9},{5... | collective-permute-start | bytes 1769480 | tf_op jit(solution)/shard_map/ppermute | solution.py:1062
  99.2 14.2 %collective-permute-start.28 = (bf16[2,8,48,384]{3,2,1,0:T(8,128)(2,1)S(1)}, bf16[2,8,48,384]{3,2,1,0:T(8,128)(2,1)S(1)}, u32[]{:S(2)}, u32[]{:S(2)}) collective-permute-start(bf16[2,8,48,384]{3,2,1,0:T(8,128)(2,1)S(1)} %pad_maximum_fusion.1.refs_3_), channel_id=1, source_target_pairs={{0,4},{4,0},{8,12},{12,8},{16,20},{20,16},{24,28},{28,24},{1,5},{5... | collective-permute-start | bytes 1769480 | tf_op jit(solution)/shard_map/ppermute | solution.py:1062
  100.0 13.4 %collective-permute-start.25 = (bf16[160,768]{1,0:T(8,128)(2,1)S(1)}, bf16[160,768]{1,0:T(8,128)(2,1)S(1)}, u32[]{:S(2)}, u32[]{:S(2)}) collective-permute-start(bf16[160,768]{1,0:T(8,128)(2,1)S(1)} %get-tuple-element.243.refs_5_), channel_id=1, source_target_pairs={{0,1},{1,0},{2,3},{3,2},{4,5},{5,4},{6,7},{7,6},{8,9},{9,8},{10,11... | collective-permute-start | bytes 737288 | tf_op jit(solution)/shard_map/ppermute | solution.py:1064
  100.0 13.4 %collective-permute-start.26 = (bf16[160,768]{1,0:T(8,128)(2,1)S(1)}, bf16[160,768]{1,0:T(8,128)(2,1)S(1)}, u32[]{:S(2)}, u32[]{:S(2)}) collective-permute-start(bf16[160,768]{1,0:T(8,128)(2,1)S(1)} %get-tuple-element.243.refs_5_), channel_id=1, source_target_pairs={{0,2},{1,3},{2,0},{3,1},{4,6},{5,7},{6,4},{7,5},{8,10},{9,11},{10,... | collective-permute-start | bytes 737288 | tf_op jit(solution)/shard_map/ppermute | solution.py:1064
  101.5 11.9 %collective-permute-start.27 = (bf16[160,768]{1,0:T(8,128)(2,1)S(1)}, bf16[160,768]{1,0:T(8,128)(2,1)S(1)}, u32[]{:S(2)}, u32[]{:S(2)}) collective-permute-start(bf16[160,768]{1,0:T(8,128)(2,1)S(1)} %get-tuple-element.243.refs_5_), channel_id=1, source_target_pairs={{0,3},{1,2},{2,1},{3,0},{4,7},{5,6},{6,5},{7,4},{8,11},{9,10},{10,... | collective-permute-start | bytes 737288 | tf_op jit(solution)/shard_map/ppermute | solution.py:1064
  120.8 15.4 %collective-permute-start.34 = (bf16[2,384,384]{2,1,0:T(8,128)(2,1)S(1)}, bf16[2,384,384]{2,1,0:T(8,128)(2,1)S(1)}, u32[]{:S(2)}, u32[]{:S(2)}) collective-permute-start(bf16[2,384,384]{2,1,0:T(8,128)(2,1)S(1)} %get-tuple-element.262), channel_id=1, source_target_pairs={{0,4},{4,0},{8,12},{12,8},{16,20},{20,16},{24,28},{28,24},{1,5},{5... | collective-permute-start | bytes 1769480 | tf_op jit(solution)/shard_map/ppermute | solution.py:1062
  121.9 15.2 %collective-permute-start.35 = (bf16[8,96,384]{2,1,0:T(8,128)(2,1)S(1)}, bf16[8,96,384]{2,1,0:T(8,128)(2,1)S(1)}, u32[]{:S(2)}, u32[]{:S(2)}) collective-permute-start(bf16[8,96,384]{2,1,0:T(8,128)(2,1)S(1)} %collective-permute-done.29.refs_7_), channel_id=1, source_target_pairs={{0,8},{4,12},{8,0},{12,4},{16,24},{20,28},{24,16},{28,20},{1,9},{5... | collective-permute-start | bytes 1769480 | tf_op jit(solution)/shard_map/ppermute | solution.py:1062
  123.2 11.9 %collective-permute-start.33 = (bf16[160,768]{1,0:T(8,128)(2,1)S(1)}, bf16[160,768]{1,0:T(8,128)(2,1)S(1)}, u32[]{:S(2)}, u32[]{:S(2)}) collective-permute-start(bf16[160,768]{1,0:T(8,128)(2,1)S(1)} %get-tuple-element.259), channel_id=1, source_target_pairs={{0,3},{1,2},{2,1},{3,0},{4,7},{5,6},{6,5},{7,4},{8,11},{9,10},{10,... | collective-permute-start | bytes 737288 | tf_op jit(solution)/shard_map/ppermute | solution.py:1064
  138.1 14.0 %collective-permute-start.37 = (bf16[2,96,384]{2,1,0:T(8,128)(2,1)S(1)}, bf16[2,96,384]{2,1,0:T(8,128)(2,1)S(1)}, u32[]{:S(2)}, u32[]{:S(2)}) collective-permute-start(bf16[2,96,384]{2,1,0:T(8,128)(2,1)S(1)} %get-tuple-element.286), channel_id=1, source_target_pairs={{0,16},{4,20},{8,24},{12,28},{16,0},{20,4},{24,8},{28,12},{1,17},{... | collective-permute-start | bytes 442376 | tf_op jit(solution)/shard_map/ppermute | solution.py:1062
  140.6 19.4 %collective-permute-start.38 = (bf16[2,96,384]{2,1,0:T(8,128)(2,1)S(1)}, bf16[2,96,384]{2,1,0:T(8,128)(2,1)S(1)}, u32[]{:S(2)}, u32[]{:S(2)}) collective-permute-start(bf16[2,96,384]{2,1,0:T(8,128)(2,1)S(1)} %get-tuple-element.287), channel_id=1, source_target_pairs={{0,24},{4,28},{8,16},{12,20},{16,8},{20,12},{24,0},{28,4},{1,25},{... | collective-permute-start | bytes 442376 | tf_op jit(solution)/shard_map/ppermute | solution.py:1062
  142.2 18.0 %collective-permute-start.39 = (bf16[2,384,384]{2,1,0:T(8,128)(2,1)S(1)}, bf16[2,384,384]{2,1,0:T(8,128)(2,1)S(1)}, u32[]{:S(2)}, u32[]{:S(2)}) collective-permute-start(bf16[2,384,384]{2,1,0:T(8,128)(2,1)S(1)} %get-tuple-element.288), channel_id=1, source_target_pairs={{0,4},{4,0},{8,12},{12,8},{16,20},{20,16},{24,28},{28,24},{1,5},{5... | collective-permute-start | bytes 1769480 | tf_op jit(solution)/shard_map/ppermute | solution.py:1062
  143.1 17.1 %collective-permute-start.40 = (bf16[160,768]{1,0:T(8,128)(2,1)S(1)}, bf16[160,768]{1,0:T(8,128)(2,1)S(1)}, u32[]{:S(2)}, u32[]{:S(2)}) collective-permute-start(bf16[160,768]{1,0:T(8,128)(2,1)S(1)} %get-tuple-element.290), channel_id=1, source_target_pairs={{0,1},{1,0},{2,3},{3,2},{4,5},{5,4},{6,7},{7,6},{8,9},{9,8},{10,11... | collective-permute-start | bytes 737288 | tf_op jit(solution)/shard_map/ppermute | solution.py:1064
  145.4 14.8 %collective-permute-start.41 = (bf16[160,768]{1,0:T(8,128)(2,1)S(1)}, bf16[160,768]{1,0:T(8,128)(2,1)S(1)}, u32[]{:S(2)}, u32[]{:S(2)}) collective-permute-start(bf16[160,768]{1,0:T(8,128)(2,1)S(1)} %get-tuple-element.291), channel_id=1, source_target_pairs={{0,2},{1,3},{2,0},{3,1},{4,6},{5,7},{6,4},{7,5},{8,10},{9,11},{10,... | collective-permute-start | bytes 737288 | tf_op jit(solution)/shard_map/ppermute | solution.py:1064
  167.5 29.4 %collective-permute-start.44 = (bf16[2,384,384]{2,1,0:T(8,128)(2,1)S(1)}, bf16[2,384,384]{2,1,0:T(8,128)(2,1)S(1)}, u32[]{:S(2)}, u32[]{:S(2)}) collective-permute-start(bf16[2,384,384]{2,1,0:T(8,128)(2,1)S(1)} %get-tuple-element.317), channel_id=1, source_target_pairs={{0,4},{4,0},{8,12},{12,8},{16,20},{20,16},{24,28},{28,24},{1,5},{5... | collective-permute-start | bytes 1769480 | tf_op jit(solution)/shard_map/ppermute | solution.py:1062
  168.6 28.2 %collective-permute-start.45 = (bf16[2,384,384]{2,1,0:T(8,128)(2,1)S(1)}, bf16[2,384,384]{2,1,0:T(8,128)(2,1)S(1)}, u32[]{:S(2)}, u32[]{:S(2)}) collective-permute-start(bf16[2,384,384]{2,1,0:T(8,128)(2,1)S(1)} %get-tuple-element.318), channel_id=1, source_target_pairs={{0,2},{1,3},{2,0},{3,1},{4,6},{5,7},{6,4},{7,5},{8,10},{9,11},{10,... | collective-permute-start | bytes 1769480 | tf_op jit(solution)/shard_map/ppermute | solution.py:1064
  169.2 27.6 %collective-permute-start.46 = (bf16[2,384,384]{2,1,0:T(8,128)(2,1)S(1)}, bf16[2,384,384]{2,1,0:T(8,128)(2,1)S(1)}, u32[]{:S(2)}, u32[]{:S(2)}) collective-permute-start(bf16[2,384,384]{2,1,0:T(8,128)(2,1)S(1)} %get-tuple-element.319), channel_id=1, source_target_pairs={{0,6},{1,7},{2,4},{3,5},{4,2},{5,3},{6,0},{7,1},{8,14},{9,15},{10,... | collective-permute-start | bytes 1769480 | tf_op jit(solution)/shard_map/ppermute | solution.py:1066
  180.6 12.5 %collective-permute-start.51 = (bf16[2,96,384]{2,1,0:T(8,128)(2,1)S(1)}, bf16[2,96,384]{2,1,0:T(8,128)(2,1)S(1)}, u32[]{:S(2)}, u32[]{:S(2)}) collective-permute-start(bf16[2,96,384]{2,1,0:T(8,128)(2,1)S(1)} %get-tuple-element.327), channel_id=1, source_target_pairs={{0,16},{4,20},{8,24},{12,28},{16,0},{20,4},{24,8},{28,12},{1,17},{... | collective-permute-start | bytes 442376 | tf_op jit(solution)/shard_map/ppermute | solution.py:1062
  180.6 12.5 %collective-permute-start.52 = (bf16[2,96,384]{2,1,0:T(8,128)(2,1)S(1)}, bf16[2,96,384]{2,1,0:T(8,128)(2,1)S(1)}, u32[]{:S(2)}, u32[]{:S(2)}) collective-permute-start(bf16[2,96,384]{2,1,0:T(8,128)(2,1)S(1)} %get-tuple-element.328), channel_id=1, source_target_pairs={{0,24},{4,28},{8,16},{12,20},{16,8},{20,12},{24,0},{28,4},{1,25},{... | collective-permute-start | bytes 442376 | tf_op jit(solution)/shard_map/ppermute | solution.py:1062
  202.0 11.4 %collective-permute-start.54 = (bf16[2,96,384]{2,1,0:T(8,128)(2,1)S(1)}, bf16[2,96,384]{2,1,0:T(8,128)(2,1)S(1)}, u32[]{:S(2)}, u32[]{:S(2)}) collective-permute-start(bf16[2,96,384]{2,1,0:T(8,128)(2,1)S(1)} %get-tuple-element.331), channel_id=1, source_target_pairs={{0,8},{4,12},{8,0},{12,4},{16,24},{20,28},{24,16},{28,20},{1,9},{5... | collective-permute-start | bytes 442376 | tf_op jit(solution)/shard_map/ppermute | solution.py:1062
  202.5 14.9 %collective-permute-start.55 = (bf16[2,96,384]{2,1,0:T(8,128)(2,1)S(1)}, bf16[2,96,384]{2,1,0:T(8,128)(2,1)S(1)}, u32[]{:S(2)}, u32[]{:S(2)}) collective-permute-start(bf16[2,96,384]{2,1,0:T(8,128)(2,1)S(1)} %get-tuple-element.332), channel_id=1, source_target_pairs={{0,16},{4,20},{8,24},{12,28},{16,0},{20,4},{24,8},{28,12},{1,17},{... | collective-permute-start | bytes 442376 | tf_op jit(solution)/shard_map/ppermute | solution.py:1062
  204.4 12.9 %collective-permute-start.56 = (bf16[2,96,384]{2,1,0:T(8,128)(2,1)S(1)}, bf16[2,96,384]{2,1,0:T(8,128)(2,1)S(1)}, u32[]{:S(2)}, u32[]{:S(2)}) collective-permute-start(bf16[2,96,384]{2,1,0:T(8,128)(2,1)S(1)} %get-tuple-element.333), channel_id=1, source_target_pairs={{0,24},{4,28},{8,16},{12,20},{16,8},{20,12},{24,0},{28,4},{1,25},{... | collective-permute-start | bytes 442376 | tf_op jit(solution)/shard_map/ppermute | solution.py:1062
  211.8 12.1 %collective-permute-start.60 = (bf16[4,2,48,384]{3,2,1,0:T(8,128)(2,1)S(1)}, bf16[4,2,48,384]{3,2,1,0:T(8,128)(2,1)S(1)}, u32[]{:S(2)}, u32[]{:S(2)}) collective-permute-start(bf16[4,2,48,384]{3,2,1,0:T(8,128)(2,1)S(1)} %get-tuple-element.342), channel_id=1, source_target_pairs={{0,4},{4,0},{8,12},{12,8},{16,20},{20,16},{24,28},{28,24},{1,5},{5... | collective-permute-start | bytes 884744 | tf_op jit(solution)/shard_map/ppermute | solution.py:1062
  213.4 10.5 %collective-permute-start.58 = (bf16[2,96,384]{2,1,0:T(8,128)(2,1)S(1)}, bf16[2,96,384]{2,1,0:T(8,128)(2,1)S(1)}, u32[]{:S(2)}, u32[]{:S(2)}) collective-permute-start(bf16[2,96,384]{2,1,0:T(8,128)(2,1)S(1)} %add_convert_fusion.1.refs_1_), channel_id=1, source_target_pairs={{0,16},{4,20},{8,24},{12,28},{16,0},{20,4},{24,8},{28,12},{1,17},{... | collective-permute-start | bytes 442376 | tf_op jit(solution)/shard_map/ppermute | solution.py:1062
  223.9 9.8 %collective-permute-start.63 = (bf16[2,96,384]{2,1,0:T(8,128)(2,1)S(1)}, bf16[2,96,384]{2,1,0:T(8,128)(2,1)S(1)}, u32[]{:S(2)}, u32[]{:S(2)}) collective-permute-start(bf16[2,96,384]{2,1,0:T(8,128)(2,1)S(1)} %add_convert_fusion.refs_1_), channel_id=1, source_target_pairs={{0,16},{4,20},{8,24},{12,28},{16,0},{20,4},{24,8},{28,12},{1,17},{... | collective-permute-start | bytes 442376 | tf_op jit(solution)/shard_map/ppermute | solution.py:1062
  241.7 18.2 %collective-permute-start.76 = (f32[13,768]{1,0:T(8,128)S(1)}, f32[13,768]{1,0:T(8,128)S(1)}, u32[]{:S(2)}, u32[]{:S(2)}) collective-permute-start(f32[13,768]{1,0:T(8,128)S(1)} %add.65.refs_0_), channel_id=1, source_target_pairs={{0,8},{4,12},{8,0},{12,4},{16,24},{20,28},{24,16},{28,20},{1,9},{5... | collective-permute-start | bytes 119816 | tf_op jit(solution)/shard_map/ppermute | solution.py:1062
  242.6 17.3 %collective-permute-start.77 = (f32[13,768]{1,0:T(8,128)S(1)}, f32[13,768]{1,0:T(8,128)S(1)}, u32[]{:S(2)}, u32[]{:S(2)}) collective-permute-start(f32[13,768]{1,0:T(8,128)S(1)} %add.65.refs_0_), channel_id=1, source_target_pairs={{0,16},{4,20},{8,24},{12,28},{16,0},{20,4},{24,8},{28,12},{1,17},{... | collective-permute-start | bytes 119816 | tf_op jit(solution)/shard_map/ppermute | solution.py:1062
  257.9 13.9 %collective-permute-start.72 = (bf16[4,2,48,384]{3,2,1,0:T(8,128)(2,1)S(1)}, bf16[4,2,48,384]{3,2,1,0:T(8,128)(2,1)S(1)}, u32[]{:S(2)}, u32[]{:S(2)}) collective-permute-start(bf16[4,2,48,384]{3,2,1,0:T(8,128)(2,1)S(1)} %get-tuple-element.364), channel_id=1, source_target_pairs={{0,4},{4,0},{8,12},{12,8},{16,20},{20,16},{24,28},{28,24},{1,5},{5... | collective-permute-start | bytes 884744 | tf_op jit(solution)/shard_map/ppermute | solution.py:1062
  259.1 10.9 %collective-permute-start.71 = (bf16[4,2,48,384]{3,2,1,0:T(8,128)(2,1)S(1)}, bf16[4,2,48,384]{3,2,1,0:T(8,128)(2,1)S(1)}, u32[]{:S(2)}, u32[]{:S(2)}) collective-permute-start(bf16[4,2,48,384]{3,2,1,0:T(8,128)(2,1)S(1)} %get-tuple-element.356), channel_id=1, source_target_pairs={{0,4},{4,0},{8,12},{12,8},{16,20},{20,16},{24,28},{28,24},{1,5},{5... | collective-permute-start | bytes 884744 | tf_op jit(solution)/shard_map/ppermute | solution.py:1062
  (50 other events, 453.7 us)

commit v3 on v2

--- a/solution.py
+++ b/solution.py
@@ -658,13 +658,14 @@
 def hidden_kernel(order, group, pieces, place_ref, *refs):
     piece_refs, refs = refs[: len(pieces)], refs[len(pieces) :]
     row_refs, refs = refs[:group], refs[group:]
-    grad_refs, refs = refs[:group], refs[group:]
+    grad_refs, refs = refs[: group // PAIR], refs[group // PAIR :]
     vec_ref = refs[0]
     back_refs, refs = refs[1 : 1 + group], refs[1 + group :]
     rows_ref, grads_ref, active_ref, hidden_ref, down_hbm = refs[:5]
     weights, sems, out_sem = refs[5:]
     z, x, m = place_ref[0], place_ref[1], place_ref[2]
     piece = piece_refs[0].shape[2]
+    local = weights.shape[0] // 2
     bias = jnp.sum(bias_row(m, vec_ref[9:, :], vec_ref.shape[0] - 9), axis=0, keepdims=True)
     copies = []
     for ref, (slots, dx) in zip(piece_refs, pieces):
@@ -677,7 +678,7 @@
     count = row_refs[0].shape[0]
     for index in range(group):
         rows_ref[index * count : (index + 1) * count, :] = row_refs[index][...]
-        grads_ref[index * count : (index + 1) * count, :] = grad_refs[index][...]
+        grads_ref[index * count : (index + 1) * count, :] = grad_refs[index // PAIR][index % PAIR]
     for copy in copies:
         copy.wait()
     local = weights.shape[0] // 2
@@ -714,10 +715,12 @@
     keep_down.wait()
 
 
-def share_blocks(place_ref, blocks, kept_ref, sent_ref):
+def share_blocks(place_ref, blocks, kept_ref, *sent_refs):
     own, x = kept_ref.shape[0], place_ref[1]
     kept_ref[...] = blocks[pl.ds(x * own, own)]
-    sent_ref[...] = blocks[pl.ds((1 - x) * own, own)]
+    count = own // len(sent_refs)
+    for index, ref in enumerate(sent_refs):
+        ref[...] = blocks[pl.ds((1 - x) * own + index * count, count)]
 
 
 def up_grads_kernel(order, place_ref, rows_ref, hidden_ref, kept_ref, sent_ref, bias_ref, blocks):
@@ -734,7 +737,7 @@
 
 
 def down_grads_kernel(order, group, place_ref, grads_ref, active_ref, down_ref, *refs):
-    feed_refs, (kept_ref, sent_ref, blocks) = refs[:group], refs[group:]
+    feed_kept_ref, feed_sent_ref, kept_ref, first_ref, second_ref, blocks = refs
     count = grads_ref.shape[0] // group
     row_blocks = grads_ref.shape[1] // order
     col_blocks = down_ref.shape[0] // row_blocks
@@ -746,7 +749,8 @@
             )
             total = part if total is None else total + part
         for index in range(group):
-            feed_refs[index][:, row * order : (row + 1) * order] = to_half(
+            target = (feed_kept_ref, feed_sent_ref)[index % PAIR]
+            target[index // PAIR, :, row * order : (row + 1) * order] = to_half(
                 total[index * count : (index + 1) * count, :]
             )
     for col in range(col_blocks):
@@ -756,7 +760,7 @@
             blocks[col * row_blocks + row] = to_half(
                 row_product(active_ref[:, lanes], grads_ref[:, others])
             )
-    share_blocks(place_ref, blocks, kept_ref, sent_ref)
+    share_blocks(place_ref, blocks, kept_ref, first_ref, second_ref)
 
 
 def backward_kernel(order, group, place_ref, *refs):
@@ -892,95 +896,132 @@
 def core_sum_kernel(place_ref, kept_ref, came_ref, *out_refs):
     x, m = place_ref[1], place_ref[2]
     own = kept_ref.shape[1] // PAIR
-    for index, out_ref in enumerate(out_refs):
+    chips = len(out_refs) // 2
+    for index in range(chips):
         dy, dx = index // PAIR, index % PAIR
         high = (m // PAIR) ^ dy
         for block in range(own):
             at = (x ^ dx) * own + block
-            out_ref[block] = to_half(
+            out_ref = out_refs[block // (own // 2) * chips + index]
+            out_ref[block % (own // 2)] = to_half(
                 kept_ref[high, at].astype(full) + came_ref[high, at].astype(full)
             )
 
 
-def row_sum_kernel(count, place_ref, *refs):
-    ins, outs = refs[:count], refs[count:]
-    rows = outs[0].shape[1]
-    for slot, out_ref in enumerate(outs):
+def row_sum_kernel(groups, count, place_ref, *refs):
+    ins, outs = refs[: groups * count], refs[groups * count :]
+    rows = outs[0].shape[-2]
+    near = len(outs) == 2
+    slots = outs[0].shape[0] * 2 if near else len(outs)
+    for slot in range(slots):
+        out_ref = outs[slot % 2].at[slot // 2] if near else outs[slot]
         start = pl.multiple_of((place_ref[0] ^ slot) * rows, 16)
-        for block in range(out_ref.shape[0]):
-            total = ins[0][block, pl.ds(start, rows), :].astype(full)
-            for ref in ins[1:]:
-                total = total + ref[block, pl.ds(start, rows), :].astype(full)
-            out_ref[block] = to_half(total)
-
-
-def whole_step_kernel(count, first, place_ref, *refs):
+        at = 0
+        for group in range(groups):
+            parts = ins[group * count : (group + 1) * count]
+            for block in range(parts[0].shape[0]):
+                total = parts[0][block, pl.ds(start, rows), :].astype(full)
+                for ref in parts[1:]:
+                    total = total + ref[block, pl.ds(start, rows), :].astype(full)
+                out_ref[at] = to_half(total)
+                at += 1
+
+
+def line_blocks(z, refs, target, first=0):
+    for slot, ref in enumerate(refs):
+        rows = ref.shape[-2]
+        start = pl.multiple_of((z ^ slot) * rows, 16)
+        for block in range(target.shape[0]):
+            target[block, pl.ds(start, rows), :] = ref[first + block]
+
+
+def line_roots(z, refs, target, first):
+    for slot, ref in enumerate(refs):
+        rows = ref.shape[1]
+        for block in range(target.shape[0]):
+            for part in range(PAIR):
+                start = pl.multiple_of((z ^ slot) * (PAIR * rows) + part * rows, 16)
+                at = (first + block) * PAIR + part
+                target[block, pl.ds(start, rows), :] = ref[at]
+
+
+def step_parts(z, x, own, whole, step, terms, found, block, kept_ref, sent_ref):
+    rows, order = own.shape
+    mine = pl.multiple_of(z * rows, 16)
+    half_rows = rows // PAIR
+    terms[...] = row_product(whole, whole)
+    found[0] = own.astype(full)
+    found[1] = times_transpose(own, whole)
+    found[2] = terms[pl.ds(mine, rows), :]
+    found[3] = step
+    for target, part in ((kept_ref, x), (sent_ref, 1 - x)):
+        start = pl.multiple_of(part * half_rows, 16)
+        for kind in range(4):
+            target[kind, block] = to_half(found[kind, pl.ds(start, half_rows), :])
+
+
+def whole_step_kernel(count, left_first, place_ref, *refs):
     grad_refs, refs = refs[:count], refs[count:]
     root_refs, refs = refs[:count], refs[count:]
-    kept_ref, sent_ref, grads, rights, lefts, terms, found = refs
+    kept_ref, sent_ref, grads, lefts, rights, terms, found, steps = refs
     z, x = place_ref[0], place_ref[1]
     blocks, rows, order = grad_refs[0].shape
-    for slot in range(count):
-        start = pl.multiple_of((z ^ slot) * rows, 16)
-        for block in range(blocks):
-            grads[block, pl.ds(start, rows), :] = grad_refs[slot][block]
-            rights[block, pl.ds(start, rows), :] = root_refs[slot][block]
-            lefts[block, pl.ds(start, rows), :] = root_refs[slot][first + block]
+    line_blocks(z, grad_refs, grads)
+    line_roots(z, root_refs, rights, 0)
+    line_roots(z, root_refs, lefts, left_first)
     mine = pl.multiple_of(z * rows, 16)
     for block in range(blocks):
         whole = grads[block]
-        own = grad_refs[0][block]
         step = to_half(dot32(lefts[block], whole))
         step = dot32(step, rights[block])
         mean = jnp.mean(jnp.mean(step * step, axis=1, keepdims=True), axis=0, keepdims=True)
-        terms[0] = row_product(whole, whole)
-        terms[1] = step * lax.rsqrt(mean + 1e-06)
-        found[0] = own.astype(full)
-        found[1] = times_transpose(own, whole)
-        found[2] = terms[0, pl.ds(mine, rows), :]
-        found[3] = terms[1, pl.ds(mine, rows), :]
-        half_rows = rows // PAIR
-        for target, part in ((kept_ref, x), (sent_ref, 1 - x)):
-            start = pl.multiple_of(part * half_rows, 16)
-            for kind in range(4):
-                target[kind, block] = to_half(found[kind, pl.ds(start, half_rows), :])
+        steps[...] = step * lax.rsqrt(mean + 1e-06)
+        step = steps[pl.ds(mine, rows), :]
+        step_parts(z, x, grad_refs[0][block], whole, step, terms, found, block, kept_ref, sent_ref)
 
 
 def step_kernel(count, first, place_ref, *refs):
     grad_refs, refs = refs[:count], refs[count:]
-    right_refs, refs = refs[:count], refs[count:]
+    root_refs, refs = refs[:count], refs[count:]
     left_ref, kept_ref, sent_ref, square_ref, grads, rights, terms, found = refs
     z, x = place_ref[0], place_ref[1]
     blocks, rows, order = grad_refs[0].shape
-    for slot in range(count):
-        start = pl.multiple_of((z ^ slot) * rows, 16)
-        for block in range(blocks):
-            grads[block, pl.ds(start, rows), :] = grad_refs[slot][block]
-            rights[block, pl.ds(start, rows), :] = right_refs[slot][first + block]
-    mine = pl.multiple_of(z * rows, 16)
+    line_blocks(z, grad_refs, grads)
+    line_roots(z, root_refs, rights, first)
     square_ref[...] = jnp.zeros_like(square_ref)
     for block in range(blocks):
         whole = grads[block]
-        own = grad_refs[0][block]
         step = to_half(dot32(left_ref[first + block], whole))
         step = dot32(step, rights[block])
-        square_ref[block : block + 1, :] = jnp.broadcast_to(
-            jnp.sum(jnp.sum(step * step, axis=1, keepdims=True), axis=0, keepdims=True), (1, 128)
-        )
-        terms[...] = row_product(whole, whole)
-        found[0] = own.astype(full)
-        found[1] = times_transpose(own, whole)
-        found[2] = terms[pl.ds(mine, rows), :]
-        found[3] = step
-        half_rows = rows // PAIR
-        for target, part in ((kept_ref, x), (sent_ref, 1 - x)):
-            start = pl.multiple_of(part * half_rows, 16)
-            for kind in range(4):
-                target[kind, block] = to_half(found[kind, pl.ds(start, half_rows), :])
+        total = jnp.sum(jnp.sum(step * step, axis=1, keepdims=True), axis=0, keepdims=True)
+        square_ref[block : block + 1, :] = jnp.broadcast_to(total, (1, 128))
+        step_parts(z, x, grad_refs[0][block], whole, step, terms, found, block, kept_ref, sent_ref)
+        total = jnp.broadcast_to(total, (16, order))
+        terms_of = jnp.zeros((16, order), full)
+        row = lax.broadcasted_iota(jnp.int32, (16, order), 0)
+        for index in range(3):
+            part = to_half(total).astype(full)
+            terms_of = jnp.where(row == index, part, terms_of)
+            total = total - part
+        sent_ref[4, block, :16, :] = to_half(terms_of)
+        sent_ref[4, block, 16:, :] = jnp.zeros((sent_ref.shape[2] - 16, order), half)
+
+
+def squares_kernel(*refs):
+    count = len(refs) // 2
+    mine_refs, came_refs, out_ref = refs[:count], refs[count:-1], refs[-1]
+    blocks = came_refs[0].shape[1]
+    for matrix in range(count):
+        for block in range(blocks):
+            at = matrix * blocks + block
+            out_ref[at : at + 1, :] = mine_refs[matrix][block : block + 1, :]
+            terms = came_refs[matrix][4, block, 0:16, 0:128].astype(full)
+            at += count * blocks
+            out_ref[at : at + 1, :] = jnp.sum(terms, axis=0, keepdims=True)
 
 
 def apply_kernel(
-    first, order, rates, place_ref, weight_ref, left_ref, right_ref, kept_ref, came_ref, *refs
+    order, rates, matrix, place_ref, weight_ref, left_ref, right_ref, kept_ref, came_ref, *refs
 ):
     total_ref = refs[0] if len(refs) == 6 else None
     grad_ref, new_left_ref, new_right_ref, new_ref, half_ref = refs[-5:]
@@ -990,15 +1031,15 @@
     for side, ref in ((0, kept_ref), (1, came_ref)):
         for block in range(own):
             at = (x ^ side) * own + block
-            index = first + block
             rate = jnp.where(m * local + at < rates[0], rates[1], rates[2])
-            scale = 1.0
             if total_ref is not None:
-                scale = lax.rsqrt(total_ref[side, index : index + 1, 0:1] / (order * order) + 1e-06)
-            grad_ref[at] = ref[0, index].astype(full)
-            new_left_ref[at] = 0.95 * left_ref[at] + 0.05 * ref[1, index].astype(full)
-            new_right_ref[at] = 0.95 * right_ref[at] + 0.05 * ref[2, index].astype(full)
-            new = weight_ref[at] - (rate * scale) * ref[3, index].astype(full)
+                row = (side * 2 + matrix) * own + block
+                total = total_ref[row : row + 1, 0:1]
+                rate = rate * lax.rsqrt(total / (order * order) + 1e-06)
+            grad_ref[at] = ref[0, block].astype(full)
+            new_left_ref[at] = 0.95 * left_ref[at] + 0.05 * ref[1, block].astype(full)
+            new_right_ref[at] = 0.95 * right_ref[at] + 0.05 * ref[2, block].astype(full)
+            new = weight_ref[at] - rate * ref[3, block].astype(full)
             new_ref[at] = new
             half_ref[at] = to_half(new)
 
@@ -1025,35 +1066,44 @@
         new_ref[:, lanes] = vec_ref[:, lanes] - 0.05 * (block * scale)
 
 
-def weights_kernel(attn_ref, up_ref, down_ref, attn_out, feed_out):
-    attn_out[...] = to_half(attn_ref[...])
-    local = up_ref.shape[0]
-    feed_out[:local] = to_half(up_ref[...])
-    feed_out[local:] = to_half(down_ref[...])
-
-
-def roots_kernel(place_ref, *refs):
-    ins, (kept_ref, sent_ref) = refs[:6], refs[6:]
+def first_kernel(place_ref, *refs):
+    ins, refs = refs[:9], refs[9:]
+    attn_out, feed_out, kept_ref, sent_ref = refs[:4]
+    held, sems = refs[4:]
+    copies = [
+        pltpu.make_async_copy(ref, held.at[index], sems.at[index])
+        for index, ref in enumerate(ins)
+    ]
+    for copy in copies:
+        copy.start()
+    local, own = attn_out.shape[0], kept_ref.shape[1]
     x = place_ref[1]
-    own = ins[0].shape[0] // PAIR
-    for index, ref in enumerate(ins):
-        kept_ref[index] = to_half(ref[pl.ds(x * own, own)])
-        sent_ref[index] = to_half(ref[pl.ds((1 - x) * own, own)])
-
-
-def roots_join_kernel(place_ref, kept_ref, came_ref, left_ref, right_ref):
+    for index, copy in enumerate(copies):
+        copy.wait()
+        if index == 0:
+            attn_out[...] = to_half(held[index])
+        elif index < 3:
+            feed_out[(index - 1) * local : index * local] = to_half(held[index])
+        else:
+            kept_ref[index - 3] = to_half(held[index, pl.ds(x * own, own)])
+            sent_ref[index - 3] = to_half(held[index, pl.ds((1 - x) * own, own)])
+
+
+def bundle_kernel(place_ref, kept_ref, came_ref, feed_ref, left_ref, bundle_ref):
     x = place_ref[1]
     kinds, own, piece, order = kept_ref.shape
+    feed = feed_ref.shape[0]
+    bundle_ref[:feed] = feed_ref[...]
     for index in range(kinds):
         for block in range(own):
-            at = (index % 3) * own + block
-            targets = [(left_ref, at)] if index < 3 else [(right_ref, at)]
-            if index == 0:
-                targets.append((right_ref, 3 * own + block))
-            for target, place in targets:
-                for side, ref in ((0, kept_ref), (1, came_ref)):
+            for side, ref in ((0, kept_ref), (1, came_ref)):
+                value = ref[index, block]
+                if index < 3:
                     start = pl.multiple_of((x ^ side) * piece, 16)
-                    target[place, pl.ds(start, piece), :] = ref[index, block]
+                    left_ref[index * own + block, pl.ds(start, piece), :] = value
+                if index == 0 or index >= 3:
+                    at = (index - 3 if index else 3) * own + block
+                    bundle_ref[feed + at * PAIR + (x ^ side)] = value
 
 
 def move(values, dp_mask, mp_mask):
@@ -1110,44 +1160,52 @@
     tok, cot, mask = tokens[0], cotangent[0], keep_mask
     line, member = lax.axis_index("dp"), lax.axis_index("mp")
     place = jnp.stack([line >> 1, line & 1, member, member & 1]).astype(jnp.int32)
-    w_attn_first, place = phase(w_attn, place)
-
-    attn_half, feed_half = local_call(
-        weights_kernel,
-        (w_attn_first, w_fc1, w_fc2),
-        (shape((local, piece, order)), shape((2 * local, piece, order))),
-        in_smem=(),
-    )
-    line_came = [move(attn_half, k * PAIR, 0) for k in lines]
-    plane = [(dx, high * PAIR) for high in range(group // PAIR) for dx in range(PAIR)]
-    first = attn_half[None]
-    first_pieces = [first] + [move(first, dx, dm) for dx, dm in plane[1:]]
-    root_kept, root_sent = local_call(
-        roots_kernel,
+
+    attn_half, feed_half, root_kept, root_sent = local_call(
+        first_kernel,
         (
             place,
-            root_left_attn,
-            root_left_fc1,
-            root_left_fc2,
-            root_right_attn,
-            root_right_fc1,
-            root_right_fc2,
+            *[
+                pltpu.with_memory_space_constraint(value, pltpu.HBM)
+                for value in (
+                    w_attn,
+                    w_fc1,
+                    w_fc2,
+                    root_left_attn,
+                    root_left_fc1,
+                    root_left_fc2,
+                    root_right_attn,
+                    root_right_fc1,
+                    root_right_fc2,
+                )
+            ],
         ),
-        (shape((6, own, piece, order)),) * 2,
-    )
+        (
+            shape((local, piece, order)),
+            shape((2 * local, piece, order)),
+            shape((6, own, piece, order)),
+            shape((6, own, piece, order)),
+        ),
+        scratch=(pltpu.VMEM((9, local, piece, order), full), pltpu.SemaphoreType.DMA((9,))),
+        in_hbm=range(1, 10),
+    )
+    line_came = [move(attn_half, k * PAIR, 0) for k in lines]
     root_came = move(root_sent, 1, 0)
-    second = jnp.stack(line_came)
-    second, first_pieces, root_came, feed_half = phase(
-        second, first_pieces, root_came, feed_half
-    )
-
-    feed_far, feed_near = move(feed_half, 2 * PAIR, 0), move(feed_half, PAIR, 0)
-    second_pieces = [second] + [move(second, dx, dm) for dx, dm in plane[1:]]
-    pieces, piece_info = [], []
-    for slots, found in (((0,), first_pieces), (tuple(lines), second_pieces)):
-        for (dx, dm), part in zip(plane, found):
-            pieces += [part, move(part, 0, 1)]
-            piece_info += [(slots, dx, dm), (slots, dx, dm + 1)]
+    line_came, root_came, attn_half, mask = phase(line_came, root_came, attn_half, mask)
+
+    plane = [(dx, high * PAIR) for high in range(group // PAIR) for dx in range(PAIR)]
+    feed_far = move(feed_half, 2 * PAIR, 0)
+    left_roots, bundle = local_call(
+        bundle_kernel,
+        (place, root_kept, root_came, feed_half),
+        (
+            shape((3 * own, PAIR * piece, order)),
+            shape((2 * local + 4 * own * PAIR, piece, order)),
+        ),
+    )
+    bundle_near = move(bundle, PAIR, 0)
+    stack = jnp.stack([attn_half, *line_came])
+    found = [stack] + [move(stack, dx, dm) for dx, dm in plane[1:]]
     normed, grad_sent, chosen = local_call(
         prepare_kernel,
         (mask, tok, cot, vectors),
@@ -1155,14 +1213,29 @@
         in_smem=(),
         micros=1.5,
     )
-    feed_near = jnp.stack([feed_half, feed_near])
-    pieces, feed_near, feed_far, normed, grad_sent, chosen = phase(
-        pieces, feed_near, feed_far, normed, grad_sent, chosen
-    )
-
-    near_came = move(feed_near, 1, 0)
+    found, grad_sent, normed, chosen, feed_far, bundle_near = phase(
+        found, grad_sent, normed, chosen, feed_far, bundle_near
+    )
+
+    pieces, piece_info = [], []
+    for (dx, dm), part in zip(plane, found):
+        pieces += [part, move(part, 0, 1)]
+        piece_info += [(range(z_count), dx, dm), (range(z_count), dx, dm + 1)]
+    grad_came = move(grad_sent, 0, 1)
+    feed_count = 2 * local
+    feed_near = jnp.stack([feed_half, bundle_near[:feed_count]])
+    roots, roots_near = bundle[feed_count:], bundle_near[feed_count:]
+    half_roots = roots.shape[0] // 2
+    roots_first, roots_second = roots[:half_roots], roots[half_roots:]
+    pieces, grad_came, feed_near, roots_first, roots_second, roots, roots_near = phase(
+        pieces, grad_came, feed_near, roots_first, roots_second, roots, roots_near
+    )
+
+    feed_near_came = move(feed_near, 1, 0)
     feed_last = move(feed_far, PAIR, 0)
-    group_grads = [grad_sent] + [move(grad_sent, 0, k) for k in others]
+    roots_first_far = move(roots_first, 2 * PAIR, 0)
+    pair = jnp.stack([grad_sent, grad_came])
+    group_grads = [pair] + [move(pair, 0, dm) for dm in range(PAIR, group, PAIR)]
     count = len(pieces)
     rows_sent, qkv, probs, attended, branch, weights = local_call(
         lambda *refs: forward_kernel(order, piece_info, *refs),
@@ -1178,7 +1251,7 @@
         scratch=(
             pltpu.VMEM((group * local, order, order), half),
             pltpu.VMEM(heads, full),
-            pltpu.SemaphoreType.DMA((count * z_count // 2,)),
+            pltpu.SemaphoreType.DMA((count * z_count,)),
             pltpu.SemaphoreType.DMA(()),
             pltpu.SemaphoreType.DMA((HEADS // 2,)),
         ),
@@ -1186,28 +1259,20 @@
         out_hbm=(2, 5),
         micros=8,
     )
+    rows_sent, group_grads, feed_near_came, feed_last, roots_first_far = phase(
+        rows_sent, group_grads, feed_near_came, feed_last, roots_first_far
+    )
+
+    group_rows = [rows_sent] + [move(rows_sent, 0, k) for k in others]
     feed_far = jnp.stack([feed_far, feed_last])
-    rows_sent, near_came, feed_far, group_grads = phase(
-        rows_sent, near_came, feed_far, group_grads
-    )
-
-    group_rows = [rows_sent] + [move(rows_sent, 0, k) for k in others]
-    far_came = move(feed_far, 1, 0)
-    left_roots, right_root = local_call(
-        roots_join_kernel,
-        (place, root_kept, root_came),
-        (shape((3 * own, PAIR * piece, order)), shape((4 * own, PAIR * piece, order))),
-    )
-    roots_far = move(right_root, 2 * PAIR, 0)
-    roots_near = move(right_root, PAIR, 0)
-    group_rows, far_came, roots_far, roots_near = phase(
-        group_rows, far_came, roots_far, roots_near
-    )
-
-    feed_pieces = [feed_near, near_came, feed_far, far_came]
-    near_slots, far_slots = (0, 1), (2, 3)
-    feed_info = [(near_slots, 0), (near_slots, 1), (far_slots, 0), (far_slots, 1)]
-    count = len(feed_pieces)
+    feed_far_came = move(feed_far, 1, 0)
+    roots_second_far = move(roots_second, 2 * PAIR, 0)
+    group_rows, feed_far_came, roots_second_far = phase(
+        group_rows, feed_far_came, roots_second_far
+    )
+
+    feed_pieces = [feed_near, feed_near_came, feed_far, feed_far_came]
+    feed_info = [((0, 1), 0), ((0, 1), 1), ((2, 3), 0), ((2, 3), 1)]
     outs = local_call(
         lambda *refs: hidden_kernel(order, group, feed_info, *refs),
         (place, *feed_pieces, *group_rows, *group_grads, vectors),
@@ -1220,7 +1285,7 @@
             pltpu.SemaphoreType.DMA((PAIR * z_count,)),
             pltpu.SemaphoreType.DMA(()),
         ),
-        in_hbm=range(1, 1 + count),
+        in_hbm=(1, 2, 3, 4),
         out_hbm=(group + 4,),
         micros=5,
     )
@@ -1228,8 +1293,9 @@
     back, all_rows = phase(back, all_rows)
 
     back = [back[0]] + [move(back[k], 0, k) for k in others]
+    roots_far = jnp.concatenate([roots_first_far, roots_second_far])
     roots_last = move(roots_far, PAIR, 0)
-    right_roots = [right_root, roots_near, roots_far, roots_last]
+    all_roots = [roots, roots_near, roots_far, roots_last]
     up_kept, up_sent, bias_sums = local_call(
         lambda *refs: up_grads_kernel(order, *refs),
         (place, all_rows, grad_hidden),
@@ -1238,33 +1304,68 @@
         micros=1,
     )
     up_came = move(up_sent, 1, 0)
-    outs = local_call(
+    feed_kept, feed_sent, down_kept, down_first, down_second = local_call(
         lambda *refs: down_grads_kernel(order, group, *refs),
         (place, all_grads, active, down),
-        (shape((SLOTS, width)),) * group + (shape((own, order, order)),) * 2,
+        (shape((group // PAIR, SLOTS, width)),) * 2
+        + (shape((own, order, order)),)
+        + (shape((own // 2, order, order)),) * 2,
         scratch=(pltpu.VMEM((local, order, order), half),),
         micros=2,
     )
-    feed, down_kept, down_sent = outs[:group], outs[group], outs[group + 1]
-    back, up_came, down_sent, feed, roots_last = phase(back, up_came, down_sent, feed, roots_last)
-
-    def split_rows_of(parts):
+    back, up_came, down_first, down_second, feed_sent, all_roots = phase(
+        back, up_came, down_first, down_second, feed_sent, all_roots
+    )
+
+    def rows_of(*groups):
+        blocks = sum(parts[0].shape[0] for parts in groups)
         return local_call(
-            lambda *refs: row_sum_kernel(len(parts), *refs),
-            (place, *parts),
-            (shape((own, line_rows, order)),) * z_count,
+            lambda *refs: row_sum_kernel(len(groups), len(groups[0]), *refs),
+            (place, *[part for parts in groups for part in parts]),
+            (shape((blocks, line_rows, order)),) * z_count,
         )
 
-    def total_of(split):
-        parts = [split[0]] + [move(split[k], k * PAIR, 0) for k in lines]
+    def pairs_of(*groups):
+        blocks = sum(parts[0].shape[0] for parts in groups)
+        return local_call(
+            lambda *refs: row_sum_kernel(len(groups), len(groups[0]), *refs),
+            (place, *[part for parts in groups for part in parts]),
+            (shape((z_count // 2, blocks, line_rows, order)),) * 2,
+        )
+
+    def add_near(kept, came):
+        return [
+            to_half(kept[k].astype(full) + came[k].astype(full)) for k in range(z_count // 2)
+        ]
+
+    def total_of(parts):
         total = parts[0].astype(full)
         for part in parts[1:]:
             total = total + part.astype(full)
         return to_half(total)
 
-    up_rows = total_of(split_rows_of([up_kept, up_came]))
-    down_came = move(down_sent, 1, 0)
-    feed = [feed[0]] + [move(feed[k], 0, k) for k in others]
+    def step_of(parts, matrix):
+        return local_call(
+            lambda *refs: step_kernel(z_count, matrix * own, *refs),
+            (place, *parts, *all_roots, left_roots),
+            (
+                shape((4, own, piece, order)),
+                shape((5, own, piece, order)),
+                shape((8, 128), full),
+            ),
+            scratch=(
+                pltpu.VMEM((own, order, order), half),
+                pltpu.VMEM((own, order, order), half),
+                pltpu.VMEM((order, order), full),
+                pltpu.VMEM((4, line_rows, order), full),
+            ),
+            micros=2,
+        )
+
+    up_near_kept, up_near_sent = pairs_of((up_kept, up_came))
+    up_near = move(up_near_sent, PAIR, 0)
+    down_first_came = move(down_first, 1, 0)
+    feed_came = move(feed_sent, 0, 1)
     attn_kept, attn_sent, mixed, grad_middle, sums_two = local_call(
         lambda *refs: backward_kernel(order, group, *refs),
         (place, *back, chosen, tok, cot, branch, vectors, qkv, probs, attended, normed, weights),
@@ -1287,11 +1388,41 @@
         in_hbm=(1 + group + 6, 1 + group + 9),
         micros=8,
     )
-    attn_sent, up_rows, down_came, feed = phase(attn_sent, up_rows, down_came, feed)
+    attn_sent, up_near, down_first_came, feed_came = phase(
+        attn_sent, up_near, down_first_came, feed_came
+    )
 
     attn_came = move(attn_sent, 0, 1)
+    up_mine, up_other = add_near(up_near_kept, up_near)
+    up_far = move(up_other, 2 * PAIR, 0)
+    down_second_came = move(down_second, 1, 0)
+    feed_pairs = [
+        to_half(feed_kept[k].astype(full) + feed_came[k].astype(full))
+        for k in range(group // PAIR)
+    ]
+    feed = [feed_pairs[0]] + [
+        move(part, 0, (k + 1) * PAIR) for k, part in enumerate(feed_pairs[1:])
+    ]
+    core_parts = local_call(
+        core_sum_kernel,
+        (place, attn_kept, attn_came),
+        (shape((own // 2, order, order)),) * (2 * group),
+    )
+    core_parts, up_far, up_mine, down_second_came, feed = phase(
+        core_parts, up_far, up_mine, down_second_came, feed
+    )
+    first_half, second_half = core_parts[:group], core_parts[group:]
+
+    first_came = [move(part, dx, dm) for (dx, dm), part in zip(plane[1:], first_half[1:])]
+    middle = own // 2
+    down_near_kept, down_near_sent = pairs_of(
+        (down_kept[:middle], down_first_came), (down_kept[middle:], down_second_came)
+    )
+    down_near = move(down_near_sent, PAIR, 0)
+    up_rows = total_of([up_mine, up_far])
+    up_whole_far = move(up_rows, 2 * PAIR, 0)
     block_out, input_grad, sums_one = local_call(
-        lambda *refs: input_kernel(order, group, *refs),
+        lambda *refs: input_kernel(order, group // PAIR, *refs),
         (*feed, mixed, grad_middle, tok, cot, chosen, vectors, branch, weights),
         (
             shape((patches, width)),
@@ -1302,97 +1433,89 @@
             pltpu.VMEM((3 * local, order, order), half),
             pltpu.SemaphoreType.DMA(()),
         ),
-        in_hbm=(group + 7,),
+        in_hbm=(group // PAIR + 7,),
         in_smem=(),
-        micros=4,
+        micros=2,
     )
     (vector_sum,) = local_call(
         vector_part_kernel,
         (place, sums_one, sums_two, bias_sums),
         (shape(vectors.shape, full),),
     )
-    down_split = split_rows_of([down_kept, down_came])
-    core_parts = local_call(
-        core_sum_kernel,
-        (place, attn_kept, attn_came),
-        (shape((own, order, order)),) * group,
-    )
-    core_parts, down_split, vector_sum = phase(core_parts, down_split, vector_sum)
-
-    attn_parts = [core_parts[0]]
-    for (dx, dm), part in zip(plane[1:], core_parts[1:]):
-        attn_parts.append(move(part, dx, dm))
-    up_near, up_far = move(up_rows, PAIR, 0), move(up_rows, 2 * PAIR, 0)
-    down_rows = total_of(down_split)
-    up_last = move(up_far, PAIR, 0)
-    vector_sum = vector_sum + move(vector_sum, 0, 1)
-    attn_split = split_rows_of(attn_parts)
-    up_parts = [up_rows, up_near, up_far, up_last]
-    attn_split, up_parts, down_rows, vector_sum = phase(
-        attn_split, up_parts, down_rows, vector_sum
-    )
-
-    def step_of(parts, first):
-        return local_call(
-            lambda *refs: step_kernel(z_count, first, *refs),
-            (place, *parts, *right_roots, left_roots),
-            (shape((4, own, line_rows // PAIR, order)),) * 2 + (shape((8, 128), full),),
-            scratch=(
-                pltpu.VMEM((own, order, order), half),
-                pltpu.VMEM((own, order, order), half),
-                pltpu.VMEM((order, order), full),
-                pltpu.VMEM((4, line_rows, order), full),
-            ),
-            micros=2,
-        )
-
-    def line_total(values):
-        total = values
-        for k in lines:
-            total = total + move(values, k * PAIR, 0)
-        return total
+    first_came, down_near, up_whole_far, up_rows, vector_sum = phase(
+        first_came, down_near, up_whole_far, up_rows, vector_sum
+    )
+    second_came = [move(part, dx, dm) for (dx, dm), part in zip(plane[1:], second_half[1:])]
+    down_mine, down_other = add_near(down_near_kept, down_near)
+    down_far = move(down_other, 2 * PAIR, 0)
+    up_pair = jnp.stack([up_rows, up_whole_far])
+    up_pair_came = move(up_pair, PAIR, 0)
+    second_came, down_far, up_pair_came, down_mine = phase(
+        second_came, down_far, up_pair_came, down_mine
+    )
+
+    attn_split = rows_of((first_half[0], *first_came), (second_half[0], *second_came))
+    attn_split = [attn_split[0]] + [move(attn_split[k], k * PAIR, 0) for k in lines]
+    down_rows = total_of([down_mine, down_far])
+    down_whole_far = move(down_rows, 2 * PAIR, 0)
+    vector_came = move(vector_sum, 0, 1)
+    up_mine, up_sent, up_squares = step_of(
+        [up_rows, up_pair_came[0], up_whole_far, up_pair_came[1]], 1
+    )
+    attn_split, down_whole_far, vector_came, up_sent, up_mine, up_squares = phase(
+        attn_split, down_whole_far, vector_came, up_sent, up_mine, up_squares
+    )
 
     attn_rows = total_of(attn_split)
-    down_near, down_far = move(down_rows, PAIR, 0), move(down_rows, 2 * PAIR, 0)
-    up_mine, up_sent, up_squares = step_of(up_parts, own)
-    up_squares = jnp.stack([up_squares, move(up_squares, 1, 0)])
+    attn_far = move(attn_rows, 2 * PAIR, 0)
     up_found = move(up_sent, 1, 0)
-    for dm in range(PAIR, group, PAIR):
-        vector_sum = vector_sum + move(vector_sum, 0, dm)
-    attn_rows, down_near, down_far, up_squares, up_found, vector_sum = phase(
-        attn_rows, down_near, down_far, up_squares, up_found, vector_sum
-    )
-
-    attn_near, attn_far = move(attn_rows, PAIR, 0), move(attn_rows, 2 * PAIR, 0)
-    down_last = move(down_far, PAIR, 0)
-    attn_last = move(attn_far, PAIR, 0)
-    vector_sum = vector_sum + move(vector_sum, 1, 0)
-    up_total = line_total(up_squares)
-    attn_near, attn_far, attn_last, down_last, vector_sum, up_total = phase(
-        attn_near, attn_far, attn_last, down_last, vector_sum, up_total
-    )
+    down_pair = jnp.stack([down_rows, down_whole_far])
+    down_pair_came = move(down_pair, PAIR, 0)
+    vector_sum = vector_sum + vector_came
+    vector_later = [move(vector_sum, 0, dm) for dm in range(PAIR, group, PAIR)]
+    attn_far, up_found, down_pair_came, vector_later = phase(
+        attn_far, up_found, down_pair_came, vector_later
+    )
+    attn_pair = jnp.stack([attn_rows, attn_far])
+    attn_pair_came = move(attn_pair, PAIR, 0)
+    down_mine, down_sent, down_squares = step_of(
+        [down_rows, down_pair_came[0], down_whole_far, down_pair_came[1]], 2
+    )
+    down_found = move(down_sent, 1, 0)
+    vector_sum = sum(vector_later, vector_sum)
+    vector_line = [move(vector_sum, k * PAIR, 0) for k in lines]
+    attn_pair_came, down_found, vector_line = phase(attn_pair_came, down_found, vector_line)
 
     kept, sent = local_call(
         lambda *refs: whole_step_kernel(z_count, 3 * own, *refs),
-        (place, attn_rows, attn_near, attn_far, attn_last, *right_roots),
-        (shape((4, own, line_rows // PAIR, order)),) * 2,
+        (place, attn_rows, attn_pair_came[0], attn_far, attn_pair_came[1], *all_roots),
+        (shape((4, own, piece, order)),) * 2,
         scratch=(pltpu.VMEM((own, order, order), half),) * 3
-        + (pltpu.VMEM((2, order, order), full), pltpu.VMEM((4, line_rows, order), full)),
+        + (
+            pltpu.VMEM((order, order), full),
+            pltpu.VMEM((4, line_rows, order), full),
+            pltpu.VMEM((order, order), full),
+        ),
         micros=2,
     )
-    down_mine, down_sent, down_squares = step_of(
-        [down_rows, down_near, down_far, down_last], 2 * own
-    )
-    down_squares = jnp.stack([down_squares, move(down_squares, 1, 0)])
-    came = move(after(sent, down_squares), 1, 0)
-    down_found = move(after(down_sent, down_squares), 1, 0)
-    vector_parts = [vector_sum] + [move(vector_sum, k * PAIR, 0) for k in lines]
-    down_total = line_total(down_squares)
-
-    def apply(first, rates, weight, left, right, found):
+    sent, down_found, vector_line = phase(sent, down_found, vector_line)
+    came = move(sent, 1, 0)
+    (squares,) = local_call(
+        squares_kernel,
+        (up_squares, down_squares, up_found, down_found),
+        (shape((8, 128), full),),
+        in_smem=(),
+    )
+    total = squares
+    for k in lines:
+        total = total + move(squares, k * PAIR, 0)
+    vector_sum = sum(vector_line, vector_sum)
+    vector_parts = [vector_sum, move(vector_sum, 1, 0)]
+
+    def apply(rates, matrix, weight, left, right, *found):
         stat = shape(weight.shape, full)
         return local_call(
-            lambda *refs: apply_kernel(first, order, rates, *refs),
+            lambda *refs: apply_kernel(order, rates, matrix, *refs),
             (place, weight, left, right, *found),
             (stat,) * 4 + (shape(weight.shape),),
         )
@@ -1406,11 +1529,9 @@
         (shape(vectors.shape, full),) * 2,
         in_smem=(),
     )
-    done_attn = apply(0, attn_rates, w_attn, left_attn, right_attn, (kept, came))
-    done_fc1 = apply(0, fc1_rates, w_fc1, left_fc1, right_fc1, (up_mine, up_found, up_total))
-    done_fc2 = apply(
-        0, fc2_rates, w_fc2, left_fc2, right_fc2, (down_mine, down_found, down_total)
-    )
+    done_attn = apply(attn_rates, 0, w_attn, left_attn, right_attn, kept, came)
+    done_fc1 = apply(fc1_rates, 0, w_fc1, left_fc1, right_fc1, up_mine, up_found, total)
+    done_fc2 = apply(fc2_rates, 1, w_fc2, left_fc2, right_fc2, down_mine, down_found, total)
     return (
         block_out[None],
         input_grad[None],

time: 274 us -> 225 us (0.82)
  waiting for transfers between devices: 137 us -> 94.3 us
  local copies, waits for them, and re-layouts: 7.27 us -> 1.96 us
  starting transfers between devices: 76.8 us -> 73.8 us
    ppermute x50 -> x41, waiting for transfers between devices: 111 us -> 69.5 us  [move(): return lax.ppermute(values, 'dp', [(s, s ^ dp_mask) for s in range(dp)])]
    ppermute x3, waiting for transfers between devices: 5.88 us -> 0.01 us  [move(): lax.ppermute(values, ('dp', 'mp'), [(s, s ^ mask) for s in range(dp * mp)])]
    unnamed x39 -> x28, local copies, waits for them, and re-layouts: 7.27 us -> 1.54 us
    ppermute x26 -> x20, waiting for transfers between devices: 20.6 us -> 24.7 us  [move(): return lax.ppermute(values, 'mp', [(s, s ^ mp_mask) for s in range(mp)])]
    ppermute x26 -> x20, starting transfers between devices: 13 us -> 11.2 us  [move(): return lax.ppermute(values, 'mp', [(s, s ^ mp_mask) for s in range(mp)])]
    ppermute x50 -> x41, starting transfers between devices: 59.1 us -> 57.9 us  [move(): return lax.ppermute(values, 'dp', [(s, s ^ dp_mask) for s in range(dp)])]
  transfers between devices with their start and end apart: 79 -> 64, of which waited for: 36 -> 26; matrix products, arithmetic and copies ran while one was open for 1% -> 1% of each run, Pallas kernels for 14% -> 19%
where the time goes in v3:
time: 225 us; the launch traced here: 224 us
  waiting for transfers between devices  94.3 us (42%)
  starting transfers between devices  73.8 us (33%)
  Pallas kernels  52.3 us (23%)
    ppermute x41, waiting for transfers between devices, move(): return lax.ppermute(values, 'dp', [(s, s ^ dp_mask) for s in range(dp)])  69.5 us
    ppermute x41, starting transfers between devices, move(): return lax.ppermute(values, 'dp', [(s, s ^ dp_mask) for s in range(dp)])  57.9 us
    pallas_call x22, Pallas kernels, local_call(): pl.pallas_call(kernel, out_shape=list(outs), in_specs=[place_of(i, in_hbm...  52.3 us
    ppermute x20, waiting for transfers between devices, move(): return lax.ppermute(values, 'mp', [(s, s ^ mp_mask) for s in range(mp)])  24.7 us
    ppermute x20, starting transfers between devices, move(): return lax.ppermute(values, 'mp', [(s, s ^ mp_mask) for s in range(mp)])  11.2 us
    ppermute x3, starting transfers between devices, move(): lax.ppermute(values, ('dp', 'mp'), [(s, s ^ mask) for s in range(dp * mp)])  4.77 us
  transfers between devices with their start and end apart: 64, of which 26 were waited for; matrix products, arithmetic and copies ran while one was open for 1% of the time, Pallas kernels for 19%

profile of v3, /device:TPU:0, one launch (start us, length us, event | category | flops | bytes accessed | tf_op | source)
XLA Modules:
  0.0 224.4 jit_solution(2182054280128945303)
XLA Ops:
  0.7 2.3 %shard_map.330 = (bf16[4,48,384]{2,1,0:T(8,128)(2,1)S(1)}, bf16[8,48,384]{2,1,0:T(8,128)(2,1)S(1)}, bf16[6,2,48,384]{3,2,1,0:T(8,128)(2,1)S(1)}, bf16[6,2,48,384]{3,2,1,0:T(8,128)(2,1)S(1)}) custom-call(s32[4]{0:T(128)S(1)} %pad_add_fusion.place_ref.refs_0_, f32[4,48,384]{2,1,0:T(8,128)} %refs_1_.5, f32[4,48,384]{2,1,0:T(8,128)} %refs_1_.6, ...), custom_call_target="tpu_custom_call" | custom-call | flops 1000000000 | bytes 3981328 | tf_op jit(solution)/shard_map/pallas_call | solution.py:518
  3.1 3.0 %collective-permute-start.3 = (bf16[6,2,48,384]{3,2,1,0:T(8,128)(2,1)S(1)}, bf16[6,2,48,384]{3,2,1,0:T(8,128)(2,1)S(1)}, u32[]{:S(2)}, u32[]{:S(2)}) collective-permute-start(bf16[6,2,48,384]{3,2,1,0:T(8,128)(2,1)S(1)} %get-tuple-element.212), channel_id=1, source_target_pairs={{0,4},{4,0},{8,12},{12,8},{16,20},{20,16},{24,28},{28,24},{1,5},{5... | collective-permute-start | bytes 1327112 | tf_op jit(solution)/shard_map/ppermute | solution.py:1112
  6.1 3.6 %collective-permute-start.2 = (bf16[4,48,384]{2,1,0:T(8,128)(2,1)S(1)}, bf16[4,48,384]{2,1,0:T(8,128)(2,1)S(1)}, u32[]{:S(2)}, u32[]{:S(2)}) collective-permute-start(bf16[4,48,384]{2,1,0:T(8,128)(2,1)S(1)} %get-tuple-element.213), channel_id=1, source_target_pairs={{0,24},{4,28},{8,16},{12,20},{16,8},{20,12},{24,0},{28,4},{1,25},{... | collective-permute-start | bytes 442376 | tf_op jit(solution)/shard_map/ppermute | solution.py:1112
  10.4 4.2 %collective-permute-done.2 = bf16[4,48,384]{2,1,0:T(8,128)(2,1)S(1)} collective-permute-done((bf16[4,48,384]{2,1,0:T(8,128)(2,1)S(1)}, bf16[4,48,384]{2,1,0:T(8,128)(2,1)S(1)}, u32[]{:S(2)}, u32[]{:S(2)}) %collective-permute-start.2) | collective-permute-done | bytes 147488 | tf_op jit(solution)/shard_map/ppermute | solution.py:1112
  14.7 7.2 %collective-permute-done.1 = bf16[4,48,384]{2,1,0:T(8,128)(2,1)S(1)} collective-permute-done((bf16[4,48,384]{2,1,0:T(8,128)(2,1)S(1)}, bf16[4,48,384]{2,1,0:T(8,128)(2,1)S(1)}, u32[]{:S(2)}, u32[]{:S(2)}) %collective-permute-start.1) | collective-permute-done | bytes 147488 | tf_op jit(solution)/shard_map/ppermute | solution.py:1112
  26.3 3.0 %collective-permute-start.7 = (bf16[8,48,384]{2,1,0:T(8,128)(2,1)S(1)}, bf16[8,48,384]{2,1,0:T(8,128)(2,1)S(1)}, u32[]{:S(2)}, u32[]{:S(2)}) collective-permute-start(bf16[8,48,384]{2,1,0:T(8,128)(2,1)S(1)} %get-tuple-element.221.feed_ref), channel_id=1, source_target_pairs={{0,16},{4,20},{8,24},{12,28},{16,0},{20,4},{24,8},{28,12},{1,17},{... | collective-permute-start | bytes 884744 | tf_op jit(solution)/shard_map/ppermute | solution.py:1112
  30.2 17.3 %collective-permute-done.7 = bf16[8,48,384]{2,1,0:T(8,128)(2,1)S(1)} collective-permute-done((bf16[8,48,384]{2,1,0:T(8,128)(2,1)S(1)}, bf16[8,48,384]{2,1,0:T(8,128)(2,1)S(1)}, u32[]{:S(2)}, u32[]{:S(2)}) %collective-permute-start.7) | collective-permute-done | bytes 294944 | tf_op jit(solution)/shard_map/ppermute | solution.py:1112
  47.4 3.3 %collective-permute-done.5.refs_5_ = bf16[4,4,48,384]{3,2,1,0:T(8,128)(2,1)S(1)} collective-permute-done((bf16[4,4,48,384]{3,2,1,0:T(8,128)(2,1)S(1)}, bf16[4,4,48,384]{3,2,1,0:T(8,128)(2,1)S(1)}, u32[]{:S(2)}, u32[]{:S(2)}) %collective-permute-start.5) | collective-permute-done | bytes 589856 | tf_op jit(solution)/shard_map/ppermute | solution.py:1114
  52.2 3.5 %collective-permute-done.13 = bf16[160,768]{1,0:T(8,128)(2,1)S(1)} collective-permute-done((bf16[160,768]{1,0:T(8,128)(2,1)S(1)}, bf16[160,768]{1,0:T(8,128)(2,1)S(1)}, u32[]{:S(2)}, u32[]{:S(2)}) %collective-permute-start.13) | collective-permute-done | bytes 245792 | tf_op jit(solution)/shard_map/ppermute | solution.py:1114
  55.7 1.7 collective-permute-start.16
  60.4 10.9 %shard_map.333 = (bf16[160,768]{1,0:T(8,128)(2,1)S(1)}, bf16[197,2304]{1,0:T(8,128)(2,1)S(1)}, f32[12,197,197]{2,1,0:T(8,128)S(1)}, bf16[197,768]{1,0:T(8,128)(2...) custom-call(s32[4]{0:T(128)S(1)} %pad_add_fusion.place_ref.refs_0_, ...), custom_call_target="tpu_custom_call" | custom-call | flops 8000000000 | bytes 14070292 | tf_op jit(solution)/shard_map/pallas_call | solution.py:518
  71.4 2.2 collective-permute-done.17
  75.1 2.1 collective-permute-start.22
  79.1 10.3 %collective-permute-done.22 = bf16[8,48,384]{2,1,0:T(8,128)(2,1)S(1)} collective-permute-done((bf16[8,48,384]{2,1,0:T(8,128)(2,1)S(1)}, bf16[8,48,384]{2,1,0:T(8,128)(2,1)S(1)}, u32[]{:S(2)}, u32[]{:S(2)}) %collective-permute-start.22) | collective-permute-done | bytes 294944 | tf_op jit(solution)/shard_map/ppermute | solution.py:1112
  89.8 5.2 %shard_map.334 = (bf16[160,768]{1,0:T(8,128)(2,1)S(1)}, bf16[160,768]{1,0:T(8,128)(2,1)S(1)}, bf16[160,768]{1,0:T(8,128)(2,1)S(1)}, bf16[160,768]{1,0:T(8,128)(2...) custom-call(s32[4]{0:T(128)S(1)} %pad_add_fusion.place_ref.refs_0_, ...), custom_call_target="tpu_custom_call" | custom-call | flops 5000000000 | bytes 10460176 | tf_op jit(solution)/shard_map/pallas_call | solution.py:518
  95.0 2.0 shard_map.335
  97.0 1.9 collective-permute-start.26
  100.8 3.1 %shard_map.336 = (bf16[2,160,768]{2,1,0:T(8,128)(2,1)S(1)}, bf16[2,160,768]{2,1,0:T(8,128)(2,1)S(1)}, bf16[2,384,384]{2,1,0:T(8,128)(2,1)S(1)}, bf16[1,384,384]{2,1,0:T(8,128)(2,1)S(1)}, bf16[1,384,384]{2,1,0:T(8,128)(2,1)S(1)}) custom-call(s32[4]{0:T(128)S(1)} %pad_add_fusion.place_ref.refs_0_, bf16[640,768]{1,0:T(8,128)(2,1)S(1)} %get-tuple-element.269.refs_1_, ...), custom_call_target="tpu_custom_call" | custom-call | flops 2000000000 | bytes 5308432 | tf_op jit(solution)/shard_map/pallas_call | solution.py:518
  104.0 3.7 %collective-permute-done.24.refs_3_ = bf16[160,768]{1,0:T(8,128)(2,1)S(1)} collective-permute-done((bf16[160,768]{1,0:T(8,128)(2,1)S(1)}, bf16[160,768]{1,0:T(8,128)(2,1)S(1)}, u32[]{:S(2)}, u32[]{:S(2)}) %collective-permute-start.24) | collective-permute-done | bytes 245792 | tf_op jit(solution)/shard_map/ppermute | solution.py:1114
  107.7 4.5 %collective-permute-done.25.refs_4_ = bf16[160,768]{1,0:T(8,128)(2,1)S(1)} collective-permute-done((bf16[160,768]{1,0:T(8,128)(2,1)S(1)}, bf16[160,768]{1,0:T(8,128)(2,1)S(1)}, u32[]{:S(2)}, u32[]{:S(2)}) %collective-permute-start.25) | collective-permute-done | bytes 245792 | tf_op jit(solution)/shard_map/ppermute | solution.py:1114
  116.5 8.2 %shard_map.337 = (bf16[2,4,384,384]{3,2,1,0:T(8,128)(2,1)S(1)}, bf16[2,4,384,384]{3,2,1,0:T(8,128)(2,1)S(1)}, bf16[197,2304]{1,0:T(8,128)(2,1)S(1)}, f32[197,768]{1,0:T(8,128)S(1)}, f32[4,768]{1,0:T(4,128)S(1)}) custom-call(s32[4]{0:T(128)S(1)} %pad_add_fusion.place_ref.refs_0_, bf16[160,768]{1,0:T(8,128)(2,1)S(1)} %get-tuple-element.279.refs_1_, ...), custom_call_target="tpu_custom_call" | custom-call | flops 8000000000 | bytes 16634624 | tf_op jit(solution)/shard_map/pallas_call | solution.py:518
  126.8 1.8 collective-permute-start.34
  130.6 3.7 %collective-permute-done.33.refs_4_ = bf16[1,384,384]{2,1,0:T(8,128)(2,1)S(1)} collective-permute-done((bf16[1,384,384]{2,1,0:T(8,128)(2,1)S(1)}, bf16[1,384,384]{2,1,0:T(8,128)(2,1)S(1)}, u32[]{:S(2)}, u32[]{:S(2)}) %collective-permute-start.33) | collective-permute-done | bytes 294944 | tf_op jit(solution)/shard_map/ppermute | solution.py:1112
  140.3 1.8 collective-permute-start.39
  142.1 3.4 %shard_map.340 = (bf16[197,768]{1,0:T(8,128)(2,1)}, f32[197,768]{1,0:T(8,128)S(1)}, f32[5,768]{1,0:T(8,128)S(1)}) custom-call(bf16[160,768]{1,0:T(8,128)(2,1)S(1)} %get-tuple-element.309.refs_0_, bf16[160,768]{1,0:T(8,128)(2,1)S(1)} %collective-permute-done.34.refs_1_, bf16[197,2304]{1,0:T(8,128)(2,1)S(1)} %get-tuple-element.311.refs_2_, ...), custom_call_target="tpu_custom_call" | custom-call | flops 2000000000 | bytes 8959552 | tf_op jit(solution)/shard_map/pallas_call | solution.py:518
  146.2 2.5 %collective-permute-done.39.refs_3_ = bf16[2,96,384]{2,1,0:T(8,128)(2,1)S(1)} collective-permute-done((bf16[2,96,384]{2,1,0:T(8,128)(2,1)S(1)}, bf16[2,96,384]{2,1,0:T(8,128)(2,1)S(1)}, u32[]{:S(2)}, u32[]{:S(2)}) %collective-permute-start.39) | collective-permute-done | bytes 147488 | tf_op jit(solution)/shard_map/ppermute | solution.py:1112
  151.2 1.8 collective-permute-start.42
  153.0 2.1 collective-permute-start.44
  155.8 2.7 %collective-permute-done.40.refs_6_ = bf16[1,384,384]{2,1,0:T(8,128)(2,1)S(1)} collective-permute-done((bf16[1,384,384]{2,1,0:T(8,128)(2,1)S(1)}, bf16[1,384,384]{2,1,0:T(8,128)(2,1)S(1)}, u32[]{:S(2)}, u32[]{:S(2)}) %collective-permute-start.40) | collective-permute-done | bytes 294944 | tf_op jit(solution)/shard_map/ppermute | solution.py:1112
  158.6 5.8 %collective-permute-done.41.refs_7_ = bf16[1,384,384]{2,1,0:T(8,128)(2,1)S(1)} collective-permute-done((bf16[1,384,384]{2,1,0:T(8,128)(2,1)S(1)}, bf16[1,384,384]{2,1,0:T(8,128)(2,1)S(1)}, u32[]{:S(2)}, u32[]{:S(2)}) %collective-permute-start.41) | collective-permute-done | bytes 294944 | tf_op jit(solution)/shard_map/ppermute | solution.py:1114
  164.5 1.8 collective-permute-start.48
  168.1 2.0 collective-permute-start.46
  171.7 1.8 shard_map.344
  173.5 6.5 %collective-permute-done.48.refs_3_ = bf16[2,96,384]{2,1,0:T(8,128)(2,1)S(1)} collective-permute-done((bf16[2,96,384]{2,1,0:T(8,128)(2,1)S(1)}, bf16[2,96,384]{2,1,0:T(8,128)(2,1)S(1)}, u32[]{:S(2)}, u32[]{:S(2)}) %collective-permute-start.48) | collective-permute-done | bytes 147488 | tf_op jit(solution)/shard_map/ppermute | solution.py:1112
  180.0 3.2 %collective-permute-done.46 = bf16[2,96,384]{2,1,0:T(8,128)(2,1)S(1)} collective-permute-done((bf16[2,96,384]{2,1,0:T(8,128)(2,1)S(1)}, bf16[2,96,384]{2,1,0:T(8,128)(2,1)S(1)}, u32[]{:S(2)}, u32[]{:S(2)}) %collective-permute-start.46) | collective-permute-done | bytes 147488 | tf_op jit(solution)/shard_map/ppermute | solution.py:1112
  183.2 2.4 %collective-permute-start.52 = (bf16[2,2,96,384]{3,2,1,0:T(8,128)(2,1)S(1)}, bf16[2,2,96,384]{3,2,1,0:T(8,128)(2,1)S(1)}, u32[]{:S(2)}, u32[]{:S(2)}) collective-permute-start(bf16[2,2,96,384]{3,2,1,0:T(8,128)(2,1)S(1)} %pad_maximum_fusion.5), channel_id=1, source_target_pairs={{0,8},{4,12},{8,0},{12,4},{16,24},{20,28},{24,16},{28,20},{1,9},{5... | collective-permute-start | bytes 884744 | tf_op jit(solution)/shard_map/ppermute | solution.py:1112
  188.4 2.6 %collective-permute-done.53 = f32[13,768]{1,0:T(8,128)S(1)} collective-permute-done((f32[13,768]{1,0:T(8,128)S(1)}, f32[13,768]{1,0:T(8,128)S(1)}, u32[]{:S(2)}, u32[]{:S(2)}) %collective-permute-start.53) | collective-permute-done | bytes 39968 | tf_op jit(solution)/shard_map/ppermute | solution.py:1114
  190.9 3.2 %collective-permute-done.50.refs_3_ = bf16[2,96,384]{2,1,0:T(8,128)(2,1)S(1)} collective-permute-done((bf16[2,96,384]{2,1,0:T(8,128)(2,1)S(1)}, bf16[2,96,384]{2,1,0:T(8,128)(2,1)S(1)}, u32[]{:S(2)}, u32[]{:S(2)}) %collective-permute-start.50) | collective-permute-done | bytes 147488 | tf_op jit(solution)/shard_map/ppermute | solution.py:1112
  194.7 1.8 shard_map.345
  197.4 1.9 collective-permute-start.54
  199.3 2.3 %collective-permute-start.58 = (f32[13,768]{1,0:T(8,128)S(1)}, f32[13,768]{1,0:T(8,128)S(1)}, u32[]{:S(2)}, u32[]{:S(2)}) collective-permute-start(f32[13,768]{1,0:T(8,128)S(1)} %add.75), channel_id=1, source_target_pairs={{0,24},{4,28},{8,16},{12,20},{16,8},{20,12},{24,0},{28,4},{1,25},{... | collective-permute-start | bytes 119816 | tf_op jit(solution)/shard_map/ppermute | solution.py:1112
  201.6 2.1 collective-permute-start.56
  205.1 2.8 %collective-permute-done.58 = f32[13,768]{1,0:T(8,128)S(1)} collective-permute-done((f32[13,768]{1,0:T(8,128)S(1)}, f32[13,768]{1,0:T(8,128)S(1)}, u32[]{:S(2)}, u32[]{:S(2)}) %collective-permute-start.58) | collective-permute-done | bytes 39968 | tf_op jit(solution)/shard_map/ppermute | solution.py:1112
  208.0 2.2 %shard_map.346 = (bf16[4,2,48,384]{3,2,1,0:T(8,128)(2,1)S(1)}, bf16[4,2,48,384]{3,2,1,0:T(8,128)(2,1)S(1)}) custom-call(s32[4]{0:T(128)S(1)} %pad_add_fusion.place_ref.refs_0_, bf16[2,96,384]{2,1,0:T(8,128)(2,1)S(1)} %add_convert_fusion.2.refs_1_, bf16[2,96,384]{2,1,0:T(8,128)(2,1)S(1)} %get-tuple-element.433.refs_2_, ...), custom_call_target="tpu_custom_call" | custom-call | flops 2000000000 | bytes 3538960 | tf_op jit(solution)/shard_map/pallas_call | solution.py:518
  212.9 1.8 collective-permute-start.60
  216.9 1.7 shard_map.350
  218.7 1.7 shard_map.349
  222.7 1.7 shard_map.347
  (157 shorter events, 50.7 us)
Async XLA Ops:
  3.1 18.8 %collective-permute-start.3 = (bf16[6,2,48,384]{3,2,1,0:T(8,128)(2,1)S(1)}, bf16[6,2,48,384]{3,2,1,0:T(8,128)(2,1)S(1)}, u32[]{:S(2)}, u32[]{:S(2)}) collective-permute-start(bf16[6,2,48,384]{3,2,1,0:T(8,128)(2,1)S(1)} %get-tuple-element.212), channel_id=1, source_target_pairs={{0,4},{4,0},{8,12},{12,8},{16,20},{20,16},{24,28},{28,24},{1,5},{5... | collective-permute-start | bytes 1327112 | tf_op jit(solution)/shard_map/ppermute | solution.py:1112
  6.1 8.6 %collective-permute-start.2 = (bf16[4,48,384]{2,1,0:T(8,128)(2,1)S(1)}, bf16[4,48,384]{2,1,0:T(8,128)(2,1)S(1)}, u32[]{:S(2)}, u32[]{:S(2)}) collective-permute-start(bf16[4,48,384]{2,1,0:T(8,128)(2,1)S(1)} %get-tuple-element.213), channel_id=1, source_target_pairs={{0,24},{4,28},{8,16},{12,20},{16,8},{20,12},{24,0},{28,4},{1,25},{... | collective-permute-start | bytes 442376 | tf_op jit(solution)/shard_map/ppermute | solution.py:1112
  9.7 12.2 %collective-permute-start.1 = (bf16[4,48,384]{2,1,0:T(8,128)(2,1)S(1)}, bf16[4,48,384]{2,1,0:T(8,128)(2,1)S(1)}, u32[]{:S(2)}, u32[]{:S(2)}) collective-permute-start(bf16[4,48,384]{2,1,0:T(8,128)(2,1)S(1)} %get-tuple-element.213), channel_id=1, source_target_pairs={{0,16},{4,20},{8,24},{12,28},{16,0},{20,4},{24,8},{28,12},{1,17},{... | collective-permute-start | bytes 442376 | tf_op jit(solution)/shard_map/ppermute | solution.py:1112
  9.7 12.2 %collective-permute-start = (bf16[4,48,384]{2,1,0:T(8,128)(2,1)S(1)}, bf16[4,48,384]{2,1,0:T(8,128)(2,1)S(1)}, u32[]{:S(2)}, u32[]{:S(2)}) collective-permute-start(bf16[4,48,384]{2,1,0:T(8,128)(2,1)S(1)} %get-tuple-element.213), channel_id=1, source_target_pairs={{0,8},{4,12},{8,0},{12,4},{16,24},{20,28},{24,16},{28,20},{1,9},{5... | collective-permute-start | bytes 442376 | tf_op jit(solution)/shard_map/ppermute | solution.py:1112
  22.6 28.2 %collective-permute-start.8 = (bf16[24,48,384]{2,1,0:T(8,128)(2,1)S(1)}, bf16[24,48,384]{2,1,0:T(8,128)(2,1)S(1)}, u32[]{:S(2)}, u32[]{:S(2)}) collective-permute-start(bf16[24,48,384]{2,1,0:T(8,128)(2,1)S(1)} %get-tuple-element.224), channel_id=1, source_target_pairs={{0,8},{4,12},{8,0},{12,4},{16,24},{20,28},{24,16},{28,20},{1,9},{5... | collective-permute-start | bytes 2654216 | tf_op jit(solution)/shard_map/ppermute | solution.py:1112
  22.8 24.7 %collective-permute-start.6 = (bf16[4,4,48,384]{3,2,1,0:T(8,128)(2,1)S(1)}, bf16[4,4,48,384]{3,2,1,0:T(8,128)(2,1)S(1)}, u32[]{:S(2)}, u32[]{:S(2)}) collective-permute-start(bf16[4,4,48,384]{3,2,1,0:T(8,128)(2,1)S(1)} %pad_maximum_fusion.refs_1_), channel_id=1, source_target_pairs={{0,6},{1,7},{2,4},{3,5},{4,2},{5,3},{6,0},{7,1},{8,14},{9,15},{10,... | collective-permute-start | bytes 1769480 | tf_op jit(solution)/shard_map/ppermute | solution.py:1116
  24.3 26.4 %collective-permute-start.5 = (bf16[4,4,48,384]{3,2,1,0:T(8,128)(2,1)S(1)}, bf16[4,4,48,384]{3,2,1,0:T(8,128)(2,1)S(1)}, u32[]{:S(2)}, u32[]{:S(2)}) collective-permute-start(bf16[4,4,48,384]{3,2,1,0:T(8,128)(2,1)S(1)} %pad_maximum_fusion.refs_1_), channel_id=1, source_target_pairs={{0,2},{1,3},{2,0},{3,1},{4,6},{5,7},{6,4},{7,5},{8,10},{9,11},{10,... | collective-permute-start | bytes 1769480 | tf_op jit(solution)/shard_map/ppermute | solution.py:1114
  24.8 26.0 %collective-permute-start.4 = (bf16[4,4,48,384]{3,2,1,0:T(8,128)(2,1)S(1)}, bf16[4,4,48,384]{3,2,1,0:T(8,128)(2,1)S(1)}, u32[]{:S(2)}, u32[]{:S(2)}) collective-permute-start(bf16[4,4,48,384]{3,2,1,0:T(8,128)(2,1)S(1)} %pad_maximum_fusion.refs_1_), channel_id=1, source_target_pairs={{0,4},{4,0},{8,12},{12,8},{16,20},{20,16},{24,28},{28,24},{1,5},{5... | collective-permute-start | bytes 1769480 | tf_op jit(solution)/shard_map/ppermute | solution.py:1112
  26.3 21.1 %collective-permute-start.7 = (bf16[8,48,384]{2,1,0:T(8,128)(2,1)S(1)}, bf16[8,48,384]{2,1,0:T(8,128)(2,1)S(1)}, u32[]{:S(2)}, u32[]{:S(2)}) collective-permute-start(bf16[8,48,384]{2,1,0:T(8,128)(2,1)S(1)} %get-tuple-element.221.feed_ref), channel_id=1, source_target_pairs={{0,16},{4,20},{8,24},{12,28},{16,0},{20,4},{24,8},{28,12},{1,17},{... | collective-permute-start | bytes 884744 | tf_op jit(solution)/shard_map/ppermute | solution.py:1112
  55.7 15.7 %collective-permute-start.16 = (bf16[8,48,384]{2,1,0:T(8,128)(2,1)S(1)}, bf16[8,48,384]{2,1,0:T(8,128)(2,1)S(1)}, u32[]{:S(2)}, u32[]{:S(2)}) collective-permute-start(bf16[8,48,384]{2,1,0:T(8,128)(2,1)S(1)} %collective-permute-done.7), channel_id=1, source_target_pairs={{0,8},{4,12},{8,0},{12,4},{16,24},{20,28},{24,16},{28,20},{1,9},{5... | collective-permute-start | bytes 884744 | tf_op jit(solution)/shard_map/ppermute | solution.py:1112
  57.4 16.1 %collective-permute-start.17 = (bf16[8,48,384]{2,1,0:T(8,128)(2,1)S(1)}, bf16[8,48,384]{2,1,0:T(8,128)(2,1)S(1)}, u32[]{:S(2)}, u32[]{:S(2)}) collective-permute-start(bf16[8,48,384]{2,1,0:T(8,128)(2,1)S(1)} %get-tuple-element.245), channel_id=1, source_target_pairs={{0,16},{4,20},{8,24},{12,28},{16,0},{20,4},{24,8},{28,12},{1,17},{... | collective-permute-start | bytes 884744 | tf_op jit(solution)/shard_map/ppermute | solution.py:1112
  58.4 15.1 %collective-permute-start.14 = (bf16[2,160,768]{2,1,0:T(8,128)(2,1)S(1)}, bf16[2,160,768]{2,1,0:T(8,128)(2,1)S(1)}, u32[]{:S(2)}, u32[]{:S(2)}) collective-permute-start(bf16[2,160,768]{2,1,0:T(8,128)(2,1)S(1)} %pad_maximum_fusion.3.refs_9_), channel_id=1, source_target_pairs={{0,2},{1,3},{2,0},{3,1},{4,6},{5,7},{6,4},{7,5},{8,10},{9,11},{10,... | collective-permute-start | bytes 1474568 | tf_op jit(solution)/shard_map/ppermute | solution.py:1114
  59.2 14.5 %collective-permute-start.15 = (bf16[2,8,48,384]{3,2,1,0:T(8,128)(2,1)S(1)}, bf16[2,8,48,384]{3,2,1,0:T(8,128)(2,1)S(1)}, u32[]{:S(2)}, u32[]{:S(2)}) collective-permute-start(bf16[2,8,48,384]{3,2,1,0:T(8,128)(2,1)S(1)} %pad_maximum_fusion.1.refs_1_), channel_id=1, source_target_pairs={{0,4},{4,0},{8,12},{12,8},{16,20},{20,16},{24,28},{28,24},{1,5},{5... | collective-permute-start | bytes 1769480 | tf_op jit(solution)/shard_map/ppermute | solution.py:1112
  73.8 15.5 %collective-permute-start.21 = (bf16[2,8,48,384]{3,2,1,0:T(8,128)(2,1)S(1)}, bf16[2,8,48,384]{3,2,1,0:T(8,128)(2,1)S(1)}, u32[]{:S(2)}, u32[]{:S(2)}) collective-permute-start(bf16[2,8,48,384]{3,2,1,0:T(8,128)(2,1)S(1)} %pad_maximum_fusion.2.refs_3_), channel_id=1, source_target_pairs={{0,4},{4,0},{8,12},{12,8},{16,20},{20,16},{24,28},{28,24},{1,5},{5... | collective-permute-start | bytes 1769480 | tf_op jit(solution)/shard_map/ppermute | solution.py:1112
  75.1 14.2 %collective-permute-start.22 = (bf16[8,48,384]{2,1,0:T(8,128)(2,1)S(1)}, bf16[8,48,384]{2,1,0:T(8,128)(2,1)S(1)}, u32[]{:S(2)}, u32[]{:S(2)}) collective-permute-start(bf16[8,48,384]{2,1,0:T(8,128)(2,1)S(1)} %get-tuple-element.249), channel_id=1, source_target_pairs={{0,16},{4,20},{8,24},{12,28},{16,0},{20,4},{24,8},{28,12},{1,17},{... | collective-permute-start | bytes 884744 | tf_op jit(solution)/shard_map/ppermute | solution.py:1112
  77.2 12.2 %collective-permute-start.20 = (bf16[160,768]{1,0:T(8,128)(2,1)S(1)}, bf16[160,768]{1,0:T(8,128)(2,1)S(1)}, u32[]{:S(2)}, u32[]{:S(2)}) collective-permute-start(bf16[160,768]{1,0:T(8,128)(2,1)S(1)} %get-tuple-element.251.refs_5_), channel_id=1, source_target_pairs={{0,3},{1,2},{2,1},{3,0},{4,7},{5,6},{6,5},{7,4},{8,11},{9,10},{10,... | collective-permute-start | bytes 737288 | tf_op jit(solution)/shard_map/ppermute | solution.py:1114
  77.2 12.2 %collective-permute-start.19 = (bf16[160,768]{1,0:T(8,128)(2,1)S(1)}, bf16[160,768]{1,0:T(8,128)(2,1)S(1)}, u32[]{:S(2)}, u32[]{:S(2)}) collective-permute-start(bf16[160,768]{1,0:T(8,128)(2,1)S(1)} %get-tuple-element.251.refs_5_), channel_id=1, source_target_pairs={{0,2},{1,3},{2,0},{3,1},{4,6},{5,7},{6,4},{7,5},{8,10},{9,11},{10,... | collective-permute-start | bytes 737288 | tf_op jit(solution)/shard_map/ppermute | solution.py:1114
  77.8 11.5 %collective-permute-start.18 = (bf16[160,768]{1,0:T(8,128)(2,1)S(1)}, bf16[160,768]{1,0:T(8,128)(2,1)S(1)}, u32[]{:S(2)}, u32[]{:S(2)}) collective-permute-start(bf16[160,768]{1,0:T(8,128)(2,1)S(1)} %get-tuple-element.251.refs_5_), channel_id=1, source_target_pairs={{0,1},{1,0},{2,3},{3,2},{4,5},{5,4},{6,7},{7,6},{8,9},{9,8},{10,11... | collective-permute-start | bytes 737288 | tf_op jit(solution)/shard_map/ppermute | solution.py:1114
  89.4 22.8 %collective-permute-start.27 = (bf16[16,48,384]{2,1,0:T(8,128)(2,1)S(1)}, bf16[16,48,384]{2,1,0:T(8,128)(2,1)S(1)}, u32[]{:S(2)}, u32[]{:S(2)}) collective-permute-start(bf16[16,48,384]{2,1,0:T(8,128)(2,1)S(1)} %constant_dynamic-update-slice_fusion.refs_7_), channel_id=1, source_target_pairs={{0,8},{4,12},{8,0},{12,4},{16,24},{20,28},{24,16},{28,20},{1,9},{5... | collective-permute-start | bytes 1769480 | tf_op jit(solution)/shard_map/ppermute | solution.py:1112
  97.0 15.5 %collective-permute-start.26 = (bf16[2,384,384]{2,1,0:T(8,128)(2,1)S(1)}, bf16[2,384,384]{2,1,0:T(8,128)(2,1)S(1)}, u32[]{:S(2)}, u32[]{:S(2)}) collective-permute-start(bf16[2,384,384]{2,1,0:T(8,128)(2,1)S(1)} %get-tuple-element.268), channel_id=1, source_target_pairs={{0,4},{4,0},{8,12},{12,8},{16,20},{20,16},{24,28},{28,24},{1,5},{5... | collective-permute-start | bytes 1769480 | tf_op jit(solution)/shard_map/ppermute | solution.py:1112
  99.0 8.8 %collective-permute-start.24 = (bf16[160,768]{1,0:T(8,128)(2,1)S(1)}, bf16[160,768]{1,0:T(8,128)(2,1)S(1)}, u32[]{:S(2)}, u32[]{:S(2)}) collective-permute-start(bf16[160,768]{1,0:T(8,128)(2,1)S(1)} %get-tuple-element.264), channel_id=1, source_target_pairs={{0,2},{1,3},{2,0},{3,1},{4,6},{5,7},{6,4},{7,5},{8,10},{9,11},{10,... | collective-permute-start | bytes 737288 | tf_op jit(solution)/shard_map/ppermute | solution.py:1114
  99.2 13.0 %collective-permute-start.25 = (bf16[160,768]{1,0:T(8,128)(2,1)S(1)}, bf16[160,768]{1,0:T(8,128)(2,1)S(1)}, u32[]{:S(2)}, u32[]{:S(2)}) collective-permute-start(bf16[160,768]{1,0:T(8,128)(2,1)S(1)} %get-tuple-element.265), channel_id=1, source_target_pairs={{0,3},{1,2},{2,1},{3,0},{4,7},{5,6},{6,5},{7,4},{8,11},{9,10},{10,... | collective-permute-start | bytes 737288 | tf_op jit(solution)/shard_map/ppermute | solution.py:1114
  113.2 11.5 %collective-permute-start.28 = (bf16[2,2,96,384]{3,2,1,0:T(8,128)(2,1)S(1)}, bf16[2,2,96,384]{3,2,1,0:T(8,128)(2,1)S(1)}, u32[]{:S(2)}, u32[]{:S(2)}) collective-permute-start(bf16[2,2,96,384]{3,2,1,0:T(8,128)(2,1)S(1)} %get-tuple-element.292), channel_id=1, source_target_pairs={{0,8},{4,12},{8,0},{12,4},{16,24},{20,28},{24,16},{28,20},{1,9},{5... | collective-permute-start | bytes 884744 | tf_op jit(solution)/shard_map/ppermute | solution.py:1112
  114.9 9.8 %collective-permute-start.29 = (bf16[1,384,384]{2,1,0:T(8,128)(2,1)S(1)}, bf16[1,384,384]{2,1,0:T(8,128)(2,1)S(1)}, u32[]{:S(2)}, u32[]{:S(2)}) collective-permute-start(bf16[1,384,384]{2,1,0:T(8,128)(2,1)S(1)} %get-tuple-element.293), channel_id=1, source_target_pairs={{0,4},{4,0},{8,12},{12,8},{16,20},{20,16},{24,28},{28,24},{1,5},{5... | collective-permute-start | bytes 884744 | tf_op jit(solution)/shard_map/ppermute | solution.py:1112
  116.5 8.2 %collective-permute-start.30 = (bf16[2,160,768]{2,1,0:T(8,128)(2,1)S(1)}, bf16[2,160,768]{2,1,0:T(8,128)(2,1)S(1)}, u32[]{:S(2)}, u32[]{:S(2)}) collective-permute-start(bf16[2,160,768]{2,1,0:T(8,128)(2,1)S(1)} %get-tuple-element.294), channel_id=1, source_target_pairs={{0,1},{1,0},{2,3},{3,2},{4,5},{5,4},{6,7},{7,6},{8,9},{9,8},{10,11... | collective-permute-start | bytes 1474568 | tf_op jit(solution)/shard_map/ppermute | solution.py:1114
  125.3 9.0 %collective-permute-start.33 = (bf16[1,384,384]{2,1,0:T(8,128)(2,1)S(1)}, bf16[1,384,384]{2,1,0:T(8,128)(2,1)S(1)}, u32[]{:S(2)}, u32[]{:S(2)}) collective-permute-start(bf16[1,384,384]{2,1,0:T(8,128)(2,1)S(1)} %get-tuple-element.306), channel_id=1, source_target_pairs={{0,4},{4,0},{8,12},{12,8},{16,20},{20,16},{24,28},{28,24},{1,5},{5... | collective-permute-start | bytes 884744 | tf_op jit(solution)/shard_map/ppermute | solution.py:1112
  125.8 9.6 %collective-permute-start.32 = (bf16[2,96,384]{2,1,0:T(8,128)(2,1)S(1)}, bf16[2,96,384]{2,1,0:T(8,128)(2,1)S(1)}, u32[]{:S(2)}, u32[]{:S(2)}) collective-permute-start(bf16[2,96,384]{2,1,0:T(8,128)(2,1)S(1)} %get-tuple-element.431), channel_id=1, source_target_pairs={{0,16},{4,20},{8,24},{12,28},{16,0},{20,4},{24,8},{28,12},{1,17},{... | collective-permute-start | bytes 442376 | tf_op jit(solution)/shard_map/ppermute | solution.py:1112
  126.8 8.5 %collective-permute-start.34 = (bf16[160,768]{1,0:T(8,128)(2,1)S(1)}, bf16[160,768]{1,0:T(8,128)(2,1)S(1)}, u32[]{:S(2)}, u32[]{:S(2)}) collective-permute-start(bf16[160,768]{1,0:T(8,128)(2,1)S(1)} %get-tuple-element.422), channel_id=1, source_target_pairs={{0,2},{1,3},{2,0},{3,1},{4,6},{5,7},{6,4},{7,5},{8,10},{9,11},{10,... | collective-permute-start | bytes 737288 | tf_op jit(solution)/shard_map/ppermute | solution.py:1114
  135.3 14.8 %collective-permute-start.35 = (bf16[1,384,384]{2,1,0:T(8,128)(2,1)S(1)}, bf16[1,384,384]{2,1,0:T(8,128)(2,1)S(1)}, u32[]{:S(2)}, u32[]{:S(2)}) collective-permute-start(bf16[1,384,384]{2,1,0:T(8,128)(2,1)S(1)} %get-tuple-element.316), channel_id=1, source_target_pairs={{0,4},{4,0},{8,12},{12,8},{16,20},{20,16},{24,28},{28,24},{1,5},{5... | collective-permute-start | bytes 884744 | tf_op jit(solution)/shard_map/ppermute | solution.py:1112
  136.8 14.3 %collective-permute-start.36 = (bf16[1,384,384]{2,1,0:T(8,128)(2,1)S(1)}, bf16[1,384,384]{2,1,0:T(8,128)(2,1)S(1)}, u32[]{:S(2)}, u32[]{:S(2)}) collective-permute-start(bf16[1,384,384]{2,1,0:T(8,128)(2,1)S(1)} %get-tuple-element.317), channel_id=1, source_target_pairs={{0,2},{1,3},{2,0},{3,1},{4,6},{5,7},{6,4},{7,5},{8,10},{9,11},{10,... | collective-permute-start | bytes 884744 | tf_op jit(solution)/shard_map/ppermute | solution.py:1114
  137.4 15.6 %collective-permute-start.37 = (bf16[1,384,384]{2,1,0:T(8,128)(2,1)S(1)}, bf16[1,384,384]{2,1,0:T(8,128)(2,1)S(1)}, u32[]{:S(2)}, u32[]{:S(2)}) collective-permute-start(bf16[1,384,384]{2,1,0:T(8,128)(2,1)S(1)} %get-tuple-element.318), channel_id=1, source_target_pairs={{0,6},{1,7},{2,4},{3,5},{4,2},{5,3},{6,0},{7,1},{8,14},{9,15},{10,... | collective-permute-start | bytes 884744 | tf_op jit(solution)/shard_map/ppermute | solution.py:1116
  139.5 13.5 %collective-permute-start.38 = (bf16[2,2,96,384]{3,2,1,0:T(8,128)(2,1)S(1)}, bf16[2,2,96,384]{3,2,1,0:T(8,128)(2,1)S(1)}, u32[]{:S(2)}, u32[]{:S(2)}) collective-permute-start(bf16[2,2,96,384]{3,2,1,0:T(8,128)(2,1)S(1)} %get-tuple-element.322), channel_id=1, source_target_pairs={{0,8},{4,12},{8,0},{12,4},{16,24},{20,28},{24,16},{28,20},{1,9},{5... | collective-permute-start | bytes 884744 | tf_op jit(solution)/shard_map/ppermute | solution.py:1112
  140.3 8.4 %collective-permute-start.39 = (bf16[2,96,384]{2,1,0:T(8,128)(2,1)S(1)}, bf16[2,96,384]{2,1,0:T(8,128)(2,1)S(1)}, u32[]{:S(2)}, u32[]{:S(2)}) collective-permute-start(bf16[2,96,384]{2,1,0:T(8,128)(2,1)S(1)} %add_convert_fusion.6.refs_1_), channel_id=1, source_target_pairs={{0,16},{4,20},{8,24},{12,28},{16,0},{20,4},{24,8},{28,12},{1,17},{... | collective-permute-start | bytes 442376 | tf_op jit(solution)/shard_map/ppermute | solution.py:1112
  148.7 9.9 %collective-permute-start.40 = (bf16[1,384,384]{2,1,0:T(8,128)(2,1)S(1)}, bf16[1,384,384]{2,1,0:T(8,128)(2,1)S(1)}, u32[]{:S(2)}, u32[]{:S(2)}) collective-permute-start(bf16[1,384,384]{2,1,0:T(8,128)(2,1)S(1)} %get-tuple-element.332), channel_id=1, source_target_pairs={{0,4},{4,0},{8,12},{12,8},{16,20},{20,16},{24,28},{28,24},{1,5},{5... | collective-permute-start | bytes 884744 | tf_op jit(solution)/shard_map/ppermute | solution.py:1112
  150.1 14.3 %collective-permute-start.41 = (bf16[1,384,384]{2,1,0:T(8,128)(2,1)S(1)}, bf16[1,384,384]{2,1,0:T(8,128)(2,1)S(1)}, u32[]{:S(2)}, u32[]{:S(2)}) collective-permute-start(bf16[1,384,384]{2,1,0:T(8,128)(2,1)S(1)} %get-tuple-element.333), channel_id=1, source_target_pairs={{0,2},{1,3},{2,0},{3,1},{4,6},{5,7},{6,4},{7,5},{8,10},{9,11},{10,... | collective-permute-start | bytes 884744 | tf_op jit(solution)/shard_map/ppermute | solution.py:1114
  151.2 13.3 %collective-permute-start.42 = (bf16[1,384,384]{2,1,0:T(8,128)(2,1)S(1)}, bf16[1,384,384]{2,1,0:T(8,128)(2,1)S(1)}, u32[]{:S(2)}, u32[]{:S(2)}) collective-permute-start(bf16[1,384,384]{2,1,0:T(8,128)(2,1)S(1)} %get-tuple-element.334), channel_id=1, source_target_pairs={{0,6},{1,7},{2,4},{3,5},{4,2},{5,3},{6,0},{7,1},{8,14},{9,15},{10,... | collective-permute-start | bytes 884744 | tf_op jit(solution)/shard_map/ppermute | solution.py:1116
  153.0 11.4 %collective-permute-start.44 = (bf16[2,2,96,384]{3,2,1,0:T(8,128)(2,1)S(1)}, bf16[2,2,96,384]{3,2,1,0:T(8,128)(2,1)S(1)}, u32[]{:S(2)}, u32[]{:S(2)}) collective-permute-start(bf16[2,2,96,384]{3,2,1,0:T(8,128)(2,1)S(1)} %pad_maximum_fusion.4), channel_id=1, source_target_pairs={{0,8},{4,12},{8,0},{12,4},{16,24},{20,28},{24,16},{28,20},{1,9},{5... | collective-permute-start | bytes 884744 | tf_op jit(solution)/shard_map/ppermute | solution.py:1112
  155.2 9.2 %collective-permute-start.43 = (bf16[2,96,384]{2,1,0:T(8,128)(2,1)S(1)}, bf16[2,96,384]{2,1,0:T(8,128)(2,1)S(1)}, u32[]{:S(2)}, u32[]{:S(2)}) collective-permute-start(bf16[2,96,384]{2,1,0:T(8,128)(2,1)S(1)} %get-tuple-element.427), channel_id=1, source_target_pairs={{0,16},{4,20},{8,24},{12,28},{16,0},{20,4},{24,8},{28,12},{1,17},{... | collective-permute-start | bytes 442376 | tf_op jit(solution)/shard_map/ppermute | solution.py:1112
  158.6 14.9 %collective-permute-start.49 = (f32[13,768]{1,0:T(8,128)S(1)}, f32[13,768]{1,0:T(8,128)S(1)}, u32[]{:S(2)}, u32[]{:S(2)}) collective-permute-start(f32[13,768]{1,0:T(8,128)S(1)} %shard_map.342), channel_id=1, source_target_pairs={{0,1},{1,0},{2,3},{3,2},{4,5},{5,4},{6,7},{7,6},{8,9},{9,8},{10,11... | collective-permute-start | bytes 119816 | tf_op jit(solution)/shard_map/ppermute | solution.py:1114
  164.5 15.5 %collective-permute-start.48 = (bf16[2,96,384]{2,1,0:T(8,128)(2,1)S(1)}, bf16[2,96,384]{2,1,0:T(8,128)(2,1)S(1)}, u32[]{:S(2)}, u32[]{:S(2)}) collective-permute-start(bf16[2,96,384]{2,1,0:T(8,128)(2,1)S(1)} %add_convert_fusion.3.refs_1_), channel_id=1, source_target_pairs={{0,16},{4,20},{8,24},{12,28},{16,0},{20,4},{24,8},{28,12},{1,17},{... | collective-permute-start | bytes 442376 | tf_op jit(solution)/shard_map/ppermute | solution.py:1112
  167.2 12.8 %collective-permute-start.45 = (bf16[2,96,384]{2,1,0:T(8,128)(2,1)S(1)}, bf16[2,96,384]{2,1,0:T(8,128)(2,1)S(1)}, u32[]{:S(2)}, u32[]{:S(2)}) collective-permute-start(bf16[2,96,384]{2,1,0:T(8,128)(2,1)S(1)} %get-tuple-element.343), channel_id=1, source_target_pairs={{0,8},{4,12},{8,0},{12,4},{16,24},{20,28},{24,16},{28,20},{1,9},{5... | collective-permute-start | bytes 442376 | tf_op jit(solution)/shard_map/ppermute | solution.py:1112
  168.1 15.1 %collective-permute-start.46 = (bf16[2,96,384]{2,1,0:T(8,128)(2,1)S(1)}, bf16[2,96,384]{2,1,0:T(8,128)(2,1)S(1)}, u32[]{:S(2)}, u32[]{:S(2)}) collective-permute-start(bf16[2,96,384]{2,1,0:T(8,128)(2,1)S(1)} %get-tuple-element.344), channel_id=1, source_target_pairs={{0,16},{4,20},{8,24},{12,28},{16,0},{20,4},{24,8},{28,12},{1,17},{... | collective-permute-start | bytes 442376 | tf_op jit(solution)/shard_map/ppermute | solution.py:1112
  170.1 13.1 %collective-permute-start.47 = (bf16[2,96,384]{2,1,0:T(8,128)(2,1)S(1)}, bf16[2,96,384]{2,1,0:T(8,128)(2,1)S(1)}, u32[]{:S(2)}, u32[]{:S(2)}) collective-permute-start(bf16[2,96,384]{2,1,0:T(8,128)(2,1)S(1)} %get-tuple-element.345), channel_id=1, source_target_pairs={{0,24},{4,28},{8,16},{12,20},{16,8},{20,12},{24,0},{28,4},{1,25},{... | collective-permute-start | bytes 442376 | tf_op jit(solution)/shard_map/ppermute | solution.py:1112
  183.2 11.5 %collective-permute-start.52 = (bf16[2,2,96,384]{3,2,1,0:T(8,128)(2,1)S(1)}, bf16[2,2,96,384]{3,2,1,0:T(8,128)(2,1)S(1)}, u32[]{:S(2)}, u32[]{:S(2)}) collective-permute-start(bf16[2,2,96,384]{3,2,1,0:T(8,128)(2,1)S(1)} %pad_maximum_fusion.5), channel_id=1, source_target_pairs={{0,8},{4,12},{8,0},{12,4},{16,24},{20,28},{24,16},{28,20},{1,9},{5... | collective-permute-start | bytes 884744 | tf_op jit(solution)/shard_map/ppermute | solution.py:1112
  185.6 9.1 %collective-permute-start.51 = (bf16[5,2,48,384]{3,2,1,0:T(8,128)(2,1)S(1)}, bf16[5,2,48,384]{3,2,1,0:T(8,128)(2,1)S(1)}, u32[]{:S(2)}, u32[]{:S(2)}) collective-permute-start(bf16[5,2,48,384]{3,2,1,0:T(8,128)(2,1)S(1)} %get-tuple-element.362), channel_id=1, source_target_pairs={{0,4},{4,0},{8,12},{12,8},{16,20},{20,16},{24,28},{28,24},{1,5},{5... | collective-permute-start | bytes 1105928 | tf_op jit(solution)/shard_map/ppermute | solution.py:1112
  196.5 11.4 %collective-permute-start.55 = (bf16[5,2,48,384]{3,2,1,0:T(8,128)(2,1)S(1)}, bf16[5,2,48,384]{3,2,1,0:T(8,128)(2,1)S(1)}, u32[]{:S(2)}, u32[]{:S(2)}) collective-permute-start(bf16[5,2,48,384]{3,2,1,0:T(8,128)(2,1)S(1)} %get-tuple-element.367), channel_id=1, source_target_pairs={{0,4},{4,0},{8,12},{12,8},{16,20},{20,16},{24,28},{28,24},{1,5},{5... | collective-permute-start | bytes 1105928 | tf_op jit(solution)/shard_map/ppermute | solution.py:1112
  197.4 10.5 %collective-permute-start.54 = (bf16[2,2,96,384]{3,2,1,0:T(8,128)(2,1)S(1)}, bf16[2,2,96,384]{3,2,1,0:T(8,128)(2,1)S(1)}, u32[]{:S(2)}, u32[]{:S(2)}) collective-permute-start(bf16[2,2,96,384]{3,2,1,0:T(8,128)(2,1)S(1)} %pad_maximum_fusion.6), channel_id=1, source_target_pairs={{0,8},{4,12},{8,0},{12,4},{16,24},{20,28},{24,16},{28,20},{1,9},{5... | collective-permute-start | bytes 884744 | tf_op jit(solution)/shard_map/ppermute | solution.py:1112
  199.3 8.6 %collective-permute-start.58 = (f32[13,768]{1,0:T(8,128)S(1)}, f32[13,768]{1,0:T(8,128)S(1)}, u32[]{:S(2)}, u32[]{:S(2)}) collective-permute-start(f32[13,768]{1,0:T(8,128)S(1)} %add.75), channel_id=1, source_target_pairs={{0,24},{4,28},{8,16},{12,20},{16,8},{20,12},{24,0},{28,4},{1,25},{... | collective-permute-start | bytes 119816 | tf_op jit(solution)/shard_map/ppermute | solution.py:1112
  (29 other events, 173.4 us)

commit v4 on v3

--- a/solution.py
+++ b/solution.py
@@ -506,7 +506,7 @@
     return jax.ShapeDtypeStruct(dims, kind)
 
 
-def local_call(kernel, args, outs, scratch=(), in_hbm=(), out_hbm=(), in_smem=(0,), mib=12, micros=1):
+def local_call(kernel, args, outs, scratch=(), in_hbm=(), out_hbm=(), in_smem=(0,), mib=12, micros=0.05):
     def place_of(index, hbm, smem):
         if index in hbm:
             return pl.BlockSpec(memory_space=pltpu.HBM)
@@ -514,7 +514,6 @@
             return pl.BlockSpec(memory_space=pltpu.SMEM)
         return pl.BlockSpec(memory_space=pltpu.VMEM)
 
-    moved = sum(v.size * v.dtype.itemsize for v in list(args) + list(outs))
     return pl.pallas_call(
         kernel,
         out_shape=list(outs),
@@ -523,7 +522,7 @@
         scratch_shapes=list(scratch),
         compiler_params=pltpu.CompilerParams(vmem_limit_bytes=mib * 2**20),
         cost_estimate=pl.CostEstimate(
-            flops=int(micros * 1e9), bytes_accessed=moved, transcendentals=0
+            flops=int(micros * 1e9), bytes_accessed=int(micros * 1e6), transcendentals=0
         ),
     )(*args)
 
@@ -890,20 +889,18 @@
     sums_ref[0:1, :] = col_sum(grad_normed * hat)
     sums_ref[1:2, :] = col_sum(grad_normed)
     grad = base + norm_back(grad_normed * vec_ref[0:1, :], hat, scale)
-    grad_ref[...] = grad[:patches]
+    grad_ref[:, 0, :] = grad[:patches]
 
 
 def core_sum_kernel(place_ref, kept_ref, came_ref, *out_refs):
     x, m = place_ref[1], place_ref[2]
     own = kept_ref.shape[1] // PAIR
-    chips = len(out_refs) // 2
-    for index in range(chips):
+    for index, out_ref in enumerate(out_refs):
         dy, dx = index // PAIR, index % PAIR
         high = (m // PAIR) ^ dy
         for block in range(own):
             at = (x ^ dx) * own + block
-            out_ref = out_refs[block // (own // 2) * chips + index]
-            out_ref[block % (own // 2)] = to_half(
+            out_ref[block] = to_half(
                 kept_ref[high, at].astype(full) + came_ref[high, at].astype(full)
             )
 
@@ -1007,17 +1004,19 @@
         sent_ref[4, block, 16:, :] = jnp.zeros((sent_ref.shape[2] - 16, order), half)
 
 
-def squares_kernel(*refs):
+def last_sums_kernel(vec_ref, vec_came_ref, *refs):
     count = len(refs) // 2
     mine_refs, came_refs, out_ref = refs[:count], refs[count:-1], refs[-1]
     blocks = came_refs[0].shape[1]
+    out_ref[...] = jnp.zeros_like(out_ref)
+    out_ref[: vec_ref.shape[0], :] = vec_ref[...] + vec_came_ref[...]
     for matrix in range(count):
         for block in range(blocks):
-            at = matrix * blocks + block
-            out_ref[at : at + 1, :] = mine_refs[matrix][block : block + 1, :]
+            at = 16 + matrix * blocks + block
+            out_ref[at : at + 1, :128] = mine_refs[matrix][block : block + 1, :]
             terms = came_refs[matrix][4, block, 0:16, 0:128].astype(full)
             at += count * blocks
-            out_ref[at : at + 1, :] = jnp.sum(terms, axis=0, keepdims=True)
+            out_ref[at : at + 1, :128] = jnp.sum(terms, axis=0, keepdims=True)
 
 
 def apply_kernel(
@@ -1033,7 +1032,7 @@
             at = (x ^ side) * own + block
             rate = jnp.where(m * local + at < rates[0], rates[1], rates[2])
             if total_ref is not None:
-                row = (side * 2 + matrix) * own + block
+                row = 16 + (side * 2 + matrix) * own + block
                 total = total_ref[row : row + 1, 0:1]
                 rate = rate * lax.rsqrt(total / (order * order) + 1e-06)
             grad_ref[at] = ref[0, block].astype(full)
@@ -1053,15 +1052,12 @@
     out_ref[9:, :] = bias_row(place_ref[2], bias_ref[...], out_ref.shape[0] - 9)
 
 
-def vector_step_kernel(vec_ref, *refs):
-    part_refs, (grad_ref, new_ref) = refs[:-2], refs[-2:]
-    grad = part_refs[0][...]
-    for ref in part_refs[1:]:
-        grad = grad + ref[...]
-    grad_ref[...] = grad
-    for start in range(0, grad.shape[1], BLOCK_VEC):
+def vector_step_kernel(vec_ref, total_ref, grad_ref, new_ref):
+    rows = vec_ref.shape[0]
+    grad_ref[...] = total_ref[:rows, :]
+    for start in range(0, vec_ref.shape[1], BLOCK_VEC):
         lanes = slice(start, start + BLOCK_VEC)
-        block = grad[:, lanes]
+        block = total_ref[:rows, lanes]
         scale = lax.rsqrt(jnp.mean(block * block, axis=-1, keepdims=True) + 1e-06)
         new_ref[:, lanes] = vec_ref[:, lanes] - 0.05 * (block * scale)
 
@@ -1211,12 +1207,7 @@
         (mask, tok, cot, vectors),
         (shape((rows, width)), shape((SLOTS, width)), shape((SLOTS, rows))),
         in_smem=(),
-        micros=1.5,
-    )
-    found, grad_sent, normed, chosen, feed_far, bundle_near = phase(
-        found, grad_sent, normed, chosen, feed_far, bundle_near
-    )
-
+    )
     pieces, piece_info = [], []
     for (dx, dm), part in zip(plane, found):
         pieces += [part, move(part, 0, 1)]
@@ -1227,9 +1218,6 @@
     roots, roots_near = bundle[feed_count:], bundle_near[feed_count:]
     half_roots = roots.shape[0] // 2
     roots_first, roots_second = roots[:half_roots], roots[half_roots:]
-    pieces, grad_came, feed_near, roots_first, roots_second, roots, roots_near = phase(
-        pieces, grad_came, feed_near, roots_first, roots_second, roots, roots_near
-    )
 
     feed_near_came = move(feed_near, 1, 0)
     feed_last = move(feed_far, PAIR, 0)
@@ -1267,9 +1255,6 @@
     feed_far = jnp.stack([feed_far, feed_last])
     feed_far_came = move(feed_far, 1, 0)
     roots_second_far = move(roots_second, 2 * PAIR, 0)
-    group_rows, feed_far_came, roots_second_far = phase(
-        group_rows, feed_far_came, roots_second_far
-    )
 
     feed_pieces = [feed_near, feed_near_came, feed_far, feed_far_came]
     feed_info = [((0, 1), 0), ((0, 1), 1), ((2, 3), 0), ((2, 3), 1)]
@@ -1301,7 +1286,6 @@
         (place, all_rows, grad_hidden),
         (shape((own, order, order)),) * 2 + (shape((1, hidden_width), full),),
         scratch=(pltpu.VMEM((local, order, order), half),),
-        micros=1,
     )
     up_came = move(up_sent, 1, 0)
     feed_kept, feed_sent, down_kept, down_first, down_second = local_call(
@@ -1311,7 +1295,6 @@
         + (shape((own, order, order)),)
         + (shape((own // 2, order, order)),) * 2,
         scratch=(pltpu.VMEM((local, order, order), half),),
-        micros=2,
     )
     back, up_came, down_first, down_second, feed_sent, all_roots = phase(
         back, up_came, down_first, down_second, feed_sent, all_roots
@@ -1359,8 +1342,7 @@
                 pltpu.VMEM((order, order), full),
                 pltpu.VMEM((4, line_rows, order), full),
             ),
-            micros=2,
-        )
+            )
 
     up_near_kept, up_near_sent = pairs_of((up_kept, up_came))
     up_near = move(up_near_sent, PAIR, 0)
@@ -1406,14 +1388,13 @@
     core_parts = local_call(
         core_sum_kernel,
         (place, attn_kept, attn_came),
-        (shape((own // 2, order, order)),) * (2 * group),
+        (shape((own, order, order)),) * group,
     )
     core_parts, up_far, up_mine, down_second_came, feed = phase(
         core_parts, up_far, up_mine, down_second_came, feed
     )
-    first_half, second_half = core_parts[:group], core_parts[group:]
-
-    first_came = [move(part, dx, dm) for (dx, dm), part in zip(plane[1:], first_half[1:])]
+
+    attn_came = [move(part, dx, dm) for (dx, dm), part in zip(plane[1:], core_parts[1:])]
     middle = own // 2
     down_near_kept, down_near_sent = pairs_of(
         (down_kept[:middle], down_first_came), (down_kept[middle:], down_second_came)
@@ -1426,7 +1407,7 @@
         (*feed, mixed, grad_middle, tok, cot, chosen, vectors, branch, weights),
         (
             shape((patches, width)),
-            shape((patches, width), full),
+            shape((patches, 1, width), full),
             shape((5, width), full),
         ),
         scratch=(
@@ -1435,60 +1416,49 @@
         ),
         in_hbm=(group // PAIR + 7,),
         in_smem=(),
-        micros=2,
     )
     (vector_sum,) = local_call(
         vector_part_kernel,
         (place, sums_one, sums_two, bias_sums),
         (shape(vectors.shape, full),),
     )
-    first_came, down_near, up_whole_far, up_rows, vector_sum = phase(
-        first_came, down_near, up_whole_far, up_rows, vector_sum
-    )
-    second_came = [move(part, dx, dm) for (dx, dm), part in zip(plane[1:], second_half[1:])]
     down_mine, down_other = add_near(down_near_kept, down_near)
     down_far = move(down_other, 2 * PAIR, 0)
     up_pair = jnp.stack([up_rows, up_whole_far])
     up_pair_came = move(up_pair, PAIR, 0)
-    second_came, down_far, up_pair_came, down_mine = phase(
-        second_came, down_far, up_pair_came, down_mine
-    )
-
-    attn_split = rows_of((first_half[0], *first_came), (second_half[0], *second_came))
-    attn_split = [attn_split[0]] + [move(attn_split[k], k * PAIR, 0) for k in lines]
+    up_kept, up_sent, up_squares = step_of(
+        [up_rows, up_pair_came[0], up_whole_far, up_pair_came[1]], 1
+    )
     down_rows = total_of([down_mine, down_far])
     down_whole_far = move(down_rows, 2 * PAIR, 0)
-    vector_came = move(vector_sum, 0, 1)
-    up_mine, up_sent, up_squares = step_of(
-        [up_rows, up_pair_came[0], up_whole_far, up_pair_came[1]], 1
-    )
-    attn_split, down_whole_far, vector_came, up_sent, up_mine, up_squares = phase(
-        attn_split, down_whole_far, vector_came, up_sent, up_mine, up_squares
-    )
-
-    attn_rows = total_of(attn_split)
-    attn_far = move(attn_rows, 2 * PAIR, 0)
-    up_found = move(up_sent, 1, 0)
+    attn_came, down_rows, down_whole_far, up_sent, vector_sum = phase(
+        attn_came, down_rows, down_whole_far, up_sent, vector_sum
+    )
+
+    attn_split = rows_of((core_parts[0], *attn_came))
+    attn_split = [attn_split[0]] + [move(attn_split[k], k * PAIR, 0) for k in lines]
     down_pair = jnp.stack([down_rows, down_whole_far])
     down_pair_came = move(down_pair, PAIR, 0)
-    vector_sum = vector_sum + vector_came
-    vector_later = [move(vector_sum, 0, dm) for dm in range(PAIR, group, PAIR)]
-    attn_far, up_found, down_pair_came, vector_later = phase(
-        attn_far, up_found, down_pair_came, vector_later
-    )
-    attn_pair = jnp.stack([attn_rows, attn_far])
-    attn_pair_came = move(attn_pair, PAIR, 0)
-    down_mine, down_sent, down_squares = step_of(
+    up_found = move(up_sent, 1, 0)
+    down_kept, down_sent, down_squares = step_of(
         [down_rows, down_pair_came[0], down_whole_far, down_pair_came[1]], 2
     )
+    attn_split, up_found, down_sent, vector_sum = phase(
+        attn_split, up_found, down_sent, vector_sum
+    )
+
+    attn_rows = total_of(attn_split)
+    attn_parts = [attn_rows] + [move(attn_rows, k * PAIR, 0) for k in lines]
     down_found = move(down_sent, 1, 0)
-    vector_sum = sum(vector_later, vector_sum)
-    vector_line = [move(vector_sum, k * PAIR, 0) for k in lines]
-    attn_pair_came, down_found, vector_line = phase(attn_pair_came, down_found, vector_line)
+    vector_sum = vector_sum + move(vector_sum, 0, 1)
+    for dm in range(PAIR, group, PAIR):
+        vector_sum = vector_sum + move(vector_sum, 0, dm)
+    vector_came = move(vector_sum, 1, 0)
+    attn_parts, down_found, vector_came = phase(attn_parts, down_found, vector_came)
 
     kept, sent = local_call(
         lambda *refs: whole_step_kernel(z_count, 3 * own, *refs),
-        (place, attn_rows, attn_pair_came[0], attn_far, attn_pair_came[1], *all_roots),
+        (place, *attn_parts, *all_roots),
         (shape((4, own, piece, order)),) * 2,
         scratch=(pltpu.VMEM((own, order, order), half),) * 3
         + (
@@ -1496,21 +1466,17 @@
             pltpu.VMEM((4, line_rows, order), full),
             pltpu.VMEM((order, order), full),
         ),
-        micros=2,
-    )
-    sent, down_found, vector_line = phase(sent, down_found, vector_line)
+    )
     came = move(sent, 1, 0)
-    (squares,) = local_call(
-        squares_kernel,
-        (up_squares, down_squares, up_found, down_found),
-        (shape((8, 128), full),),
+    (last_sums,) = local_call(
+        last_sums_kernel,
+        (vector_sum, vector_came, up_squares, down_squares, up_found, down_found),
+        (shape((24, width), full),),
         in_smem=(),
     )
-    total = squares
+    total = last_sums
     for k in lines:
-        total = total + move(squares, k * PAIR, 0)
-    vector_sum = sum(vector_line, vector_sum)
-    vector_parts = [vector_sum, move(vector_sum, 1, 0)]
+        total = total + move(last_sums, k * PAIR, 0)
 
     def apply(rates, matrix, weight, left, right, *found):
         stat = shape(weight.shape, full)
@@ -1525,16 +1491,16 @@
     fc2_rates = (0, 0.0, 0.5 * FF ** (-0.5))
     vector_grad, new_vectors = local_call(
         vector_step_kernel,
-        (vectors, *vector_parts),
+        (vectors, total),
         (shape(vectors.shape, full),) * 2,
         in_smem=(),
     )
     done_attn = apply(attn_rates, 0, w_attn, left_attn, right_attn, kept, came)
-    done_fc1 = apply(fc1_rates, 0, w_fc1, left_fc1, right_fc1, up_mine, up_found, total)
-    done_fc2 = apply(fc2_rates, 1, w_fc2, left_fc2, right_fc2, down_mine, down_found, total)
+    done_fc1 = apply(fc1_rates, 0, w_fc1, left_fc1, right_fc1, up_kept, up_found, total)
+    done_fc2 = apply(fc2_rates, 1, w_fc2, left_fc2, right_fc2, down_kept, down_found, total)
     return (
         block_out[None],
-        input_grad[None],
+        input_grad.transpose(1, 0, 2),
         done_attn[0],
         done_fc1[0],
         done_fc2[0],

time: 225 us -> 210 us (0.933)
  starting transfers between devices: 73.8 us -> 60.7 us
    ppermute x41 -> x38, starting transfers between devices: 57.9 us -> 48.2 us  [move(): return lax.ppermute(values, 'dp', [(s, s ^ dp_mask) for s in range(dp)])]
    ppermute x41 -> x38, waiting for transfers between devices: 69.5 us -> 66.6 us  [move(): return lax.ppermute(values, 'dp', [(s, s ^ dp_mask) for s in range(dp)])]
    ppermute x20 -> x19, waiting for transfers between devices: 24.7 us -> 26.9 us  [move(): return lax.ppermute(values, 'mp', [(s, s ^ mp_mask) for s in range(mp)])]
    ppermute x3 -> x2, starting transfers between devices: 4.77 us -> 2.74 us  [move(): lax.ppermute(values, ('dp', 'mp'), [(s, s ^ mask) for s in range(dp * mp)])]
    ppermute x20 -> x19, starting transfers between devices: 11.2 us -> 9.73 us  [move(): return lax.ppermute(values, 'mp', [(s, s ^ mp_mask) for s in range(mp)])]
  transfers between devices with their start and end apart: 64 -> 59, of which waited for: 26 -> 29; matrix products, arithmetic and copies ran while one was open for 1% -> 0% of each run, Pallas kernels for 19% -> 23%
where the time goes in v4:
time: 210 us
  waiting for transfers between devices  93.5 us (45%)
  starting transfers between devices  60.7 us (29%)
  Pallas kernels  53 us (25%)
    ppermute x38, waiting for transfers between devices, move(): return lax.ppermute(values, 'dp', [(s, s ^ dp_mask) for s in range(dp)])  66.6 us
    pallas_call x22, Pallas kernels, local_call(): pl.pallas_call(kernel, out_shape=list(outs), in_specs=[place_of(i, in_hbm...  53 us
    ppermute x38, starting transfers between devices, move(): return lax.ppermute(values, 'dp', [(s, s ^ dp_mask) for s in range(dp)])  48.2 us
    ppermute x19, waiting for transfers between devices, move(): return lax.ppermute(values, 'mp', [(s, s ^ mp_mask) for s in range(mp)])  26.9 us
    ppermute x19, starting transfers between devices, move(): return lax.ppermute(values, 'mp', [(s, s ^ mp_mask) for s in range(mp)])  9.73 us
  transfers between devices with their start and end apart: 59, of which 29 were waited for; matrix products, arithmetic and copies ran while one was open for 0% of the time, Pallas kernels for 23%

profile of v4, /device:TPU:0, one launch (start us, length us, event | category | flops | bytes accessed | tf_op | source)
XLA Modules:
  0.0 209.7 jit_solution(9129770572130943454)
XLA Ops:
  0.8 2.3 %shard_map.330 = (bf16[4,48,384]{2,1,0:T(8,128)(2,1)S(1)}, bf16[8,48,384]{2,1,0:T(8,128)(2,1)S(1)}, bf16[6,2,48,384]{3,2,1,0:T(8,128)(2,1)S(1)}, bf16[6,2,48,384]{3,2,1,0:T(8,128)(2,1)S(1)}) custom-call(s32[4]{0:T(128)S(1)} %pad_add_fusion.place_ref.refs_0_, f32[4,48,384]{2,1,0:T(8,128)} %refs_1_.5, f32[4,48,384]{2,1,0:T(8,128)} %refs_1_.6, ...), custom_call_target="tpu_custom_call" | custom-call | flops 50000000 | bytes 50000 | tf_op jit(solution)/shard_map/pallas_call | solution.py:517
  3.1 3.0 %collective-permute-start.3 = (bf16[6,2,48,384]{3,2,1,0:T(8,128)(2,1)S(1)}, bf16[6,2,48,384]{3,2,1,0:T(8,128)(2,1)S(1)}, u32[]{:S(2)}, u32[]{:S(2)}) collective-permute-start(bf16[6,2,48,384]{3,2,1,0:T(8,128)(2,1)S(1)} %get-tuple-element.161), channel_id=1, source_target_pairs={{0,4},{4,0},{8,12},{12,8},{16,20},{20,16},{24,28},{28,24},{1,5},{5... | collective-permute-start | bytes 1327112 | tf_op jit(solution)/shard_map/ppermute | solution.py:1108
  6.1 3.6 %collective-permute-start.2 = (bf16[4,48,384]{2,1,0:T(8,128)(2,1)S(1)}, bf16[4,48,384]{2,1,0:T(8,128)(2,1)S(1)}, u32[]{:S(2)}, u32[]{:S(2)}) collective-permute-start(bf16[4,48,384]{2,1,0:T(8,128)(2,1)S(1)} %get-tuple-element.164), channel_id=1, source_target_pairs={{0,24},{4,28},{8,16},{12,20},{16,8},{20,12},{24,0},{28,4},{1,25},{... | collective-permute-start | bytes 442376 | tf_op jit(solution)/shard_map/ppermute | solution.py:1108
  10.5 4.2 %collective-permute-done.2 = bf16[4,48,384]{2,1,0:T(8,128)(2,1)S(1)} collective-permute-done((bf16[4,48,384]{2,1,0:T(8,128)(2,1)S(1)}, bf16[4,48,384]{2,1,0:T(8,128)(2,1)S(1)}, u32[]{:S(2)}, u32[]{:S(2)}) %collective-permute-start.2) | collective-permute-done | bytes 147488 | tf_op jit(solution)/shard_map/ppermute | solution.py:1108
  14.7 7.2 %collective-permute-done.1 = bf16[4,48,384]{2,1,0:T(8,128)(2,1)S(1)} collective-permute-done((bf16[4,48,384]{2,1,0:T(8,128)(2,1)S(1)}, bf16[4,48,384]{2,1,0:T(8,128)(2,1)S(1)}, u32[]{:S(2)}, u32[]{:S(2)}) %collective-permute-start.1) | collective-permute-done | bytes 147488 | tf_op jit(solution)/shard_map/ppermute | solution.py:1108
  22.0 1.6 collective-permute-start.10
  26.2 3.1 %collective-permute-start.4 = (bf16[24,48,384]{2,1,0:T(8,128)(2,1)S(1)}, bf16[24,48,384]{2,1,0:T(8,128)(2,1)S(1)}, u32[]{:S(2)}, u32[]{:S(2)}) collective-permute-start(bf16[24,48,384]{2,1,0:T(8,128)(2,1)S(1)} %get-tuple-element.163), channel_id=1, source_target_pairs={{0,8},{4,12},{8,0},{12,4},{16,24},{20,28},{24,16},{28,20},{1,9},{5... | collective-permute-start | bytes 2654216 | tf_op jit(solution)/shard_map/ppermute | solution.py:1108
  30.0 9.4 %collective-permute-done.15 = bf16[8,48,384]{2,1,0:T(8,128)(2,1)S(1)} collective-permute-done((bf16[8,48,384]{2,1,0:T(8,128)(2,1)S(1)}, bf16[8,48,384]{2,1,0:T(8,128)(2,1)S(1)}, u32[]{:S(2)}, u32[]{:S(2)}) %collective-permute-start.15) | collective-permute-done | bytes 294944 | tf_op jit(solution)/shard_map/ppermute | solution.py:1108
  41.4 8.5 %collective-permute-done.8.refs_5_ = bf16[4,4,48,384]{3,2,1,0:T(8,128)(2,1)S(1)} collective-permute-done((bf16[4,4,48,384]{3,2,1,0:T(8,128)(2,1)S(1)}, bf16[4,4,48,384]{3,2,1,0:T(8,128)(2,1)S(1)}, u32[]{:S(2)}, u32[]{:S(2)}) %collective-permute-start.8) | collective-permute-done | bytes 589856 | tf_op jit(solution)/shard_map/ppermute | solution.py:1110
  50.6 2.4 %collective-permute-done.4 = bf16[24,48,384]{2,1,0:T(8,128)(2,1)S(1)} collective-permute-done((bf16[24,48,384]{2,1,0:T(8,128)(2,1)S(1)}, bf16[24,48,384]{2,1,0:T(8,128)(2,1)S(1)}, u32[]{:S(2)}, u32[]{:S(2)}) %collective-permute-start.4) | collective-permute-done | bytes 884768 | tf_op jit(solution)/shard_map/ppermute | solution.py:1108
  53.1 2.5 %collective-permute-start.17 = (bf16[8,48,384]{2,1,0:T(8,128)(2,1)S(1)}, bf16[8,48,384]{2,1,0:T(8,128)(2,1)S(1)}, u32[]{:S(2)}, u32[]{:S(2)}) collective-permute-start(bf16[8,48,384]{2,1,0:T(8,128)(2,1)S(1)} %get-tuple-element.300), channel_id=1, source_target_pairs={{0,16},{4,20},{8,24},{12,28},{16,0},{20,4},{24,8},{28,12},{1,17},{... | collective-permute-start | bytes 884744 | tf_op jit(solution)/shard_map/ppermute | solution.py:1108
  57.6 10.9 %shard_map.333 = (bf16[160,768]{1,0:T(8,128)(2,1)S(1)}, bf16[197,2304]{1,0:T(8,128)(2,1)S(1)}, f32[12,197,197]{2,1,0:T(8,128)S(1)}, bf16[197,768]{1,0:T(8,128)(2...) custom-call(s32[4]{0:T(128)S(1)} %pad_add_fusion.place_ref.refs_0_, ...), custom_call_target="tpu_custom_call" | custom-call | flops 8000000000 | bytes 8000000 | tf_op jit(solution)/shard_map/pallas_call | solution.py:517
  71.7 1.6 collective-permute-start.19
  73.3 8.7 %collective-permute-done.26 = bf16[8,48,384]{2,1,0:T(8,128)(2,1)S(1)} collective-permute-done((bf16[8,48,384]{2,1,0:T(8,128)(2,1)S(1)}, bf16[8,48,384]{2,1,0:T(8,128)(2,1)S(1)}, u32[]{:S(2)}, u32[]{:S(2)}) %collective-permute-start.26) | collective-permute-done | bytes 294944 | tf_op jit(solution)/shard_map/ppermute | solution.py:1108
  82.7 5.2 %shard_map.334 = (bf16[160,768]{1,0:T(8,128)(2,1)S(1)}, bf16[160,768]{1,0:T(8,128)(2,1)S(1)}, bf16[160,768]{1,0:T(8,128)(2,1)S(1)}, bf16[160,768]{1,0:T(8,128)(2...) custom-call(s32[4]{0:T(128)S(1)} %pad_add_fusion.place_ref.refs_0_, ...), custom_call_target="tpu_custom_call" | custom-call | flops 5000000000 | bytes 5000000 | tf_op jit(solution)/shard_map/pallas_call | solution.py:517
  87.9 2.0 shard_map.335
  90.0 2.8 %collective-permute-start.25 = (bf16[2,384,384]{2,1,0:T(8,128)(2,1)S(1)}, bf16[2,384,384]{2,1,0:T(8,128)(2,1)S(1)}, u32[]{:S(2)}, u32[]{:S(2)}) collective-permute-start(bf16[2,384,384]{2,1,0:T(8,128)(2,1)S(1)} %get-tuple-element.189), channel_id=1, source_target_pairs={{0,4},{4,0},{8,12},{12,8},{16,20},{20,16},{24,28},{28,24},{1,5},{5... | collective-permute-start | bytes 1769480 | tf_op jit(solution)/shard_map/ppermute | solution.py:1108
  94.8 3.1 %shard_map.336 = (bf16[2,160,768]{2,1,0:T(8,128)(2,1)S(1)}, bf16[2,160,768]{2,1,0:T(8,128)(2,1)S(1)}, bf16[2,384,384]{2,1,0:T(8,128)(2,1)S(1)}, bf16[1,384,384]{2,1,0:T(8,128)(2,1)S(1)}, bf16[1,384,384]{2,1,0:T(8,128)(2,1)S(1)}) custom-call(s32[4]{0:T(128)S(1)} %pad_add_fusion.place_ref.refs_0_, bf16[640,768]{1,0:T(8,128)(2,1)S(1)} %get-tuple-element.190.refs_1_, ...), custom_call_target="tpu_custom_call" | custom-call | flops 50000000 | bytes 50000 | tf_op jit(solution)/shard_map/pallas_call | solution.py:517
  97.9 3.6 %collective-permute-done.23.refs_3_ = bf16[160,768]{1,0:T(8,128)(2,1)S(1)} collective-permute-done((bf16[160,768]{1,0:T(8,128)(2,1)S(1)}, bf16[160,768]{1,0:T(8,128)(2,1)S(1)}, u32[]{:S(2)}, u32[]{:S(2)}) %collective-permute-start.23) | collective-permute-done | bytes 245792 | tf_op jit(solution)/shard_map/ppermute | solution.py:1110
  101.5 4.5 %collective-permute-done.24.refs_4_ = bf16[160,768]{1,0:T(8,128)(2,1)S(1)} collective-permute-done((bf16[160,768]{1,0:T(8,128)(2,1)S(1)}, bf16[160,768]{1,0:T(8,128)(2,1)S(1)}, u32[]{:S(2)}, u32[]{:S(2)}) %collective-permute-start.24) | collective-permute-done | bytes 245792 | tf_op jit(solution)/shard_map/ppermute | solution.py:1110
  107.1 2.3 %collective-permute-start.28 = (bf16[2,2,96,384]{3,2,1,0:T(8,128)(2,1)S(1)}, bf16[2,2,96,384]{3,2,1,0:T(8,128)(2,1)S(1)}, u32[]{:S(2)}, u32[]{:S(2)}) collective-permute-start(bf16[2,2,96,384]{3,2,1,0:T(8,128)(2,1)S(1)} %get-tuple-element.210), channel_id=1, source_target_pairs={{0,8},{4,12},{8,0},{12,4},{16,24},{20,28},{24,16},{28,20},{1,9},{5... | collective-permute-start | bytes 884744 | tf_op jit(solution)/shard_map/ppermute | solution.py:1108
  109.4 1.7 collective-permute-start.29
  111.1 8.2 %shard_map.337 = (bf16[2,4,384,384]{3,2,1,0:T(8,128)(2,1)S(1)}, bf16[2,4,384,384]{3,2,1,0:T(8,128)(2,1)S(1)}, bf16[197,2304]{1,0:T(8,128)(2,1)S(1)}, f32[197,768]{1,0:T(8,128)S(1)}, f32[4,768]{1,0:T(4,128)S(1)}) custom-call(s32[4]{0:T(128)S(1)} %pad_add_fusion.place_ref.refs_0_, bf16[160,768]{1,0:T(8,128)(2,1)S(1)} %get-tuple-element.197.refs_1_, ...), custom_call_target="tpu_custom_call" | custom-call | flops 8000000000 | bytes 8000000 | tf_op jit(solution)/shard_map/pallas_call | solution.py:517
  122.0 2.1 collective-permute-done.31.came_ref
  125.2 3.7 %collective-permute-done.33.refs_4_ = bf16[1,384,384]{2,1,0:T(8,128)(2,1)S(1)} collective-permute-done((bf16[1,384,384]{2,1,0:T(8,128)(2,1)S(1)}, bf16[1,384,384]{2,1,0:T(8,128)(2,1)S(1)}, u32[]{:S(2)}, u32[]{:S(2)}) %collective-permute-start.33) | collective-permute-done | bytes 294944 | tf_op jit(solution)/shard_map/ppermute | solution.py:1108
  131.0 1.6 collective-permute-start.41
  132.6 1.7 collective-permute-start.35
  136.1 6.3 %collective-permute-done.38 = bf16[2,2,96,384]{3,2,1,0:T(8,128)(2,1)S(1)} collective-permute-done((bf16[2,2,96,384]{3,2,1,0:T(8,128)(2,1)S(1)}, bf16[2,2,96,384]{3,2,1,0:T(8,128)(2,1)S(1)}, u32[]{:S(2)}, u32[]{:S(2)}) %collective-permute-start.38) | collective-permute-done | bytes 294944 | tf_op jit(solution)/shard_map/ppermute | solution.py:1108
  142.5 2.3 %collective-permute-start.42 = (bf16[2,2,96,384]{3,2,1,0:T(8,128)(2,1)S(1)}, bf16[2,2,96,384]{3,2,1,0:T(8,128)(2,1)S(1)}, u32[]{:S(2)}, u32[]{:S(2)}) collective-permute-start(bf16[2,2,96,384]{3,2,1,0:T(8,128)(2,1)S(1)} %pad_maximum_fusion.4), channel_id=1, source_target_pairs={{0,8},{4,12},{8,0},{12,4},{16,24},{20,28},{24,16},{28,20},{1,9},{5... | collective-permute-start | bytes 884744 | tf_op jit(solution)/shard_map/ppermute | solution.py:1108
  144.8 4.4 %shard_map.340 = (bf16[197,768]{1,0:T(8,128)(2,1)}, f32[197,1,768]{2,1,0:T(1,128)}, f32[5,768]{1,0:T(8,128)S(1)}) custom-call(bf16[160,768]{1,0:T(8,128)(2,1)S(1)} %get-tuple-element.223.refs_0_, bf16[160,768]{1,0:T(8,128)(2,1)S(1)} %collective-permute-done.34.refs_1_, bf16[197,2304]{1,0:T(8,128)(2,1)S(1)} %get-tuple-element.225.refs_2_, ...), custom_call_target="tpu_custom_call" | custom-call | flops 50000000 | bytes 50000 | tf_op jit(solution)/shard_map/pallas_call | solution.py:517
  150.7 3.6 %collective-permute-done.42 = bf16[2,2,96,384]{3,2,1,0:T(8,128)(2,1)S(1)} collective-permute-done((bf16[2,2,96,384]{3,2,1,0:T(8,128)(2,1)S(1)}, bf16[2,2,96,384]{3,2,1,0:T(8,128)(2,1)S(1)}, u32[]{:S(2)}, u32[]{:S(2)}) %collective-permute-start.42) | collective-permute-done | bytes 294944 | tf_op jit(solution)/shard_map/ppermute | solution.py:1108
  154.3 1.8 shard_map.342
  156.1 3.8 %collective-permute-done.40.refs_3_ = bf16[2,96,384]{2,1,0:T(8,128)(2,1)S(1)} collective-permute-done((bf16[2,96,384]{2,1,0:T(8,128)(2,1)S(1)}, bf16[2,96,384]{2,1,0:T(8,128)(2,1)S(1)}, u32[]{:S(2)}, u32[]{:S(2)}) %collective-permute-start.40) | collective-permute-done | bytes 147488 | tf_op jit(solution)/shard_map/ppermute | solution.py:1108
  162.9 1.8 collective-permute-start.43
  165.7 1.7 collective-permute-start.45
  167.4 6.1 %collective-permute-done.47 = bf16[2,2,96,384]{3,2,1,0:T(8,128)(2,1)S(1)} collective-permute-done((bf16[2,2,96,384]{3,2,1,0:T(8,128)(2,1)S(1)}, bf16[2,2,96,384]{3,2,1,0:T(8,128)(2,1)S(1)}, u32[]{:S(2)}, u32[]{:S(2)}) %collective-permute-start.47) | collective-permute-done | bytes 294944 | tf_op jit(solution)/shard_map/ppermute | solution.py:1108
  173.6 1.8 shard_map.345
  176.7 1.8 collective-permute-done.45
  178.5 1.7 collective-permute-start.51
  180.4 2.1 collective-permute-start.50
  186.7 3.5 %collective-permute-done.53 = f32[13,768]{1,0:T(8,128)S(1)} collective-permute-done((f32[13,768]{1,0:T(8,128)S(1)}, f32[13,768]{1,0:T(8,128)S(1)}, u32[]{:S(2)}, u32[]{:S(2)}) %collective-permute-start.53) | collective-permute-done | bytes 39968 | tf_op jit(solution)/shard_map/ppermute | solution.py:1110
  191.0 3.4 %collective-permute-done.54.vec_came_ref = f32[13,768]{1,0:T(8,128)S(1)} collective-permute-done((f32[13,768]{1,0:T(8,128)S(1)}, f32[13,768]{1,0:T(8,128)S(1)}, u32[]{:S(2)}, u32[]{:S(2)}) %collective-permute-start.54) | collective-permute-done | bytes 39968 | tf_op jit(solution)/shard_map/ppermute | solution.py:1108
  194.4 2.2 %collective-permute-start.58 = (f32[24,768]{1,0:T(8,128)S(1)}, f32[24,768]{1,0:T(8,128)S(1)}, u32[]{:S(2)}, u32[]{:S(2)}) collective-permute-start(f32[24,768]{1,0:T(8,128)S(1)} %shard_map.348), channel_id=1, source_target_pairs={{0,24},{4,28},{8,16},{12,20},{16,8},{20,12},{24,0},{28,4},{1,25},{... | collective-permute-start | bytes 221192 | tf_op jit(solution)/shard_map/ppermute | solution.py:1108
  196.7 2.2 %collective-permute-start.56 = (f32[24,768]{1,0:T(8,128)S(1)}, f32[24,768]{1,0:T(8,128)S(1)}, u32[]{:S(2)}, u32[]{:S(2)}) collective-permute-start(f32[24,768]{1,0:T(8,128)S(1)} %shard_map.348), channel_id=1, source_target_pairs={{0,8},{4,12},{8,0},{12,4},{16,24},{20,28},{24,16},{28,20},{1,9},{5... | collective-permute-start | bytes 221192 | tf_op jit(solution)/shard_map/ppermute | solution.py:1108
  198.9 2.3 %shard_map.346 = (bf16[4,2,48,384]{3,2,1,0:T(8,128)(2,1)S(1)}, bf16[4,2,48,384]{3,2,1,0:T(8,128)(2,1)S(1)}) custom-call(s32[4]{0:T(128)S(1)} %pad_add_fusion.place_ref.refs_0_, bf16[2,96,384]{2,1,0:T(8,128)(2,1)S(1)} %add_convert_fusion.2.refs_1_, bf16[2,96,384]{2,1,0:T(8,128)(2,1)S(1)} %collective-permute-done.48.refs_2_, ...), custom_call_target="tpu_custom_call" | custom-call | flops 50000000 | bytes 50000 | tf_op jit(solution)/shard_map/pallas_call | solution.py:517
  203.6 1.7 shard_map.350
  205.2 1.7 shard_map.349
  208.0 1.7 shard_map.347
  (143 shorter events, 39.3 us)
Async XLA Ops:
  3.1 18.8 %collective-permute-start.3 = (bf16[6,2,48,384]{3,2,1,0:T(8,128)(2,1)S(1)}, bf16[6,2,48,384]{3,2,1,0:T(8,128)(2,1)S(1)}, u32[]{:S(2)}, u32[]{:S(2)}) collective-permute-start(bf16[6,2,48,384]{3,2,1,0:T(8,128)(2,1)S(1)} %get-tuple-element.161), channel_id=1, source_target_pairs={{0,4},{4,0},{8,12},{12,8},{16,20},{20,16},{24,28},{28,24},{1,5},{5... | collective-permute-start | bytes 1327112 | tf_op jit(solution)/shard_map/ppermute | solution.py:1108
  6.1 8.6 %collective-permute-start.2 = (bf16[4,48,384]{2,1,0:T(8,128)(2,1)S(1)}, bf16[4,48,384]{2,1,0:T(8,128)(2,1)S(1)}, u32[]{:S(2)}, u32[]{:S(2)}) collective-permute-start(bf16[4,48,384]{2,1,0:T(8,128)(2,1)S(1)} %get-tuple-element.164), channel_id=1, source_target_pairs={{0,24},{4,28},{8,16},{12,20},{16,8},{20,12},{24,0},{28,4},{1,25},{... | collective-permute-start | bytes 442376 | tf_op jit(solution)/shard_map/ppermute | solution.py:1108
  9.7 12.2 %collective-permute-start.1 = (bf16[4,48,384]{2,1,0:T(8,128)(2,1)S(1)}, bf16[4,48,384]{2,1,0:T(8,128)(2,1)S(1)}, u32[]{:S(2)}, u32[]{:S(2)}) collective-permute-start(bf16[4,48,384]{2,1,0:T(8,128)(2,1)S(1)} %get-tuple-element.164), channel_id=1, source_target_pairs={{0,16},{4,20},{8,24},{12,28},{16,0},{20,4},{24,8},{28,12},{1,17},{... | collective-permute-start | bytes 442376 | tf_op jit(solution)/shard_map/ppermute | solution.py:1108
  9.7 12.2 %collective-permute-start = (bf16[4,48,384]{2,1,0:T(8,128)(2,1)S(1)}, bf16[4,48,384]{2,1,0:T(8,128)(2,1)S(1)}, u32[]{:S(2)}, u32[]{:S(2)}) collective-permute-start(bf16[4,48,384]{2,1,0:T(8,128)(2,1)S(1)} %get-tuple-element.164), channel_id=1, source_target_pairs={{0,8},{4,12},{8,0},{12,4},{16,24},{20,28},{24,16},{28,20},{1,9},{5... | collective-permute-start | bytes 442376 | tf_op jit(solution)/shard_map/ppermute | solution.py:1108
  22.0 19.1 %collective-permute-start.10 = (bf16[4,4,48,384]{3,2,1,0:T(8,128)(2,1)S(1)}, bf16[4,4,48,384]{3,2,1,0:T(8,128)(2,1)S(1)}, u32[]{:S(2)}, u32[]{:S(2)}) collective-permute-start(bf16[4,4,48,384]{3,2,1,0:T(8,128)(2,1)S(1)} %pad_maximum_fusion.1.refs_1_), channel_id=1, source_target_pairs={{0,6},{1,7},{2,4},{3,5},{4,2},{5,3},{6,0},{7,1},{8,14},{9,15},{10,... | collective-permute-start | bytes 1769480 | tf_op jit(solution)/shard_map/ppermute | solution.py:1112
  23.5 26.4 %collective-permute-start.8 = (bf16[4,4,48,384]{3,2,1,0:T(8,128)(2,1)S(1)}, bf16[4,4,48,384]{3,2,1,0:T(8,128)(2,1)S(1)}, u32[]{:S(2)}, u32[]{:S(2)}) collective-permute-start(bf16[4,4,48,384]{3,2,1,0:T(8,128)(2,1)S(1)} %pad_maximum_fusion.1.refs_1_), channel_id=1, source_target_pairs={{0,2},{1,3},{2,0},{3,1},{4,6},{5,7},{6,4},{7,5},{8,10},{9,11},{10,... | collective-permute-start | bytes 1769480 | tf_op jit(solution)/shard_map/ppermute | solution.py:1110
  24.0 26.0 %collective-permute-start.6 = (bf16[4,4,48,384]{3,2,1,0:T(8,128)(2,1)S(1)}, bf16[4,4,48,384]{3,2,1,0:T(8,128)(2,1)S(1)}, u32[]{:S(2)}, u32[]{:S(2)}) collective-permute-start(bf16[4,4,48,384]{3,2,1,0:T(8,128)(2,1)S(1)} %pad_maximum_fusion.1.refs_1_), channel_id=1, source_target_pairs={{0,4},{4,0},{8,12},{12,8},{16,20},{20,16},{24,28},{28,24},{1,5},{5... | collective-permute-start | bytes 1769480 | tf_op jit(solution)/shard_map/ppermute | solution.py:1108
  25.5 13.9 %collective-permute-start.15 = (bf16[8,48,384]{2,1,0:T(8,128)(2,1)S(1)}, bf16[8,48,384]{2,1,0:T(8,128)(2,1)S(1)}, u32[]{:S(2)}, u32[]{:S(2)}) collective-permute-start(bf16[8,48,384]{2,1,0:T(8,128)(2,1)S(1)} %get-tuple-element.158.feed_ref), channel_id=1, source_target_pairs={{0,16},{4,20},{8,24},{12,28},{16,0},{20,4},{24,8},{28,12},{1,17},{... | collective-permute-start | bytes 884744 | tf_op jit(solution)/shard_map/ppermute | solution.py:1108
  26.2 26.7 %collective-permute-start.4 = (bf16[24,48,384]{2,1,0:T(8,128)(2,1)S(1)}, bf16[24,48,384]{2,1,0:T(8,128)(2,1)S(1)}, u32[]{:S(2)}, u32[]{:S(2)}) collective-permute-start(bf16[24,48,384]{2,1,0:T(8,128)(2,1)S(1)} %get-tuple-element.163), channel_id=1, source_target_pairs={{0,8},{4,12},{8,0},{12,4},{16,24},{20,28},{24,16},{28,20},{1,9},{5... | collective-permute-start | bytes 2654216 | tf_op jit(solution)/shard_map/ppermute | solution.py:1108
  40.9 12.1 %collective-permute-start.5 = (bf16[4,4,48,384]{3,2,1,0:T(8,128)(2,1)S(1)}, bf16[4,4,48,384]{3,2,1,0:T(8,128)(2,1)S(1)}, u32[]{:S(2)}, u32[]{:S(2)}) collective-permute-start(bf16[4,4,48,384]{3,2,1,0:T(8,128)(2,1)S(1)} %pad_maximum_fusion.1.refs_1_), channel_id=1, source_target_pairs={{0,1},{1,0},{2,3},{3,2},{4,5},{5,4},{6,7},{7,6},{8,9},{9,8},{10,11... | collective-permute-start | bytes 1769480 | tf_op jit(solution)/shard_map/ppermute | solution.py:1110
  41.1 14.4 %collective-permute-start.11 = (bf16[4,4,48,384]{3,2,1,0:T(8,128)(2,1)S(1)}, bf16[4,4,48,384]{3,2,1,0:T(8,128)(2,1)S(1)}, u32[]{:S(2)}, u32[]{:S(2)}) collective-permute-start(bf16[4,4,48,384]{3,2,1,0:T(8,128)(2,1)S(1)} %collective-permute-done.10.refs_7_), channel_id=1, source_target_pairs={{0,1},{1,0},{2,3},{3,2},{4,5},{5,4},{6,7},{7,6},{8,9},{9,8},{10,11... | collective-permute-start | bytes 1769480 | tf_op jit(solution)/shard_map/ppermute | solution.py:1110
  50.0 7.5 %collective-permute-start.7 = (bf16[4,4,48,384]{3,2,1,0:T(8,128)(2,1)S(1)}, bf16[4,4,48,384]{3,2,1,0:T(8,128)(2,1)S(1)}, u32[]{:S(2)}, u32[]{:S(2)}) collective-permute-start(bf16[4,4,48,384]{3,2,1,0:T(8,128)(2,1)S(1)} %collective-permute-done.6.refs_3_), channel_id=1, source_target_pairs={{0,1},{1,0},{2,3},{3,2},{4,5},{5,4},{6,7},{7,6},{8,9},{9,8},{10,11... | collective-permute-start | bytes 1769480 | tf_op jit(solution)/shard_map/ppermute | solution.py:1110
  52.9 15.6 %collective-permute-start.16 = (bf16[8,48,384]{2,1,0:T(8,128)(2,1)S(1)}, bf16[8,48,384]{2,1,0:T(8,128)(2,1)S(1)}, u32[]{:S(2)}, u32[]{:S(2)}) collective-permute-start(bf16[8,48,384]{2,1,0:T(8,128)(2,1)S(1)} %collective-permute-done.15), channel_id=1, source_target_pairs={{0,8},{4,12},{8,0},{12,4},{16,24},{20,28},{24,16},{28,20},{1,9},{5... | collective-permute-start | bytes 884744 | tf_op jit(solution)/shard_map/ppermute | solution.py:1108
  53.1 15.4 %collective-permute-start.17 = (bf16[8,48,384]{2,1,0:T(8,128)(2,1)S(1)}, bf16[8,48,384]{2,1,0:T(8,128)(2,1)S(1)}, u32[]{:S(2)}, u32[]{:S(2)}) collective-permute-start(bf16[8,48,384]{2,1,0:T(8,128)(2,1)S(1)} %get-tuple-element.300), channel_id=1, source_target_pairs={{0,16},{4,20},{8,24},{12,28},{16,0},{20,4},{24,8},{28,12},{1,17},{... | collective-permute-start | bytes 884744 | tf_op jit(solution)/shard_map/ppermute | solution.py:1108
  55.5 13.0 %collective-permute-start.13 = (bf16[2,160,768]{2,1,0:T(8,128)(2,1)S(1)}, bf16[2,160,768]{2,1,0:T(8,128)(2,1)S(1)}, u32[]{:S(2)}, u32[]{:S(2)}) collective-permute-start(bf16[2,160,768]{2,1,0:T(8,128)(2,1)S(1)} %pad_maximum_fusion.3.refs_9_), channel_id=1, source_target_pairs={{0,2},{1,3},{2,0},{3,1},{4,6},{5,7},{6,4},{7,5},{8,10},{9,11},{10,... | collective-permute-start | bytes 1474568 | tf_op jit(solution)/shard_map/ppermute | solution.py:1110
  57.1 12.3 %collective-permute-start.14 = (bf16[2,8,48,384]{3,2,1,0:T(8,128)(2,1)S(1)}, bf16[2,8,48,384]{3,2,1,0:T(8,128)(2,1)S(1)}, u32[]{:S(2)}, u32[]{:S(2)}) collective-permute-start(bf16[2,8,48,384]{3,2,1,0:T(8,128)(2,1)S(1)} %pad_maximum_fusion.refs_1_), channel_id=1, source_target_pairs={{0,4},{4,0},{8,12},{12,8},{16,20},{20,16},{24,28},{28,24},{1,5},{5... | collective-permute-start | bytes 1769480 | tf_op jit(solution)/shard_map/ppermute | solution.py:1108
  69.4 13.3 %collective-permute-start.18 = (bf16[2,8,48,384]{3,2,1,0:T(8,128)(2,1)S(1)}, bf16[2,8,48,384]{3,2,1,0:T(8,128)(2,1)S(1)}, u32[]{:S(2)}, u32[]{:S(2)}) collective-permute-start(bf16[2,8,48,384]{3,2,1,0:T(8,128)(2,1)S(1)} %pad_maximum_fusion.2.refs_3_), channel_id=1, source_target_pairs={{0,4},{4,0},{8,12},{12,8},{16,20},{20,16},{24,28},{28,24},{1,5},{5... | collective-permute-start | bytes 1769480 | tf_op jit(solution)/shard_map/ppermute | solution.py:1108
  70.9 11.2 %collective-permute-start.26 = (bf16[8,48,384]{2,1,0:T(8,128)(2,1)S(1)}, bf16[8,48,384]{2,1,0:T(8,128)(2,1)S(1)}, u32[]{:S(2)}, u32[]{:S(2)}) collective-permute-start(bf16[8,48,384]{2,1,0:T(8,128)(2,1)S(1)} %get-tuple-element.299), channel_id=1, source_target_pairs={{0,16},{4,20},{8,24},{12,28},{16,0},{20,4},{24,8},{28,12},{1,17},{... | collective-permute-start | bytes 884744 | tf_op jit(solution)/shard_map/ppermute | solution.py:1108
  71.4 10.8 %collective-permute-start.21 = (bf16[160,768]{1,0:T(8,128)(2,1)S(1)}, bf16[160,768]{1,0:T(8,128)(2,1)S(1)}, u32[]{:S(2)}, u32[]{:S(2)}) collective-permute-start(bf16[160,768]{1,0:T(8,128)(2,1)S(1)} %get-tuple-element.175.refs_5_), channel_id=1, source_target_pairs={{0,3},{1,2},{2,1},{3,0},{4,7},{5,6},{6,5},{7,4},{8,11},{9,10},{10,... | collective-permute-start | bytes 737288 | tf_op jit(solution)/shard_map/ppermute | solution.py:1110
  71.4 11.3 %collective-permute-start.20 = (bf16[160,768]{1,0:T(8,128)(2,1)S(1)}, bf16[160,768]{1,0:T(8,128)(2,1)S(1)}, u32[]{:S(2)}, u32[]{:S(2)}) collective-permute-start(bf16[160,768]{1,0:T(8,128)(2,1)S(1)} %get-tuple-element.175.refs_5_), channel_id=1, source_target_pairs={{0,2},{1,3},{2,0},{3,1},{4,6},{5,7},{6,4},{7,5},{8,10},{9,11},{10,... | collective-permute-start | bytes 737288 | tf_op jit(solution)/shard_map/ppermute | solution.py:1110
  71.7 11.0 %collective-permute-start.19 = (bf16[160,768]{1,0:T(8,128)(2,1)S(1)}, bf16[160,768]{1,0:T(8,128)(2,1)S(1)}, u32[]{:S(2)}, u32[]{:S(2)}) collective-permute-start(bf16[160,768]{1,0:T(8,128)(2,1)S(1)} %get-tuple-element.175.refs_5_), channel_id=1, source_target_pairs={{0,1},{1,0},{2,3},{3,2},{4,5},{5,4},{6,7},{7,6},{8,9},{9,8},{10,11... | collective-permute-start | bytes 737288 | tf_op jit(solution)/shard_map/ppermute | solution.py:1110
  82.1 15.8 %collective-permute-start.27 = (bf16[16,48,384]{2,1,0:T(8,128)(2,1)S(1)}, bf16[16,48,384]{2,1,0:T(8,128)(2,1)S(1)}, u32[]{:S(2)}, u32[]{:S(2)}) collective-permute-start(bf16[16,48,384]{2,1,0:T(8,128)(2,1)S(1)} %constant_dynamic-update-slice_fusion.refs_7_), channel_id=1, source_target_pairs={{0,8},{4,12},{8,0},{12,4},{16,24},{20,28},{24,16},{28,20},{1,9},{5... | collective-permute-start | bytes 1769480 | tf_op jit(solution)/shard_map/ppermute | solution.py:1108
  90.0 16.4 %collective-permute-start.25 = (bf16[2,384,384]{2,1,0:T(8,128)(2,1)S(1)}, bf16[2,384,384]{2,1,0:T(8,128)(2,1)S(1)}, u32[]{:S(2)}, u32[]{:S(2)}) collective-permute-start(bf16[2,384,384]{2,1,0:T(8,128)(2,1)S(1)} %get-tuple-element.189), channel_id=1, source_target_pairs={{0,4},{4,0},{8,12},{12,8},{16,20},{20,16},{24,28},{28,24},{1,5},{5... | collective-permute-start | bytes 1769480 | tf_op jit(solution)/shard_map/ppermute | solution.py:1108
  92.8 8.8 %collective-permute-start.23 = (bf16[160,768]{1,0:T(8,128)(2,1)S(1)}, bf16[160,768]{1,0:T(8,128)(2,1)S(1)}, u32[]{:S(2)}, u32[]{:S(2)}) collective-permute-start(bf16[160,768]{1,0:T(8,128)(2,1)S(1)} %get-tuple-element.185), channel_id=1, source_target_pairs={{0,2},{1,3},{2,0},{3,1},{4,6},{5,7},{6,4},{7,5},{8,10},{9,11},{10,... | collective-permute-start | bytes 737288 | tf_op jit(solution)/shard_map/ppermute | solution.py:1110
  93.4 12.6 %collective-permute-start.24 = (bf16[160,768]{1,0:T(8,128)(2,1)S(1)}, bf16[160,768]{1,0:T(8,128)(2,1)S(1)}, u32[]{:S(2)}, u32[]{:S(2)}) collective-permute-start(bf16[160,768]{1,0:T(8,128)(2,1)S(1)} %get-tuple-element.186), channel_id=1, source_target_pairs={{0,3},{1,2},{2,1},{3,0},{4,7},{5,6},{6,5},{7,4},{8,11},{9,10},{10,... | collective-permute-start | bytes 737288 | tf_op jit(solution)/shard_map/ppermute | solution.py:1110
  107.1 12.2 %collective-permute-start.28 = (bf16[2,2,96,384]{3,2,1,0:T(8,128)(2,1)S(1)}, bf16[2,2,96,384]{3,2,1,0:T(8,128)(2,1)S(1)}, u32[]{:S(2)}, u32[]{:S(2)}) collective-permute-start(bf16[2,2,96,384]{3,2,1,0:T(8,128)(2,1)S(1)} %get-tuple-element.210), channel_id=1, source_target_pairs={{0,8},{4,12},{8,0},{12,4},{16,24},{20,28},{24,16},{28,20},{1,9},{5... | collective-permute-start | bytes 884744 | tf_op jit(solution)/shard_map/ppermute | solution.py:1108
  109.4 9.9 %collective-permute-start.29 = (bf16[1,384,384]{2,1,0:T(8,128)(2,1)S(1)}, bf16[1,384,384]{2,1,0:T(8,128)(2,1)S(1)}, u32[]{:S(2)}, u32[]{:S(2)}) collective-permute-start(bf16[1,384,384]{2,1,0:T(8,128)(2,1)S(1)} %get-tuple-element.211), channel_id=1, source_target_pairs={{0,4},{4,0},{8,12},{12,8},{16,20},{20,16},{24,28},{28,24},{1,5},{5... | collective-permute-start | bytes 884744 | tf_op jit(solution)/shard_map/ppermute | solution.py:1108
  111.1 8.2 %collective-permute-start.30 = (bf16[2,160,768]{2,1,0:T(8,128)(2,1)S(1)}, bf16[2,160,768]{2,1,0:T(8,128)(2,1)S(1)}, u32[]{:S(2)}, u32[]{:S(2)}) collective-permute-start(bf16[2,160,768]{2,1,0:T(8,128)(2,1)S(1)} %get-tuple-element.212), channel_id=1, source_target_pairs={{0,1},{1,0},{2,3},{3,2},{4,5},{5,4},{6,7},{7,6},{8,9},{9,8},{10,11... | collective-permute-start | bytes 1474568 | tf_op jit(solution)/shard_map/ppermute | solution.py:1110
  119.9 9.0 %collective-permute-start.33 = (bf16[1,384,384]{2,1,0:T(8,128)(2,1)S(1)}, bf16[1,384,384]{2,1,0:T(8,128)(2,1)S(1)}, u32[]{:S(2)}, u32[]{:S(2)}) collective-permute-start(bf16[1,384,384]{2,1,0:T(8,128)(2,1)S(1)} %get-tuple-element.220), channel_id=1, source_target_pairs={{0,4},{4,0},{8,12},{12,8},{16,20},{20,16},{24,28},{28,24},{1,5},{5... | collective-permute-start | bytes 884744 | tf_op jit(solution)/shard_map/ppermute | solution.py:1108
  120.3 9.2 %collective-permute-start.32 = (bf16[2,96,384]{2,1,0:T(8,128)(2,1)S(1)}, bf16[2,96,384]{2,1,0:T(8,128)(2,1)S(1)}, u32[]{:S(2)}, u32[]{:S(2)}) collective-permute-start(bf16[2,96,384]{2,1,0:T(8,128)(2,1)S(1)} %get-tuple-element.304), channel_id=1, source_target_pairs={{0,16},{4,20},{8,24},{12,28},{16,0},{20,4},{24,8},{28,12},{1,17},{... | collective-permute-start | bytes 442376 | tf_op jit(solution)/shard_map/ppermute | solution.py:1108
  120.8 8.7 %collective-permute-start.34 = (bf16[160,768]{1,0:T(8,128)(2,1)S(1)}, bf16[160,768]{1,0:T(8,128)(2,1)S(1)}, u32[]{:S(2)}, u32[]{:S(2)}) collective-permute-start(bf16[160,768]{1,0:T(8,128)(2,1)S(1)} %get-tuple-element.297), channel_id=1, source_target_pairs={{0,2},{1,3},{2,0},{3,1},{4,6},{5,7},{6,4},{7,5},{8,10},{9,11},{10,... | collective-permute-start | bytes 737288 | tf_op jit(solution)/shard_map/ppermute | solution.py:1110
  130.2 12.2 %collective-permute-start.38 = (bf16[2,2,96,384]{3,2,1,0:T(8,128)(2,1)S(1)}, bf16[2,2,96,384]{3,2,1,0:T(8,128)(2,1)S(1)}, u32[]{:S(2)}, u32[]{:S(2)}) collective-permute-start(bf16[2,2,96,384]{3,2,1,0:T(8,128)(2,1)S(1)} %get-tuple-element.237), channel_id=1, source_target_pairs={{0,8},{4,12},{8,0},{12,4},{16,24},{20,28},{24,16},{28,20},{1,9},{5... | collective-permute-start | bytes 884744 | tf_op jit(solution)/shard_map/ppermute | solution.py:1108
  131.0 11.5 %collective-permute-start.41 = (bf16[2,96,384]{2,1,0:T(8,128)(2,1)S(1)}, bf16[2,96,384]{2,1,0:T(8,128)(2,1)S(1)}, u32[]{:S(2)}, u32[]{:S(2)}) collective-permute-start(bf16[2,96,384]{2,1,0:T(8,128)(2,1)S(1)} %add_convert_fusion.3.refs_1_), channel_id=1, source_target_pairs={{0,16},{4,20},{8,24},{12,28},{16,0},{20,4},{24,8},{28,12},{1,17},{... | collective-permute-start | bytes 442376 | tf_op jit(solution)/shard_map/ppermute | solution.py:1108
  132.6 27.4 %collective-permute-start.35 = (bf16[2,384,384]{2,1,0:T(8,128)(2,1)S(1)}, bf16[2,384,384]{2,1,0:T(8,128)(2,1)S(1)}, u32[]{:S(2)}, u32[]{:S(2)}) collective-permute-start(bf16[2,384,384]{2,1,0:T(8,128)(2,1)S(1)} %get-tuple-element.230), channel_id=1, source_target_pairs={{0,4},{4,0},{8,12},{12,8},{16,20},{20,16},{24,28},{28,24},{1,5},{5... | collective-permute-start | bytes 1769480 | tf_op jit(solution)/shard_map/ppermute | solution.py:1108
  134.3 27.1 %collective-permute-start.36 = (bf16[2,384,384]{2,1,0:T(8,128)(2,1)S(1)}, bf16[2,384,384]{2,1,0:T(8,128)(2,1)S(1)}, u32[]{:S(2)}, u32[]{:S(2)}) collective-permute-start(bf16[2,384,384]{2,1,0:T(8,128)(2,1)S(1)} %get-tuple-element.231), channel_id=1, source_target_pairs={{0,2},{1,3},{2,0},{3,1},{4,6},{5,7},{6,4},{7,5},{8,10},{9,11},{10,... | collective-permute-start | bytes 1769480 | tf_op jit(solution)/shard_map/ppermute | solution.py:1110
  134.9 26.5 %collective-permute-start.37 = (bf16[2,384,384]{2,1,0:T(8,128)(2,1)S(1)}, bf16[2,384,384]{2,1,0:T(8,128)(2,1)S(1)}, u32[]{:S(2)}, u32[]{:S(2)}) collective-permute-start(bf16[2,384,384]{2,1,0:T(8,128)(2,1)S(1)} %get-tuple-element.232), channel_id=1, source_target_pairs={{0,6},{1,7},{2,4},{3,5},{4,2},{5,3},{6,0},{7,1},{8,14},{9,15},{10,... | collective-permute-start | bytes 1769480 | tf_op jit(solution)/shard_map/ppermute | solution.py:1112
  142.4 8.1 %collective-permute-start.39 = (bf16[2,96,384]{2,1,0:T(8,128)(2,1)S(1)}, bf16[2,96,384]{2,1,0:T(8,128)(2,1)S(1)}, u32[]{:S(2)}, u32[]{:S(2)}) collective-permute-start(bf16[2,96,384]{2,1,0:T(8,128)(2,1)S(1)} %fusion.6), channel_id=1, source_target_pairs={{0,16},{4,20},{8,24},{12,28},{16,0},{20,4},{24,8},{28,12},{1,17},{... | collective-permute-start | bytes 442376 | tf_op jit(solution)/shard_map/ppermute | solution.py:1108
  142.5 11.8 %collective-permute-start.42 = (bf16[2,2,96,384]{3,2,1,0:T(8,128)(2,1)S(1)}, bf16[2,2,96,384]{3,2,1,0:T(8,128)(2,1)S(1)}, u32[]{:S(2)}, u32[]{:S(2)}) collective-permute-start(bf16[2,2,96,384]{3,2,1,0:T(8,128)(2,1)S(1)} %pad_maximum_fusion.4), channel_id=1, source_target_pairs={{0,8},{4,12},{8,0},{12,4},{16,24},{20,28},{24,16},{28,20},{1,9},{5... | collective-permute-start | bytes 884744 | tf_op jit(solution)/shard_map/ppermute | solution.py:1108
  150.6 9.4 %collective-permute-start.40 = (bf16[2,96,384]{2,1,0:T(8,128)(2,1)S(1)}, bf16[2,96,384]{2,1,0:T(8,128)(2,1)S(1)}, u32[]{:S(2)}, u32[]{:S(2)}) collective-permute-start(bf16[2,96,384]{2,1,0:T(8,128)(2,1)S(1)} %fusion.refs_1_), channel_id=1, source_target_pairs={{0,16},{4,20},{8,24},{12,28},{16,0},{20,4},{24,8},{28,12},{1,17},{... | collective-permute-start | bytes 442376 | tf_op jit(solution)/shard_map/ppermute | solution.py:1108
  161.4 12.1 %collective-permute-start.47 = (bf16[2,2,96,384]{3,2,1,0:T(8,128)(2,1)S(1)}, bf16[2,2,96,384]{3,2,1,0:T(8,128)(2,1)S(1)}, u32[]{:S(2)}, u32[]{:S(2)}) collective-permute-start(bf16[2,2,96,384]{3,2,1,0:T(8,128)(2,1)S(1)} %pad_maximum_fusion.5), channel_id=1, source_target_pairs={{0,8},{4,12},{8,0},{12,4},{16,24},{20,28},{24,16},{28,20},{1,9},{5... | collective-permute-start | bytes 884744 | tf_op jit(solution)/shard_map/ppermute | solution.py:1108
  161.8 16.7 %collective-permute-start.46 = (bf16[5,2,48,384]{3,2,1,0:T(8,128)(2,1)S(1)}, bf16[5,2,48,384]{3,2,1,0:T(8,128)(2,1)S(1)}, u32[]{:S(2)}, u32[]{:S(2)}) collective-permute-start(bf16[5,2,48,384]{3,2,1,0:T(8,128)(2,1)S(1)} %get-tuple-element.256), channel_id=1, source_target_pairs={{0,4},{4,0},{8,12},{12,8},{16,20},{20,16},{24,28},{28,24},{1,5},{5... | collective-permute-start | bytes 1105928 | tf_op jit(solution)/shard_map/ppermute | solution.py:1108
  162.9 13.8 %collective-permute-start.43 = (bf16[2,96,384]{2,1,0:T(8,128)(2,1)S(1)}, bf16[2,96,384]{2,1,0:T(8,128)(2,1)S(1)}, u32[]{:S(2)}, u32[]{:S(2)}) collective-permute-start(bf16[2,96,384]{2,1,0:T(8,128)(2,1)S(1)} %get-tuple-element.253), channel_id=1, source_target_pairs={{0,8},{4,12},{8,0},{12,4},{16,24},{20,28},{24,16},{28,20},{1,9},{5... | collective-permute-start | bytes 442376 | tf_op jit(solution)/shard_map/ppermute | solution.py:1108
  164.7 12.0 %collective-permute-start.44 = (bf16[2,96,384]{2,1,0:T(8,128)(2,1)S(1)}, bf16[2,96,384]{2,1,0:T(8,128)(2,1)S(1)}, u32[]{:S(2)}, u32[]{:S(2)}) collective-permute-start(bf16[2,96,384]{2,1,0:T(8,128)(2,1)S(1)} %get-tuple-element.254), channel_id=1, source_target_pairs={{0,16},{4,20},{8,24},{12,28},{16,0},{20,4},{24,8},{28,12},{1,17},{... | collective-permute-start | bytes 442376 | tf_op jit(solution)/shard_map/ppermute | solution.py:1108
  165.7 12.8 %collective-permute-start.45 = (bf16[2,96,384]{2,1,0:T(8,128)(2,1)S(1)}, bf16[2,96,384]{2,1,0:T(8,128)(2,1)S(1)}, u32[]{:S(2)}, u32[]{:S(2)}) collective-permute-start(bf16[2,96,384]{2,1,0:T(8,128)(2,1)S(1)} %get-tuple-element.255), channel_id=1, source_target_pairs={{0,24},{4,28},{8,16},{12,20},{16,8},{20,12},{24,0},{28,4},{1,25},{... | collective-permute-start | bytes 442376 | tf_op jit(solution)/shard_map/ppermute | solution.py:1108
  178.5 15.9 %collective-permute-start.51 = (bf16[5,2,48,384]{3,2,1,0:T(8,128)(2,1)S(1)}, bf16[5,2,48,384]{3,2,1,0:T(8,128)(2,1)S(1)}, u32[]{:S(2)}, u32[]{:S(2)}) collective-permute-start(bf16[5,2,48,384]{3,2,1,0:T(8,128)(2,1)S(1)} %get-tuple-element.265), channel_id=1, source_target_pairs={{0,4},{4,0},{8,12},{12,8},{16,20},{20,16},{24,28},{28,24},{1,5},{5... | collective-permute-start | bytes 1105928 | tf_op jit(solution)/shard_map/ppermute | solution.py:1108
  180.4 14.0 %collective-permute-start.50 = (bf16[2,96,384]{2,1,0:T(8,128)(2,1)S(1)}, bf16[2,96,384]{2,1,0:T(8,128)(2,1)S(1)}, u32[]{:S(2)}, u32[]{:S(2)}) collective-permute-start(bf16[2,96,384]{2,1,0:T(8,128)(2,1)S(1)} %add_convert_fusion.2.refs_1_), channel_id=1, source_target_pairs={{0,24},{4,28},{8,16},{12,20},{16,8},{20,12},{24,0},{28,4},{1,25},{... | collective-permute-start | bytes 442376 | tf_op jit(solution)/shard_map/ppermute | solution.py:1108
  182.4 12.0 %collective-permute-start.49 = (bf16[2,96,384]{2,1,0:T(8,128)(2,1)S(1)}, bf16[2,96,384]{2,1,0:T(8,128)(2,1)S(1)}, u32[]{:S(2)}, u32[]{:S(2)}) collective-permute-start(bf16[2,96,384]{2,1,0:T(8,128)(2,1)S(1)} %add_convert_fusion.2.refs_1_), channel_id=1, source_target_pairs={{0,16},{4,20},{8,24},{12,28},{16,0},{20,4},{24,8},{28,12},{1,17},{... | collective-permute-start | bytes 442376 | tf_op jit(solution)/shard_map/ppermute | solution.py:1108
  183.5 10.9 %collective-permute-start.48 = (bf16[2,96,384]{2,1,0:T(8,128)(2,1)S(1)}, bf16[2,96,384]{2,1,0:T(8,128)(2,1)S(1)}, u32[]{:S(2)}, u32[]{:S(2)}) collective-permute-start(bf16[2,96,384]{2,1,0:T(8,128)(2,1)S(1)} %add_convert_fusion.2.refs_1_), channel_id=1, source_target_pairs={{0,8},{4,12},{8,0},{12,4},{16,24},{20,28},{24,16},{28,20},{1,9},{5... | collective-permute-start | bytes 442376 | tf_op jit(solution)/shard_map/ppermute | solution.py:1108
  (24 other events, 291.6 us)

commit v5 on v4

--- a/solution.py
+++ b/solution.py
@@ -11,6 +11,7 @@
 BLOCK_VEC = 128
 KEPT_MOST = 157
 SLOTS = 160
+TILE = 256
 PAIR = 2
 
 highest = lax.Precision.HIGHEST
@@ -506,7 +507,7 @@
     return jax.ShapeDtypeStruct(dims, kind)
 
 
-def local_call(kernel, args, outs, scratch=(), in_hbm=(), out_hbm=(), in_smem=(0,), mib=12, micros=0.05):
+def local_call(kernel, args, outs, scratch=(), in_hbm=(), out_hbm=(), in_smem=(0,), mib=20, micros=0.05):
     def place_of(index, hbm, smem):
         if index in hbm:
             return pl.BlockSpec(memory_space=pltpu.HBM)
@@ -571,36 +572,45 @@
         copy.wait()
 
 
+def matrix_of(weights, kind, row_blocks):
+    blocks = weights[kind * row_blocks : (kind + 1) * row_blocks]
+    return blocks.reshape(row_blocks * blocks.shape[1], blocks.shape[2])
+
+
 def forward_kernel(order, pieces, place_ref, *refs):
     piece_refs, refs = refs[: len(pieces)], refs[len(pieces) :]
     normed_ref, tok_ref, mask_ref, chosen_ref, vec_ref = refs[:5]
     rows_ref, qkv_ref, probs_ref, attended_ref, branch_ref, weights_hbm = refs[5:11]
     weights, probs_all, sems, out_sem, probs_sems = refs[11:]
     z, x, m = place_ref[0], place_ref[1], place_ref[2]
-    local, piece = piece_refs[0].shape[1], piece_refs[0].shape[2]
+    piece = piece_refs[0].shape[2]
+    width = normed_ref.shape[1]
+    row_blocks = width // order
     copies = []
     for ref, (slots, dx, dm) in zip(piece_refs, pieces):
         for index, slot in enumerate(slots):
             row = pl.multiple_of(((z ^ slot) * PAIR + (x ^ dx)) * piece, 16)
-            target = weights.at[pl.ds((m ^ dm) * local, local), pl.ds(row, piece), :]
-            copies.append(pltpu.make_async_copy(ref.at[index], target, sems.at[len(copies)]))
+            for col in range(row_blocks):
+                target = weights.at[
+                    pl.ds((m ^ dm) * row_blocks, row_blocks),
+                    pl.ds(row, piece),
+                    pl.ds(col * order, order),
+                ]
+                source = ref.at[index, pl.ds(col * row_blocks, row_blocks)]
+                copies.append(pltpu.make_async_copy(source, target, sems.at[len(copies)]))
     copy_all(copies)
     keep_whole = pltpu.make_async_copy(weights, weights_hbm, out_sem)
     keep_whole.start()
-    width = normed_ref.shape[1]
-    row_blocks = width // order
     normed = normed_ref[...]
-    for col in range(3 * row_blocks):
-        part = jnp.zeros((normed.shape[0], order), full)
-        for row in range(row_blocks):
-            part = part + dot32(
-                normed[:, row * order : (row + 1) * order], weights[col * row_blocks + row]
-            )
-        kind, start = col // row_blocks, (col % row_blocks) * order
-        if kind != 1:
-            bias_row = 4 if kind == 0 else 5
-            part = part + vec_ref[bias_row : bias_row + 1, start : start + order]
-        qkv_ref[:, col * order : (col + 1) * order] = to_half(part)
+    for kind in range(3):
+        matrix = matrix_of(weights, kind, row_blocks)
+        for start in range(0, width, TILE):
+            lanes = slice(start, start + TILE)
+            part = dot32(normed, matrix[:, lanes])
+            if kind != 1:
+                bias_row = 4 if kind == 0 else 5
+                part = part + vec_ref[bias_row : bias_row + 1, lanes]
+            qkv_ref[:, kind * width + start : kind * width + start + TILE] = to_half(part)
     keep_probs = []
     head = width // HEADS
     scale = head ** (-0.5)
@@ -626,15 +636,10 @@
         )
         keep_probs[-1].start()
     attended = attended_ref[...]
-    for col in range(row_blocks):
-        part = jnp.zeros((normed.shape[0], order), full)
-        for row in range(row_blocks):
-            part = part + dot32(
-                attended[:, row * order : (row + 1) * order],
-                weights[(3 * row_blocks + col) * row_blocks + row],
-            )
-        lanes = slice(col * order, (col + 1) * order)
-        branch_ref[:, lanes] = part + vec_ref[6:7, lanes]
+    matrix = matrix_of(weights, 3, row_blocks)
+    for start in range(0, width, TILE):
+        lanes = slice(start, start + TILE)
+        branch_ref[:, lanes] = dot32(attended, matrix[:, lanes]) + vec_ref[6:7, lanes]
     hat, _ = normalized(tok_ref[...].astype(full) + branch_ref[...])
     second = to_half(hat * vec_ref[2:3, :] + vec_ref[3:4, :])
     rows_ref[...] = to_half(dot32(chosen_ref[...], second))
@@ -661,17 +666,28 @@
     vec_ref = refs[0]
     back_refs, refs = refs[1 : 1 + group], refs[1 + group :]
     rows_ref, grads_ref, active_ref, hidden_ref, down_hbm = refs[:5]
-    weights, sems, out_sem = refs[5:]
+    up, down, sems, out_sem = refs[5:]
     z, x, m = place_ref[0], place_ref[1], place_ref[2]
     piece = piece_refs[0].shape[2]
-    local = weights.shape[0] // 2
+    width = rows_ref.shape[1]
+    row_blocks = width // order
+    col_blocks = active_ref.shape[1] // order
+    local = row_blocks * col_blocks
     bias = jnp.sum(bias_row(m, vec_ref[9:, :], vec_ref.shape[0] - 9), axis=0, keepdims=True)
     copies = []
     for ref, (slots, dx) in zip(piece_refs, pieces):
         for index, slot in enumerate(slots):
             row = pl.multiple_of(((z ^ slot) * PAIR + (x ^ dx)) * piece, 16)
-            target = weights.at[:, pl.ds(row, piece), :]
-            copies.append(pltpu.make_async_copy(ref.at[index], target, sems.at[len(copies)]))
+            span = pl.ds(row, piece)
+            for col in range(col_blocks):
+                lanes = pl.ds(col * order, order)
+                source = ref.at[index, pl.ds(col * row_blocks, row_blocks)]
+                pairs = [(source, up.at[:, span, lanes])]
+                for other in range(row_blocks):
+                    source = ref.at[index, local + col * row_blocks + other]
+                    pairs.append((source, down.at[col, span, pl.ds(other * order, order)]))
+                for source, target in pairs:
+                    copies.append(pltpu.make_async_copy(source, target, sems.at[len(copies)]))
     for copy in copies:
         copy.start()
     count = row_refs[0].shape[0]
@@ -680,37 +696,22 @@
         grads_ref[index * count : (index + 1) * count, :] = grad_refs[index // PAIR][index % PAIR]
     for copy in copies:
         copy.wait()
-    local = weights.shape[0] // 2
-    keep_down = pltpu.make_async_copy(weights.at[pl.ds(local, local)], down_hbm, out_sem)
+    keep_down = pltpu.make_async_copy(down, down_hbm, out_sem)
     keep_down.start()
-    row_blocks = rows_ref.shape[1] // order
-    for col in range(local // row_blocks):
-        lanes = slice(col * order, (col + 1) * order)
-        hidden = bias[:, lanes]
-        for row in range(row_blocks):
-            hidden = hidden + dot32(
-                rows_ref[:, row * order : (row + 1) * order], weights[col * row_blocks + row]
-            )
+    up_matrix = matrix_of(up, 0, row_blocks)
+    down_matrix = matrix_of(down, 0, col_blocks)
+    for start in range(0, active_ref.shape[1], TILE):
+        lanes = slice(start, start + TILE)
+        hidden = dot32(rows_ref[...], up_matrix[:, lanes]) + bias[:, lanes]
         active, slope = gelu_parts(hidden)
         active_ref[:, lanes] = to_half(active)
-        grad = jnp.zeros_like(slope)
-        for row in range(row_blocks):
-            grad = grad + times_transpose(
-                grads_ref[:, row * order : (row + 1) * order],
-                weights[local + col * row_blocks + row],
-            )
+        grad = times_transpose(grads_ref[...], down_matrix[lanes, :])
         hidden_ref[:, lanes] = to_half(grad * slope)
-    for row in range(row_blocks):
-        total = None
-        for col in range(local // row_blocks):
-            part = times_transpose(
-                hidden_ref[:, col * order : (col + 1) * order], weights[col * row_blocks + row]
-            )
-            total = part if total is None else total + part
+    for start in range(0, width, TILE):
+        lanes = slice(start, start + TILE)
+        total = times_transpose(hidden_ref[...], up_matrix[lanes, :])
         for index in range(group):
-            back_refs[index][:, row * order : (row + 1) * order] = to_half(
-                total[index * count : (index + 1) * count, :]
-            )
+            back_refs[index][:, lanes] = to_half(total[index * count : (index + 1) * count, :])
     keep_down.wait()
 
 
@@ -722,44 +723,34 @@
         ref[...] = blocks[pl.ds((1 - x) * own + index * count, count)]
 
 
-def up_grads_kernel(order, place_ref, rows_ref, hidden_ref, kept_ref, sent_ref, bias_ref, blocks):
-    row_blocks = rows_ref.shape[1] // order
-    for col in range(blocks.shape[0] // row_blocks):
-        lanes = slice(col * order, (col + 1) * order)
-        for row in range(row_blocks):
-            others = slice(row * order, (row + 1) * order)
-            blocks[col * row_blocks + row] = to_half(
-                row_product(rows_ref[:, others], hidden_ref[:, lanes])
+def store_blocks(blocks, order, product, by_rows):
+    rows, cols = product.shape[0] // order, product.shape[1] // order
+    for row in range(rows):
+        for col in range(cols):
+            at = row * cols + col if by_rows else col * rows + row
+            blocks[at] = to_half(
+                product[row * order : (row + 1) * order, col * order : (col + 1) * order]
             )
+
+
+def up_grads_kernel(order, place_ref, rows_ref, hidden_ref, kept_ref, sent_ref, blocks):
+    store_blocks(blocks, order, row_product(rows_ref[...], hidden_ref[...]), False)
     share_blocks(place_ref, blocks, kept_ref, sent_ref)
-    bias_ref[...] = col_sum(hidden_ref[...].astype(full))
-
-
-def down_grads_kernel(order, group, place_ref, grads_ref, active_ref, down_ref, *refs):
-    feed_kept_ref, feed_sent_ref, kept_ref, first_ref, second_ref, blocks = refs
+
+
+def down_grads_kernel(order, group, place_ref, grads_ref, active_ref, hidden_ref, down_ref, *refs):
+    feed_kept_ref, feed_sent_ref, kept_ref, first_ref, second_ref, bias_ref, blocks = refs
     count = grads_ref.shape[0] // group
-    row_blocks = grads_ref.shape[1] // order
-    col_blocks = down_ref.shape[0] // row_blocks
-    for row in range(row_blocks):
-        total = None
-        for col in range(col_blocks):
-            part = dot32(
-                active_ref[:, col * order : (col + 1) * order], down_ref[col * row_blocks + row]
-            )
-            total = part if total is None else total + part
+    down_matrix = matrix_of(down_ref, 0, down_ref.shape[0])
+    for start in range(0, down_matrix.shape[1], TILE):
+        lanes = slice(start, start + TILE)
+        total = dot32(active_ref[...], down_matrix[:, lanes])
         for index in range(group):
             target = (feed_kept_ref, feed_sent_ref)[index % PAIR]
-            target[index // PAIR, :, row * order : (row + 1) * order] = to_half(
-                total[index * count : (index + 1) * count, :]
-            )
-    for col in range(col_blocks):
-        lanes = slice(col * order, (col + 1) * order)
-        for row in range(row_blocks):
-            others = slice(row * order, (row + 1) * order)
-            blocks[col * row_blocks + row] = to_half(
-                row_product(active_ref[:, lanes], grads_ref[:, others])
-            )
+            target[index // PAIR, :, lanes] = to_half(total[index * count : (index + 1) * count, :])
+    store_blocks(blocks, order, row_product(active_ref[...], grads_ref[...]), True)
     share_blocks(place_ref, blocks, kept_ref, first_ref, second_ref)
+    bias_ref[...] = col_sum(hidden_ref[...].astype(full))
 
 
 def backward_kernel(order, group, place_ref, *refs):
@@ -770,8 +761,9 @@
     weights, left, right, grad_attended, probs_all, sem, probs_sem = refs[15:]
     width = tok_ref.shape[1]
     row_blocks = width // order
-    local = weights.shape[0]
-    fetch = pltpu.make_async_copy(weights_hbm.at[pl.ds(3 * local, local)], weights, sem)
+    fetch = pltpu.make_async_copy(
+        weights_hbm.at[pl.ds(3 * row_blocks, row_blocks)], weights, sem
+    )
     fetch.start()
     fetch_probs = pltpu.make_async_copy(probs_ref, probs_all, probs_sem)
     fetch_probs.start()
@@ -796,14 +788,10 @@
     left[1] = attended_ref[...]
     right[3] = grad_branch
     fetch.wait()
-    for row in range(row_blocks):
-        total = None
-        for col in range(row_blocks):
-            part = times_transpose(
-                grad_branch[:, col * order : (col + 1) * order], weights[col * row_blocks + row]
-            )
-            total = part if total is None else total + part
-        grad_attended[:, row * order : (row + 1) * order] = to_half(total)
+    matrix = matrix_of(weights, 0, row_blocks)
+    for start in range(0, width, TILE):
+        lanes = slice(start, start + TILE)
+        grad_attended[:, lanes] = to_half(times_transpose(grad_branch, matrix[lanes, :]))
     fetch_probs.wait()
     head = width // HEADS
     factor = head ** (-0.5)
@@ -835,16 +823,8 @@
     for high_part in range(kept_ref.shape[0]):
         for target, low_part in ((kept_ref, core), (sent_ref, 1 - core)):
             kind = high_part * PAIR + low_part
-            rows = left[kind // 3]
-            cols = right[kind]
-            for col in range(row_blocks):
-                for row in range(row_blocks):
-                    target[high_part, col * row_blocks + row] = to_half(
-                        row_product(
-                            rows[:, row * order : (row + 1) * order],
-                            cols[:, col * order : (col + 1) * order],
-                        )
-                    )
+            product = row_product(left[kind // 3], right[kind])
+            store_blocks(target.at[high_part], order, product, False)
 
 
 def input_kernel(order, group, *refs):
@@ -876,16 +856,12 @@
     sums_ref[3:4, :] = col_sum(mixed_ref[:, 2 * width :].astype(full))
     hat, scale = normalized(tokens)
     fetch.wait()
-    parts = []
-    for row in range(row_blocks):
-        total = None
-        for col in range(3 * row_blocks):
-            part = times_transpose(
-                mixed_ref[:, col * order : (col + 1) * order], weights[col * row_blocks + row]
-            )
-            total = part if total is None else total + part
-        parts.append(total)
-    grad_normed = jnp.concatenate(parts, axis=1)
+    grad_normed = None
+    for kind in range(3):
+        part = times_transpose(
+            mixed_ref[:, kind * width : (kind + 1) * width], matrix_of(weights, kind, row_blocks)
+        )
+        grad_normed = part if grad_normed is None else grad_normed + part
     sums_ref[0:1, :] = col_sum(grad_normed * hat)
     sums_ref[1:2, :] = col_sum(grad_normed)
     grad = base + norm_back(grad_normed * vec_ref[0:1, :], hat, scale)
@@ -1234,12 +1210,12 @@
             shape(heads, full),
             shape((rows, width)),
             shape((rows, width), full),
-            shape((group * local, order, order)),
+            shape((group * row_blocks, order, width)),
         ),
         scratch=(
-            pltpu.VMEM((group * local, order, order), half),
+            pltpu.VMEM((group * row_blocks, order, width), half),
             pltpu.VMEM(heads, full),
-            pltpu.SemaphoreType.DMA((count * z_count,)),
+            pltpu.SemaphoreType.DMA((count * z_count * row_blocks,)),
             pltpu.SemaphoreType.DMA(()),
             pltpu.SemaphoreType.DMA((HEADS // 2,)),
         ),
@@ -1247,8 +1223,8 @@
         out_hbm=(2, 5),
         micros=8,
     )
-    rows_sent, group_grads, feed_near_came, feed_last, roots_first_far = phase(
-        rows_sent, group_grads, feed_near_came, feed_last, roots_first_far
+    rows_sent, group_grads, feed_last, roots_first_far = phase(
+        rows_sent, group_grads, feed_last, roots_first_far
     )
 
     group_rows = [rows_sent] + [move(rows_sent, 0, k) for k in others]
@@ -1264,10 +1240,11 @@
         (shape((SLOTS, width)),) * group
         + (shape((total_rows, width)),) * 2
         + (shape((total_rows, hidden_width)),) * 2
-        + (shape((local, order, order)),),
+        + (shape((local // row_blocks, order, width)),),
         scratch=(
-            pltpu.VMEM((2 * local, order, order), half),
-            pltpu.SemaphoreType.DMA((PAIR * z_count,)),
+            pltpu.VMEM((row_blocks, order, hidden_width), half),
+            pltpu.VMEM((local // row_blocks, order, width), half),
+            pltpu.SemaphoreType.DMA((PAIR * z_count * (local // row_blocks + local),)),
             pltpu.SemaphoreType.DMA(()),
         ),
         in_hbm=(1, 2, 3, 4),
@@ -1281,23 +1258,24 @@
     roots_far = jnp.concatenate([roots_first_far, roots_second_far])
     roots_last = move(roots_far, PAIR, 0)
     all_roots = [roots, roots_near, roots_far, roots_last]
-    up_kept, up_sent, bias_sums = local_call(
+    up_kept, up_sent = local_call(
         lambda *refs: up_grads_kernel(order, *refs),
         (place, all_rows, grad_hidden),
-        (shape((own, order, order)),) * 2 + (shape((1, hidden_width), full),),
+        (shape((own, order, order)),) * 2,
         scratch=(pltpu.VMEM((local, order, order), half),),
     )
     up_came = move(up_sent, 1, 0)
-    feed_kept, feed_sent, down_kept, down_first, down_second = local_call(
+    feed_kept, feed_sent, down_kept, down_first, down_second, bias_sums = local_call(
         lambda *refs: down_grads_kernel(order, group, *refs),
-        (place, all_grads, active, down),
+        (place, all_grads, active, grad_hidden, down),
         (shape((group // PAIR, SLOTS, width)),) * 2
         + (shape((own, order, order)),)
-        + (shape((own // 2, order, order)),) * 2,
+        + (shape((own // 2, order, order)),) * 2
+        + (shape((1, hidden_width), full),),
         scratch=(pltpu.VMEM((local, order, order), half),),
     )
-    back, up_came, down_first, down_second, feed_sent, all_roots = phase(
-        back, up_came, down_first, down_second, feed_sent, all_roots
+    back, down_first, down_second, feed_sent, all_roots = phase(
+        back, down_first, down_second, feed_sent, all_roots
     )
 
     def rows_of(*groups):
@@ -1359,7 +1337,7 @@
             shape((4, width), full),
         ),
         scratch=(
-            pltpu.VMEM((local, order, order), half),
+            pltpu.VMEM((row_blocks, order, width), half),
             pltpu.VMEM((2, rows, width), half),
             pltpu.VMEM((4, rows, width), half),
             pltpu.VMEM((rows, width), half),
@@ -1390,8 +1368,8 @@
         (place, attn_kept, attn_came),
         (shape((own, order, order)),) * group,
     )
-    core_parts, up_far, up_mine, down_second_came, feed = phase(
-        core_parts, up_far, up_mine, down_second_came, feed
+    core_parts, up_mine, down_second_came, feed = phase(
+        core_parts, up_mine, down_second_came, feed
     )
 
     attn_came = [move(part, dx, dm) for (dx, dm), part in zip(plane[1:], core_parts[1:])]
@@ -1411,7 +1389,7 @@
             shape((5, width), full),
         ),
         scratch=(
-            pltpu.VMEM((3 * local, order, order), half),
+            pltpu.VMEM((3 * row_blocks, order, width), half),
             pltpu.SemaphoreType.DMA(()),
         ),
         in_hbm=(group // PAIR + 7,),

time: 210 us -> 204 us (0.971)
  waiting for transfers between devices: 93.5 us -> 88.3 us
  Pallas kernels: 53 us -> 49.5 us
  starting transfers between devices: 60.7 us -> 63.4 us
    ppermute x38, waiting for transfers between devices: 66.6 us -> 62.3 us  [move(): return lax.ppermute(values, 'dp', [(s, s ^ dp_mask) for s in range(dp)])]
    pallas_call x22, Pallas kernels: 53 us -> 49.5 us  [local_call(): pl.pallas_call(kernel, out_shape=list(outs), in_specs=[place_of(i, in_hbm...]
  transfers between devices with their start and end apart: 59 -> 59, of which waited for: 29 -> 28; matrix products, arithmetic and copies ran while one was open for 0% -> 1% of each run, Pallas kernels for 23% -> 22%
where the time goes in v5:
time: 204 us
  waiting for transfers between devices  88.3 us (43%)
  starting transfers between devices  63.4 us (31%)
  Pallas kernels  49.5 us (24%)
    ppermute x38, waiting for transfers between devices, move(): return lax.ppermute(values, 'dp', [(s, s ^ dp_mask) for s in range(dp)])  62.3 us
    ppermute x38, starting transfers between devices, move(): return lax.ppermute(values, 'dp', [(s, s ^ dp_mask) for s in range(dp)])  49.8 us
    pallas_call x22, Pallas kernels, local_call(): pl.pallas_call(kernel, out_shape=list(outs), in_specs=[place_of(i, in_hbm...  49.5 us
    ppermute x19, waiting for transfers between devices, move(): return lax.ppermute(values, 'mp', [(s, s ^ mp_mask) for s in range(mp)])  26 us
    ppermute x19, starting transfers between devices, move(): return lax.ppermute(values, 'mp', [(s, s ^ mp_mask) for s in range(mp)])  11.7 us
  transfers between devices with their start and end apart: 59, of which 28 were waited for; matrix products, arithmetic and copies ran while one was open for 1% of the time, Pallas kernels for 22%

profile of v5, /device:TPU:0, one launch (start us, length us, event | category | flops | bytes accessed | tf_op | source)
XLA Modules:
  0.0 203.7 jit_solution(4724396857899407214)
XLA Ops:
  0.8 2.3 %shard_map.330 = (bf16[4,48,384]{2,1,0:T(8,128)(2,1)S(1)}, bf16[8,48,384]{2,1,0:T(8,128)(2,1)S(1)}, bf16[6,2,48,384]{3,2,1,0:T(8,128)(2,1)S(1)}, bf16[6,2,48,384]{3,2,1,0:T(8,128)(2,1)S(1)}) custom-call(s32[4]{0:T(128)S(1)} %pad_add_fusion.place_ref.refs_0_, f32[4,48,384]{2,1,0:T(8,128)} %refs_1_.5, f32[4,48,384]{2,1,0:T(8,128)} %refs_1_.6, ...), custom_call_target="tpu_custom_call" | custom-call | flops 50000000 | bytes 50000 | tf_op jit(solution)/shard_map/pallas_call | solution.py:518
  3.1 3.0 %collective-permute-start.3 = (bf16[6,2,48,384]{3,2,1,0:T(8,128)(2,1)S(1)}, bf16[6,2,48,384]{3,2,1,0:T(8,128)(2,1)S(1)}, u32[]{:S(2)}, u32[]{:S(2)}) collective-permute-start(bf16[6,2,48,384]{3,2,1,0:T(8,128)(2,1)S(1)} %get-tuple-element.158), channel_id=1, source_target_pairs={{0,4},{4,0},{8,12},{12,8},{16,20},{20,16},{24,28},{28,24},{1,5},{5... | collective-permute-start | bytes 1327112 | tf_op jit(solution)/shard_map/ppermute | solution.py:1084
  6.1 3.6 %collective-permute-start.2 = (bf16[4,48,384]{2,1,0:T(8,128)(2,1)S(1)}, bf16[4,48,384]{2,1,0:T(8,128)(2,1)S(1)}, u32[]{:S(2)}, u32[]{:S(2)}) collective-permute-start(bf16[4,48,384]{2,1,0:T(8,128)(2,1)S(1)} %get-tuple-element.161), channel_id=1, source_target_pairs={{0,24},{4,28},{8,16},{12,20},{16,8},{20,12},{24,0},{28,4},{1,25},{... | collective-permute-start | bytes 442376 | tf_op jit(solution)/shard_map/ppermute | solution.py:1084
  10.5 4.2 %collective-permute-done.2 = bf16[4,48,384]{2,1,0:T(8,128)(2,1)S(1)} collective-permute-done((bf16[4,48,384]{2,1,0:T(8,128)(2,1)S(1)}, bf16[4,48,384]{2,1,0:T(8,128)(2,1)S(1)}, u32[]{:S(2)}, u32[]{:S(2)}) %collective-permute-start.2) | collective-permute-done | bytes 147488 | tf_op jit(solution)/shard_map/ppermute | solution.py:1084
  14.7 7.2 %collective-permute-done.1 = bf16[4,48,384]{2,1,0:T(8,128)(2,1)S(1)} collective-permute-done((bf16[4,48,384]{2,1,0:T(8,128)(2,1)S(1)}, bf16[4,48,384]{2,1,0:T(8,128)(2,1)S(1)}, u32[]{:S(2)}, u32[]{:S(2)}) %collective-permute-start.1) | collective-permute-done | bytes 147488 | tf_op jit(solution)/shard_map/ppermute | solution.py:1084
  26.2 3.1 %collective-permute-start.4 = (bf16[24,48,384]{2,1,0:T(8,128)(2,1)S(1)}, bf16[24,48,384]{2,1,0:T(8,128)(2,1)S(1)}, u32[]{:S(2)}, u32[]{:S(2)}) collective-permute-start(bf16[24,48,384]{2,1,0:T(8,128)(2,1)S(1)} %get-tuple-element.160), channel_id=1, source_target_pairs={{0,8},{4,12},{8,0},{12,4},{16,24},{20,28},{24,16},{28,20},{1,9},{5... | collective-permute-start | bytes 2654216 | tf_op jit(solution)/shard_map/ppermute | solution.py:1084
  30.0 9.4 %collective-permute-done.6 = bf16[8,48,384]{2,1,0:T(8,128)(2,1)S(1)} collective-permute-done((bf16[8,48,384]{2,1,0:T(8,128)(2,1)S(1)}, bf16[8,48,384]{2,1,0:T(8,128)(2,1)S(1)}, u32[]{:S(2)}, u32[]{:S(2)}) %collective-permute-start.6) | collective-permute-done | bytes 294944 | tf_op jit(solution)/shard_map/ppermute | solution.py:1084
  41.4 8.5 %collective-permute-done.10.refs_5_ = bf16[4,4,48,384]{3,2,1,0:T(8,128)(2,1)S(1)} collective-permute-done((bf16[4,4,48,384]{3,2,1,0:T(8,128)(2,1)S(1)}, bf16[4,4,48,384]{3,2,1,0:T(8,128)(2,1)S(1)}, u32[]{:S(2)}, u32[]{:S(2)}) %collective-permute-start.10) | collective-permute-done | bytes 589856 | tf_op jit(solution)/shard_map/ppermute | solution.py:1086
  50.6 2.4 %collective-permute-done.4 = bf16[24,48,384]{2,1,0:T(8,128)(2,1)S(1)} collective-permute-done((bf16[24,48,384]{2,1,0:T(8,128)(2,1)S(1)}, bf16[24,48,384]{2,1,0:T(8,128)(2,1)S(1)}, u32[]{:S(2)}, u32[]{:S(2)}) %collective-permute-start.4) | collective-permute-done | bytes 884768 | tf_op jit(solution)/shard_map/ppermute | solution.py:1084
  53.1 2.5 %collective-permute-start.17 = (bf16[8,48,384]{2,1,0:T(8,128)(2,1)S(1)}, bf16[8,48,384]{2,1,0:T(8,128)(2,1)S(1)}, u32[]{:S(2)}, u32[]{:S(2)}) collective-permute-start(bf16[8,48,384]{2,1,0:T(8,128)(2,1)S(1)} %get-tuple-element.294), channel_id=1, source_target_pairs={{0,16},{4,20},{8,24},{12,28},{16,0},{20,4},{24,8},{28,12},{1,17},{... | collective-permute-start | bytes 884744 | tf_op jit(solution)/shard_map/ppermute | solution.py:1084
  57.6 9.7 %shard_map.333 = (bf16[160,768]{1,0:T(8,128)(2,1)S(1)}, bf16[197,2304]{1,0:T(8,128)(2,1)S(1)}, f32[12,197,197]{2,1,0:T(8,128)S(1)}, bf16[197,768]{1,0:T(8,128)(2...) custom-call(s32[4]{0:T(128)S(1)} %pad_add_fusion.place_ref.refs_0_, ...), custom_call_target="tpu_custom_call" | custom-call | flops 8000000000 | bytes 8000000 | tf_op jit(solution)/shard_map/pallas_call | solution.py:518
  67.4 1.6 collective-permute-start.18
  70.0 10.7 %collective-permute-done.25 = bf16[8,48,384]{2,1,0:T(8,128)(2,1)S(1)} collective-permute-done((bf16[8,48,384]{2,1,0:T(8,128)(2,1)S(1)}, bf16[8,48,384]{2,1,0:T(8,128)(2,1)S(1)}, u32[]{:S(2)}, u32[]{:S(2)}) %collective-permute-start.25) | collective-permute-done | bytes 294944 | tf_op jit(solution)/shard_map/ppermute | solution.py:1084
  82.2 4.6 %shard_map.334 = (bf16[160,768]{1,0:T(8,128)(2,1)S(1)}, bf16[160,768]{1,0:T(8,128)(2,1)S(1)}, bf16[160,768]{1,0:T(8,128)(2,1)S(1)}, bf16[160,768]{1,0:T(8,128)(2...) custom-call(s32[4]{0:T(128)S(1)} %pad_add_fusion.place_ref.refs_0_, ...), custom_call_target="tpu_custom_call" | custom-call | flops 5000000000 | bytes 5000000 | tf_op jit(solution)/shard_map/pallas_call | solution.py:518
  86.8 1.8 shard_map.337
  91.8 2.6 %shard_map.335 = (bf16[2,160,768]{2,1,0:T(8,128)(2,1)S(1)}, bf16[2,160,768]{2,1,0:T(8,128)(2,1)S(1)}, bf16[2,384,384]{2,1,0:T(8,128)(2,1)S(1)}, bf16[1,384,384]{...) custom-call(s32[4]{0:T(128)S(1)} %pad_add_fusion.place_ref.refs_0_, ...), custom_call_target="tpu_custom_call" | custom-call | flops 50000000 | bytes 50000 | tf_op jit(solution)/shard_map/pallas_call | solution.py:518
  94.4 2.3 %collective-permute-done.26.refs_8_ = bf16[16,48,384]{2,1,0:T(8,128)(2,1)S(1)} collective-permute-done((bf16[16,48,384]{2,1,0:T(8,128)(2,1)S(1)}, bf16[16,48,384]{2,1,0:T(8,128)(2,1)S(1)}, u32[]{:S(2)}, u32[]{:S(2)}) %collective-permute-start.26) | collective-permute-done | bytes 589856 | tf_op jit(solution)/shard_map/ppermute | solution.py:1084
  96.6 1.9 collective-permute-done.23.refs_3_
  98.6 4.5 %collective-permute-done.24.refs_4_ = bf16[160,768]{1,0:T(8,128)(2,1)S(1)} collective-permute-done((bf16[160,768]{1,0:T(8,128)(2,1)S(1)}, bf16[160,768]{1,0:T(8,128)(2,1)S(1)}, u32[]{:S(2)}, u32[]{:S(2)}) %collective-permute-start.24) | collective-permute-done | bytes 245792 | tf_op jit(solution)/shard_map/ppermute | solution.py:1086
  104.9 1.7 collective-permute-start.28
  106.5 7.8 %shard_map.336 = (bf16[2,4,384,384]{3,2,1,0:T(8,128)(2,1)S(1)}, bf16[2,4,384,384]{3,2,1,0:T(8,128)(2,1)S(1)}, bf16[197,2304]{1,0:T(8,128)(2,1)S(1)}, f32[197,768]{1,0:T(8,128)S(1)}, f32[4,768]{1,0:T(4,128)S(1)}) custom-call(s32[4]{0:T(128)S(1)} %pad_add_fusion.place_ref.refs_0_, bf16[160,768]{1,0:T(8,128)(2,1)S(1)} %get-tuple-element.191.refs_1_, ...), custom_call_target="tpu_custom_call" | custom-call | flops 8000000000 | bytes 8000000 | tf_op jit(solution)/shard_map/pallas_call | solution.py:518
  116.7 1.9 collective-permute-start.33
  120.1 3.7 %collective-permute-done.32.refs_4_ = bf16[1,384,384]{2,1,0:T(8,128)(2,1)S(1)} collective-permute-done((bf16[1,384,384]{2,1,0:T(8,128)(2,1)S(1)}, bf16[1,384,384]{2,1,0:T(8,128)(2,1)S(1)}, u32[]{:S(2)}, u32[]{:S(2)}) %collective-permute-start.32) | collective-permute-done | bytes 294944 | tf_op jit(solution)/shard_map/ppermute | solution.py:1084
  126.6 1.6 collective-permute-start.41
  129.8 1.6 collective-permute-start.35
  131.7 5.0 %collective-permute-done.37 = bf16[2,2,96,384]{3,2,1,0:T(8,128)(2,1)S(1)} collective-permute-done((bf16[2,2,96,384]{3,2,1,0:T(8,128)(2,1)S(1)}, bf16[2,2,96,384]{3,2,1,0:T(8,128)(2,1)S(1)}, u32[]{:S(2)}, u32[]{:S(2)}) %collective-permute-start.37) | collective-permute-done | bytes 294944 | tf_op jit(solution)/shard_map/ppermute | solution.py:1084
  136.9 2.5 %collective-permute-start.42 = (bf16[2,2,96,384]{3,2,1,0:T(8,128)(2,1)S(1)}, bf16[2,2,96,384]{3,2,1,0:T(8,128)(2,1)S(1)}, u32[]{:S(2)}, u32[]{:S(2)}) collective-permute-start(bf16[2,2,96,384]{3,2,1,0:T(8,128)(2,1)S(1)} %pad_maximum_fusion.4), channel_id=1, source_target_pairs={{0,8},{4,12},{8,0},{12,4},{16,24},{20,28},{24,16},{28,20},{1,9},{5... | collective-permute-start | bytes 884744 | tf_op jit(solution)/shard_map/ppermute | solution.py:1084
  139.5 3.9 %shard_map.340 = (bf16[197,768]{1,0:T(8,128)(2,1)}, f32[197,1,768]{2,1,0:T(1,128)}, f32[5,768]{1,0:T(8,128)S(1)}) custom-call(bf16[160,768]{1,0:T(8,128)(2,1)S(1)} %get-tuple-element.218.refs_0_, bf16[160,768]{1,0:T(8,128)(2,1)S(1)} %collective-permute-done.33.refs_1_, bf16[197,2304]{1,0:T(8,128)(2,1)S(1)} %get-tuple-element.220.refs_2_, ...), custom_call_target="tpu_custom_call" | custom-call | flops 50000000 | bytes 50000 | tf_op jit(solution)/shard_map/pallas_call | solution.py:518
  144.6 5.2 %collective-permute-done.42 = bf16[2,2,96,384]{3,2,1,0:T(8,128)(2,1)S(1)} collective-permute-done((bf16[2,2,96,384]{3,2,1,0:T(8,128)(2,1)S(1)}, bf16[2,2,96,384]{3,2,1,0:T(8,128)(2,1)S(1)}, u32[]{:S(2)}, u32[]{:S(2)}) %collective-permute-start.42) | collective-permute-done | bytes 294944 | tf_op jit(solution)/shard_map/ppermute | solution.py:1084
  149.8 1.8 shard_map.342
  152.1 3.8 %collective-permute-done.35.refs_3_ = bf16[2,384,384]{2,1,0:T(8,128)(2,1)S(1)} collective-permute-done((bf16[2,384,384]{2,1,0:T(8,128)(2,1)S(1)}, bf16[2,384,384]{2,1,0:T(8,128)(2,1)S(1)}, u32[]{:S(2)}, u32[]{:S(2)}) %collective-permute-start.35) | collective-permute-done | bytes 589856 | tf_op jit(solution)/shard_map/ppermute | solution.py:1086
  161.3 2.0 collective-permute-start.45
  163.3 3.1 %collective-permute-done.47 = bf16[2,2,96,384]{3,2,1,0:T(8,128)(2,1)S(1)} collective-permute-done((bf16[2,2,96,384]{3,2,1,0:T(8,128)(2,1)S(1)}, bf16[2,2,96,384]{3,2,1,0:T(8,128)(2,1)S(1)}, u32[]{:S(2)}, u32[]{:S(2)}) %collective-permute-start.47) | collective-permute-done | bytes 294944 | tf_op jit(solution)/shard_map/ppermute | solution.py:1084
  166.5 1.8 shard_map.345
  168.3 2.1 %collective-permute-done.43 = bf16[2,96,384]{2,1,0:T(8,128)(2,1)S(1)} collective-permute-done((bf16[2,96,384]{2,1,0:T(8,128)(2,1)S(1)}, bf16[2,96,384]{2,1,0:T(8,128)(2,1)S(1)}, u32[]{:S(2)}, u32[]{:S(2)}) %collective-permute-start.43) | collective-permute-done | bytes 147488 | tf_op jit(solution)/shard_map/ppermute | solution.py:1084
  170.4 2.8 %collective-permute-done.45 = bf16[2,96,384]{2,1,0:T(8,128)(2,1)S(1)} collective-permute-done((bf16[2,96,384]{2,1,0:T(8,128)(2,1)S(1)}, bf16[2,96,384]{2,1,0:T(8,128)(2,1)S(1)}, u32[]{:S(2)}, u32[]{:S(2)}) %collective-permute-start.45) | collective-permute-done | bytes 147488 | tf_op jit(solution)/shard_map/ppermute | solution.py:1084
  173.9 2.1 %collective-permute-start.50 = (bf16[2,96,384]{2,1,0:T(8,128)(2,1)S(1)}, bf16[2,96,384]{2,1,0:T(8,128)(2,1)S(1)}, u32[]{:S(2)}, u32[]{:S(2)}) collective-permute-start(bf16[2,96,384]{2,1,0:T(8,128)(2,1)S(1)} %add_convert_fusion.2.refs_1_), channel_id=1, source_target_pairs={{0,24},{4,28},{8,16},{12,20},{16,8},{20,12},{24,0},{28,4},{1,25},{... | collective-permute-start | bytes 442376 | tf_op jit(solution)/shard_map/ppermute | solution.py:1084
  176.8 1.6 collective-permute-start.48
  179.6 2.5 %collective-permute-start.53 = (f32[13,768]{1,0:T(8,128)S(1)}, f32[13,768]{1,0:T(8,128)S(1)}, u32[]{:S(2)}, u32[]{:S(2)}) collective-permute-start(f32[13,768]{1,0:T(8,128)S(1)} %add.65), channel_id=1, source_target_pairs={{0,2},{1,3},{2,0},{3,1},{4,6},{5,7},{6,4},{7,5},{8,10},{9,11},{10,... | collective-permute-start | bytes 119816 | tf_op jit(solution)/shard_map/ppermute | solution.py:1086
  182.1 2.1 %collective-permute-done.53 = f32[13,768]{1,0:T(8,128)S(1)} collective-permute-done((f32[13,768]{1,0:T(8,128)S(1)}, f32[13,768]{1,0:T(8,128)S(1)}, u32[]{:S(2)}, u32[]{:S(2)}) %collective-permute-start.53) | collective-permute-done | bytes 39968 | tf_op jit(solution)/shard_map/ppermute | solution.py:1086
  184.2 1.7 collective-permute-start.54
  185.9 2.4 %collective-permute-done.54.vec_came_ref = f32[13,768]{1,0:T(8,128)S(1)} collective-permute-done((f32[13,768]{1,0:T(8,128)S(1)}, f32[13,768]{1,0:T(8,128)S(1)}, u32[]{:S(2)}, u32[]{:S(2)}) %collective-permute-start.54) | collective-permute-done | bytes 39968 | tf_op jit(solution)/shard_map/ppermute | solution.py:1084
  188.4 2.3 %collective-permute-start.58 = (f32[24,768]{1,0:T(8,128)S(1)}, f32[24,768]{1,0:T(8,128)S(1)}, u32[]{:S(2)}, u32[]{:S(2)}) collective-permute-start(f32[24,768]{1,0:T(8,128)S(1)} %shard_map.348), channel_id=1, source_target_pairs={{0,24},{4,28},{8,16},{12,20},{16,8},{20,12},{24,0},{28,4},{1,25},{... | collective-permute-start | bytes 221192 | tf_op jit(solution)/shard_map/ppermute | solution.py:1084
  192.9 2.3 %shard_map.346 = (bf16[4,2,48,384]{3,2,1,0:T(8,128)(2,1)S(1)}, bf16[4,2,48,384]{3,2,1,0:T(8,128)(2,1)S(1)}) custom-call(s32[4]{0:T(128)S(1)} %pad_add_fusion.place_ref.refs_0_, bf16[2,96,384]{2,1,0:T(8,128)(2,1)S(1)} %add_convert_fusion.2.refs_1_, bf16[2,96,384]{2,1,0:T(8,128)(2,1)S(1)} %collective-permute-done.48.refs_2_, ...), custom_call_target="tpu_custom_call" | custom-call | flops 50000000 | bytes 50000 | tf_op jit(solution)/shard_map/pallas_call | solution.py:518
  195.2 1.7 collective-permute-start.55
  197.7 1.7 shard_map.350
  199.4 1.7 shard_map.349
  202.0 1.7 shard_map.347
  (143 shorter events, 40.8 us)
Async XLA Ops:
  3.1 18.8 %collective-permute-start.3 = (bf16[6,2,48,384]{3,2,1,0:T(8,128)(2,1)S(1)}, bf16[6,2,48,384]{3,2,1,0:T(8,128)(2,1)S(1)}, u32[]{:S(2)}, u32[]{:S(2)}) collective-permute-start(bf16[6,2,48,384]{3,2,1,0:T(8,128)(2,1)S(1)} %get-tuple-element.158), channel_id=1, source_target_pairs={{0,4},{4,0},{8,12},{12,8},{16,20},{20,16},{24,28},{28,24},{1,5},{5... | collective-permute-start | bytes 1327112 | tf_op jit(solution)/shard_map/ppermute | solution.py:1084
  6.1 8.6 %collective-permute-start.2 = (bf16[4,48,384]{2,1,0:T(8,128)(2,1)S(1)}, bf16[4,48,384]{2,1,0:T(8,128)(2,1)S(1)}, u32[]{:S(2)}, u32[]{:S(2)}) collective-permute-start(bf16[4,48,384]{2,1,0:T(8,128)(2,1)S(1)} %get-tuple-element.161), channel_id=1, source_target_pairs={{0,24},{4,28},{8,16},{12,20},{16,8},{20,12},{24,0},{28,4},{1,25},{... | collective-permute-start | bytes 442376 | tf_op jit(solution)/shard_map/ppermute | solution.py:1084
  9.7 12.2 %collective-permute-start.1 = (bf16[4,48,384]{2,1,0:T(8,128)(2,1)S(1)}, bf16[4,48,384]{2,1,0:T(8,128)(2,1)S(1)}, u32[]{:S(2)}, u32[]{:S(2)}) collective-permute-start(bf16[4,48,384]{2,1,0:T(8,128)(2,1)S(1)} %get-tuple-element.161), channel_id=1, source_target_pairs={{0,16},{4,20},{8,24},{12,28},{16,0},{20,4},{24,8},{28,12},{1,17},{... | collective-permute-start | bytes 442376 | tf_op jit(solution)/shard_map/ppermute | solution.py:1084
  9.7 12.2 %collective-permute-start = (bf16[4,48,384]{2,1,0:T(8,128)(2,1)S(1)}, bf16[4,48,384]{2,1,0:T(8,128)(2,1)S(1)}, u32[]{:S(2)}, u32[]{:S(2)}) collective-permute-start(bf16[4,48,384]{2,1,0:T(8,128)(2,1)S(1)} %get-tuple-element.161), channel_id=1, source_target_pairs={{0,8},{4,12},{8,0},{12,4},{16,24},{20,28},{24,16},{28,20},{1,9},{5... | collective-permute-start | bytes 442376 | tf_op jit(solution)/shard_map/ppermute | solution.py:1084
  22.0 19.1 %collective-permute-start.12 = (bf16[4,4,48,384]{3,2,1,0:T(8,128)(2,1)S(1)}, bf16[4,4,48,384]{3,2,1,0:T(8,128)(2,1)S(1)}, u32[]{:S(2)}, u32[]{:S(2)}) collective-permute-start(bf16[4,4,48,384]{3,2,1,0:T(8,128)(2,1)S(1)} %pad_maximum_fusion.1.refs_1_), channel_id=1, source_target_pairs={{0,6},{1,7},{2,4},{3,5},{4,2},{5,3},{6,0},{7,1},{8,14},{9,15},{10,... | collective-permute-start | bytes 1769480 | tf_op jit(solution)/shard_map/ppermute | solution.py:1088
  23.5 26.4 %collective-permute-start.10 = (bf16[4,4,48,384]{3,2,1,0:T(8,128)(2,1)S(1)}, bf16[4,4,48,384]{3,2,1,0:T(8,128)(2,1)S(1)}, u32[]{:S(2)}, u32[]{:S(2)}) collective-permute-start(bf16[4,4,48,384]{3,2,1,0:T(8,128)(2,1)S(1)} %pad_maximum_fusion.1.refs_1_), channel_id=1, source_target_pairs={{0,2},{1,3},{2,0},{3,1},{4,6},{5,7},{6,4},{7,5},{8,10},{9,11},{10,... | collective-permute-start | bytes 1769480 | tf_op jit(solution)/shard_map/ppermute | solution.py:1086
  24.0 26.0 %collective-permute-start.8 = (bf16[4,4,48,384]{3,2,1,0:T(8,128)(2,1)S(1)}, bf16[4,4,48,384]{3,2,1,0:T(8,128)(2,1)S(1)}, u32[]{:S(2)}, u32[]{:S(2)}) collective-permute-start(bf16[4,4,48,384]{3,2,1,0:T(8,128)(2,1)S(1)} %pad_maximum_fusion.1.refs_1_), channel_id=1, source_target_pairs={{0,4},{4,0},{8,12},{12,8},{16,20},{20,16},{24,28},{28,24},{1,5},{5... | collective-permute-start | bytes 1769480 | tf_op jit(solution)/shard_map/ppermute | solution.py:1084
  25.5 13.9 %collective-permute-start.6 = (bf16[8,48,384]{2,1,0:T(8,128)(2,1)S(1)}, bf16[8,48,384]{2,1,0:T(8,128)(2,1)S(1)}, u32[]{:S(2)}, u32[]{:S(2)}) collective-permute-start(bf16[8,48,384]{2,1,0:T(8,128)(2,1)S(1)} %get-tuple-element.155.feed_ref), channel_id=1, source_target_pairs={{0,16},{4,20},{8,24},{12,28},{16,0},{20,4},{24,8},{28,12},{1,17},{... | collective-permute-start | bytes 884744 | tf_op jit(solution)/shard_map/ppermute | solution.py:1084
  26.2 26.7 %collective-permute-start.4 = (bf16[24,48,384]{2,1,0:T(8,128)(2,1)S(1)}, bf16[24,48,384]{2,1,0:T(8,128)(2,1)S(1)}, u32[]{:S(2)}, u32[]{:S(2)}) collective-permute-start(bf16[24,48,384]{2,1,0:T(8,128)(2,1)S(1)} %get-tuple-element.160), channel_id=1, source_target_pairs={{0,8},{4,12},{8,0},{12,4},{16,24},{20,28},{24,16},{28,20},{1,9},{5... | collective-permute-start | bytes 2654216 | tf_op jit(solution)/shard_map/ppermute | solution.py:1084
  40.9 12.1 %collective-permute-start.7 = (bf16[4,4,48,384]{3,2,1,0:T(8,128)(2,1)S(1)}, bf16[4,4,48,384]{3,2,1,0:T(8,128)(2,1)S(1)}, u32[]{:S(2)}, u32[]{:S(2)}) collective-permute-start(bf16[4,4,48,384]{3,2,1,0:T(8,128)(2,1)S(1)} %pad_maximum_fusion.1.refs_1_), channel_id=1, source_target_pairs={{0,1},{1,0},{2,3},{3,2},{4,5},{5,4},{6,7},{7,6},{8,9},{9,8},{10,11... | collective-permute-start | bytes 1769480 | tf_op jit(solution)/shard_map/ppermute | solution.py:1086
  41.1 14.4 %collective-permute-start.13 = (bf16[4,4,48,384]{3,2,1,0:T(8,128)(2,1)S(1)}, bf16[4,4,48,384]{3,2,1,0:T(8,128)(2,1)S(1)}, u32[]{:S(2)}, u32[]{:S(2)}) collective-permute-start(bf16[4,4,48,384]{3,2,1,0:T(8,128)(2,1)S(1)} %collective-permute-done.12.refs_7_), channel_id=1, source_target_pairs={{0,1},{1,0},{2,3},{3,2},{4,5},{5,4},{6,7},{7,6},{8,9},{9,8},{10,11... | collective-permute-start | bytes 1769480 | tf_op jit(solution)/shard_map/ppermute | solution.py:1086
  50.0 7.5 %collective-permute-start.9 = (bf16[4,4,48,384]{3,2,1,0:T(8,128)(2,1)S(1)}, bf16[4,4,48,384]{3,2,1,0:T(8,128)(2,1)S(1)}, u32[]{:S(2)}, u32[]{:S(2)}) collective-permute-start(bf16[4,4,48,384]{3,2,1,0:T(8,128)(2,1)S(1)} %collective-permute-done.8.refs_3_), channel_id=1, source_target_pairs={{0,1},{1,0},{2,3},{3,2},{4,5},{5,4},{6,7},{7,6},{8,9},{9,8},{10,11... | collective-permute-start | bytes 1769480 | tf_op jit(solution)/shard_map/ppermute | solution.py:1086
  52.9 14.3 %collective-permute-start.16 = (bf16[8,48,384]{2,1,0:T(8,128)(2,1)S(1)}, bf16[8,48,384]{2,1,0:T(8,128)(2,1)S(1)}, u32[]{:S(2)}, u32[]{:S(2)}) collective-permute-start(bf16[8,48,384]{2,1,0:T(8,128)(2,1)S(1)} %collective-permute-done.6), channel_id=1, source_target_pairs={{0,8},{4,12},{8,0},{12,4},{16,24},{20,28},{24,16},{28,20},{1,9},{5... | collective-permute-start | bytes 884744 | tf_op jit(solution)/shard_map/ppermute | solution.py:1084
  53.1 14.2 %collective-permute-start.17 = (bf16[8,48,384]{2,1,0:T(8,128)(2,1)S(1)}, bf16[8,48,384]{2,1,0:T(8,128)(2,1)S(1)}, u32[]{:S(2)}, u32[]{:S(2)}) collective-permute-start(bf16[8,48,384]{2,1,0:T(8,128)(2,1)S(1)} %get-tuple-element.294), channel_id=1, source_target_pairs={{0,16},{4,20},{8,24},{12,28},{16,0},{20,4},{24,8},{28,12},{1,17},{... | collective-permute-start | bytes 884744 | tf_op jit(solution)/shard_map/ppermute | solution.py:1084
  55.5 11.8 %collective-permute-start.15 = (bf16[2,160,768]{2,1,0:T(8,128)(2,1)S(1)}, bf16[2,160,768]{2,1,0:T(8,128)(2,1)S(1)}, u32[]{:S(2)}, u32[]{:S(2)}) collective-permute-start(bf16[2,160,768]{2,1,0:T(8,128)(2,1)S(1)} %pad_maximum_fusion.3.refs_9_), channel_id=1, source_target_pairs={{0,2},{1,3},{2,0},{3,1},{4,6},{5,7},{6,4},{7,5},{8,10},{9,11},{10,... | collective-permute-start | bytes 1474568 | tf_op jit(solution)/shard_map/ppermute | solution.py:1086
  57.1 25.2 %collective-permute-start.5 = (bf16[2,8,48,384]{3,2,1,0:T(8,128)(2,1)S(1)}, bf16[2,8,48,384]{3,2,1,0:T(8,128)(2,1)S(1)}, u32[]{:S(2)}, u32[]{:S(2)}) collective-permute-start(bf16[2,8,48,384]{3,2,1,0:T(8,128)(2,1)S(1)} %pad_maximum_fusion.refs_1_), channel_id=1, source_target_pairs={{0,4},{4,0},{8,12},{12,8},{16,20},{20,16},{24,28},{28,24},{1,5},{5... | collective-permute-start | bytes 1769480 | tf_op jit(solution)/shard_map/ppermute | solution.py:1084
  67.4 14.8 %collective-permute-start.18 = (bf16[2,8,48,384]{3,2,1,0:T(8,128)(2,1)S(1)}, bf16[2,8,48,384]{3,2,1,0:T(8,128)(2,1)S(1)}, u32[]{:S(2)}, u32[]{:S(2)}) collective-permute-start(bf16[2,8,48,384]{3,2,1,0:T(8,128)(2,1)S(1)} %pad_maximum_fusion.2.refs_3_), channel_id=1, source_target_pairs={{0,4},{4,0},{8,12},{12,8},{16,20},{20,16},{24,28},{28,24},{1,5},{5... | collective-permute-start | bytes 1769480 | tf_op jit(solution)/shard_map/ppermute | solution.py:1084
  69.0 11.7 %collective-permute-start.25 = (bf16[8,48,384]{2,1,0:T(8,128)(2,1)S(1)}, bf16[8,48,384]{2,1,0:T(8,128)(2,1)S(1)}, u32[]{:S(2)}, u32[]{:S(2)}) collective-permute-start(bf16[8,48,384]{2,1,0:T(8,128)(2,1)S(1)} %get-tuple-element.293), channel_id=1, source_target_pairs={{0,16},{4,20},{8,24},{12,28},{16,0},{20,4},{24,8},{28,12},{1,17},{... | collective-permute-start | bytes 884744 | tf_op jit(solution)/shard_map/ppermute | solution.py:1084
  69.6 11.2 %collective-permute-start.21 = (bf16[160,768]{1,0:T(8,128)(2,1)S(1)}, bf16[160,768]{1,0:T(8,128)(2,1)S(1)}, u32[]{:S(2)}, u32[]{:S(2)}) collective-permute-start(bf16[160,768]{1,0:T(8,128)(2,1)S(1)} %get-tuple-element.171.refs_5_), channel_id=1, source_target_pairs={{0,3},{1,2},{2,1},{3,0},{4,7},{5,6},{6,5},{7,4},{8,11},{9,10},{10,... | collective-permute-start | bytes 737288 | tf_op jit(solution)/shard_map/ppermute | solution.py:1086
  69.6 11.5 %collective-permute-start.20 = (bf16[160,768]{1,0:T(8,128)(2,1)S(1)}, bf16[160,768]{1,0:T(8,128)(2,1)S(1)}, u32[]{:S(2)}, u32[]{:S(2)}) collective-permute-start(bf16[160,768]{1,0:T(8,128)(2,1)S(1)} %get-tuple-element.171.refs_5_), channel_id=1, source_target_pairs={{0,2},{1,3},{2,0},{3,1},{4,6},{5,7},{6,4},{7,5},{8,10},{9,11},{10,... | collective-permute-start | bytes 737288 | tf_op jit(solution)/shard_map/ppermute | solution.py:1086
  80.8 15.8 %collective-permute-start.26 = (bf16[16,48,384]{2,1,0:T(8,128)(2,1)S(1)}, bf16[16,48,384]{2,1,0:T(8,128)(2,1)S(1)}, u32[]{:S(2)}, u32[]{:S(2)}) collective-permute-start(bf16[16,48,384]{2,1,0:T(8,128)(2,1)S(1)} %constant_dynamic-update-slice_fusion.refs_7_), channel_id=1, source_target_pairs={{0,8},{4,12},{8,0},{12,4},{16,24},{20,28},{24,16},{28,20},{1,9},{5... | collective-permute-start | bytes 1769480 | tf_op jit(solution)/shard_map/ppermute | solution.py:1084
  88.6 15.6 %collective-permute-start.27 = (bf16[2,384,384]{2,1,0:T(8,128)(2,1)S(1)}, bf16[2,384,384]{2,1,0:T(8,128)(2,1)S(1)}, u32[]{:S(2)}, u32[]{:S(2)}) collective-permute-start(bf16[2,384,384]{2,1,0:T(8,128)(2,1)S(1)} %get-tuple-element.204), channel_id=1, source_target_pairs={{0,4},{4,0},{8,12},{12,8},{16,20},{20,16},{24,28},{28,24},{1,5},{5... | collective-permute-start | bytes 1769480 | tf_op jit(solution)/shard_map/ppermute | solution.py:1084
  89.8 8.8 %collective-permute-start.23 = (bf16[160,768]{1,0:T(8,128)(2,1)S(1)}, bf16[160,768]{1,0:T(8,128)(2,1)S(1)}, u32[]{:S(2)}, u32[]{:S(2)}) collective-permute-start(bf16[160,768]{1,0:T(8,128)(2,1)S(1)} %get-tuple-element.181), channel_id=1, source_target_pairs={{0,2},{1,3},{2,0},{3,1},{4,6},{5,7},{6,4},{7,5},{8,10},{9,11},{10,... | collective-permute-start | bytes 737288 | tf_op jit(solution)/shard_map/ppermute | solution.py:1086
  90.5 12.5 %collective-permute-start.24 = (bf16[160,768]{1,0:T(8,128)(2,1)S(1)}, bf16[160,768]{1,0:T(8,128)(2,1)S(1)}, u32[]{:S(2)}, u32[]{:S(2)}) collective-permute-start(bf16[160,768]{1,0:T(8,128)(2,1)S(1)} %get-tuple-element.182), channel_id=1, source_target_pairs={{0,3},{1,2},{2,1},{3,0},{4,7},{5,6},{6,5},{7,4},{8,11},{9,10},{10,... | collective-permute-start | bytes 737288 | tf_op jit(solution)/shard_map/ppermute | solution.py:1086
  103.1 11.3 %collective-permute-start.29 = (bf16[1,384,384]{2,1,0:T(8,128)(2,1)S(1)}, bf16[1,384,384]{2,1,0:T(8,128)(2,1)S(1)}, u32[]{:S(2)}, u32[]{:S(2)}) collective-permute-start(bf16[1,384,384]{2,1,0:T(8,128)(2,1)S(1)} %get-tuple-element.206), channel_id=1, source_target_pairs={{0,4},{4,0},{8,12},{12,8},{16,20},{20,16},{24,28},{28,24},{1,5},{5... | collective-permute-start | bytes 884744 | tf_op jit(solution)/shard_map/ppermute | solution.py:1084
  103.9 10.4 %collective-permute-start.30 = (bf16[2,160,768]{2,1,0:T(8,128)(2,1)S(1)}, bf16[2,160,768]{2,1,0:T(8,128)(2,1)S(1)}, u32[]{:S(2)}, u32[]{:S(2)}) collective-permute-start(bf16[2,160,768]{2,1,0:T(8,128)(2,1)S(1)} %get-tuple-element.207), channel_id=1, source_target_pairs={{0,1},{1,0},{2,3},{3,2},{4,5},{5,4},{6,7},{7,6},{8,9},{9,8},{10,11... | collective-permute-start | bytes 1474568 | tf_op jit(solution)/shard_map/ppermute | solution.py:1086
  104.9 9.5 %collective-permute-start.28 = (bf16[2,2,96,384]{3,2,1,0:T(8,128)(2,1)S(1)}, bf16[2,2,96,384]{3,2,1,0:T(8,128)(2,1)S(1)}, u32[]{:S(2)}, u32[]{:S(2)}) collective-permute-start(bf16[2,2,96,384]{3,2,1,0:T(8,128)(2,1)S(1)} %get-tuple-element.205), channel_id=1, source_target_pairs={{0,8},{4,12},{8,0},{12,4},{16,24},{20,28},{24,16},{28,20},{1,9},{5... | collective-permute-start | bytes 884744 | tf_op jit(solution)/shard_map/ppermute | solution.py:1084
  114.5 9.4 %collective-permute-start.32 = (bf16[1,384,384]{2,1,0:T(8,128)(2,1)S(1)}, bf16[1,384,384]{2,1,0:T(8,128)(2,1)S(1)}, u32[]{:S(2)}, u32[]{:S(2)}) collective-permute-start(bf16[1,384,384]{2,1,0:T(8,128)(2,1)S(1)} %get-tuple-element.215), channel_id=1, source_target_pairs={{0,4},{4,0},{8,12},{12,8},{16,20},{20,16},{24,28},{28,24},{1,5},{5... | collective-permute-start | bytes 884744 | tf_op jit(solution)/shard_map/ppermute | solution.py:1084
  115.3 11.2 %collective-permute-start.40 = (bf16[2,96,384]{2,1,0:T(8,128)(2,1)S(1)}, bf16[2,96,384]{2,1,0:T(8,128)(2,1)S(1)}, u32[]{:S(2)}, u32[]{:S(2)}) collective-permute-start(bf16[2,96,384]{2,1,0:T(8,128)(2,1)S(1)} %get-tuple-element.295), channel_id=1, source_target_pairs={{0,16},{4,20},{8,24},{12,28},{16,0},{20,4},{24,8},{28,12},{1,17},{... | collective-permute-start | bytes 442376 | tf_op jit(solution)/shard_map/ppermute | solution.py:1084
  116.7 8.0 %collective-permute-start.33 = (bf16[160,768]{1,0:T(8,128)(2,1)S(1)}, bf16[160,768]{1,0:T(8,128)(2,1)S(1)}, u32[]{:S(2)}, u32[]{:S(2)}) collective-permute-start(bf16[160,768]{1,0:T(8,128)(2,1)S(1)} %get-tuple-element.291), channel_id=1, source_target_pairs={{0,2},{1,3},{2,0},{3,1},{4,6},{5,7},{6,4},{7,5},{8,10},{9,11},{10,... | collective-permute-start | bytes 737288 | tf_op jit(solution)/shard_map/ppermute | solution.py:1086
  125.3 11.3 %collective-permute-start.37 = (bf16[2,2,96,384]{3,2,1,0:T(8,128)(2,1)S(1)}, bf16[2,2,96,384]{3,2,1,0:T(8,128)(2,1)S(1)}, u32[]{:S(2)}, u32[]{:S(2)}) collective-permute-start(bf16[2,2,96,384]{3,2,1,0:T(8,128)(2,1)S(1)} %get-tuple-element.232), channel_id=1, source_target_pairs={{0,8},{4,12},{8,0},{12,4},{16,24},{20,28},{24,16},{28,20},{1,9},{5... | collective-permute-start | bytes 884744 | tf_op jit(solution)/shard_map/ppermute | solution.py:1084
  126.6 10.3 %collective-permute-start.41 = (bf16[2,96,384]{2,1,0:T(8,128)(2,1)S(1)}, bf16[2,96,384]{2,1,0:T(8,128)(2,1)S(1)}, u32[]{:S(2)}, u32[]{:S(2)}) collective-permute-start(bf16[2,96,384]{2,1,0:T(8,128)(2,1)S(1)} %add_convert_fusion.3.refs_1_), channel_id=1, source_target_pairs={{0,16},{4,20},{8,24},{12,28},{16,0},{20,4},{24,8},{28,12},{1,17},{... | collective-permute-start | bytes 442376 | tf_op jit(solution)/shard_map/ppermute | solution.py:1084
  128.2 23.9 %collective-permute-start.34 = (bf16[2,384,384]{2,1,0:T(8,128)(2,1)S(1)}, bf16[2,384,384]{2,1,0:T(8,128)(2,1)S(1)}, u32[]{:S(2)}, u32[]{:S(2)}) collective-permute-start(bf16[2,384,384]{2,1,0:T(8,128)(2,1)S(1)} %get-tuple-element.225), channel_id=1, source_target_pairs={{0,4},{4,0},{8,12},{12,8},{16,20},{20,16},{24,28},{28,24},{1,5},{5... | collective-permute-start | bytes 1769480 | tf_op jit(solution)/shard_map/ppermute | solution.py:1084
  129.8 26.1 %collective-permute-start.35 = (bf16[2,384,384]{2,1,0:T(8,128)(2,1)S(1)}, bf16[2,384,384]{2,1,0:T(8,128)(2,1)S(1)}, u32[]{:S(2)}, u32[]{:S(2)}) collective-permute-start(bf16[2,384,384]{2,1,0:T(8,128)(2,1)S(1)} %get-tuple-element.226), channel_id=1, source_target_pairs={{0,2},{1,3},{2,0},{3,1},{4,6},{5,7},{6,4},{7,5},{8,10},{9,11},{10,... | collective-permute-start | bytes 1769480 | tf_op jit(solution)/shard_map/ppermute | solution.py:1086
  131.4 24.5 %collective-permute-start.36 = (bf16[2,384,384]{2,1,0:T(8,128)(2,1)S(1)}, bf16[2,384,384]{2,1,0:T(8,128)(2,1)S(1)}, u32[]{:S(2)}, u32[]{:S(2)}) collective-permute-start(bf16[2,384,384]{2,1,0:T(8,128)(2,1)S(1)} %get-tuple-element.227), channel_id=1, source_target_pairs={{0,6},{1,7},{2,4},{3,5},{4,2},{5,3},{6,0},{7,1},{8,14},{9,15},{10,... | collective-permute-start | bytes 1769480 | tf_op jit(solution)/shard_map/ppermute | solution.py:1088
  136.7 7.5 %collective-permute-start.38 = (bf16[2,96,384]{2,1,0:T(8,128)(2,1)S(1)}, bf16[2,96,384]{2,1,0:T(8,128)(2,1)S(1)}, u32[]{:S(2)}, u32[]{:S(2)}) collective-permute-start(bf16[2,96,384]{2,1,0:T(8,128)(2,1)S(1)} %fusion.5), channel_id=1, source_target_pairs={{0,16},{4,20},{8,24},{12,28},{16,0},{20,4},{24,8},{28,12},{1,17},{... | collective-permute-start | bytes 442376 | tf_op jit(solution)/shard_map/ppermute | solution.py:1084
  136.9 12.9 %collective-permute-start.42 = (bf16[2,2,96,384]{3,2,1,0:T(8,128)(2,1)S(1)}, bf16[2,2,96,384]{3,2,1,0:T(8,128)(2,1)S(1)}, u32[]{:S(2)}, u32[]{:S(2)}) collective-permute-start(bf16[2,2,96,384]{3,2,1,0:T(8,128)(2,1)S(1)} %pad_maximum_fusion.4), channel_id=1, source_target_pairs={{0,8},{4,12},{8,0},{12,4},{16,24},{20,28},{24,16},{28,20},{1,9},{5... | collective-permute-start | bytes 884744 | tf_op jit(solution)/shard_map/ppermute | solution.py:1084
  144.3 7.8 %collective-permute-start.39 = (bf16[2,96,384]{2,1,0:T(8,128)(2,1)S(1)}, bf16[2,96,384]{2,1,0:T(8,128)(2,1)S(1)}, u32[]{:S(2)}, u32[]{:S(2)}) collective-permute-start(bf16[2,96,384]{2,1,0:T(8,128)(2,1)S(1)} %fusion.refs_1_), channel_id=1, source_target_pairs={{0,16},{4,20},{8,24},{12,28},{16,0},{20,4},{24,8},{28,12},{1,17},{... | collective-permute-start | bytes 442376 | tf_op jit(solution)/shard_map/ppermute | solution.py:1084
  156.0 10.5 %collective-permute-start.47 = (bf16[2,2,96,384]{3,2,1,0:T(8,128)(2,1)S(1)}, bf16[2,2,96,384]{3,2,1,0:T(8,128)(2,1)S(1)}, u32[]{:S(2)}, u32[]{:S(2)}) collective-permute-start(bf16[2,2,96,384]{3,2,1,0:T(8,128)(2,1)S(1)} %pad_maximum_fusion.5), channel_id=1, source_target_pairs={{0,8},{4,12},{8,0},{12,4},{16,24},{20,28},{24,16},{28,20},{1,9},{5... | collective-permute-start | bytes 884744 | tf_op jit(solution)/shard_map/ppermute | solution.py:1084
  156.7 16.4 %collective-permute-start.46 = (bf16[5,2,48,384]{3,2,1,0:T(8,128)(2,1)S(1)}, bf16[5,2,48,384]{3,2,1,0:T(8,128)(2,1)S(1)}, u32[]{:S(2)}, u32[]{:S(2)}) collective-permute-start(bf16[5,2,48,384]{3,2,1,0:T(8,128)(2,1)S(1)} %get-tuple-element.250), channel_id=1, source_target_pairs={{0,4},{4,0},{8,12},{12,8},{16,20},{20,16},{24,28},{28,24},{1,5},{5... | collective-permute-start | bytes 1105928 | tf_op jit(solution)/shard_map/ppermute | solution.py:1084
  158.9 11.5 %collective-permute-start.43 = (bf16[2,96,384]{2,1,0:T(8,128)(2,1)S(1)}, bf16[2,96,384]{2,1,0:T(8,128)(2,1)S(1)}, u32[]{:S(2)}, u32[]{:S(2)}) collective-permute-start(bf16[2,96,384]{2,1,0:T(8,128)(2,1)S(1)} %get-tuple-element.247), channel_id=1, source_target_pairs={{0,8},{4,12},{8,0},{12,4},{16,24},{20,28},{24,16},{28,20},{1,9},{5... | collective-permute-start | bytes 442376 | tf_op jit(solution)/shard_map/ppermute | solution.py:1084
  160.3 10.0 %collective-permute-start.44 = (bf16[2,96,384]{2,1,0:T(8,128)(2,1)S(1)}, bf16[2,96,384]{2,1,0:T(8,128)(2,1)S(1)}, u32[]{:S(2)}, u32[]{:S(2)}) collective-permute-start(bf16[2,96,384]{2,1,0:T(8,128)(2,1)S(1)} %get-tuple-element.248), channel_id=1, source_target_pairs={{0,16},{4,20},{8,24},{12,28},{16,0},{20,4},{24,8},{28,12},{1,17},{... | collective-permute-start | bytes 442376 | tf_op jit(solution)/shard_map/ppermute | solution.py:1084
  161.3 11.8 %collective-permute-start.45 = (bf16[2,96,384]{2,1,0:T(8,128)(2,1)S(1)}, bf16[2,96,384]{2,1,0:T(8,128)(2,1)S(1)}, u32[]{:S(2)}, u32[]{:S(2)}) collective-permute-start(bf16[2,96,384]{2,1,0:T(8,128)(2,1)S(1)} %get-tuple-element.249), channel_id=1, source_target_pairs={{0,24},{4,28},{8,16},{12,20},{16,8},{20,12},{24,0},{28,4},{1,25},{... | collective-permute-start | bytes 442376 | tf_op jit(solution)/shard_map/ppermute | solution.py:1084
  173.2 15.2 %collective-permute-start.51 = (bf16[5,2,48,384]{3,2,1,0:T(8,128)(2,1)S(1)}, bf16[5,2,48,384]{3,2,1,0:T(8,128)(2,1)S(1)}, u32[]{:S(2)}, u32[]{:S(2)}) collective-permute-start(bf16[5,2,48,384]{3,2,1,0:T(8,128)(2,1)S(1)} %get-tuple-element.259), channel_id=1, source_target_pairs={{0,4},{4,0},{8,12},{12,8},{16,20},{20,16},{24,28},{28,24},{1,5},{5... | collective-permute-start | bytes 1105928 | tf_op jit(solution)/shard_map/ppermute | solution.py:1084
  173.9 14.4 %collective-permute-start.50 = (bf16[2,96,384]{2,1,0:T(8,128)(2,1)S(1)}, bf16[2,96,384]{2,1,0:T(8,128)(2,1)S(1)}, u32[]{:S(2)}, u32[]{:S(2)}) collective-permute-start(bf16[2,96,384]{2,1,0:T(8,128)(2,1)S(1)} %add_convert_fusion.2.refs_1_), channel_id=1, source_target_pairs={{0,24},{4,28},{8,16},{12,20},{16,8},{20,12},{24,0},{28,4},{1,25},{... | collective-permute-start | bytes 442376 | tf_op jit(solution)/shard_map/ppermute | solution.py:1084
  176.0 12.4 %collective-permute-start.49 = (bf16[2,96,384]{2,1,0:T(8,128)(2,1)S(1)}, bf16[2,96,384]{2,1,0:T(8,128)(2,1)S(1)}, u32[]{:S(2)}, u32[]{:S(2)}) collective-permute-start(bf16[2,96,384]{2,1,0:T(8,128)(2,1)S(1)} %add_convert_fusion.2.refs_1_), channel_id=1, source_target_pairs={{0,16},{4,20},{8,24},{12,28},{16,0},{20,4},{24,8},{28,12},{1,17},{... | collective-permute-start | bytes 442376 | tf_op jit(solution)/shard_map/ppermute | solution.py:1084
  176.8 11.6 %collective-permute-start.48 = (bf16[2,96,384]{2,1,0:T(8,128)(2,1)S(1)}, bf16[2,96,384]{2,1,0:T(8,128)(2,1)S(1)}, u32[]{:S(2)}, u32[]{:S(2)}) collective-permute-start(bf16[2,96,384]{2,1,0:T(8,128)(2,1)S(1)} %add_convert_fusion.2.refs_1_), channel_id=1, source_target_pairs={{0,8},{4,12},{8,0},{12,4},{16,24},{20,28},{24,16},{28,20},{1,9},{5... | collective-permute-start | bytes 442376 | tf_op jit(solution)/shard_map/ppermute | solution.py:1084
  188.4 8.5 %collective-permute-start.58 = (f32[24,768]{1,0:T(8,128)S(1)}, f32[24,768]{1,0:T(8,128)S(1)}, u32[]{:S(2)}, u32[]{:S(2)}) collective-permute-start(f32[24,768]{1,0:T(8,128)S(1)} %shard_map.348), channel_id=1, source_target_pairs={{0,24},{4,28},{8,16},{12,20},{16,8},{20,12},{24,0},{28,4},{1,25},{... | collective-permute-start | bytes 221192 | tf_op jit(solution)/shard_map/ppermute | solution.py:1084
  (24 other events, 288.5 us)

commit v6 on v5

--- a/solution.py
+++ b/solution.py
@@ -581,7 +581,7 @@
     piece_refs, refs = refs[: len(pieces)], refs[len(pieces) :]
     normed_ref, tok_ref, mask_ref, chosen_ref, vec_ref = refs[:5]
     rows_ref, qkv_ref, probs_ref, attended_ref, branch_ref, weights_hbm = refs[5:11]
-    weights, probs_all, sems, out_sem, probs_sems = refs[11:]
+    weights, probs_all, sems, out_sem, probs_sem = refs[11:]
     z, x, m = place_ref[0], place_ref[1], place_ref[2]
     piece = piece_refs[0].shape[2]
     width = normed_ref.shape[1]
@@ -611,30 +611,32 @@
                 bias_row = 4 if kind == 0 else 5
                 part = part + vec_ref[bias_row : bias_row + 1, lanes]
             qkv_ref[:, kind * width + start : kind * width + start + TILE] = to_half(part)
-    keep_probs = []
     head = width // HEADS
-    scale = head ** (-0.5)
+    scale = jnp.asarray(head ** (-0.5), half)
     allowed = mask_ref[...] > 0
-    for slab in range(width // (2 * head)):
-        lanes = slice(slab * 2 * head, (slab + 1) * 2 * head)
-        queries = head_parts(qkv_ref[:, lanes])
-        keys = qkv_ref[:, width + lanes.start : width + lanes.stop]
-        values = head_parts(qkv_ref[:, 2 * width + lanes.start : 2 * width + lanes.stop])
-        total = None
-        for index in range(2):
-            scores = times_transpose(queries[index], keys) * scale
-            scores = jnp.where(allowed, scores, masked_score)
-            raised = jnp.exp(scores - jnp.max(scores, axis=-1, keepdims=True))
-            probs = raised / jnp.sum(raised, axis=-1, keepdims=True)
-            probs_all[2 * slab + index] = probs
-            part = dot32(to_half(probs), values[index])
-            total = part if total is None else total + part
-        attended_ref[:, lanes] = to_half(total)
-        pair = pl.ds(2 * slab, 2)
-        keep_probs.append(
-            pltpu.make_async_copy(probs_all.at[pair], probs_ref.at[pair], probs_sems.at[slab])
-        )
-        keep_probs[-1].start()
+    slabs = width // (2 * head)
+    together = 3
+    for first in range(0, slabs, together):
+        found = []
+        for slab in range(first, first + together):
+            lanes = slice(slab * 2 * head, (slab + 1) * 2 * head)
+            queries = head_parts(qkv_ref[:, lanes] * scale)
+            keys = qkv_ref[:, width + lanes.start : width + lanes.stop]
+            for index in range(2):
+                scores = times_transpose(queries[index], keys)
+                found.append(jnp.where(allowed, scores, masked_score))
+        found = [jnp.exp(v - jnp.max(v, axis=-1, keepdims=True)) for v in found]
+        found = [v * (1.0 / jnp.sum(v, axis=-1, keepdims=True)) for v in found]
+        for index, probs in enumerate(found):
+            probs_all[2 * first + index] = probs
+        for slab in range(first, first + together):
+            lanes = slice(slab * 2 * head, (slab + 1) * 2 * head)
+            values = head_parts(qkv_ref[:, 2 * width + lanes.start : 2 * width + lanes.stop])
+            at = 2 * (slab - first)
+            total = dot32(to_half(found[at]), values[0]) + dot32(to_half(found[at + 1]), values[1])
+            attended_ref[:, lanes] = to_half(total)
+    keep_probs = pltpu.make_async_copy(probs_all, probs_ref, probs_sem)
+    keep_probs.start()
     attended = attended_ref[...]
     matrix = matrix_of(weights, 3, row_blocks)
     for start in range(0, width, TILE):
@@ -644,8 +646,7 @@
     second = to_half(hat * vec_ref[2:3, :] + vec_ref[3:4, :])
     rows_ref[...] = to_half(dot32(chosen_ref[...], second))
     keep_whole.wait()
-    for copy in keep_probs:
-        copy.wait()
+    keep_probs.wait()
 
 
 def bias_row(m, values, count):
@@ -716,11 +717,18 @@
 
 
 def share_blocks(place_ref, blocks, kept_ref, *sent_refs):
-    own, x = kept_ref.shape[0], place_ref[1]
+    own, order, _ = kept_ref.shape
+    x = place_ref[1]
     kept_ref[...] = blocks[pl.ds(x * own, own)]
-    count = own // len(sent_refs)
-    for index, ref in enumerate(sent_refs):
-        ref[...] = blocks[pl.ds((1 - x) * own + index * count, count)]
+    at = 0
+    for ref in sent_refs:
+        stop = at + ref.shape[0]
+        for block in range(at // order, -(-stop // order)):
+            low, high = max(at, block * order), min(stop, (block + 1) * order)
+            ref[low - at : high - at] = blocks[
+                (1 - x) * own + block, low - block * order : high - block * order, :
+            ]
+        at = stop
 
 
 def store_blocks(blocks, order, product, by_rows):
@@ -795,28 +803,33 @@
     fetch_probs.wait()
     head = width // HEADS
     factor = head ** (-0.5)
-    for slab in range(width // (2 * head)):
-        start, stop = slab * 2 * head, (slab + 1) * 2 * head
-        queries = head_parts(qkv_ref[:, start:stop])
-        key_pair = qkv_ref[:, width + start : width + stop]
-        keys = head_parts(key_pair)
-        values = qkv_ref[:, 2 * width + start : 2 * width + stop]
-        grads = head_parts(grad_attended[:, start:stop])
-        sums = [None] * 3
-        for index in range(2):
-            probs = probs_all[2 * slab + index]
-            grad_probs = times_transpose(grads[index], values)
-            inner = jnp.sum(probs * grad_probs, axis=-1, keepdims=True)
-            grad_scores = to_half(probs * (grad_probs - inner))
-            parts = (
-                dot32(grad_scores, keys[index]),
-                row_product(grad_scores, queries[index]),
-                row_product(to_half(probs), grads[index]),
-            )
-            sums = [p if s is None else s + p for s, p in zip(sums, parts)]
-        right[0, :, start:stop] = to_half(sums[0] * factor)
-        right[1, :, start:stop] = to_half(sums[1] * factor)
-        right[2, :, start:stop] = to_half(sums[2])
+    slabs = width // (2 * head)
+    together = 3
+    for first in range(0, slabs, together):
+        grad_scores, probs_half = [], []
+        for slab in range(first, first + together):
+            start, stop = slab * 2 * head, (slab + 1) * 2 * head
+            values = qkv_ref[:, 2 * width + start : 2 * width + stop]
+            for index, part in enumerate(head_parts(grad_attended[:, start:stop])):
+                probs = probs_all[2 * slab + index]
+                grad_probs = times_transpose(part, values)
+                inner = jnp.sum(probs * grad_probs, axis=-1, keepdims=True)
+                grad_scores.append(to_half(probs * (grad_probs - inner)))
+                probs_half.append(to_half(probs))
+        for slab in range(first, first + together):
+            start, stop = slab * 2 * head, (slab + 1) * 2 * head
+            queries = head_parts(qkv_ref[:, start:stop])
+            keys = head_parts(qkv_ref[:, width + start : width + stop])
+            grads = head_parts(grad_attended[:, start:stop])
+            at = 2 * (slab - first)
+            sums = [0.0] * 3
+            for index in range(2):
+                sums[0] = sums[0] + dot32(grad_scores[at + index], keys[index])
+                sums[1] = sums[1] + row_product(grad_scores[at + index], queries[index])
+                sums[2] = sums[2] + row_product(probs_half[at + index], grads[index])
+            right[0, :, start:stop] = to_half(sums[0] * factor)
+            right[1, :, start:stop] = to_half(sums[1] * factor)
+            right[2, :, start:stop] = to_half(sums[2])
     for kind in range(3):
         mixed_ref[:, kind * width : (kind + 1) * width] = right[kind]
     core = place_ref[3]
@@ -900,6 +913,18 @@
                 at += 1
 
 
+def joined_sum_kernel(place_ref, kept_ref, first_ref, second_ref, near_ref, other_ref, came):
+    order = came.shape[1]
+    at = 0
+    for ref in (first_ref, second_ref):
+        stop = at + ref.shape[0]
+        for block in range(at // order, -(-stop // order)):
+            low, high = max(at, block * order), min(stop, (block + 1) * order)
+            came[block, low - block * order : high - block * order, :] = ref[low - at : high - at]
+        at = stop
+    row_sum_kernel(1, 2, place_ref, kept_ref, came, near_ref, other_ref)
+
+
 def line_blocks(z, refs, target, first=0):
     for slot, ref in enumerate(refs):
         rows = ref.shape[-2]
@@ -908,14 +933,14 @@
             target[block, pl.ds(start, rows), :] = ref[first + block]
 
 
-def line_roots(z, refs, target, first):
-    for slot, ref in enumerate(refs):
+def line_roots_kernel(place_ref, *refs):
+    root_refs, out_ref = refs[:-1], refs[-1]
+    for slot, ref in enumerate(root_refs):
         rows = ref.shape[1]
-        for block in range(target.shape[0]):
+        for block in range(out_ref.shape[0]):
             for part in range(PAIR):
-                start = pl.multiple_of((z ^ slot) * (PAIR * rows) + part * rows, 16)
-                at = (first + block) * PAIR + part
-                target[block, pl.ds(start, rows), :] = ref[at]
+                start = (place_ref[0] ^ slot) * (PAIR * rows) + part * rows
+                out_ref[block, pl.ds(pl.multiple_of(start, 16), rows), :] = ref[block * PAIR + part]
 
 
 def step_parts(z, x, own, whole, step, terms, found, block, kept_ref, sent_ref):
@@ -935,18 +960,15 @@
 
 def whole_step_kernel(count, left_first, place_ref, *refs):
     grad_refs, refs = refs[:count], refs[count:]
-    root_refs, refs = refs[:count], refs[count:]
-    kept_ref, sent_ref, grads, lefts, rights, terms, found, steps = refs
+    roots_ref, kept_ref, sent_ref, grads, terms, found, steps = refs
     z, x = place_ref[0], place_ref[1]
     blocks, rows, order = grad_refs[0].shape
     line_blocks(z, grad_refs, grads)
-    line_roots(z, root_refs, rights, 0)
-    line_roots(z, root_refs, lefts, left_first)
     mine = pl.multiple_of(z * rows, 16)
     for block in range(blocks):
         whole = grads[block]
-        step = to_half(dot32(lefts[block], whole))
-        step = dot32(step, rights[block])
+        step = to_half(dot32(roots_ref[left_first + block], whole))
+        step = dot32(step, roots_ref[block])
         mean = jnp.mean(jnp.mean(step * step, axis=1, keepdims=True), axis=0, keepdims=True)
         steps[...] = step * lax.rsqrt(mean + 1e-06)
         step = steps[pl.ds(mine, rows), :]
@@ -955,17 +977,15 @@
 
 def step_kernel(count, first, place_ref, *refs):
     grad_refs, refs = refs[:count], refs[count:]
-    root_refs, refs = refs[:count], refs[count:]
-    left_ref, kept_ref, sent_ref, square_ref, grads, rights, terms, found = refs
+    roots_ref, left_ref, kept_ref, sent_ref, square_ref, grads, terms, found = refs
     z, x = place_ref[0], place_ref[1]
     blocks, rows, order = grad_refs[0].shape
     line_blocks(z, grad_refs, grads)
-    line_roots(z, root_refs, rights, first)
     square_ref[...] = jnp.zeros_like(square_ref)
     for block in range(blocks):
         whole = grads[block]
         step = to_half(dot32(left_ref[first + block], whole))
-        step = dot32(step, rights[block])
+        step = dot32(step, roots_ref[first + block])
         total = jnp.sum(jnp.sum(step * step, axis=1, keepdims=True), axis=0, keepdims=True)
         square_ref[block : block + 1, :] = jnp.broadcast_to(total, (1, 128))
         step_parts(z, x, grad_refs[0][block], whole, step, terms, found, block, kept_ref, sent_ref)
@@ -995,28 +1015,56 @@
             out_ref[at : at + 1, :128] = jnp.sum(terms, axis=0, keepdims=True)
 
 
-def apply_kernel(
-    order, rates, matrix, place_ref, weight_ref, left_ref, right_ref, kept_ref, came_ref, *refs
-):
-    total_ref = refs[0] if len(refs) == 6 else None
-    grad_ref, new_left_ref, new_right_ref, new_ref, half_ref = refs[-5:]
-    x, m = place_ref[1], place_ref[2]
+def apply_stats(x, refs, sent_refs, out_refs):
+    left_ref, right_ref = refs
+    grad_ref, new_left_ref, new_right_ref = out_refs
+    own = left_ref.shape[0] // PAIR
+    for side, ref in enumerate(sent_refs):
+        for block in range(own):
+            at = (x ^ side) * own + block
+            grad_ref[at] = ref[0, block].astype(full)
+            new_left_ref[at] = 0.95 * left_ref[at] + 0.05 * ref[1, block].astype(full)
+            new_right_ref[at] = 0.95 * right_ref[at] + 0.05 * ref[2, block].astype(full)
+
+
+def apply_step_rows(order, rates, x, m, weight_ref, sent_refs, out_refs, total_ref=None, row=0):
+    new_ref, half_ref = out_refs
     local = weight_ref.shape[0]
     own = local // PAIR
-    for side, ref in ((0, kept_ref), (1, came_ref)):
+    for side, ref in enumerate(sent_refs):
         for block in range(own):
             at = (x ^ side) * own + block
             rate = jnp.where(m * local + at < rates[0], rates[1], rates[2])
             if total_ref is not None:
-                row = 16 + (side * 2 + matrix) * own + block
-                total = total_ref[row : row + 1, 0:1]
+                index = row + side * 2 * own + block
+                total = total_ref[index : index + 1, 0:1]
                 rate = rate * lax.rsqrt(total / (order * order) + 1e-06)
-            grad_ref[at] = ref[0, block].astype(full)
-            new_left_ref[at] = 0.95 * left_ref[at] + 0.05 * ref[1, block].astype(full)
-            new_right_ref[at] = 0.95 * right_ref[at] + 0.05 * ref[2, block].astype(full)
             new = weight_ref[at] - rate * ref[3, block].astype(full)
             new_ref[at] = new
             half_ref[at] = to_half(new)
+
+
+def apply_kernel(order, rates, place_ref, weight_ref, left_ref, right_ref, *refs):
+    sent_refs, out_refs = refs[:2], refs[2:]
+    x, m = place_ref[1], place_ref[2]
+    apply_stats(x, (left_ref, right_ref), sent_refs, out_refs[:3])
+    apply_step_rows(order, rates, x, m, weight_ref, sent_refs, out_refs[3:])
+
+
+def stats_kernel(place_ref, left_ref, right_ref, *refs):
+    apply_stats(place_ref[1], (left_ref, right_ref), refs[:2], refs[2:])
+
+
+def last_kernel(order, rates, place_ref, *refs):
+    up_weight, down_weight, left_ref, right_ref = refs[:4]
+    up_sent, down_sent, total_ref, vec_ref = refs[4:6], refs[6:8], refs[8], refs[9]
+    outs = refs[10:]
+    x, m = place_ref[1], place_ref[2]
+    own = up_weight.shape[0] // PAIR
+    apply_step_rows(order, rates[0], x, m, up_weight, up_sent, outs[0:2], total_ref, 16)
+    apply_step_rows(order, rates[1], x, m, down_weight, down_sent, outs[2:4], total_ref, 16 + own)
+    apply_stats(x, (left_ref, right_ref), down_sent, outs[4:7])
+    vector_step(vec_ref, total_ref, outs[7], outs[8])
 
 
 def vector_part_kernel(place_ref, one_ref, two_ref, bias_ref, out_ref):
@@ -1028,7 +1076,7 @@
     out_ref[9:, :] = bias_row(place_ref[2], bias_ref[...], out_ref.shape[0] - 9)
 
 
-def vector_step_kernel(vec_ref, total_ref, grad_ref, new_ref):
+def vector_step(vec_ref, total_ref, grad_ref, new_ref):
     rows = vec_ref.shape[0]
     grad_ref[...] = total_ref[:rows, :]
     for start in range(0, vec_ref.shape[1], BLOCK_VEC):
@@ -1217,7 +1265,7 @@
             pltpu.VMEM(heads, full),
             pltpu.SemaphoreType.DMA((count * z_count * row_blocks,)),
             pltpu.SemaphoreType.DMA(()),
-            pltpu.SemaphoreType.DMA((HEADS // 2,)),
+            pltpu.SemaphoreType.DMA(()),
         ),
         in_hbm=range(1, 1 + count),
         out_hbm=(2, 5),
@@ -1261,21 +1309,28 @@
     up_kept, up_sent = local_call(
         lambda *refs: up_grads_kernel(order, *refs),
         (place, all_rows, grad_hidden),
-        (shape((own, order, order)),) * 2,
+        (shape((own, order, order)), shape((own * order, order))),
         scratch=(pltpu.VMEM((local, order, order), half),),
     )
     up_came = move(up_sent, 1, 0)
+    first_rows = order + line_rows
     feed_kept, feed_sent, down_kept, down_first, down_second, bias_sums = local_call(
         lambda *refs: down_grads_kernel(order, group, *refs),
         (place, all_grads, active, grad_hidden, down),
         (shape((group // PAIR, SLOTS, width)),) * 2
         + (shape((own, order, order)),)
-        + (shape((own // 2, order, order)),) * 2
+        + (shape((first_rows, order)), shape((own * order - first_rows, order)))
         + (shape((1, hidden_width), full),),
         scratch=(pltpu.VMEM((local, order, order), half),),
     )
     back, down_first, down_second, feed_sent, all_roots = phase(
         back, down_first, down_second, feed_sent, all_roots
+    )
+
+    (joined_roots,) = local_call(
+        line_roots_kernel,
+        (place, *all_roots),
+        (shape((4 * own, order, order)),),
     )
 
     def rows_of(*groups):
@@ -1308,7 +1363,7 @@
     def step_of(parts, matrix):
         return local_call(
             lambda *refs: step_kernel(z_count, matrix * own, *refs),
-            (place, *parts, *all_roots, left_roots),
+            (place, *parts, joined_roots, left_roots),
             (
                 shape((4, own, piece, order)),
                 shape((5, own, piece, order)),
@@ -1316,13 +1371,12 @@
             ),
             scratch=(
                 pltpu.VMEM((own, order, order), half),
-                pltpu.VMEM((own, order, order), half),
                 pltpu.VMEM((order, order), full),
                 pltpu.VMEM((4, line_rows, order), full),
             ),
             )
 
-    up_near_kept, up_near_sent = pairs_of((up_kept, up_came))
+    up_near_kept, up_near_sent = pairs_of((up_kept, up_came.reshape(own, order, order)))
     up_near = move(up_near_sent, PAIR, 0)
     down_first_came = move(down_first, 1, 0)
     feed_came = move(feed_sent, 0, 1)
@@ -1346,7 +1400,7 @@
             pltpu.SemaphoreType.DMA(()),
         ),
         in_hbm=(1 + group + 6, 1 + group + 9),
-        micros=8,
+        micros=3,
     )
     attn_sent, up_near, down_first_came, feed_came = phase(
         attn_sent, up_near, down_first_came, feed_came
@@ -1373,9 +1427,11 @@
     )
 
     attn_came = [move(part, dx, dm) for (dx, dm), part in zip(plane[1:], core_parts[1:])]
-    middle = own // 2
-    down_near_kept, down_near_sent = pairs_of(
-        (down_kept[:middle], down_first_came), (down_kept[middle:], down_second_came)
+    down_near_kept, down_near_sent = local_call(
+        joined_sum_kernel,
+        (place, down_kept, down_first_came, down_second_came),
+        (shape((z_count // 2, own, line_rows, order)),) * 2,
+        scratch=(pltpu.VMEM((own, order, order), half),),
     )
     down_near = move(down_near_sent, PAIR, 0)
     up_rows = total_of([up_mine, up_far])
@@ -1421,6 +1477,7 @@
     down_kept, down_sent, down_squares = step_of(
         [down_rows, down_pair_came[0], down_whole_far, down_pair_came[1]], 2
     )
+    vector_sum = vector_sum + move(after(vector_sum, down_pair_came), 0, 1)
     attn_split, up_found, down_sent, vector_sum = phase(
         attn_split, up_found, down_sent, vector_sum
     )
@@ -1428,18 +1485,25 @@
     attn_rows = total_of(attn_split)
     attn_parts = [attn_rows] + [move(attn_rows, k * PAIR, 0) for k in lines]
     down_found = move(down_sent, 1, 0)
-    vector_sum = vector_sum + move(vector_sum, 0, 1)
     for dm in range(PAIR, group, PAIR):
         vector_sum = vector_sum + move(vector_sum, 0, dm)
     vector_came = move(vector_sum, 1, 0)
-    attn_parts, down_found, vector_came = phase(attn_parts, down_found, vector_came)
+    stat = shape(w_fc1.shape, full)
+    stats_up = local_call(
+        stats_kernel,
+        (place, left_fc1, right_fc1, up_kept, up_found),
+        (stat,) * 3,
+    )
+    attn_parts, down_found, vector_came, stats_up = phase(
+        attn_parts, down_found, vector_came, stats_up
+    )
 
     kept, sent = local_call(
         lambda *refs: whole_step_kernel(z_count, 3 * own, *refs),
-        (place, *attn_parts, *all_roots),
+        (place, *attn_parts, joined_roots),
         (shape((4, own, piece, order)),) * 2,
-        scratch=(pltpu.VMEM((own, order, order), half),) * 3
-        + (
+        scratch=(
+            pltpu.VMEM((own, order, order), half),
             pltpu.VMEM((order, order), full),
             pltpu.VMEM((4, line_rows, order), full),
             pltpu.VMEM((order, order), full),
@@ -1448,7 +1512,7 @@
     came = move(sent, 1, 0)
     (last_sums,) = local_call(
         last_sums_kernel,
-        (vector_sum, vector_came, up_squares, down_squares, up_found, down_found),
+        (after(vector_sum, sent), vector_came, up_squares, down_squares, up_found, down_found),
         (shape((24, width), full),),
         in_smem=(),
     )
@@ -1456,26 +1520,32 @@
     for k in lines:
         total = total + move(last_sums, k * PAIR, 0)
 
-    def apply(rates, matrix, weight, left, right, *found):
-        stat = shape(weight.shape, full)
-        return local_call(
-            lambda *refs: apply_kernel(order, rates, matrix, *refs),
-            (place, weight, left, right, *found),
-            (stat,) * 4 + (shape(weight.shape),),
-        )
-
     attn_rates = (3 * row_blocks * row_blocks, 0.5 * D ** (-0.5), 0.5 * (D // 16) ** (-0.5))
-    fc1_rates = (0, 0.0, 0.5 * D ** (-0.5))
-    fc2_rates = (0, 0.0, 0.5 * FF ** (-0.5))
-    vector_grad, new_vectors = local_call(
-        vector_step_kernel,
-        (vectors, total),
-        (shape(vectors.shape, full),) * 2,
-        in_smem=(),
-    )
-    done_attn = apply(attn_rates, 0, w_attn, left_attn, right_attn, kept, came)
-    done_fc1 = apply(fc1_rates, 0, w_fc1, left_fc1, right_fc1, up_kept, up_found, total)
-    done_fc2 = apply(fc2_rates, 1, w_fc2, left_fc2, right_fc2, down_kept, down_found, total)
+    fc_rates = ((0, 0.0, 0.5 * D ** (-0.5)), (0, 0.0, 0.5 * FF ** (-0.5)))
+    new_up, half_up, new_down, half_down, *stats_down, vector_grad, new_vectors = local_call(
+        lambda *refs: last_kernel(order, fc_rates, *refs),
+        (
+            place,
+            w_fc1,
+            w_fc2,
+            left_fc2,
+            right_fc2,
+            up_kept,
+            up_found,
+            down_kept,
+            down_found,
+            total,
+            vectors,
+        ),
+        (stat, shape(w_fc1.shape)) * 2 + (stat,) * 3 + (shape(vectors.shape, full),) * 2,
+    )
+    done_attn = local_call(
+        lambda *refs: apply_kernel(order, attn_rates, *refs),
+        (place, w_attn, left_attn, right_attn, kept, came),
+        (stat,) * 4 + (shape(w_attn.shape),),
+    )
+    done_fc1 = (*stats_up, new_up, half_up)
+    done_fc2 = (*stats_down, new_down, half_down)
     return (
         block_out[None],
         input_grad.transpose(1, 0, 2),

time: 204 us -> 201 us (0.985)
  Pallas kernels: 49.5 us -> 44.9 us
  waiting for transfers between devices: 88.3 us -> 91.8 us
    pallas_call x22, Pallas kernels: 49.5 us -> 44.9 us  [local_call(): pl.pallas_call(kernel, out_shape=list(outs), in_specs=[place_of(i, in_hbm...]
    ppermute x38, waiting for transfers between devices: 62.3 us -> 66.3 us  [move(): return lax.ppermute(values, 'dp', [(s, s ^ dp_mask) for s in range(dp)])]
    ppermute x19, starting transfers between devices: 11.7 us -> 9.67 us  [move(): return lax.ppermute(values, 'mp', [(s, s ^ mp_mask) for s in range(mp)])]
  transfers between devices with their start and end apart: 59 -> 59, of which waited for: 28 -> 32; matrix products, arithmetic and copies ran while one was open for 1% -> 1% of each run, Pallas kernels for 22% -> 19%
where the time goes in v6:
time: 201 us
  waiting for transfers between devices  91.8 us (46%)
  starting transfers between devices  61.8 us (31%)
  Pallas kernels  44.9 us (22%)
    ppermute x38, waiting for transfers between devices, move(): return lax.ppermute(values, 'dp', [(s, s ^ dp_mask) for s in range(dp)])  66.3 us
    ppermute x38, starting transfers between devices, move(): return lax.ppermute(values, 'dp', [(s, s ^ dp_mask) for s in range(dp)])  49.1 us
    pallas_call x22, Pallas kernels, local_call(): pl.pallas_call(kernel, out_shape=list(outs), in_specs=[place_of(i, in_hbm...  44.9 us
    ppermute x19, waiting for transfers between devices, move(): return lax.ppermute(values, 'mp', [(s, s ^ mp_mask) for s in range(mp)])  25.5 us
    ppermute x19, starting transfers between devices, move(): return lax.ppermute(values, 'mp', [(s, s ^ mp_mask) for s in range(mp)])  9.67 us
  transfers between devices with their start and end apart: 59, of which 32 were waited for; matrix products, arithmetic and copies ran while one was open for 1% of the time, Pallas kernels for 19%

profile of v6, /device:TPU:0, one launch (start us, length us, event | category | flops | bytes accessed | tf_op | source)
XLA Modules:
  0.0 200.9 jit_solution(6721942552066914106)
XLA Ops:
  0.8 2.3 %shard_map.330 = (bf16[4,48,384]{2,1,0:T(8,128)(2,1)S(1)}, bf16[8,48,384]{2,1,0:T(8,128)(2,1)S(1)}, bf16[6,2,48,384]{3,2,1,0:T(8,128)(2,1)S(1)}, bf16[6,2,48,384]{3,2,1,0:T(8,128)(2,1)S(1)}) custom-call(s32[4]{0:T(128)S(1)} %pad_add_fusion.place_ref.refs_0_, f32[4,48,384]{2,1,0:T(8,128)} %refs_1_.4, f32[4,48,384]{2,1,0:T(8,128)} %refs_1_.5, ...), custom_call_target="tpu_custom_call" | custom-call | flops 50000000 | bytes 50000 | tf_op jit(solution)/shard_map/pallas_call | solution.py:518
  3.1 3.0 %collective-permute-start.3 = (bf16[6,2,48,384]{3,2,1,0:T(8,128)(2,1)S(1)}, bf16[6,2,48,384]{3,2,1,0:T(8,128)(2,1)S(1)}, u32[]{:S(2)}, u32[]{:S(2)}) collective-permute-start(bf16[6,2,48,384]{3,2,1,0:T(8,128)(2,1)S(1)} %get-tuple-element.163), channel_id=1, source_target_pairs={{0,4},{4,0},{8,12},{12,8},{16,20},{20,16},{24,28},{28,24},{1,5},{5... | collective-permute-start | bytes 1327112 | tf_op jit(solution)/shard_map/ppermute | solution.py:1132
  6.1 3.6 %collective-permute-start.2 = (bf16[4,48,384]{2,1,0:T(8,128)(2,1)S(1)}, bf16[4,48,384]{2,1,0:T(8,128)(2,1)S(1)}, u32[]{:S(2)}, u32[]{:S(2)}) collective-permute-start(bf16[4,48,384]{2,1,0:T(8,128)(2,1)S(1)} %get-tuple-element.166), channel_id=1, source_target_pairs={{0,24},{4,28},{8,16},{12,20},{16,8},{20,12},{24,0},{28,4},{1,25},{... | collective-permute-start | bytes 442376 | tf_op jit(solution)/shard_map/ppermute | solution.py:1132
  10.5 4.2 %collective-permute-done.2 = bf16[4,48,384]{2,1,0:T(8,128)(2,1)S(1)} collective-permute-done((bf16[4,48,384]{2,1,0:T(8,128)(2,1)S(1)}, bf16[4,48,384]{2,1,0:T(8,128)(2,1)S(1)}, u32[]{:S(2)}, u32[]{:S(2)}) %collective-permute-start.2) | collective-permute-done | bytes 147488 | tf_op jit(solution)/shard_map/ppermute | solution.py:1132
  14.7 7.2 %collective-permute-done.1 = bf16[4,48,384]{2,1,0:T(8,128)(2,1)S(1)} collective-permute-done((bf16[4,48,384]{2,1,0:T(8,128)(2,1)S(1)}, bf16[4,48,384]{2,1,0:T(8,128)(2,1)S(1)}, u32[]{:S(2)}, u32[]{:S(2)}) %collective-permute-start.1) | collective-permute-done | bytes 147488 | tf_op jit(solution)/shard_map/ppermute | solution.py:1132
  22.0 1.6 collective-permute-start.12
  26.2 3.1 %collective-permute-start.4 = (bf16[24,48,384]{2,1,0:T(8,128)(2,1)S(1)}, bf16[24,48,384]{2,1,0:T(8,128)(2,1)S(1)}, u32[]{:S(2)}, u32[]{:S(2)}) collective-permute-start(bf16[24,48,384]{2,1,0:T(8,128)(2,1)S(1)} %get-tuple-element.165), channel_id=1, source_target_pairs={{0,8},{4,12},{8,0},{12,4},{16,24},{20,28},{24,16},{28,20},{1,9},{5... | collective-permute-start | bytes 2654216 | tf_op jit(solution)/shard_map/ppermute | solution.py:1132
  30.0 9.4 %collective-permute-done.6 = bf16[8,48,384]{2,1,0:T(8,128)(2,1)S(1)} collective-permute-done((bf16[8,48,384]{2,1,0:T(8,128)(2,1)S(1)}, bf16[8,48,384]{2,1,0:T(8,128)(2,1)S(1)}, u32[]{:S(2)}, u32[]{:S(2)}) %collective-permute-start.6) | collective-permute-done | bytes 294944 | tf_op jit(solution)/shard_map/ppermute | solution.py:1132
  41.4 8.5 %collective-permute-done.10.refs_5_ = bf16[4,4,48,384]{3,2,1,0:T(8,128)(2,1)S(1)} collective-permute-done((bf16[4,4,48,384]{3,2,1,0:T(8,128)(2,1)S(1)}, bf16[4,4,48,384]{3,2,1,0:T(8,128)(2,1)S(1)}, u32[]{:S(2)}, u32[]{:S(2)}) %collective-permute-start.10) | collective-permute-done | bytes 589856 | tf_op jit(solution)/shard_map/ppermute | solution.py:1134
  50.6 2.4 %collective-permute-done.4 = bf16[24,48,384]{2,1,0:T(8,128)(2,1)S(1)} collective-permute-done((bf16[24,48,384]{2,1,0:T(8,128)(2,1)S(1)}, bf16[24,48,384]{2,1,0:T(8,128)(2,1)S(1)}, u32[]{:S(2)}, u32[]{:S(2)}) %collective-permute-start.4) | collective-permute-done | bytes 884768 | tf_op jit(solution)/shard_map/ppermute | solution.py:1132
  53.1 2.5 %collective-permute-start.17 = (bf16[8,48,384]{2,1,0:T(8,128)(2,1)S(1)}, bf16[8,48,384]{2,1,0:T(8,128)(2,1)S(1)}, u32[]{:S(2)}, u32[]{:S(2)}) collective-permute-start(bf16[8,48,384]{2,1,0:T(8,128)(2,1)S(1)} %get-tuple-element.304), channel_id=1, source_target_pairs={{0,16},{4,20},{8,24},{12,28},{16,0},{20,4},{24,8},{28,12},{1,17},{... | collective-permute-start | bytes 884744 | tf_op jit(solution)/shard_map/ppermute | solution.py:1132
  57.6 6.1 %shard_map.333 = (bf16[160,768]{1,0:T(8,128)(2,1)S(1)}, bf16[197,2304]{1,0:T(8,128)(2,1)S(1)}, f32[12,197,197]{2,1,0:T(8,128)S(1)}, bf16[197,768]{1,0:T(8,128)(2...) custom-call(s32[4]{0:T(128)S(1)} %pad_add_fusion.place_ref.refs_0_, ...), custom_call_target="tpu_custom_call" | custom-call | flops 8000000000 | bytes 8000000 | tf_op jit(solution)/shard_map/pallas_call | solution.py:518
  63.6 1.6 collective-permute-done.16
  65.2 1.9 collective-permute-done.17
  69.4 10.7 %collective-permute-done.25 = bf16[8,48,384]{2,1,0:T(8,128)(2,1)S(1)} collective-permute-done((bf16[8,48,384]{2,1,0:T(8,128)(2,1)S(1)}, bf16[8,48,384]{2,1,0:T(8,128)(2,1)S(1)}, u32[]{:S(2)}, u32[]{:S(2)}) %collective-permute-start.25) | collective-permute-done | bytes 294944 | tf_op jit(solution)/shard_map/ppermute | solution.py:1132
  81.6 4.6 %shard_map.334 = (bf16[160,768]{1,0:T(8,128)(2,1)S(1)}, bf16[160,768]{1,0:T(8,128)(2,1)S(1)}, bf16[160,768]{1,0:T(8,128)(2,1)S(1)}, bf16[160,768]{1,0:T(8,128)(2...) custom-call(s32[4]{0:T(128)S(1)} %pad_add_fusion.place_ref.refs_0_, ...), custom_call_target="tpu_custom_call" | custom-call | flops 5000000000 | bytes 5000000 | tf_op jit(solution)/shard_map/pallas_call | solution.py:518
  86.2 1.8 shard_map.337
  88.0 1.6 collective-permute-start.27
  91.6 2.6 %shard_map.335 = (bf16[2,160,768]{2,1,0:T(8,128)(2,1)S(1)}, bf16[2,160,768]{2,1,0:T(8,128)(2,1)S(1)}, bf16[2,384,384]{2,1,0:T(8,128)(2,1)S(1)}, bf16[480,384]{1,...) custom-call(s32[4]{0:T(128)S(1)} %pad_add_fusion.place_ref.refs_0_, ...), custom_call_target="tpu_custom_call" | custom-call | flops 50000000 | bytes 50000 | tf_op jit(solution)/shard_map/pallas_call | solution.py:518
  94.1 1.9 collective-permute-done.26.refs_3_
  96.0 2.3 %collective-permute-done.23.refs_3_ = bf16[160,768]{1,0:T(8,128)(2,1)S(1)} collective-permute-done((bf16[160,768]{1,0:T(8,128)(2,1)S(1)}, bf16[160,768]{1,0:T(8,128)(2,1)S(1)}, u32[]{:S(2)}, u32[]{:S(2)}) %collective-permute-start.23) | collective-permute-done | bytes 245792 | tf_op jit(solution)/shard_map/ppermute | solution.py:1134
  98.3 4.5 %collective-permute-done.24.refs_4_ = bf16[160,768]{1,0:T(8,128)(2,1)S(1)} collective-permute-done((bf16[160,768]{1,0:T(8,128)(2,1)S(1)}, bf16[160,768]{1,0:T(8,128)(2,1)S(1)}, u32[]{:S(2)}, u32[]{:S(2)}) %collective-permute-start.24) | collective-permute-done | bytes 245792 | tf_op jit(solution)/shard_map/ppermute | solution.py:1134
  104.5 2.3 %collective-permute-start.28 = (bf16[2,2,96,384]{3,2,1,0:T(8,128)(2,1)S(1)}, bf16[2,2,96,384]{3,2,1,0:T(8,128)(2,1)S(1)}, u32[]{:S(2)}, u32[]{:S(2)}) collective-permute-start(bf16[2,2,96,384]{3,2,1,0:T(8,128)(2,1)S(1)} %get-tuple-element.210), channel_id=1, source_target_pairs={{0,8},{4,12},{8,0},{12,4},{16,24},{20,28},{24,16},{28,20},{1,9},{5... | collective-permute-start | bytes 884744 | tf_op jit(solution)/shard_map/ppermute | solution.py:1132
  106.9 6.5 %shard_map.336 = (bf16[2,4,384,384]{3,2,1,0:T(8,128)(2,1)S(1)}, bf16[2,4,384,384]{3,2,1,0:T(8,128)(2,1)S(1)}, bf16[197,2304]{1,0:T(8,128)(2,1)S(1)}, f32[197,768]{1,0:T(8,128)S(1)}, f32[4,768]{1,0:T(4,128)S(1)}) custom-call(s32[4]{0:T(128)S(1)} %pad_add_fusion.place_ref.refs_0_, bf16[160,768]{1,0:T(8,128)(2,1)S(1)} %get-tuple-element.196.refs_1_, ...), custom_call_target="tpu_custom_call" | custom-call | flops 3000000000 | bytes 3000000 | tf_op jit(solution)/shard_map/pallas_call | solution.py:518
  116.1 1.9 collective-permute-start.40
  119.5 2.1 %collective-permute-done.32.second_ref = bf16[288,384]{1,0:T(8,128)(2,1)S(1)} collective-permute-done((bf16[288,384]{1,0:T(8,128)(2,1)S(1)}, bf16[288,384]{1,0:T(8,128)(2,1)S(1)}, u32[]{:S(2)}, u32[]{:S(2)}) %collective-permute-start.32) | collective-permute-done | bytes 221216 | tf_op jit(solution)/shard_map/ppermute | solution.py:1132
  123.8 1.9 collective-permute-start.37
  129.7 5.7 %collective-permute-done.37 = bf16[2,2,96,384]{3,2,1,0:T(8,128)(2,1)S(1)} collective-permute-done((bf16[2,2,96,384]{3,2,1,0:T(8,128)(2,1)S(1)}, bf16[2,2,96,384]{3,2,1,0:T(8,128)(2,1)S(1)}, u32[]{:S(2)}, u32[]{:S(2)}) %collective-permute-start.37) | collective-permute-done | bytes 294944 | tf_op jit(solution)/shard_map/ppermute | solution.py:1132
  136.1 1.9 collective-permute-start.42
  138.7 3.9 %shard_map.340 = (bf16[197,768]{1,0:T(8,128)(2,1)}, f32[197,1,768]{2,1,0:T(1,128)}, f32[5,768]{1,0:T(8,128)S(1)}) custom-call(bf16[160,768]{1,0:T(8,128)(2,1)S(1)} %get-tuple-element.223.refs_0_, bf16[160,768]{1,0:T(8,128)(2,1)S(1)} %collective-permute-done.33.refs_1_, bf16[197,2304]{1,0:T(8,128)(2,1)S(1)} %get-tuple-element.225.refs_2_, ...), custom_call_target="tpu_custom_call" | custom-call | flops 50000000 | bytes 50000 | tf_op jit(solution)/shard_map/pallas_call | solution.py:518
  144.1 4.4 %collective-permute-done.42 = bf16[2,2,96,384]{3,2,1,0:T(8,128)(2,1)S(1)} collective-permute-done((bf16[2,2,96,384]{3,2,1,0:T(8,128)(2,1)S(1)}, bf16[2,2,96,384]{3,2,1,0:T(8,128)(2,1)S(1)}, u32[]{:S(2)}, u32[]{:S(2)}) %collective-permute-start.42) | collective-permute-done | bytes 294944 | tf_op jit(solution)/shard_map/ppermute | solution.py:1132
  148.6 1.8 shard_map.343
  151.3 2.5 %collective-permute-done.35.refs_3_ = bf16[2,384,384]{2,1,0:T(8,128)(2,1)S(1)} collective-permute-done((bf16[2,384,384]{2,1,0:T(8,128)(2,1)S(1)}, bf16[2,384,384]{2,1,0:T(8,128)(2,1)S(1)}, u32[]{:S(2)}, u32[]{:S(2)}) %collective-permute-start.35) | collective-permute-done | bytes 589856 | tf_op jit(solution)/shard_map/ppermute | solution.py:1134
  153.9 1.8 collective-permute-start.47
  157.9 2.3 %collective-permute-start.44 = (bf16[2,96,384]{2,1,0:T(8,128)(2,1)S(1)}, bf16[2,96,384]{2,1,0:T(8,128)(2,1)S(1)}, u32[]{:S(2)}, u32[]{:S(2)}) collective-permute-start(bf16[2,96,384]{2,1,0:T(8,128)(2,1)S(1)} %get-tuple-element.253), channel_id=1, source_target_pairs={{0,16},{4,20},{8,24},{12,28},{16,0},{20,4},{24,8},{28,12},{1,17},{... | collective-permute-start | bytes 442376 | tf_op jit(solution)/shard_map/ppermute | solution.py:1132
  160.2 1.8 collective-permute-start.45
  162.0 3.2 %collective-permute-done.47 = bf16[2,2,96,384]{3,2,1,0:T(8,128)(2,1)S(1)} collective-permute-done((bf16[2,2,96,384]{3,2,1,0:T(8,128)(2,1)S(1)}, bf16[2,2,96,384]{3,2,1,0:T(8,128)(2,1)S(1)}, u32[]{:S(2)}, u32[]{:S(2)}) %collective-permute-start.47) | collective-permute-done | bytes 294944 | tf_op jit(solution)/shard_map/ppermute | solution.py:1132
  165.2 1.8 shard_map.346
  168.4 3.5 %collective-permute-done.45 = bf16[2,96,384]{2,1,0:T(8,128)(2,1)S(1)} collective-permute-done((bf16[2,96,384]{2,1,0:T(8,128)(2,1)S(1)}, bf16[2,96,384]{2,1,0:T(8,128)(2,1)S(1)}, u32[]{:S(2)}, u32[]{:S(2)}) %collective-permute-start.45) | collective-permute-done | bytes 147488 | tf_op jit(solution)/shard_map/ppermute | solution.py:1132
  173.0 2.0 collective-permute-start.51
  175.0 2.5 %collective-permute-start.49 = (bf16[2,96,384]{2,1,0:T(8,128)(2,1)S(1)}, bf16[2,96,384]{2,1,0:T(8,128)(2,1)S(1)}, u32[]{:S(2)}, u32[]{:S(2)}) collective-permute-start(bf16[2,96,384]{2,1,0:T(8,128)(2,1)S(1)} %add_convert_fusion.2.refs_1_), channel_id=1, source_target_pairs={{0,8},{4,12},{8,0},{12,4},{16,24},{20,28},{24,16},{28,20},{1,9},{5... | collective-permute-start | bytes 442376 | tf_op jit(solution)/shard_map/ppermute | solution.py:1132
  178.4 3.1 %collective-permute-done.53 = f32[13,768]{1,0:T(8,128)S(1)} collective-permute-done((f32[13,768]{1,0:T(8,128)S(1)}, f32[13,768]{1,0:T(8,128)S(1)}, u32[]{:S(2)}, u32[]{:S(2)}) %collective-permute-start.53) | collective-permute-done | bytes 39968 | tf_op jit(solution)/shard_map/ppermute | solution.py:1134
  185.7 2.2 %shard_map.348 = (bf16[4,2,48,384]{3,2,1,0:T(8,128)(2,1)S(1)}, bf16[4,2,48,384]{3,2,1,0:T(8,128)(2,1)S(1)}) custom-call(s32[4]{0:T(128)S(1)} %pad_add_fusion.place_ref.refs_0_, bf16[2,96,384]{2,1,0:T(8,128)(2,1)S(1)} %add_convert_fusion.2.refs_1_, bf16[2,96,384]{2,1,0:T(8,128)(2,1)S(1)} %collective-permute-done.49.refs_2_, ...), custom_call_target="tpu_custom_call" | custom-call | flops 50000000 | bytes 50000 | tf_op jit(solution)/shard_map/pallas_call | solution.py:518
  188.0 2.0 collective-permute-start.58
  190.0 2.5 %collective-permute-start.56 = (f32[24,768]{1,0:T(8,128)S(1)}, f32[24,768]{1,0:T(8,128)S(1)}, u32[]{:S(2)}, u32[]{:S(2)}) collective-permute-start(f32[24,768]{1,0:T(8,128)S(1)} %shard_map.350), channel_id=1, source_target_pairs={{0,8},{4,12},{8,0},{12,4},{16,24},{20,28},{24,16},{28,20},{1,9},{5... | collective-permute-start | bytes 221192 | tf_op jit(solution)/shard_map/ppermute | solution.py:1132
  194.3 1.6 collective-permute-done.57
  195.9 1.9 shard_map.351
  199.2 1.7 shard_map.349
  (142 shorter events, 43.7 us)
Async XLA Ops:
  3.1 18.8 %collective-permute-start.3 = (bf16[6,2,48,384]{3,2,1,0:T(8,128)(2,1)S(1)}, bf16[6,2,48,384]{3,2,1,0:T(8,128)(2,1)S(1)}, u32[]{:S(2)}, u32[]{:S(2)}) collective-permute-start(bf16[6,2,48,384]{3,2,1,0:T(8,128)(2,1)S(1)} %get-tuple-element.163), channel_id=1, source_target_pairs={{0,4},{4,0},{8,12},{12,8},{16,20},{20,16},{24,28},{28,24},{1,5},{5... | collective-permute-start | bytes 1327112 | tf_op jit(solution)/shard_map/ppermute | solution.py:1132
  6.1 8.6 %collective-permute-start.2 = (bf16[4,48,384]{2,1,0:T(8,128)(2,1)S(1)}, bf16[4,48,384]{2,1,0:T(8,128)(2,1)S(1)}, u32[]{:S(2)}, u32[]{:S(2)}) collective-permute-start(bf16[4,48,384]{2,1,0:T(8,128)(2,1)S(1)} %get-tuple-element.166), channel_id=1, source_target_pairs={{0,24},{4,28},{8,16},{12,20},{16,8},{20,12},{24,0},{28,4},{1,25},{... | collective-permute-start | bytes 442376 | tf_op jit(solution)/shard_map/ppermute | solution.py:1132
  9.7 12.2 %collective-permute-start.1 = (bf16[4,48,384]{2,1,0:T(8,128)(2,1)S(1)}, bf16[4,48,384]{2,1,0:T(8,128)(2,1)S(1)}, u32[]{:S(2)}, u32[]{:S(2)}) collective-permute-start(bf16[4,48,384]{2,1,0:T(8,128)(2,1)S(1)} %get-tuple-element.166), channel_id=1, source_target_pairs={{0,16},{4,20},{8,24},{12,28},{16,0},{20,4},{24,8},{28,12},{1,17},{... | collective-permute-start | bytes 442376 | tf_op jit(solution)/shard_map/ppermute | solution.py:1132
  9.7 12.2 %collective-permute-start = (bf16[4,48,384]{2,1,0:T(8,128)(2,1)S(1)}, bf16[4,48,384]{2,1,0:T(8,128)(2,1)S(1)}, u32[]{:S(2)}, u32[]{:S(2)}) collective-permute-start(bf16[4,48,384]{2,1,0:T(8,128)(2,1)S(1)} %get-tuple-element.166), channel_id=1, source_target_pairs={{0,8},{4,12},{8,0},{12,4},{16,24},{20,28},{24,16},{28,20},{1,9},{5... | collective-permute-start | bytes 442376 | tf_op jit(solution)/shard_map/ppermute | solution.py:1132
  22.0 19.1 %collective-permute-start.12 = (bf16[4,4,48,384]{3,2,1,0:T(8,128)(2,1)S(1)}, bf16[4,4,48,384]{3,2,1,0:T(8,128)(2,1)S(1)}, u32[]{:S(2)}, u32[]{:S(2)}) collective-permute-start(bf16[4,4,48,384]{3,2,1,0:T(8,128)(2,1)S(1)} %pad_maximum_fusion.1.refs_1_), channel_id=1, source_target_pairs={{0,6},{1,7},{2,4},{3,5},{4,2},{5,3},{6,0},{7,1},{8,14},{9,15},{10,... | collective-permute-start | bytes 1769480 | tf_op jit(solution)/shard_map/ppermute | solution.py:1136
  23.5 26.4 %collective-permute-start.10 = (bf16[4,4,48,384]{3,2,1,0:T(8,128)(2,1)S(1)}, bf16[4,4,48,384]{3,2,1,0:T(8,128)(2,1)S(1)}, u32[]{:S(2)}, u32[]{:S(2)}) collective-permute-start(bf16[4,4,48,384]{3,2,1,0:T(8,128)(2,1)S(1)} %pad_maximum_fusion.1.refs_1_), channel_id=1, source_target_pairs={{0,2},{1,3},{2,0},{3,1},{4,6},{5,7},{6,4},{7,5},{8,10},{9,11},{10,... | collective-permute-start | bytes 1769480 | tf_op jit(solution)/shard_map/ppermute | solution.py:1134
  24.0 26.0 %collective-permute-start.8 = (bf16[4,4,48,384]{3,2,1,0:T(8,128)(2,1)S(1)}, bf16[4,4,48,384]{3,2,1,0:T(8,128)(2,1)S(1)}, u32[]{:S(2)}, u32[]{:S(2)}) collective-permute-start(bf16[4,4,48,384]{3,2,1,0:T(8,128)(2,1)S(1)} %pad_maximum_fusion.1.refs_1_), channel_id=1, source_target_pairs={{0,4},{4,0},{8,12},{12,8},{16,20},{20,16},{24,28},{28,24},{1,5},{5... | collective-permute-start | bytes 1769480 | tf_op jit(solution)/shard_map/ppermute | solution.py:1132
  25.5 13.9 %collective-permute-start.6 = (bf16[8,48,384]{2,1,0:T(8,128)(2,1)S(1)}, bf16[8,48,384]{2,1,0:T(8,128)(2,1)S(1)}, u32[]{:S(2)}, u32[]{:S(2)}) collective-permute-start(bf16[8,48,384]{2,1,0:T(8,128)(2,1)S(1)} %get-tuple-element.160.feed_ref), channel_id=1, source_target_pairs={{0,16},{4,20},{8,24},{12,28},{16,0},{20,4},{24,8},{28,12},{1,17},{... | collective-permute-start | bytes 884744 | tf_op jit(solution)/shard_map/ppermute | solution.py:1132
  26.2 26.7 %collective-permute-start.4 = (bf16[24,48,384]{2,1,0:T(8,128)(2,1)S(1)}, bf16[24,48,384]{2,1,0:T(8,128)(2,1)S(1)}, u32[]{:S(2)}, u32[]{:S(2)}) collective-permute-start(bf16[24,48,384]{2,1,0:T(8,128)(2,1)S(1)} %get-tuple-element.165), channel_id=1, source_target_pairs={{0,8},{4,12},{8,0},{12,4},{16,24},{20,28},{24,16},{28,20},{1,9},{5... | collective-permute-start | bytes 2654216 | tf_op jit(solution)/shard_map/ppermute | solution.py:1132
  40.9 12.1 %collective-permute-start.7 = (bf16[4,4,48,384]{3,2,1,0:T(8,128)(2,1)S(1)}, bf16[4,4,48,384]{3,2,1,0:T(8,128)(2,1)S(1)}, u32[]{:S(2)}, u32[]{:S(2)}) collective-permute-start(bf16[4,4,48,384]{3,2,1,0:T(8,128)(2,1)S(1)} %pad_maximum_fusion.1.refs_1_), channel_id=1, source_target_pairs={{0,1},{1,0},{2,3},{3,2},{4,5},{5,4},{6,7},{7,6},{8,9},{9,8},{10,11... | collective-permute-start | bytes 1769480 | tf_op jit(solution)/shard_map/ppermute | solution.py:1134
  41.1 14.4 %collective-permute-start.13 = (bf16[4,4,48,384]{3,2,1,0:T(8,128)(2,1)S(1)}, bf16[4,4,48,384]{3,2,1,0:T(8,128)(2,1)S(1)}, u32[]{:S(2)}, u32[]{:S(2)}) collective-permute-start(bf16[4,4,48,384]{3,2,1,0:T(8,128)(2,1)S(1)} %collective-permute-done.12.refs_7_), channel_id=1, source_target_pairs={{0,1},{1,0},{2,3},{3,2},{4,5},{5,4},{6,7},{7,6},{8,9},{9,8},{10,11... | collective-permute-start | bytes 1769480 | tf_op jit(solution)/shard_map/ppermute | solution.py:1134
  49.9 7.1 %collective-permute-start.11 = (bf16[4,4,48,384]{3,2,1,0:T(8,128)(2,1)S(1)}, bf16[4,4,48,384]{3,2,1,0:T(8,128)(2,1)S(1)}, u32[]{:S(2)}, u32[]{:S(2)}) collective-permute-start(bf16[4,4,48,384]{3,2,1,0:T(8,128)(2,1)S(1)} %collective-permute-done.10.refs_5_), channel_id=1, source_target_pairs={{0,1},{1,0},{2,3},{3,2},{4,5},{5,4},{6,7},{7,6},{8,9},{9,8},{10,11... | collective-permute-start | bytes 1769480 | tf_op jit(solution)/shard_map/ppermute | solution.py:1134
  50.0 7.5 %collective-permute-start.9 = (bf16[4,4,48,384]{3,2,1,0:T(8,128)(2,1)S(1)}, bf16[4,4,48,384]{3,2,1,0:T(8,128)(2,1)S(1)}, u32[]{:S(2)}, u32[]{:S(2)}) collective-permute-start(bf16[4,4,48,384]{3,2,1,0:T(8,128)(2,1)S(1)} %collective-permute-done.8.refs_3_), channel_id=1, source_target_pairs={{0,1},{1,0},{2,3},{3,2},{4,5},{5,4},{6,7},{7,6},{8,9},{9,8},{10,11... | collective-permute-start | bytes 1769480 | tf_op jit(solution)/shard_map/ppermute | solution.py:1134
  52.9 12.3 %collective-permute-start.16 = (bf16[8,48,384]{2,1,0:T(8,128)(2,1)S(1)}, bf16[8,48,384]{2,1,0:T(8,128)(2,1)S(1)}, u32[]{:S(2)}, u32[]{:S(2)}) collective-permute-start(bf16[8,48,384]{2,1,0:T(8,128)(2,1)S(1)} %collective-permute-done.6), channel_id=1, source_target_pairs={{0,8},{4,12},{8,0},{12,4},{16,24},{20,28},{24,16},{28,20},{1,9},{5... | collective-permute-start | bytes 884744 | tf_op jit(solution)/shard_map/ppermute | solution.py:1132
  53.1 14.1 %collective-permute-start.17 = (bf16[8,48,384]{2,1,0:T(8,128)(2,1)S(1)}, bf16[8,48,384]{2,1,0:T(8,128)(2,1)S(1)}, u32[]{:S(2)}, u32[]{:S(2)}) collective-permute-start(bf16[8,48,384]{2,1,0:T(8,128)(2,1)S(1)} %get-tuple-element.304), channel_id=1, source_target_pairs={{0,16},{4,20},{8,24},{12,28},{16,0},{20,4},{24,8},{28,12},{1,17},{... | collective-permute-start | bytes 884744 | tf_op jit(solution)/shard_map/ppermute | solution.py:1132
  55.5 11.6 %collective-permute-start.15 = (bf16[2,160,768]{2,1,0:T(8,128)(2,1)S(1)}, bf16[2,160,768]{2,1,0:T(8,128)(2,1)S(1)}, u32[]{:S(2)}, u32[]{:S(2)}) collective-permute-start(bf16[2,160,768]{2,1,0:T(8,128)(2,1)S(1)} %pad_maximum_fusion.3.refs_9_), channel_id=1, source_target_pairs={{0,2},{1,3},{2,0},{3,1},{4,6},{5,7},{6,4},{7,5},{8,10},{9,11},{10,... | collective-permute-start | bytes 1474568 | tf_op jit(solution)/shard_map/ppermute | solution.py:1134
  57.1 24.6 %collective-permute-start.5 = (bf16[2,8,48,384]{3,2,1,0:T(8,128)(2,1)S(1)}, bf16[2,8,48,384]{3,2,1,0:T(8,128)(2,1)S(1)}, u32[]{:S(2)}, u32[]{:S(2)}) collective-permute-start(bf16[2,8,48,384]{3,2,1,0:T(8,128)(2,1)S(1)} %pad_maximum_fusion.refs_1_), channel_id=1, source_target_pairs={{0,4},{4,0},{8,12},{12,8},{16,20},{20,16},{24,28},{28,24},{1,5},{5... | collective-permute-start | bytes 1769480 | tf_op jit(solution)/shard_map/ppermute | solution.py:1132
  67.2 14.4 %collective-permute-start.18 = (bf16[2,8,48,384]{3,2,1,0:T(8,128)(2,1)S(1)}, bf16[2,8,48,384]{3,2,1,0:T(8,128)(2,1)S(1)}, u32[]{:S(2)}, u32[]{:S(2)}) collective-permute-start(bf16[2,8,48,384]{3,2,1,0:T(8,128)(2,1)S(1)} %pad_maximum_fusion.2.refs_3_), channel_id=1, source_target_pairs={{0,4},{4,0},{8,12},{12,8},{16,20},{20,16},{24,28},{28,24},{1,5},{5... | collective-permute-start | bytes 1769480 | tf_op jit(solution)/shard_map/ppermute | solution.py:1132
  67.8 12.3 %collective-permute-start.25 = (bf16[8,48,384]{2,1,0:T(8,128)(2,1)S(1)}, bf16[8,48,384]{2,1,0:T(8,128)(2,1)S(1)}, u32[]{:S(2)}, u32[]{:S(2)}) collective-permute-start(bf16[8,48,384]{2,1,0:T(8,128)(2,1)S(1)} %get-tuple-element.303), channel_id=1, source_target_pairs={{0,16},{4,20},{8,24},{12,28},{16,0},{20,4},{24,8},{28,12},{1,17},{... | collective-permute-start | bytes 884744 | tf_op jit(solution)/shard_map/ppermute | solution.py:1132
  67.9 12.3 %collective-permute-start.21 = (bf16[160,768]{1,0:T(8,128)(2,1)S(1)}, bf16[160,768]{1,0:T(8,128)(2,1)S(1)}, u32[]{:S(2)}, u32[]{:S(2)}) collective-permute-start(bf16[160,768]{1,0:T(8,128)(2,1)S(1)} %get-tuple-element.176.refs_5_), channel_id=1, source_target_pairs={{0,3},{1,2},{2,1},{3,0},{4,7},{5,6},{6,5},{7,4},{8,11},{9,10},{10,... | collective-permute-start | bytes 737288 | tf_op jit(solution)/shard_map/ppermute | solution.py:1134
  67.9 13.5 %collective-permute-start.20 = (bf16[160,768]{1,0:T(8,128)(2,1)S(1)}, bf16[160,768]{1,0:T(8,128)(2,1)S(1)}, u32[]{:S(2)}, u32[]{:S(2)}) collective-permute-start(bf16[160,768]{1,0:T(8,128)(2,1)S(1)} %get-tuple-element.176.refs_5_), channel_id=1, source_target_pairs={{0,2},{1,3},{2,0},{3,1},{4,6},{5,7},{6,4},{7,5},{8,10},{9,11},{10,... | collective-permute-start | bytes 737288 | tf_op jit(solution)/shard_map/ppermute | solution.py:1134
  80.2 15.8 %collective-permute-start.26 = (bf16[16,48,384]{2,1,0:T(8,128)(2,1)S(1)}, bf16[16,48,384]{2,1,0:T(8,128)(2,1)S(1)}, u32[]{:S(2)}, u32[]{:S(2)}) collective-permute-start(bf16[16,48,384]{2,1,0:T(8,128)(2,1)S(1)} %constant_dynamic-update-slice_fusion.refs_2_), channel_id=1, source_target_pairs={{0,8},{4,12},{8,0},{12,4},{16,24},{20,28},{24,16},{28,20},{1,9},{5... | collective-permute-start | bytes 1769480 | tf_op jit(solution)/shard_map/ppermute | solution.py:1132
  88.0 15.8 %collective-permute-start.27 = (bf16[768,384]{1,0:T(8,128)(2,1)S(1)}, bf16[768,384]{1,0:T(8,128)(2,1)S(1)}, u32[]{:S(2)}, u32[]{:S(2)}) collective-permute-start(bf16[768,384]{1,0:T(8,128)(2,1)S(1)} %get-tuple-element.209), channel_id=1, source_target_pairs={{0,4},{4,0},{8,12},{12,8},{16,20},{20,16},{24,28},{28,24},{1,5},{5... | collective-permute-start | bytes 1769480 | tf_op jit(solution)/shard_map/ppermute | solution.py:1132
  89.6 8.8 %collective-permute-start.23 = (bf16[160,768]{1,0:T(8,128)(2,1)S(1)}, bf16[160,768]{1,0:T(8,128)(2,1)S(1)}, u32[]{:S(2)}, u32[]{:S(2)}) collective-permute-start(bf16[160,768]{1,0:T(8,128)(2,1)S(1)} %get-tuple-element.186), channel_id=1, source_target_pairs={{0,2},{1,3},{2,0},{3,1},{4,6},{5,7},{6,4},{7,5},{8,10},{9,11},{10,... | collective-permute-start | bytes 737288 | tf_op jit(solution)/shard_map/ppermute | solution.py:1134
  90.1 12.7 %collective-permute-start.24 = (bf16[160,768]{1,0:T(8,128)(2,1)S(1)}, bf16[160,768]{1,0:T(8,128)(2,1)S(1)}, u32[]{:S(2)}, u32[]{:S(2)}) collective-permute-start(bf16[160,768]{1,0:T(8,128)(2,1)S(1)} %get-tuple-element.187), channel_id=1, source_target_pairs={{0,3},{1,2},{2,1},{3,0},{4,7},{5,6},{6,5},{7,4},{8,11},{9,10},{10,... | collective-permute-start | bytes 737288 | tf_op jit(solution)/shard_map/ppermute | solution.py:1134
  102.8 11.0 %collective-permute-start.30 = (bf16[2,160,768]{2,1,0:T(8,128)(2,1)S(1)}, bf16[2,160,768]{2,1,0:T(8,128)(2,1)S(1)}, u32[]{:S(2)}, u32[]{:S(2)}) collective-permute-start(bf16[2,160,768]{2,1,0:T(8,128)(2,1)S(1)} %get-tuple-element.212), channel_id=1, source_target_pairs={{0,1},{1,0},{2,3},{3,2},{4,5},{5,4},{6,7},{7,6},{8,9},{9,8},{10,11... | collective-permute-start | bytes 1474568 | tf_op jit(solution)/shard_map/ppermute | solution.py:1134
  103.3 10.5 %collective-permute-start.29 = (bf16[480,384]{1,0:T(8,128)(2,1)S(1)}, bf16[480,384]{1,0:T(8,128)(2,1)S(1)}, u32[]{:S(2)}, u32[]{:S(2)}) collective-permute-start(bf16[480,384]{1,0:T(8,128)(2,1)S(1)} %get-tuple-element.211), channel_id=1, source_target_pairs={{0,4},{4,0},{8,12},{12,8},{16,20},{20,16},{24,28},{28,24},{1,5},{5... | collective-permute-start | bytes 1105928 | tf_op jit(solution)/shard_map/ppermute | solution.py:1132
  104.5 9.3 %collective-permute-start.28 = (bf16[2,2,96,384]{3,2,1,0:T(8,128)(2,1)S(1)}, bf16[2,2,96,384]{3,2,1,0:T(8,128)(2,1)S(1)}, u32[]{:S(2)}, u32[]{:S(2)}) collective-permute-start(bf16[2,2,96,384]{3,2,1,0:T(8,128)(2,1)S(1)} %get-tuple-element.210), channel_id=1, source_target_pairs={{0,8},{4,12},{8,0},{12,4},{16,24},{20,28},{24,16},{28,20},{1,9},{5... | collective-permute-start | bytes 884744 | tf_op jit(solution)/shard_map/ppermute | solution.py:1132
  113.8 7.8 %collective-permute-start.32 = (bf16[288,384]{1,0:T(8,128)(2,1)S(1)}, bf16[288,384]{1,0:T(8,128)(2,1)S(1)}, u32[]{:S(2)}, u32[]{:S(2)}) collective-permute-start(bf16[288,384]{1,0:T(8,128)(2,1)S(1)} %get-tuple-element.220), channel_id=1, source_target_pairs={{0,4},{4,0},{8,12},{12,8},{16,20},{20,16},{24,28},{28,24},{1,5},{5... | collective-permute-start | bytes 663560 | tf_op jit(solution)/shard_map/ppermute | solution.py:1132
  114.9 8.2 %collective-permute-start.33 = (bf16[160,768]{1,0:T(8,128)(2,1)S(1)}, bf16[160,768]{1,0:T(8,128)(2,1)S(1)}, u32[]{:S(2)}, u32[]{:S(2)}) collective-permute-start(bf16[160,768]{1,0:T(8,128)(2,1)S(1)} %get-tuple-element.301), channel_id=1, source_target_pairs={{0,2},{1,3},{2,0},{3,1},{4,6},{5,7},{6,4},{7,5},{8,10},{9,11},{10,... | collective-permute-start | bytes 737288 | tf_op jit(solution)/shard_map/ppermute | solution.py:1134
  116.1 9.8 %collective-permute-start.40 = (bf16[2,96,384]{2,1,0:T(8,128)(2,1)S(1)}, bf16[2,96,384]{2,1,0:T(8,128)(2,1)S(1)}, u32[]{:S(2)}, u32[]{:S(2)}) collective-permute-start(bf16[2,96,384]{2,1,0:T(8,128)(2,1)S(1)} %get-tuple-element.305), channel_id=1, source_target_pairs={{0,16},{4,20},{8,24},{12,28},{16,0},{20,4},{24,8},{28,12},{1,17},{... | collective-permute-start | bytes 442376 | tf_op jit(solution)/shard_map/ppermute | solution.py:1132
  123.8 11.6 %collective-permute-start.37 = (bf16[2,2,96,384]{3,2,1,0:T(8,128)(2,1)S(1)}, bf16[2,2,96,384]{3,2,1,0:T(8,128)(2,1)S(1)}, u32[]{:S(2)}, u32[]{:S(2)}) collective-permute-start(bf16[2,2,96,384]{3,2,1,0:T(8,128)(2,1)S(1)} %get-tuple-element.237), channel_id=1, source_target_pairs={{0,8},{4,12},{8,0},{12,4},{16,24},{20,28},{24,16},{28,20},{1,9},{5... | collective-permute-start | bytes 884744 | tf_op jit(solution)/shard_map/ppermute | solution.py:1132
  125.9 10.2 %collective-permute-start.41 = (bf16[2,96,384]{2,1,0:T(8,128)(2,1)S(1)}, bf16[2,96,384]{2,1,0:T(8,128)(2,1)S(1)}, u32[]{:S(2)}, u32[]{:S(2)}) collective-permute-start(bf16[2,96,384]{2,1,0:T(8,128)(2,1)S(1)} %add_convert_fusion.3.refs_1_), channel_id=1, source_target_pairs={{0,16},{4,20},{8,24},{12,28},{16,0},{20,4},{24,8},{28,12},{1,17},{... | collective-permute-start | bytes 442376 | tf_op jit(solution)/shard_map/ppermute | solution.py:1132
  126.2 25.1 %collective-permute-start.34 = (bf16[2,384,384]{2,1,0:T(8,128)(2,1)S(1)}, bf16[2,384,384]{2,1,0:T(8,128)(2,1)S(1)}, u32[]{:S(2)}, u32[]{:S(2)}) collective-permute-start(bf16[2,384,384]{2,1,0:T(8,128)(2,1)S(1)} %get-tuple-element.230), channel_id=1, source_target_pairs={{0,4},{4,0},{8,12},{12,8},{16,20},{20,16},{24,28},{28,24},{1,5},{5... | collective-permute-start | bytes 1769480 | tf_op jit(solution)/shard_map/ppermute | solution.py:1132
  127.4 26.5 %collective-permute-start.35 = (bf16[2,384,384]{2,1,0:T(8,128)(2,1)S(1)}, bf16[2,384,384]{2,1,0:T(8,128)(2,1)S(1)}, u32[]{:S(2)}, u32[]{:S(2)}) collective-permute-start(bf16[2,384,384]{2,1,0:T(8,128)(2,1)S(1)} %get-tuple-element.231), channel_id=1, source_target_pairs={{0,2},{1,3},{2,0},{3,1},{4,6},{5,7},{6,4},{7,5},{8,10},{9,11},{10,... | collective-permute-start | bytes 1769480 | tf_op jit(solution)/shard_map/ppermute | solution.py:1134
  128.2 25.7 %collective-permute-start.36 = (bf16[2,384,384]{2,1,0:T(8,128)(2,1)S(1)}, bf16[2,384,384]{2,1,0:T(8,128)(2,1)S(1)}, u32[]{:S(2)}, u32[]{:S(2)}) collective-permute-start(bf16[2,384,384]{2,1,0:T(8,128)(2,1)S(1)} %get-tuple-element.232), channel_id=1, source_target_pairs={{0,6},{1,7},{2,4},{3,5},{4,2},{5,3},{6,0},{7,1},{8,14},{9,15},{10,... | collective-permute-start | bytes 1769480 | tf_op jit(solution)/shard_map/ppermute | solution.py:1136
  135.4 7.9 %collective-permute-start.38 = (bf16[2,96,384]{2,1,0:T(8,128)(2,1)S(1)}, bf16[2,96,384]{2,1,0:T(8,128)(2,1)S(1)}, u32[]{:S(2)}, u32[]{:S(2)}) collective-permute-start(bf16[2,96,384]{2,1,0:T(8,128)(2,1)S(1)} %fusion.5), channel_id=1, source_target_pairs={{0,16},{4,20},{8,24},{12,28},{16,0},{20,4},{24,8},{28,12},{1,17},{... | collective-permute-start | bytes 442376 | tf_op jit(solution)/shard_map/ppermute | solution.py:1132
  136.1 12.5 %collective-permute-start.42 = (bf16[2,2,96,384]{3,2,1,0:T(8,128)(2,1)S(1)}, bf16[2,2,96,384]{3,2,1,0:T(8,128)(2,1)S(1)}, u32[]{:S(2)}, u32[]{:S(2)}) collective-permute-start(bf16[2,2,96,384]{3,2,1,0:T(8,128)(2,1)S(1)} %pad_maximum_fusion.4), channel_id=1, source_target_pairs={{0,8},{4,12},{8,0},{12,4},{16,24},{20,28},{24,16},{28,20},{1,9},{5... | collective-permute-start | bytes 884744 | tf_op jit(solution)/shard_map/ppermute | solution.py:1132
  143.4 8.0 %collective-permute-start.39 = (bf16[2,96,384]{2,1,0:T(8,128)(2,1)S(1)}, bf16[2,96,384]{2,1,0:T(8,128)(2,1)S(1)}, u32[]{:S(2)}, u32[]{:S(2)}) collective-permute-start(bf16[2,96,384]{2,1,0:T(8,128)(2,1)S(1)} %fusion.refs_1_), channel_id=1, source_target_pairs={{0,16},{4,20},{8,24},{12,28},{16,0},{20,4},{24,8},{28,12},{1,17},{... | collective-permute-start | bytes 442376 | tf_op jit(solution)/shard_map/ppermute | solution.py:1132
  153.9 11.3 %collective-permute-start.47 = (bf16[2,2,96,384]{3,2,1,0:T(8,128)(2,1)S(1)}, bf16[2,2,96,384]{3,2,1,0:T(8,128)(2,1)S(1)}, u32[]{:S(2)}, u32[]{:S(2)}) collective-permute-start(bf16[2,2,96,384]{3,2,1,0:T(8,128)(2,1)S(1)} %pad_maximum_fusion.5), channel_id=1, source_target_pairs={{0,8},{4,12},{8,0},{12,4},{16,24},{20,28},{24,16},{28,20},{1,9},{5... | collective-permute-start | bytes 884744 | tf_op jit(solution)/shard_map/ppermute | solution.py:1132
  155.7 16.3 %collective-permute-start.46 = (bf16[5,2,48,384]{3,2,1,0:T(8,128)(2,1)S(1)}, bf16[5,2,48,384]{3,2,1,0:T(8,128)(2,1)S(1)}, u32[]{:S(2)}, u32[]{:S(2)}) collective-permute-start(bf16[5,2,48,384]{3,2,1,0:T(8,128)(2,1)S(1)} %get-tuple-element.255), channel_id=1, source_target_pairs={{0,4},{4,0},{8,12},{12,8},{16,20},{20,16},{24,28},{28,24},{1,5},{5... | collective-permute-start | bytes 1105928 | tf_op jit(solution)/shard_map/ppermute | solution.py:1132
  157.6 10.9 %collective-permute-start.43 = (bf16[2,96,384]{2,1,0:T(8,128)(2,1)S(1)}, bf16[2,96,384]{2,1,0:T(8,128)(2,1)S(1)}, u32[]{:S(2)}, u32[]{:S(2)}) collective-permute-start(bf16[2,96,384]{2,1,0:T(8,128)(2,1)S(1)} %get-tuple-element.252), channel_id=1, source_target_pairs={{0,8},{4,12},{8,0},{12,4},{16,24},{20,28},{24,16},{28,20},{1,9},{5... | collective-permute-start | bytes 442376 | tf_op jit(solution)/shard_map/ppermute | solution.py:1132
  157.9 10.5 %collective-permute-start.44 = (bf16[2,96,384]{2,1,0:T(8,128)(2,1)S(1)}, bf16[2,96,384]{2,1,0:T(8,128)(2,1)S(1)}, u32[]{:S(2)}, u32[]{:S(2)}) collective-permute-start(bf16[2,96,384]{2,1,0:T(8,128)(2,1)S(1)} %get-tuple-element.253), channel_id=1, source_target_pairs={{0,16},{4,20},{8,24},{12,28},{16,0},{20,4},{24,8},{28,12},{1,17},{... | collective-permute-start | bytes 442376 | tf_op jit(solution)/shard_map/ppermute | solution.py:1132
  160.2 11.7 %collective-permute-start.45 = (bf16[2,96,384]{2,1,0:T(8,128)(2,1)S(1)}, bf16[2,96,384]{2,1,0:T(8,128)(2,1)S(1)}, u32[]{:S(2)}, u32[]{:S(2)}) collective-permute-start(bf16[2,96,384]{2,1,0:T(8,128)(2,1)S(1)} %get-tuple-element.254), channel_id=1, source_target_pairs={{0,24},{4,28},{8,16},{12,20},{16,8},{20,12},{24,0},{28,4},{1,25},{... | collective-permute-start | bytes 442376 | tf_op jit(solution)/shard_map/ppermute | solution.py:1132
  172.0 13.7 %collective-permute-start.52 = (bf16[5,2,48,384]{3,2,1,0:T(8,128)(2,1)S(1)}, bf16[5,2,48,384]{3,2,1,0:T(8,128)(2,1)S(1)}, u32[]{:S(2)}, u32[]{:S(2)}) collective-permute-start(bf16[5,2,48,384]{3,2,1,0:T(8,128)(2,1)S(1)} %get-tuple-element.265), channel_id=1, source_target_pairs={{0,4},{4,0},{8,12},{12,8},{16,20},{20,16},{24,28},{28,24},{1,5},{5... | collective-permute-start | bytes 1105928 | tf_op jit(solution)/shard_map/ppermute | solution.py:1132
  173.0 12.7 %collective-permute-start.51 = (bf16[2,96,384]{2,1,0:T(8,128)(2,1)S(1)}, bf16[2,96,384]{2,1,0:T(8,128)(2,1)S(1)}, u32[]{:S(2)}, u32[]{:S(2)}) collective-permute-start(bf16[2,96,384]{2,1,0:T(8,128)(2,1)S(1)} %add_convert_fusion.2.refs_1_), channel_id=1, source_target_pairs={{0,24},{4,28},{8,16},{12,20},{16,8},{20,12},{24,0},{28,4},{1,25},{... | collective-permute-start | bytes 442376 | tf_op jit(solution)/shard_map/ppermute | solution.py:1132
  175.0 10.7 %collective-permute-start.50 = (bf16[2,96,384]{2,1,0:T(8,128)(2,1)S(1)}, bf16[2,96,384]{2,1,0:T(8,128)(2,1)S(1)}, u32[]{:S(2)}, u32[]{:S(2)}) collective-permute-start(bf16[2,96,384]{2,1,0:T(8,128)(2,1)S(1)} %add_convert_fusion.2.refs_1_), channel_id=1, source_target_pairs={{0,16},{4,20},{8,24},{12,28},{16,0},{20,4},{24,8},{28,12},{1,17},{... | collective-permute-start | bytes 442376 | tf_op jit(solution)/shard_map/ppermute | solution.py:1132
  175.0 10.7 %collective-permute-start.49 = (bf16[2,96,384]{2,1,0:T(8,128)(2,1)S(1)}, bf16[2,96,384]{2,1,0:T(8,128)(2,1)S(1)}, u32[]{:S(2)}, u32[]{:S(2)}) collective-permute-start(bf16[2,96,384]{2,1,0:T(8,128)(2,1)S(1)} %add_convert_fusion.2.refs_1_), channel_id=1, source_target_pairs={{0,8},{4,12},{8,0},{12,4},{16,24},{20,28},{24,16},{28,20},{1,9},{5... | collective-permute-start | bytes 442376 | tf_op jit(solution)/shard_map/ppermute | solution.py:1132
  (24 other events, 278.2 us)

commit v7 on v6

--- a/solution.py
+++ b/solution.py
@@ -1275,7 +1275,8 @@
         rows_sent, group_grads, feed_last, roots_first_far
     )
 
-    group_rows = [rows_sent] + [move(rows_sent, 0, k) for k in others]
+    rows_y = move(rows_sent, 0, PAIR)
+    group_rows = [rows_sent, move(rows_sent, 0, 1), rows_y, move(rows_y, 0, 1)]
     feed_far = jnp.stack([feed_far, feed_last])
     feed_far_came = move(feed_far, 1, 0)
     roots_second_far = move(roots_second, 2 * PAIR, 0)

time: 201 us -> 201 us (level)
    ppermute x38, waiting for transfers between devices: 66.3 us -> 63.2 us  [move(): return lax.ppermute(values, 'dp', [(s, s ^ dp_mask) for s in range(dp)])]
    ppermute x19, waiting for transfers between devices: 25.5 us -> 28.5 us  [move(): return lax.ppermute(values, 'mp', [(s, s ^ mp_mask) for s in range(mp)])]
where the time goes in v7:
time: 201 us; the launch traced here: 200 us
  waiting for transfers between devices  91.7 us (46%)
  starting transfers between devices  61.4 us (31%)
  Pallas kernels  44.9 us (22%)
    ppermute x38, waiting for transfers between devices, move(): return lax.ppermute(values, 'dp', [(s, s ^ dp_mask) for s in range(dp)])  63.2 us
    ppermute x38, starting transfers between devices, move(): return lax.ppermute(values, 'dp', [(s, s ^ dp_mask) for s in range(dp)])  48.7 us
    pallas_call x22, Pallas kernels, local_call(): pl.pallas_call(kernel, out_shape=list(outs), in_specs=[place_of(i, in_hbm...  44.9 us
    ppermute x19, waiting for transfers between devices, move(): return lax.ppermute(values, 'mp', [(s, s ^ mp_mask) for s in range(mp)])  28.5 us
    ppermute x19, starting transfers between devices, move(): return lax.ppermute(values, 'mp', [(s, s ^ mp_mask) for s in range(mp)])  9.67 us
  transfers between devices with their start and end apart: 59, of which 32 were waited for; matrix products, arithmetic and copies ran while one was open for 1% of the time, Pallas kernels for 19%

profile of v7, /device:TPU:0, one launch (start us, length us, event | category | flops | bytes accessed | tf_op | source)
XLA Modules:
  0.0 200.5 jit_solution(17426525283399606854)
XLA Ops:
  0.8 2.3 %shard_map.330 = (bf16[4,48,384]{2,1,0:T(8,128)(2,1)S(1)}, bf16[8,48,384]{2,1,0:T(8,128)(2,1)S(1)}, bf16[6,2,48,384]{3,2,1,0:T(8,128)(2,1)S(1)}, bf16[6,2,48,384]{3,2,1,0:T(8,128)(2,1)S(1)}) custom-call(s32[4]{0:T(128)S(1)} %pad_add_fusion.place_ref.refs_0_, f32[4,48,384]{2,1,0:T(8,128)} %refs_1_.4, f32[4,48,384]{2,1,0:T(8,128)} %refs_1_.5, ...), custom_call_target="tpu_custom_call" | custom-call | flops 50000000 | bytes 50000 | tf_op jit(solution)/shard_map/pallas_call | solution.py:518
  3.1 3.0 %collective-permute-start.3 = (bf16[6,2,48,384]{3,2,1,0:T(8,128)(2,1)S(1)}, bf16[6,2,48,384]{3,2,1,0:T(8,128)(2,1)S(1)}, u32[]{:S(2)}, u32[]{:S(2)}) collective-permute-start(bf16[6,2,48,384]{3,2,1,0:T(8,128)(2,1)S(1)} %get-tuple-element.163), channel_id=1, source_target_pairs={{0,4},{4,0},{8,12},{12,8},{16,20},{20,16},{24,28},{28,24},{1,5},{5... | collective-permute-start | bytes 1327112 | tf_op jit(solution)/shard_map/ppermute | solution.py:1132
  6.1 3.6 %collective-permute-start.2 = (bf16[4,48,384]{2,1,0:T(8,128)(2,1)S(1)}, bf16[4,48,384]{2,1,0:T(8,128)(2,1)S(1)}, u32[]{:S(2)}, u32[]{:S(2)}) collective-permute-start(bf16[4,48,384]{2,1,0:T(8,128)(2,1)S(1)} %get-tuple-element.166), channel_id=1, source_target_pairs={{0,24},{4,28},{8,16},{12,20},{16,8},{20,12},{24,0},{28,4},{1,25},{... | collective-permute-start | bytes 442376 | tf_op jit(solution)/shard_map/ppermute | solution.py:1132
  10.5 4.2 %collective-permute-done.2 = bf16[4,48,384]{2,1,0:T(8,128)(2,1)S(1)} collective-permute-done((bf16[4,48,384]{2,1,0:T(8,128)(2,1)S(1)}, bf16[4,48,384]{2,1,0:T(8,128)(2,1)S(1)}, u32[]{:S(2)}, u32[]{:S(2)}) %collective-permute-start.2) | collective-permute-done | bytes 147488 | tf_op jit(solution)/shard_map/ppermute | solution.py:1132
  14.7 7.2 %collective-permute-done.1 = bf16[4,48,384]{2,1,0:T(8,128)(2,1)S(1)} collective-permute-done((bf16[4,48,384]{2,1,0:T(8,128)(2,1)S(1)}, bf16[4,48,384]{2,1,0:T(8,128)(2,1)S(1)}, u32[]{:S(2)}, u32[]{:S(2)}) %collective-permute-start.1) | collective-permute-done | bytes 147488 | tf_op jit(solution)/shard_map/ppermute | solution.py:1132
  22.0 1.6 collective-permute-start.12
  26.2 3.1 %collective-permute-start.4 = (bf16[24,48,384]{2,1,0:T(8,128)(2,1)S(1)}, bf16[24,48,384]{2,1,0:T(8,128)(2,1)S(1)}, u32[]{:S(2)}, u32[]{:S(2)}) collective-permute-start(bf16[24,48,384]{2,1,0:T(8,128)(2,1)S(1)} %get-tuple-element.165), channel_id=1, source_target_pairs={{0,8},{4,12},{8,0},{12,4},{16,24},{20,28},{24,16},{28,20},{1,9},{5... | collective-permute-start | bytes 2654216 | tf_op jit(solution)/shard_map/ppermute | solution.py:1132
  30.0 9.4 %collective-permute-done.6 = bf16[8,48,384]{2,1,0:T(8,128)(2,1)S(1)} collective-permute-done((bf16[8,48,384]{2,1,0:T(8,128)(2,1)S(1)}, bf16[8,48,384]{2,1,0:T(8,128)(2,1)S(1)}, u32[]{:S(2)}, u32[]{:S(2)}) %collective-permute-start.6) | collective-permute-done | bytes 294944 | tf_op jit(solution)/shard_map/ppermute | solution.py:1132
  41.4 8.5 %collective-permute-done.10.refs_5_ = bf16[4,4,48,384]{3,2,1,0:T(8,128)(2,1)S(1)} collective-permute-done((bf16[4,4,48,384]{3,2,1,0:T(8,128)(2,1)S(1)}, bf16[4,4,48,384]{3,2,1,0:T(8,128)(2,1)S(1)}, u32[]{:S(2)}, u32[]{:S(2)}) %collective-permute-start.10) | collective-permute-done | bytes 589856 | tf_op jit(solution)/shard_map/ppermute | solution.py:1134
  50.6 2.4 %collective-permute-done.4 = bf16[24,48,384]{2,1,0:T(8,128)(2,1)S(1)} collective-permute-done((bf16[24,48,384]{2,1,0:T(8,128)(2,1)S(1)}, bf16[24,48,384]{2,1,0:T(8,128)(2,1)S(1)}, u32[]{:S(2)}, u32[]{:S(2)}) %collective-permute-start.4) | collective-permute-done | bytes 884768 | tf_op jit(solution)/shard_map/ppermute | solution.py:1132
  53.1 2.5 %collective-permute-start.17 = (bf16[8,48,384]{2,1,0:T(8,128)(2,1)S(1)}, bf16[8,48,384]{2,1,0:T(8,128)(2,1)S(1)}, u32[]{:S(2)}, u32[]{:S(2)}) collective-permute-start(bf16[8,48,384]{2,1,0:T(8,128)(2,1)S(1)} %get-tuple-element.304), channel_id=1, source_target_pairs={{0,16},{4,20},{8,24},{12,28},{16,0},{20,4},{24,8},{28,12},{1,17},{... | collective-permute-start | bytes 884744 | tf_op jit(solution)/shard_map/ppermute | solution.py:1132
  57.6 6.1 %shard_map.333 = (bf16[160,768]{1,0:T(8,128)(2,1)S(1)}, bf16[197,2304]{1,0:T(8,128)(2,1)S(1)}, f32[12,197,197]{2,1,0:T(8,128)S(1)}, bf16[197,768]{1,0:T(8,128)(2...) custom-call(s32[4]{0:T(128)S(1)} %pad_add_fusion.place_ref.refs_0_, ...), custom_call_target="tpu_custom_call" | custom-call | flops 8000000000 | bytes 8000000 | tf_op jit(solution)/shard_map/pallas_call | solution.py:518
  63.6 1.6 collective-permute-done.16
  65.2 1.9 collective-permute-done.17
  69.4 4.6 %collective-permute-done.20.refs_7_ = bf16[160,768]{1,0:T(8,128)(2,1)S(1)} collective-permute-done((bf16[160,768]{1,0:T(8,128)(2,1)S(1)}, bf16[160,768]{1,0:T(8,128)(2,1)S(1)}, u32[]{:S(2)}, u32[]{:S(2)}) %collective-permute-start.20) | collective-permute-done | bytes 245792 | tf_op jit(solution)/shard_map/ppermute | solution.py:1134
  74.0 7.2 %collective-permute-done.25 = bf16[8,48,384]{2,1,0:T(8,128)(2,1)S(1)} collective-permute-done((bf16[8,48,384]{2,1,0:T(8,128)(2,1)S(1)}, bf16[8,48,384]{2,1,0:T(8,128)(2,1)S(1)}, u32[]{:S(2)}, u32[]{:S(2)}) %collective-permute-start.25) | collective-permute-done | bytes 294944 | tf_op jit(solution)/shard_map/ppermute | solution.py:1132
  81.4 4.6 %shard_map.334 = (bf16[160,768]{1,0:T(8,128)(2,1)S(1)}, bf16[160,768]{1,0:T(8,128)(2,1)S(1)}, bf16[160,768]{1,0:T(8,128)(2,1)S(1)}, bf16[160,768]{1,0:T(8,128)(2...) custom-call(s32[4]{0:T(128)S(1)} %pad_add_fusion.place_ref.refs_0_, ...), custom_call_target="tpu_custom_call" | custom-call | flops 5000000000 | bytes 5000000 | tf_op jit(solution)/shard_map/pallas_call | solution.py:518
  86.0 1.8 shard_map.337
  90.9 2.6 %shard_map.335 = (bf16[2,160,768]{2,1,0:T(8,128)(2,1)S(1)}, bf16[2,160,768]{2,1,0:T(8,128)(2,1)S(1)}, bf16[2,384,384]{2,1,0:T(8,128)(2,1)S(1)}, bf16[480,384]{1,...) custom-call(s32[4]{0:T(128)S(1)} %pad_add_fusion.place_ref.refs_0_, ...), custom_call_target="tpu_custom_call" | custom-call | flops 50000000 | bytes 50000 | tf_op jit(solution)/shard_map/pallas_call | solution.py:518
  93.5 1.8 collective-permute-done.26.refs_3_
  95.3 2.4 %collective-permute-done.23.refs_3_ = bf16[160,768]{1,0:T(8,128)(2,1)S(1)} collective-permute-done((bf16[160,768]{1,0:T(8,128)(2,1)S(1)}, bf16[160,768]{1,0:T(8,128)(2,1)S(1)}, u32[]{:S(2)}, u32[]{:S(2)}) %collective-permute-start.23) | collective-permute-done | bytes 245792 | tf_op jit(solution)/shard_map/ppermute | solution.py:1134
  97.7 4.5 %collective-permute-done.24.refs_4_ = bf16[160,768]{1,0:T(8,128)(2,1)S(1)} collective-permute-done((bf16[160,768]{1,0:T(8,128)(2,1)S(1)}, bf16[160,768]{1,0:T(8,128)(2,1)S(1)}, u32[]{:S(2)}, u32[]{:S(2)}) %collective-permute-start.24) | collective-permute-done | bytes 245792 | tf_op jit(solution)/shard_map/ppermute | solution.py:1134
  104.0 2.1 %collective-permute-start.28 = (bf16[2,2,96,384]{3,2,1,0:T(8,128)(2,1)S(1)}, bf16[2,2,96,384]{3,2,1,0:T(8,128)(2,1)S(1)}, u32[]{:S(2)}, u32[]{:S(2)}) collective-permute-start(bf16[2,2,96,384]{3,2,1,0:T(8,128)(2,1)S(1)} %get-tuple-element.210), channel_id=1, source_target_pairs={{0,8},{4,12},{8,0},{12,4},{16,24},{20,28},{24,16},{28,20},{1,9},{5... | collective-permute-start | bytes 884744 | tf_op jit(solution)/shard_map/ppermute | solution.py:1132
  106.1 6.5 %shard_map.336 = (bf16[2,4,384,384]{3,2,1,0:T(8,128)(2,1)S(1)}, bf16[2,4,384,384]{3,2,1,0:T(8,128)(2,1)S(1)}, bf16[197,2304]{1,0:T(8,128)(2,1)S(1)}, f32[197,768]{1,0:T(8,128)S(1)}, f32[4,768]{1,0:T(4,128)S(1)}) custom-call(s32[4]{0:T(128)S(1)} %pad_add_fusion.place_ref.refs_0_, bf16[160,768]{1,0:T(8,128)(2,1)S(1)} %get-tuple-element.196.refs_1_, ...), custom_call_target="tpu_custom_call" | custom-call | flops 3000000000 | bytes 3000000 | tf_op jit(solution)/shard_map/pallas_call | solution.py:518
  115.7 2.0 collective-permute-start.40
  118.9 2.1 %collective-permute-done.32.second_ref = bf16[288,384]{1,0:T(8,128)(2,1)S(1)} collective-permute-done((bf16[288,384]{1,0:T(8,128)(2,1)S(1)}, bf16[288,384]{1,0:T(8,128)(2,1)S(1)}, u32[]{:S(2)}, u32[]{:S(2)}) %collective-permute-start.32) | collective-permute-done | bytes 221216 | tf_op jit(solution)/shard_map/ppermute | solution.py:1132
  123.2 2.0 %collective-permute-start.37 = (bf16[2,2,96,384]{3,2,1,0:T(8,128)(2,1)S(1)}, bf16[2,2,96,384]{3,2,1,0:T(8,128)(2,1)S(1)}, u32[]{:S(2)}, u32[]{:S(2)}) collective-permute-start(bf16[2,2,96,384]{3,2,1,0:T(8,128)(2,1)S(1)} %get-tuple-element.237), channel_id=1, source_target_pairs={{0,8},{4,12},{8,0},{12,4},{16,24},{20,28},{24,16},{28,20},{1,9},{5... | collective-permute-start | bytes 884744 | tf_op jit(solution)/shard_map/ppermute | solution.py:1132
  129.3 5.7 %collective-permute-done.37 = bf16[2,2,96,384]{3,2,1,0:T(8,128)(2,1)S(1)} collective-permute-done((bf16[2,2,96,384]{3,2,1,0:T(8,128)(2,1)S(1)}, bf16[2,2,96,384]{3,2,1,0:T(8,128)(2,1)S(1)}, u32[]{:S(2)}, u32[]{:S(2)}) %collective-permute-start.37) | collective-permute-done | bytes 294944 | tf_op jit(solution)/shard_map/ppermute | solution.py:1132
  135.4 2.0 %collective-permute-start.42 = (bf16[2,2,96,384]{3,2,1,0:T(8,128)(2,1)S(1)}, bf16[2,2,96,384]{3,2,1,0:T(8,128)(2,1)S(1)}, u32[]{:S(2)}, u32[]{:S(2)}) collective-permute-start(bf16[2,2,96,384]{3,2,1,0:T(8,128)(2,1)S(1)} %pad_maximum_fusion.4), channel_id=1, source_target_pairs={{0,8},{4,12},{8,0},{12,4},{16,24},{20,28},{24,16},{28,20},{1,9},{5... | collective-permute-start | bytes 884744 | tf_op jit(solution)/shard_map/ppermute | solution.py:1132
  138.2 3.9 %shard_map.340 = (bf16[197,768]{1,0:T(8,128)(2,1)}, f32[197,1,768]{2,1,0:T(1,128)}, f32[5,768]{1,0:T(8,128)S(1)}) custom-call(bf16[160,768]{1,0:T(8,128)(2,1)S(1)} %get-tuple-element.223.refs_0_, bf16[160,768]{1,0:T(8,128)(2,1)S(1)} %collective-permute-done.33.refs_1_, bf16[197,2304]{1,0:T(8,128)(2,1)S(1)} %get-tuple-element.225.refs_2_, ...), custom_call_target="tpu_custom_call" | custom-call | flops 50000000 | bytes 50000 | tf_op jit(solution)/shard_map/pallas_call | solution.py:518
  143.6 4.4 %collective-permute-done.42 = bf16[2,2,96,384]{3,2,1,0:T(8,128)(2,1)S(1)} collective-permute-done((bf16[2,2,96,384]{3,2,1,0:T(8,128)(2,1)S(1)}, bf16[2,2,96,384]{3,2,1,0:T(8,128)(2,1)S(1)}, u32[]{:S(2)}, u32[]{:S(2)}) %collective-permute-start.42) | collective-permute-done | bytes 294944 | tf_op jit(solution)/shard_map/ppermute | solution.py:1132
  148.0 1.8 shard_map.343
  150.9 2.3 %collective-permute-done.35.refs_3_ = bf16[2,384,384]{2,1,0:T(8,128)(2,1)S(1)} collective-permute-done((bf16[2,384,384]{2,1,0:T(8,128)(2,1)S(1)}, bf16[2,384,384]{2,1,0:T(8,128)(2,1)S(1)}, u32[]{:S(2)}, u32[]{:S(2)}) %collective-permute-start.35) | collective-permute-done | bytes 589856 | tf_op jit(solution)/shard_map/ppermute | solution.py:1134
  153.3 2.0 %collective-permute-start.47 = (bf16[2,2,96,384]{3,2,1,0:T(8,128)(2,1)S(1)}, bf16[2,2,96,384]{3,2,1,0:T(8,128)(2,1)S(1)}, u32[]{:S(2)}, u32[]{:S(2)}) collective-permute-start(bf16[2,2,96,384]{3,2,1,0:T(8,128)(2,1)S(1)} %pad_maximum_fusion.5), channel_id=1, source_target_pairs={{0,8},{4,12},{8,0},{12,4},{16,24},{20,28},{24,16},{28,20},{1,9},{5... | collective-permute-start | bytes 884744 | tf_op jit(solution)/shard_map/ppermute | solution.py:1132
  157.5 2.6 %collective-permute-start.44 = (bf16[2,96,384]{2,1,0:T(8,128)(2,1)S(1)}, bf16[2,96,384]{2,1,0:T(8,128)(2,1)S(1)}, u32[]{:S(2)}, u32[]{:S(2)}) collective-permute-start(bf16[2,96,384]{2,1,0:T(8,128)(2,1)S(1)} %get-tuple-element.253), channel_id=1, source_target_pairs={{0,16},{4,20},{8,24},{12,28},{16,0},{20,4},{24,8},{28,12},{1,17},{... | collective-permute-start | bytes 442376 | tf_op jit(solution)/shard_map/ppermute | solution.py:1132
  160.0 1.6 collective-permute-start.45
  161.6 2.8 %collective-permute-done.47 = bf16[2,2,96,384]{3,2,1,0:T(8,128)(2,1)S(1)} collective-permute-done((bf16[2,2,96,384]{3,2,1,0:T(8,128)(2,1)S(1)}, bf16[2,2,96,384]{3,2,1,0:T(8,128)(2,1)S(1)}, u32[]{:S(2)}, u32[]{:S(2)}) %collective-permute-start.47) | collective-permute-done | bytes 294944 | tf_op jit(solution)/shard_map/ppermute | solution.py:1132
  164.5 1.8 shard_map.346
  167.8 3.7 %collective-permute-done.45 = bf16[2,96,384]{2,1,0:T(8,128)(2,1)S(1)} collective-permute-done((bf16[2,96,384]{2,1,0:T(8,128)(2,1)S(1)}, bf16[2,96,384]{2,1,0:T(8,128)(2,1)S(1)}, u32[]{:S(2)}, u32[]{:S(2)}) %collective-permute-start.45) | collective-permute-done | bytes 147488 | tf_op jit(solution)/shard_map/ppermute | solution.py:1132
  172.5 1.7 collective-permute-start.51
  174.2 2.8 %collective-permute-start.49 = (bf16[2,96,384]{2,1,0:T(8,128)(2,1)S(1)}, bf16[2,96,384]{2,1,0:T(8,128)(2,1)S(1)}, u32[]{:S(2)}, u32[]{:S(2)}) collective-permute-start(bf16[2,96,384]{2,1,0:T(8,128)(2,1)S(1)} %add_convert_fusion.2.refs_1_), channel_id=1, source_target_pairs={{0,8},{4,12},{8,0},{12,4},{16,24},{20,28},{24,16},{28,20},{1,9},{5... | collective-permute-start | bytes 442376 | tf_op jit(solution)/shard_map/ppermute | solution.py:1132
  177.9 3.2 %collective-permute-done.53 = f32[13,768]{1,0:T(8,128)S(1)} collective-permute-done((f32[13,768]{1,0:T(8,128)S(1)}, f32[13,768]{1,0:T(8,128)S(1)}, u32[]{:S(2)}, u32[]{:S(2)}) %collective-permute-start.53) | collective-permute-done | bytes 39968 | tf_op jit(solution)/shard_map/ppermute | solution.py:1134
  185.3 2.2 %shard_map.348 = (bf16[4,2,48,384]{3,2,1,0:T(8,128)(2,1)S(1)}, bf16[4,2,48,384]{3,2,1,0:T(8,128)(2,1)S(1)}) custom-call(s32[4]{0:T(128)S(1)} %pad_add_fusion.place_ref.refs_0_, bf16[2,96,384]{2,1,0:T(8,128)(2,1)S(1)} %add_convert_fusion.2.refs_1_, bf16[2,96,384]{2,1,0:T(8,128)(2,1)S(1)} %collective-permute-done.49.refs_2_, ...), custom_call_target="tpu_custom_call" | custom-call | flops 50000000 | bytes 50000 | tf_op jit(solution)/shard_map/pallas_call | solution.py:518
  187.6 1.7 collective-permute-start.58
  189.2 2.8 %collective-permute-start.56 = (f32[24,768]{1,0:T(8,128)S(1)}, f32[24,768]{1,0:T(8,128)S(1)}, u32[]{:S(2)}, u32[]{:S(2)}) collective-permute-start(f32[24,768]{1,0:T(8,128)S(1)} %shard_map.350), channel_id=1, source_target_pairs={{0,8},{4,12},{8,0},{12,4},{16,24},{20,28},{24,16},{28,20},{1,9},{5... | collective-permute-start | bytes 221192 | tf_op jit(solution)/shard_map/ppermute | solution.py:1132
  193.8 1.6 collective-permute-done.57
  195.4 1.9 shard_map.351
  198.8 1.7 shard_map.349
  (142 shorter events, 44.0 us)
Async XLA Ops:
  3.1 18.8 %collective-permute-start.3 = (bf16[6,2,48,384]{3,2,1,0:T(8,128)(2,1)S(1)}, bf16[6,2,48,384]{3,2,1,0:T(8,128)(2,1)S(1)}, u32[]{:S(2)}, u32[]{:S(2)}) collective-permute-start(bf16[6,2,48,384]{3,2,1,0:T(8,128)(2,1)S(1)} %get-tuple-element.163), channel_id=1, source_target_pairs={{0,4},{4,0},{8,12},{12,8},{16,20},{20,16},{24,28},{28,24},{1,5},{5... | collective-permute-start | bytes 1327112 | tf_op jit(solution)/shard_map/ppermute | solution.py:1132
  6.1 8.6 %collective-permute-start.2 = (bf16[4,48,384]{2,1,0:T(8,128)(2,1)S(1)}, bf16[4,48,384]{2,1,0:T(8,128)(2,1)S(1)}, u32[]{:S(2)}, u32[]{:S(2)}) collective-permute-start(bf16[4,48,384]{2,1,0:T(8,128)(2,1)S(1)} %get-tuple-element.166), channel_id=1, source_target_pairs={{0,24},{4,28},{8,16},{12,20},{16,8},{20,12},{24,0},{28,4},{1,25},{... | collective-permute-start | bytes 442376 | tf_op jit(solution)/shard_map/ppermute | solution.py:1132
  9.7 12.2 %collective-permute-start.1 = (bf16[4,48,384]{2,1,0:T(8,128)(2,1)S(1)}, bf16[4,48,384]{2,1,0:T(8,128)(2,1)S(1)}, u32[]{:S(2)}, u32[]{:S(2)}) collective-permute-start(bf16[4,48,384]{2,1,0:T(8,128)(2,1)S(1)} %get-tuple-element.166), channel_id=1, source_target_pairs={{0,16},{4,20},{8,24},{12,28},{16,0},{20,4},{24,8},{28,12},{1,17},{... | collective-permute-start | bytes 442376 | tf_op jit(solution)/shard_map/ppermute | solution.py:1132
  9.7 12.2 %collective-permute-start = (bf16[4,48,384]{2,1,0:T(8,128)(2,1)S(1)}, bf16[4,48,384]{2,1,0:T(8,128)(2,1)S(1)}, u32[]{:S(2)}, u32[]{:S(2)}) collective-permute-start(bf16[4,48,384]{2,1,0:T(8,128)(2,1)S(1)} %get-tuple-element.166), channel_id=1, source_target_pairs={{0,8},{4,12},{8,0},{12,4},{16,24},{20,28},{24,16},{28,20},{1,9},{5... | collective-permute-start | bytes 442376 | tf_op jit(solution)/shard_map/ppermute | solution.py:1132
  22.0 19.1 %collective-permute-start.12 = (bf16[4,4,48,384]{3,2,1,0:T(8,128)(2,1)S(1)}, bf16[4,4,48,384]{3,2,1,0:T(8,128)(2,1)S(1)}, u32[]{:S(2)}, u32[]{:S(2)}) collective-permute-start(bf16[4,4,48,384]{3,2,1,0:T(8,128)(2,1)S(1)} %pad_maximum_fusion.1.refs_1_), channel_id=1, source_target_pairs={{0,6},{1,7},{2,4},{3,5},{4,2},{5,3},{6,0},{7,1},{8,14},{9,15},{10,... | collective-permute-start | bytes 1769480 | tf_op jit(solution)/shard_map/ppermute | solution.py:1136
  23.5 26.4 %collective-permute-start.10 = (bf16[4,4,48,384]{3,2,1,0:T(8,128)(2,1)S(1)}, bf16[4,4,48,384]{3,2,1,0:T(8,128)(2,1)S(1)}, u32[]{:S(2)}, u32[]{:S(2)}) collective-permute-start(bf16[4,4,48,384]{3,2,1,0:T(8,128)(2,1)S(1)} %pad_maximum_fusion.1.refs_1_), channel_id=1, source_target_pairs={{0,2},{1,3},{2,0},{3,1},{4,6},{5,7},{6,4},{7,5},{8,10},{9,11},{10,... | collective-permute-start | bytes 1769480 | tf_op jit(solution)/shard_map/ppermute | solution.py:1134
  24.0 26.0 %collective-permute-start.8 = (bf16[4,4,48,384]{3,2,1,0:T(8,128)(2,1)S(1)}, bf16[4,4,48,384]{3,2,1,0:T(8,128)(2,1)S(1)}, u32[]{:S(2)}, u32[]{:S(2)}) collective-permute-start(bf16[4,4,48,384]{3,2,1,0:T(8,128)(2,1)S(1)} %pad_maximum_fusion.1.refs_1_), channel_id=1, source_target_pairs={{0,4},{4,0},{8,12},{12,8},{16,20},{20,16},{24,28},{28,24},{1,5},{5... | collective-permute-start | bytes 1769480 | tf_op jit(solution)/shard_map/ppermute | solution.py:1132
  25.5 13.9 %collective-permute-start.6 = (bf16[8,48,384]{2,1,0:T(8,128)(2,1)S(1)}, bf16[8,48,384]{2,1,0:T(8,128)(2,1)S(1)}, u32[]{:S(2)}, u32[]{:S(2)}) collective-permute-start(bf16[8,48,384]{2,1,0:T(8,128)(2,1)S(1)} %get-tuple-element.160.feed_ref), channel_id=1, source_target_pairs={{0,16},{4,20},{8,24},{12,28},{16,0},{20,4},{24,8},{28,12},{1,17},{... | collective-permute-start | bytes 884744 | tf_op jit(solution)/shard_map/ppermute | solution.py:1132
  26.2 26.7 %collective-permute-start.4 = (bf16[24,48,384]{2,1,0:T(8,128)(2,1)S(1)}, bf16[24,48,384]{2,1,0:T(8,128)(2,1)S(1)}, u32[]{:S(2)}, u32[]{:S(2)}) collective-permute-start(bf16[24,48,384]{2,1,0:T(8,128)(2,1)S(1)} %get-tuple-element.165), channel_id=1, source_target_pairs={{0,8},{4,12},{8,0},{12,4},{16,24},{20,28},{24,16},{28,20},{1,9},{5... | collective-permute-start | bytes 2654216 | tf_op jit(solution)/shard_map/ppermute | solution.py:1132
  40.9 12.1 %collective-permute-start.7 = (bf16[4,4,48,384]{3,2,1,0:T(8,128)(2,1)S(1)}, bf16[4,4,48,384]{3,2,1,0:T(8,128)(2,1)S(1)}, u32[]{:S(2)}, u32[]{:S(2)}) collective-permute-start(bf16[4,4,48,384]{3,2,1,0:T(8,128)(2,1)S(1)} %pad_maximum_fusion.1.refs_1_), channel_id=1, source_target_pairs={{0,1},{1,0},{2,3},{3,2},{4,5},{5,4},{6,7},{7,6},{8,9},{9,8},{10,11... | collective-permute-start | bytes 1769480 | tf_op jit(solution)/shard_map/ppermute | solution.py:1134
  41.1 14.4 %collective-permute-start.13 = (bf16[4,4,48,384]{3,2,1,0:T(8,128)(2,1)S(1)}, bf16[4,4,48,384]{3,2,1,0:T(8,128)(2,1)S(1)}, u32[]{:S(2)}, u32[]{:S(2)}) collective-permute-start(bf16[4,4,48,384]{3,2,1,0:T(8,128)(2,1)S(1)} %collective-permute-done.12.refs_7_), channel_id=1, source_target_pairs={{0,1},{1,0},{2,3},{3,2},{4,5},{5,4},{6,7},{7,6},{8,9},{9,8},{10,11... | collective-permute-start | bytes 1769480 | tf_op jit(solution)/shard_map/ppermute | solution.py:1134
  49.9 7.1 %collective-permute-start.11 = (bf16[4,4,48,384]{3,2,1,0:T(8,128)(2,1)S(1)}, bf16[4,4,48,384]{3,2,1,0:T(8,128)(2,1)S(1)}, u32[]{:S(2)}, u32[]{:S(2)}) collective-permute-start(bf16[4,4,48,384]{3,2,1,0:T(8,128)(2,1)S(1)} %collective-permute-done.10.refs_5_), channel_id=1, source_target_pairs={{0,1},{1,0},{2,3},{3,2},{4,5},{5,4},{6,7},{7,6},{8,9},{9,8},{10,11... | collective-permute-start | bytes 1769480 | tf_op jit(solution)/shard_map/ppermute | solution.py:1134
  50.0 7.5 %collective-permute-start.9 = (bf16[4,4,48,384]{3,2,1,0:T(8,128)(2,1)S(1)}, bf16[4,4,48,384]{3,2,1,0:T(8,128)(2,1)S(1)}, u32[]{:S(2)}, u32[]{:S(2)}) collective-permute-start(bf16[4,4,48,384]{3,2,1,0:T(8,128)(2,1)S(1)} %collective-permute-done.8.refs_3_), channel_id=1, source_target_pairs={{0,1},{1,0},{2,3},{3,2},{4,5},{5,4},{6,7},{7,6},{8,9},{9,8},{10,11... | collective-permute-start | bytes 1769480 | tf_op jit(solution)/shard_map/ppermute | solution.py:1134
  52.9 12.3 %collective-permute-start.16 = (bf16[8,48,384]{2,1,0:T(8,128)(2,1)S(1)}, bf16[8,48,384]{2,1,0:T(8,128)(2,1)S(1)}, u32[]{:S(2)}, u32[]{:S(2)}) collective-permute-start(bf16[8,48,384]{2,1,0:T(8,128)(2,1)S(1)} %collective-permute-done.6), channel_id=1, source_target_pairs={{0,8},{4,12},{8,0},{12,4},{16,24},{20,28},{24,16},{28,20},{1,9},{5... | collective-permute-start | bytes 884744 | tf_op jit(solution)/shard_map/ppermute | solution.py:1132
  53.1 14.1 %collective-permute-start.17 = (bf16[8,48,384]{2,1,0:T(8,128)(2,1)S(1)}, bf16[8,48,384]{2,1,0:T(8,128)(2,1)S(1)}, u32[]{:S(2)}, u32[]{:S(2)}) collective-permute-start(bf16[8,48,384]{2,1,0:T(8,128)(2,1)S(1)} %get-tuple-element.304), channel_id=1, source_target_pairs={{0,16},{4,20},{8,24},{12,28},{16,0},{20,4},{24,8},{28,12},{1,17},{... | collective-permute-start | bytes 884744 | tf_op jit(solution)/shard_map/ppermute | solution.py:1132
  55.5 11.6 %collective-permute-start.15 = (bf16[2,160,768]{2,1,0:T(8,128)(2,1)S(1)}, bf16[2,160,768]{2,1,0:T(8,128)(2,1)S(1)}, u32[]{:S(2)}, u32[]{:S(2)}) collective-permute-start(bf16[2,160,768]{2,1,0:T(8,128)(2,1)S(1)} %pad_maximum_fusion.3.refs_9_), channel_id=1, source_target_pairs={{0,2},{1,3},{2,0},{3,1},{4,6},{5,7},{6,4},{7,5},{8,10},{9,11},{10,... | collective-permute-start | bytes 1474568 | tf_op jit(solution)/shard_map/ppermute | solution.py:1134
  57.1 24.3 %collective-permute-start.5 = (bf16[2,8,48,384]{3,2,1,0:T(8,128)(2,1)S(1)}, bf16[2,8,48,384]{3,2,1,0:T(8,128)(2,1)S(1)}, u32[]{:S(2)}, u32[]{:S(2)}) collective-permute-start(bf16[2,8,48,384]{3,2,1,0:T(8,128)(2,1)S(1)} %pad_maximum_fusion.refs_1_), channel_id=1, source_target_pairs={{0,4},{4,0},{8,12},{12,8},{16,20},{20,16},{24,28},{28,24},{1,5},{5... | collective-permute-start | bytes 1769480 | tf_op jit(solution)/shard_map/ppermute | solution.py:1132
  67.2 14.2 %collective-permute-start.18 = (bf16[2,8,48,384]{3,2,1,0:T(8,128)(2,1)S(1)}, bf16[2,8,48,384]{3,2,1,0:T(8,128)(2,1)S(1)}, u32[]{:S(2)}, u32[]{:S(2)}) collective-permute-start(bf16[2,8,48,384]{3,2,1,0:T(8,128)(2,1)S(1)} %pad_maximum_fusion.2.refs_3_), channel_id=1, source_target_pairs={{0,4},{4,0},{8,12},{12,8},{16,20},{20,16},{24,28},{28,24},{1,5},{5... | collective-permute-start | bytes 1769480 | tf_op jit(solution)/shard_map/ppermute | solution.py:1132
  69.2 12.0 %collective-permute-start.25 = (bf16[8,48,384]{2,1,0:T(8,128)(2,1)S(1)}, bf16[8,48,384]{2,1,0:T(8,128)(2,1)S(1)}, u32[]{:S(2)}, u32[]{:S(2)}) collective-permute-start(bf16[8,48,384]{2,1,0:T(8,128)(2,1)S(1)} %get-tuple-element.303), channel_id=1, source_target_pairs={{0,16},{4,20},{8,24},{12,28},{16,0},{20,4},{24,8},{28,12},{1,17},{... | collective-permute-start | bytes 884744 | tf_op jit(solution)/shard_map/ppermute | solution.py:1132
  69.4 12.0 %collective-permute-start.19 = (bf16[160,768]{1,0:T(8,128)(2,1)S(1)}, bf16[160,768]{1,0:T(8,128)(2,1)S(1)}, u32[]{:S(2)}, u32[]{:S(2)}) collective-permute-start(bf16[160,768]{1,0:T(8,128)(2,1)S(1)} %get-tuple-element.176.refs_5_), channel_id=1, source_target_pairs={{0,1},{1,0},{2,3},{3,2},{4,5},{5,4},{6,7},{7,6},{8,9},{9,8},{10,11... | collective-permute-start | bytes 737288 | tf_op jit(solution)/shard_map/ppermute | solution.py:1134
  74.0 7.4 %collective-permute-start.21 = (bf16[160,768]{1,0:T(8,128)(2,1)S(1)}, bf16[160,768]{1,0:T(8,128)(2,1)S(1)}, u32[]{:S(2)}, u32[]{:S(2)}) collective-permute-start(bf16[160,768]{1,0:T(8,128)(2,1)S(1)} %collective-permute-done.20.refs_7_), channel_id=1, source_target_pairs={{0,1},{1,0},{2,3},{3,2},{4,5},{5,4},{6,7},{7,6},{8,9},{9,8},{10,11... | collective-permute-start | bytes 737288 | tf_op jit(solution)/shard_map/ppermute | solution.py:1134
  81.3 14.0 %collective-permute-start.26 = (bf16[16,48,384]{2,1,0:T(8,128)(2,1)S(1)}, bf16[16,48,384]{2,1,0:T(8,128)(2,1)S(1)}, u32[]{:S(2)}, u32[]{:S(2)}) collective-permute-start(bf16[16,48,384]{2,1,0:T(8,128)(2,1)S(1)} %constant_dynamic-update-slice_fusion.refs_2_), channel_id=1, source_target_pairs={{0,8},{4,12},{8,0},{12,4},{16,24},{20,28},{24,16},{28,20},{1,9},{5... | collective-permute-start | bytes 1769480 | tf_op jit(solution)/shard_map/ppermute | solution.py:1132
  87.7 15.6 %collective-permute-start.27 = (bf16[768,384]{1,0:T(8,128)(2,1)S(1)}, bf16[768,384]{1,0:T(8,128)(2,1)S(1)}, u32[]{:S(2)}, u32[]{:S(2)}) collective-permute-start(bf16[768,384]{1,0:T(8,128)(2,1)S(1)} %get-tuple-element.209), channel_id=1, source_target_pairs={{0,4},{4,0},{8,12},{12,8},{16,20},{20,16},{24,28},{28,24},{1,5},{5... | collective-permute-start | bytes 1769480 | tf_op jit(solution)/shard_map/ppermute | solution.py:1132
  88.9 8.8 %collective-permute-start.23 = (bf16[160,768]{1,0:T(8,128)(2,1)S(1)}, bf16[160,768]{1,0:T(8,128)(2,1)S(1)}, u32[]{:S(2)}, u32[]{:S(2)}) collective-permute-start(bf16[160,768]{1,0:T(8,128)(2,1)S(1)} %get-tuple-element.186), channel_id=1, source_target_pairs={{0,2},{1,3},{2,0},{3,1},{4,6},{5,7},{6,4},{7,5},{8,10},{9,11},{10,... | collective-permute-start | bytes 737288 | tf_op jit(solution)/shard_map/ppermute | solution.py:1134
  90.0 12.2 %collective-permute-start.24 = (bf16[160,768]{1,0:T(8,128)(2,1)S(1)}, bf16[160,768]{1,0:T(8,128)(2,1)S(1)}, u32[]{:S(2)}, u32[]{:S(2)}) collective-permute-start(bf16[160,768]{1,0:T(8,128)(2,1)S(1)} %get-tuple-element.187), channel_id=1, source_target_pairs={{0,3},{1,2},{2,1},{3,0},{4,7},{5,6},{6,5},{7,4},{8,11},{9,10},{10,... | collective-permute-start | bytes 737288 | tf_op jit(solution)/shard_map/ppermute | solution.py:1134
  102.2 11.0 %collective-permute-start.30 = (bf16[2,160,768]{2,1,0:T(8,128)(2,1)S(1)}, bf16[2,160,768]{2,1,0:T(8,128)(2,1)S(1)}, u32[]{:S(2)}, u32[]{:S(2)}) collective-permute-start(bf16[2,160,768]{2,1,0:T(8,128)(2,1)S(1)} %get-tuple-element.212), channel_id=1, source_target_pairs={{0,1},{1,0},{2,3},{3,2},{4,5},{5,4},{6,7},{7,6},{8,9},{9,8},{10,11... | collective-permute-start | bytes 1474568 | tf_op jit(solution)/shard_map/ppermute | solution.py:1134
  102.4 10.8 %collective-permute-start.29 = (bf16[480,384]{1,0:T(8,128)(2,1)S(1)}, bf16[480,384]{1,0:T(8,128)(2,1)S(1)}, u32[]{:S(2)}, u32[]{:S(2)}) collective-permute-start(bf16[480,384]{1,0:T(8,128)(2,1)S(1)} %get-tuple-element.211), channel_id=1, source_target_pairs={{0,4},{4,0},{8,12},{12,8},{16,20},{20,16},{24,28},{28,24},{1,5},{5... | collective-permute-start | bytes 1105928 | tf_op jit(solution)/shard_map/ppermute | solution.py:1132
  104.0 9.3 %collective-permute-start.28 = (bf16[2,2,96,384]{3,2,1,0:T(8,128)(2,1)S(1)}, bf16[2,2,96,384]{3,2,1,0:T(8,128)(2,1)S(1)}, u32[]{:S(2)}, u32[]{:S(2)}) collective-permute-start(bf16[2,2,96,384]{3,2,1,0:T(8,128)(2,1)S(1)} %get-tuple-element.210), channel_id=1, source_target_pairs={{0,8},{4,12},{8,0},{12,4},{16,24},{20,28},{24,16},{28,20},{1,9},{5... | collective-permute-start | bytes 884744 | tf_op jit(solution)/shard_map/ppermute | solution.py:1132
  113.3 7.8 %collective-permute-start.32 = (bf16[288,384]{1,0:T(8,128)(2,1)S(1)}, bf16[288,384]{1,0:T(8,128)(2,1)S(1)}, u32[]{:S(2)}, u32[]{:S(2)}) collective-permute-start(bf16[288,384]{1,0:T(8,128)(2,1)S(1)} %get-tuple-element.220), channel_id=1, source_target_pairs={{0,4},{4,0},{8,12},{12,8},{16,20},{20,16},{24,28},{28,24},{1,5},{5... | collective-permute-start | bytes 663560 | tf_op jit(solution)/shard_map/ppermute | solution.py:1132
  114.3 8.1 %collective-permute-start.33 = (bf16[160,768]{1,0:T(8,128)(2,1)S(1)}, bf16[160,768]{1,0:T(8,128)(2,1)S(1)}, u32[]{:S(2)}, u32[]{:S(2)}) collective-permute-start(bf16[160,768]{1,0:T(8,128)(2,1)S(1)} %get-tuple-element.301), channel_id=1, source_target_pairs={{0,2},{1,3},{2,0},{3,1},{4,6},{5,7},{6,4},{7,5},{8,10},{9,11},{10,... | collective-permute-start | bytes 737288 | tf_op jit(solution)/shard_map/ppermute | solution.py:1134
  115.7 9.8 %collective-permute-start.40 = (bf16[2,96,384]{2,1,0:T(8,128)(2,1)S(1)}, bf16[2,96,384]{2,1,0:T(8,128)(2,1)S(1)}, u32[]{:S(2)}, u32[]{:S(2)}) collective-permute-start(bf16[2,96,384]{2,1,0:T(8,128)(2,1)S(1)} %get-tuple-element.305), channel_id=1, source_target_pairs={{0,16},{4,20},{8,24},{12,28},{16,0},{20,4},{24,8},{28,12},{1,17},{... | collective-permute-start | bytes 442376 | tf_op jit(solution)/shard_map/ppermute | solution.py:1132
  123.2 11.8 %collective-permute-start.37 = (bf16[2,2,96,384]{3,2,1,0:T(8,128)(2,1)S(1)}, bf16[2,2,96,384]{3,2,1,0:T(8,128)(2,1)S(1)}, u32[]{:S(2)}, u32[]{:S(2)}) collective-permute-start(bf16[2,2,96,384]{3,2,1,0:T(8,128)(2,1)S(1)} %get-tuple-element.237), channel_id=1, source_target_pairs={{0,8},{4,12},{8,0},{12,4},{16,24},{20,28},{24,16},{28,20},{1,9},{5... | collective-permute-start | bytes 884744 | tf_op jit(solution)/shard_map/ppermute | solution.py:1132
  125.6 9.8 %collective-permute-start.41 = (bf16[2,96,384]{2,1,0:T(8,128)(2,1)S(1)}, bf16[2,96,384]{2,1,0:T(8,128)(2,1)S(1)}, u32[]{:S(2)}, u32[]{:S(2)}) collective-permute-start(bf16[2,96,384]{2,1,0:T(8,128)(2,1)S(1)} %add_convert_fusion.3.refs_1_), channel_id=1, source_target_pairs={{0,16},{4,20},{8,24},{12,28},{16,0},{20,4},{24,8},{28,12},{1,17},{... | collective-permute-start | bytes 442376 | tf_op jit(solution)/shard_map/ppermute | solution.py:1132
  125.8 25.1 %collective-permute-start.34 = (bf16[2,384,384]{2,1,0:T(8,128)(2,1)S(1)}, bf16[2,384,384]{2,1,0:T(8,128)(2,1)S(1)}, u32[]{:S(2)}, u32[]{:S(2)}) collective-permute-start(bf16[2,384,384]{2,1,0:T(8,128)(2,1)S(1)} %get-tuple-element.230), channel_id=1, source_target_pairs={{0,4},{4,0},{8,12},{12,8},{16,20},{20,16},{24,28},{28,24},{1,5},{5... | collective-permute-start | bytes 1769480 | tf_op jit(solution)/shard_map/ppermute | solution.py:1132
  126.8 26.4 %collective-permute-start.35 = (bf16[2,384,384]{2,1,0:T(8,128)(2,1)S(1)}, bf16[2,384,384]{2,1,0:T(8,128)(2,1)S(1)}, u32[]{:S(2)}, u32[]{:S(2)}) collective-permute-start(bf16[2,384,384]{2,1,0:T(8,128)(2,1)S(1)} %get-tuple-element.231), channel_id=1, source_target_pairs={{0,2},{1,3},{2,0},{3,1},{4,6},{5,7},{6,4},{7,5},{8,10},{9,11},{10,... | collective-permute-start | bytes 1769480 | tf_op jit(solution)/shard_map/ppermute | solution.py:1134
  127.8 25.4 %collective-permute-start.36 = (bf16[2,384,384]{2,1,0:T(8,128)(2,1)S(1)}, bf16[2,384,384]{2,1,0:T(8,128)(2,1)S(1)}, u32[]{:S(2)}, u32[]{:S(2)}) collective-permute-start(bf16[2,384,384]{2,1,0:T(8,128)(2,1)S(1)} %get-tuple-element.232), channel_id=1, source_target_pairs={{0,6},{1,7},{2,4},{3,5},{4,2},{5,3},{6,0},{7,1},{8,14},{9,15},{10,... | collective-permute-start | bytes 1769480 | tf_op jit(solution)/shard_map/ppermute | solution.py:1136
  135.0 7.7 %collective-permute-start.38 = (bf16[2,96,384]{2,1,0:T(8,128)(2,1)S(1)}, bf16[2,96,384]{2,1,0:T(8,128)(2,1)S(1)}, u32[]{:S(2)}, u32[]{:S(2)}) collective-permute-start(bf16[2,96,384]{2,1,0:T(8,128)(2,1)S(1)} %fusion.5), channel_id=1, source_target_pairs={{0,16},{4,20},{8,24},{12,28},{16,0},{20,4},{24,8},{28,12},{1,17},{... | collective-permute-start | bytes 442376 | tf_op jit(solution)/shard_map/ppermute | solution.py:1132
  135.4 12.5 %collective-permute-start.42 = (bf16[2,2,96,384]{3,2,1,0:T(8,128)(2,1)S(1)}, bf16[2,2,96,384]{3,2,1,0:T(8,128)(2,1)S(1)}, u32[]{:S(2)}, u32[]{:S(2)}) collective-permute-start(bf16[2,2,96,384]{3,2,1,0:T(8,128)(2,1)S(1)} %pad_maximum_fusion.4), channel_id=1, source_target_pairs={{0,8},{4,12},{8,0},{12,4},{16,24},{20,28},{24,16},{28,20},{1,9},{5... | collective-permute-start | bytes 884744 | tf_op jit(solution)/shard_map/ppermute | solution.py:1132
  142.8 8.1 %collective-permute-start.39 = (bf16[2,96,384]{2,1,0:T(8,128)(2,1)S(1)}, bf16[2,96,384]{2,1,0:T(8,128)(2,1)S(1)}, u32[]{:S(2)}, u32[]{:S(2)}) collective-permute-start(bf16[2,96,384]{2,1,0:T(8,128)(2,1)S(1)} %fusion.refs_1_), channel_id=1, source_target_pairs={{0,16},{4,20},{8,24},{12,28},{16,0},{20,4},{24,8},{28,12},{1,17},{... | collective-permute-start | bytes 442376 | tf_op jit(solution)/shard_map/ppermute | solution.py:1132
  153.3 11.1 %collective-permute-start.47 = (bf16[2,2,96,384]{3,2,1,0:T(8,128)(2,1)S(1)}, bf16[2,2,96,384]{3,2,1,0:T(8,128)(2,1)S(1)}, u32[]{:S(2)}, u32[]{:S(2)}) collective-permute-start(bf16[2,2,96,384]{3,2,1,0:T(8,128)(2,1)S(1)} %pad_maximum_fusion.5), channel_id=1, source_target_pairs={{0,8},{4,12},{8,0},{12,4},{16,24},{20,28},{24,16},{28,20},{1,9},{5... | collective-permute-start | bytes 884744 | tf_op jit(solution)/shard_map/ppermute | solution.py:1132
  155.3 16.1 %collective-permute-start.46 = (bf16[5,2,48,384]{3,2,1,0:T(8,128)(2,1)S(1)}, bf16[5,2,48,384]{3,2,1,0:T(8,128)(2,1)S(1)}, u32[]{:S(2)}, u32[]{:S(2)}) collective-permute-start(bf16[5,2,48,384]{3,2,1,0:T(8,128)(2,1)S(1)} %get-tuple-element.255), channel_id=1, source_target_pairs={{0,4},{4,0},{8,12},{12,8},{16,20},{20,16},{24,28},{28,24},{1,5},{5... | collective-permute-start | bytes 1105928 | tf_op jit(solution)/shard_map/ppermute | solution.py:1132
  157.2 10.6 %collective-permute-start.43 = (bf16[2,96,384]{2,1,0:T(8,128)(2,1)S(1)}, bf16[2,96,384]{2,1,0:T(8,128)(2,1)S(1)}, u32[]{:S(2)}, u32[]{:S(2)}) collective-permute-start(bf16[2,96,384]{2,1,0:T(8,128)(2,1)S(1)} %get-tuple-element.252), channel_id=1, source_target_pairs={{0,8},{4,12},{8,0},{12,4},{16,24},{20,28},{24,16},{28,20},{1,9},{5... | collective-permute-start | bytes 442376 | tf_op jit(solution)/shard_map/ppermute | solution.py:1132
  157.5 10.3 %collective-permute-start.44 = (bf16[2,96,384]{2,1,0:T(8,128)(2,1)S(1)}, bf16[2,96,384]{2,1,0:T(8,128)(2,1)S(1)}, u32[]{:S(2)}, u32[]{:S(2)}) collective-permute-start(bf16[2,96,384]{2,1,0:T(8,128)(2,1)S(1)} %get-tuple-element.253), channel_id=1, source_target_pairs={{0,16},{4,20},{8,24},{12,28},{16,0},{20,4},{24,8},{28,12},{1,17},{... | collective-permute-start | bytes 442376 | tf_op jit(solution)/shard_map/ppermute | solution.py:1132
  160.0 11.4 %collective-permute-start.45 = (bf16[2,96,384]{2,1,0:T(8,128)(2,1)S(1)}, bf16[2,96,384]{2,1,0:T(8,128)(2,1)S(1)}, u32[]{:S(2)}, u32[]{:S(2)}) collective-permute-start(bf16[2,96,384]{2,1,0:T(8,128)(2,1)S(1)} %get-tuple-element.254), channel_id=1, source_target_pairs={{0,24},{4,28},{8,16},{12,20},{16,8},{20,12},{24,0},{28,4},{1,25},{... | collective-permute-start | bytes 442376 | tf_op jit(solution)/shard_map/ppermute | solution.py:1132
  171.4 13.8 %collective-permute-start.52 = (bf16[5,2,48,384]{3,2,1,0:T(8,128)(2,1)S(1)}, bf16[5,2,48,384]{3,2,1,0:T(8,128)(2,1)S(1)}, u32[]{:S(2)}, u32[]{:S(2)}) collective-permute-start(bf16[5,2,48,384]{3,2,1,0:T(8,128)(2,1)S(1)} %get-tuple-element.265), channel_id=1, source_target_pairs={{0,4},{4,0},{8,12},{12,8},{16,20},{20,16},{24,28},{28,24},{1,5},{5... | collective-permute-start | bytes 1105928 | tf_op jit(solution)/shard_map/ppermute | solution.py:1132
  172.5 12.7 %collective-permute-start.51 = (bf16[2,96,384]{2,1,0:T(8,128)(2,1)S(1)}, bf16[2,96,384]{2,1,0:T(8,128)(2,1)S(1)}, u32[]{:S(2)}, u32[]{:S(2)}) collective-permute-start(bf16[2,96,384]{2,1,0:T(8,128)(2,1)S(1)} %add_convert_fusion.2.refs_1_), channel_id=1, source_target_pairs={{0,24},{4,28},{8,16},{12,20},{16,8},{20,12},{24,0},{28,4},{1,25},{... | collective-permute-start | bytes 442376 | tf_op jit(solution)/shard_map/ppermute | solution.py:1132
  174.2 11.0 %collective-permute-start.50 = (bf16[2,96,384]{2,1,0:T(8,128)(2,1)S(1)}, bf16[2,96,384]{2,1,0:T(8,128)(2,1)S(1)}, u32[]{:S(2)}, u32[]{:S(2)}) collective-permute-start(bf16[2,96,384]{2,1,0:T(8,128)(2,1)S(1)} %add_convert_fusion.2.refs_1_), channel_id=1, source_target_pairs={{0,16},{4,20},{8,24},{12,28},{16,0},{20,4},{24,8},{28,12},{1,17},{... | collective-permute-start | bytes 442376 | tf_op jit(solution)/shard_map/ppermute | solution.py:1132
  174.2 11.0 %collective-permute-start.49 = (bf16[2,96,384]{2,1,0:T(8,128)(2,1)S(1)}, bf16[2,96,384]{2,1,0:T(8,128)(2,1)S(1)}, u32[]{:S(2)}, u32[]{:S(2)}) collective-permute-start(bf16[2,96,384]{2,1,0:T(8,128)(2,1)S(1)} %add_convert_fusion.2.refs_1_), channel_id=1, source_target_pairs={{0,8},{4,12},{8,0},{12,4},{16,24},{20,28},{24,16},{28,20},{1,9},{5... | collective-permute-start | bytes 442376 | tf_op jit(solution)/shard_map/ppermute | solution.py:1132
  (24 other events, 284.2 us)
